TPU v7x, 32 devices: a whole 2x2x4 slice. The times are simulated.
32 devices in a mesh: grp: 4 (over x, core), tile: 8 (over z, y).
Axes of the slice: x: 2, y: 2, z: 4, core: 2. Of those that a mesh axis runs over, the one named last changes fastest.
Arguments:
- raw: bfloat16 [16, 256, 3840], P('grp', 'tile'), may hold values from 0.25 to 4
- scales: bfloat16 [16, 64, 120], P('grp', 'tile'), may hold values from 0.29882812 to 1.1953125
- flat: float32 [256, 3840], P(None, 'tile'), may hold values from 0.25 to 1.75
- spectrum: float32 [8, 2, 256, 512], P('tile'), may hold values from -5 to 5
- pupil: float32 [2, 64, 128], replicated, may hold values from -5 to 5
- patterns: int32 [16, 4], replicated, may hold values from 0 to 31, all different within a row
- led_row: int32 [32], replicated, may hold values from 0 to 192
- led_col: int32 [32], replicated, may hold values from 0 to 384
Outputs:
- new_spectrum: float32 [8, 2, 256, 512], P('tile')
- stitched: float32 [2, 256, 3840], P(None, None, 'tile')
Inputs may be any that keep to these rules, and one draw needn't show every extreme that they name: `patterns`: each frame lights 4 different LEDs, and every LED is lit in some frame.
All inputs are finite; a program needn't handle non-finite values.
Results may differ from a plain program's by a relative error of at most 0.0003.
Values may be sent and summed in bfloat16 or wider, within the bound.
No kernel may reach another device: no remote copies, remote signals or barrier semaphores. Data moves between devices by JAX's collectives and lax.ppermute only.
A program may use at most 128 MiB of HBM per device.

v0:
```python
import math

import jax
import jax.numpy as jnp
from jax import lax
from jax.sharding import PartitionSpec as P

TH = 256
TW = 512
OV = 32
BR = 4
BC = 32
FR_G = 4
LEDS = 4


step_size = 0.02
highest = lax.Precision.HIGHEST


def padded(block, sides, width):
    for axis, dim in sides:
        count = lax.axis_size(axis)
        forward = [(i, i + 1) for i in range(count - 1)]
        backward = [(target, source) for source, target in forward]
        low = lax.ppermute(
            lax.slice_in_dim(block, block.shape[dim] - width, None, axis=dim), axis, forward
        )
        high = lax.ppermute(lax.slice_in_dim(block, 0, width, axis=dim), axis, backward)
        block = jnp.concatenate([low, block, high], axis=dim)
    return block


def wave_table(length, band):
    places = jnp.arange(length, dtype=jnp.int32)[:, None]
    freqs = jnp.arange(band, dtype=jnp.int32)[None, :] - band // 2
    turns = places * freqs % length
    angle = turns.astype(jnp.float32) * (2.0 * math.pi / length)
    factor = 1.0 / math.sqrt(band)
    return (jnp.cos(angle) * factor, jnp.sin(angle) * factor)


def complex_product(form, left_pair, right_pair):
    left_re, left_im = left_pair
    right_re, right_im = right_pair

    def einsum_pair(first, second):
        return jnp.einsum(form, first, second, precision=highest)

    return (
        einsum_pair(left_re, right_re) - einsum_pair(left_im, right_im),
        einsum_pair(left_re, right_im) + einsum_pair(left_im, right_re),
    )


def remove_tilt(flattened):
    rows_n = flattened.shape[1]
    cols_n = flattened.shape[2]
    ycentre = jnp.arange(rows_n, dtype=jnp.float32) - (rows_n - 1) / 2.0
    xcentre = jnp.arange(cols_n, dtype=jnp.float32) - (cols_n - 1) / 2.0
    slope_y = jnp.sum(flattened * ycentre[None, :, None], axis=(1, 2)) / (
        jnp.sum(ycentre * ycentre) * cols_n
    )
    slope_x = jnp.sum(flattened * xcentre[None, None, :], axis=(1, 2)) / (
        jnp.sum(xcentre * xcentre) * rows_n
    )
    return (
        flattened
        - slope_y[:, None, None] * ycentre[None, :, None]
        - slope_x[:, None, None] * xcentre[None, None, :]
    )


def box_gradients(spectrum_tile, window, pupil, row_starts, col_starts, lit_count):
    band_rows = pupil.shape[1]
    band_cols = pupil.shape[2]
    height = window.shape[1]
    width = window.shape[2]
    frames_n = window.shape[0]
    anchor = jnp.zeros((), jnp.int32)

    def cut_box(row_top, col_left):
        return lax.dynamic_slice(
            spectrum_tile, (anchor, row_top, col_left), (2, band_rows, band_cols)
        )

    boxes = jax.vmap(cut_box)(row_starts, col_starts)
    pupil_re = pupil[0]
    pupil_im = pupil[1]
    lit_re = pupil_re * boxes[:, 0] - pupil_im * boxes[:, 1]
    lit_im = pupil_re * boxes[:, 1] + pupil_im * boxes[:, 0]
    rows_re, rows_im = wave_table(height, band_rows)
    cols_re, cols_im = wave_table(width, band_cols)
    spread = complex_product("bup,xp->bux", (lit_re, lit_im), (cols_re, cols_im))
    field_re, field_im = complex_product("yu,bux->byx", (rows_re, rows_im), spread)
    field_re = field_re.reshape(frames_n, lit_count, height, width)
    field_im = field_im.reshape(frames_n, lit_count, height, width)
    estimate = jnp.sum(field_re * field_re + field_im * field_im, axis=1)
    misfit = estimate - window
    weighted_re = (misfit[:, None] * field_re).reshape(frames_n * lit_count, height, width)
    weighted_im = (misfit[:, None] * field_im).reshape(frames_n * lit_count, height, width)
    back = complex_product("yu,byx->bux", (rows_re, -rows_im), (weighted_re, weighted_im))
    tile_re, tile_im = complex_product("bux,xp->bup", back, (cols_re, -cols_im))
    grad_re = pupil_re * tile_re + pupil_im * tile_im
    grad_im = pupil_re * tile_im - pupil_im * tile_re
    return jnp.stack([grad_re, grad_im], axis=1)


def place_boxes(grads, row_starts, col_starts, height, width):
    anchor = jnp.zeros((), jnp.int32)

    def add_box(number, total):
        corner = (anchor, row_starts[number], col_starts[number])
        current = lax.dynamic_slice(total, corner, grads.shape[1:])
        return lax.dynamic_update_slice(total, current + grads[number], corner)

    return lax.fori_loop(0, grads.shape[0], add_box, jnp.zeros((2, height, width), jnp.float32))


def object_tile(spectrum_tile):
    height = spectrum_tile.shape[1]
    width = spectrum_tile.shape[2]
    rows_re, rows_im = wave_table(height, height)
    cols_re, cols_im = wave_table(width, width)
    partial_field = complex_product(
        "yu,uv->yv", (rows_re, rows_im), (spectrum_tile[0], spectrum_tile[1])
    )
    return jnp.stack(complex_product("yv,xv->yx", partial_field, (cols_re, cols_im)))


def blend_core(own, left_part, right_part, has_left, has_right, core):
    margin = left_part.shape[-1]
    correlation = 2 * margin
    positions = jnp.arange(margin, dtype=jnp.float32)
    left_own = (positions + margin + 0.5) / correlation
    left_other = (margin - positions - 0.5) / correlation
    right_own = (correlation - positions - 0.5) / correlation
    right_other = (positions + 0.5) / correlation
    middle = own[..., margin : margin + core]
    head = middle[..., :margin] * (left_own * has_left + (1.0 - has_left)) + left_part * (
        left_other * has_left
    )
    tail = middle[..., core - margin :] * (
        right_own * has_right + (1.0 - has_right)
    ) + right_part * (right_other * has_right)
    return jnp.concatenate([head, middle[..., margin : core - margin], tail], axis=-1)


def lookup_offsets(lit_ids, led_row, led_col):
    choose = (lit_ids[:, None] == jnp.arange(led_row.shape[0], dtype=jnp.int32)[None, :]).astype(
        jnp.int32
    )
    return (jnp.sum(choose * led_row[None, :], axis=1), jnp.sum(choose * led_col[None, :], axis=1))


def spread_factors(coarse):
    return jnp.repeat(jnp.repeat(coarse.astype(jnp.float32), BR, axis=1), BC, axis=2)


def body(raw, scales, flat, spectrum, pupil, patterns, led_row, led_col):
    core = TW - OV
    margin = OV // 2
    tile_count = lax.axis_size("tile")
    tile_number = lax.axis_index("tile")
    rows_here = raw.shape[1]
    frames_here = raw.shape[0]
    dequant = raw.astype(jnp.float32) * spread_factors(scales)
    value_blocks = dequant.reshape(frames_here, rows_here, tile_count, core)
    arrived = lax.all_to_all(
        value_blocks.astype(jnp.bfloat16), "tile", split_axis=2, concat_axis=1, tiled=True
    ).astype(value_blocks.dtype)
    values = arrived.reshape(frames_here, TH, arrived.shape[-1])
    measured = remove_tilt(values * flat[None])
    window = padded(measured.astype(jnp.bfloat16), (("tile", 2),), margin).astype(measured.dtype)
    group = lax.axis_index("grp")
    own_ids = lax.dynamic_slice_in_dim(patterns, group * FR_G, FR_G, 0).reshape(-1)
    row_starts, col_starts = lookup_offsets(own_ids, led_row, led_col)
    spectrum_tile = spectrum[0]
    grads = box_gradients(spectrum_tile, window, pupil, row_starts, col_starts, LEDS)
    local_total = place_boxes(grads, row_starts, col_starts, TH, TW)
    total = lax.psum(local_total, "grp")
    fresh = spectrum_tile - step_size * total
    image = object_tile(fresh)
    extended = padded(image, (("tile", 2),), margin)
    has_left = (tile_number > 0).astype(jnp.float32)
    has_right = (tile_number < tile_count - 1).astype(jnp.float32)
    stitched = blend_core(
        image, extended[..., :margin], extended[..., margin + TW :], has_left, has_right, core
    )
    return (fresh[None], stitched)


def solution(mesh):
    return jax.shard_map(
        body,
        mesh=mesh,
        in_specs=(
            P("grp", "tile", None),
            P("grp", "tile", None),
            P(None, "tile"),
            P("tile", None, None, None),
            P(),
            P(),
            P(),
            P(),
        ),
        out_specs=(P("tile", None, None, None), P(None, None, "tile")),
        check_vma=False,
    )
```

profile of v0, /device:TPU:24, one launch (start us, length us, event | category | flops | bytes accessed | tf_op | source)
XLA Modules:
  0.0 440.8 jit_solution(17291537043906018549)
XLA Ops:
  7.9 5.1 %broadcast_in_dim.10 = f32[4,32,120,32]{3,2,1,0:T(8,128)} broadcast(f32[4,32,120]{2,1,0:T(8,128)S(1)} %bitcast.181), dimensions={0,1,2} | broadcast | bytes 2027520 | tf_op jit(solution)/shard_map/broadcast_in_dim | solution.py:157
  13.0 4.8 %reshape.196 = f32[4,32,3840]{2,1,0:T(8,128)S(1)} reshape(f32[4,32,120,32]{3,2,1,0:T(8,128)} %broadcast_in_dim.10) | data formatting | bytes 3932160 | tf_op jit(solution)/shard_map/reshape | solution.py:157
  22.5 6.1 %all-to-all-start = ((bf16[4,32,8,480]{3,1,0,2:T(8,128)(2,1)}), bf16[4,32,8,480]{3,1,0,2:T(8,128)(2,1)S(1)}, u32[]{:S(2)}, u32[]{:S(2)}) async-start(bf16[4,32,8,480]{3,1,0,2:T(8,128)(2,1)} %copy.49), calls=%async_computation | async-start | bytes 2097152 | tf_op jit(solution)/shard_map/all_to_all | solution.py:169
  30.4 55.5 %while.15 = (s32[]{:T(128)}, f32[2,256,512]{2,1,0:T(8,128)}, s32[16,3]{0,1:T(4,128)S(1)}, f32[16,2,64,128]{3,2,0,1:T(8,128)}, s32[]{:T(128)}) while((s32[]{:T(128)}, f32[2,256,512]{2,1,0:T(8,128)}, s32[16,3]{0,1:T(4,128)S(1)}, f32[16,2,64,128]{3,2,0,1:T(8,128)}, s32[]{:T(128)}) %tuple.74), condition=%wide.while_cond, body=%wide.while_body.sunk | while | flops 2 | bytes 132213 | solution.py:83
  31.1 2.8 bitcast_dynamic-update-slice_fusion.2
  41.4 2.8 bitcast_dynamic-update-slice_fusion.2
  51.8 2.8 bitcast_dynamic-update-slice_fusion.2
  86.0 4.1 fusion.59
  90.0 4.1 fusion.53
  96.1 5.4 %convolution_subtract_fusion.1 = f32[16,64,512]{2,1,0:T(8,128)} fusion(f32[16,64,512]{2,1,0:T(8,128)S(1)} %fusion.59, s32[128]{0:T(128)S(1)} %iota_add_fusion.5, f32[16,2,64,128]{3,2,0,1:T(8,128)} %get-tuple-element.104, f32[64,128]{1,0:T(8,128)S(1)} %get-tuple-element.166, f32[64,128]{1,0:T(8,128)S(1)} %get-tuple-element.165), kind=kOutput, calls=%fused_computation.34 | convolution fusion | flops 807206912 | bytes 5308928 | tf_op jit(solution)/shard_map/bup,xp->bux/dot_general | solution.py:48
  102.9 4.9 %convolution_add_fusion.1 = f32[16,64,512]{2,1,0:T(8,128)S(1)} fusion(f32[16,64,512]{2,1,0:T(8,128)} %fusion.53, s32[128]{0:T(128)S(1)} %iota_add_fusion.5, f32[16,2,64,128]{3,2,0,1:T(8,128)} %get-tuple-element.104, f32[64,128]{1,0:T(8,128)S(1)} %get-tuple-element.166, f32[64,128]{1,0:T(8,128)S(1)} %get-tuple-element.165), kind=kOutput, calls=%fused_computation.33 | convolution fusion | flops 807206912 | bytes 5308928 | tf_op jit(solution)/shard_map/bup,xp->bux/dot_general | solution.py:48
  107.8 10.1 %fusion.104 = f32[16,512,256]{2,1,0:T(8,128)} fusion(f32[16,64,512]{2,1,0:T(8,128)S(1)} %copy-done.4, s32[64]{0:T(128)S(1)} %iota_add_fusion.4), kind=kOutput, calls=%fused_computation.140 | convolution fusion | flops 1610858496 | bytes 10486016 | tf_op jit(solution)/shard_map/yu,bux->byx/dot_general | solution.py:48
  117.9 9.5 %fusion.112 = f32[16,512,256]{2,1,0:T(8,128)} fusion(f32[16,64,512]{2,1,0:T(8,128)S(1)} %copy-done.4, s32[64]{0:T(128)S(1)} %iota_add_fusion.4), kind=kOutput, calls=%fused_computation.148 | convolution fusion | flops 1610858496 | bytes 10486016 | tf_op jit(solution)/shard_map/yu,bux->byx/dot_general | solution.py:48
  127.4 9.7 %fusion.106 = f32[16,512,256]{2,1,0:T(8,128)} fusion(f32[16,64,512]{2,1,0:T(8,128)S(1)} %convolution_add_fusion.1, s32[64]{0:T(128)S(1)} %iota_add_fusion.4), kind=kOutput, calls=%fused_computation.142 | convolution fusion | flops 1610858496 | bytes 10486016 | tf_op jit(solution)/shard_map/yu,bux->byx/dot_general | solution.py:48
  140.8 2.9 copy.51
  145.7 3.4 collective-permute-start
  149.1 3.4 collective-permute-start.1
  152.4 16.9 %bitcast_reduce_fusion = (f32[4,256,512]{1,2,0:T(8,128)}, f32[16,512,256]{2,1,0:T(8,128)}) fusion(f32[16,512,256]{2,1,0:T(8,128)} %fusion.104, f32[16,512,256]{2,1,0:T(8,128)} %fusion.112, f32[16,512,256]{2,1,0:T(8,128)} %fusion.106, f32[16,64,512]{2,1,0:T(8,128)S(1)} %convolution_add_fusion.1, s32[64]{0:T(128)S(1)} %iota_add_fusion.4), kind=kOutput, calls=%fused_computation.5 | convolution fusion | flops 1622917120 | bytes 37748992 | tf_op jit(solution)/shard_map/yu,bux->byx/dot_general | solution.py:48
  171.1 18.1 %bitcast_multiply_fusion = (f32[16,256,512]{1,2,0:T(8,128)}, f32[16,256,512]{1,2,0:T(8,128)}) fusion(f32[4,256,512]{1,2,0:T(8,128)S(1)} %convert_subtract_fusion, f32[16,512,256]{2,1,0:T(8,128)} %get-tuple-element.168, f32[16,512,256]{2,1,0:T(8,128)} %fusion.104, f32[16,512,256]{2,1,0:T(8,128)} %fusion.112, f32[16,512,256]{2,1,0:T(8,128)} %fusion.106), kind=kLoop, calls=%fused_computation.3 | loop fusion | flops 8388608 | bytes 52428800 | tf_op jit(solution)/shard_map/mul | solution.py:101
  189.2 11.6 %fusion.102 = f32[16,512,64]{1,2,0:T(8,128)S(1)} fusion(f32[16,256,512]{1,2,0:T(8,128)} %get-tuple-element.157, s32[64]{0:T(128)S(1)} %iota_add_fusion.4), kind=kOutput, calls=%fused_computation.138 | convolution fusion | flops 1610874880 | bytes 10486016 | tf_op jit(solution)/shard_map/yu,byx->bux/dot_general | solution.py:48
  200.9 8.5 %fusion.100 = f32[16,512,64]{1,2,0:T(8,128)S(1)} fusion(f32[16,256,512]{1,2,0:T(8,128)S(1)} %copy-done.2, s32[64]{0:T(128)S(1)} %iota_add_fusion.4), kind=kOutput, calls=%fused_computation.136 | convolution fusion | flops 1610874880 | bytes 10486016 | tf_op jit(solution)/shard_map/yu,byx->bux/dot_general | solution.py:48
  209.4 8.9 %convolution_add_fusion = f32[16,512,64]{1,2,0:T(8,128)S(1)} fusion(f32[16,512,64]{1,2,0:T(8,128)S(1)} %fusion.100, f32[16,256,512]{1,2,0:T(8,128)S(1)} %copy-done.3, s32[64]{0:T(128)S(1)} %iota_add_fusion.4), kind=kOutput, calls=%fused_computation.31 | convolution fusion | flops 1611382784 | bytes 12583168 | tf_op jit(solution)/shard_map/yu,byx->bux/dot_general | solution.py:48
  223.8 8.7 %convolution_subtract_fusion = f32[16,512,64]{1,2,0:T(8,128)S(1)} fusion(f32[16,512,64]{1,2,0:T(8,128)S(1)} %fusion.102, f32[16,256,512]{1,2,0:T(8,128)S(1)} %copy-done.2, s32[64]{0:T(128)S(1)} %iota_add_fusion.4), kind=kOutput, calls=%fused_computation.32 | convolution fusion | flops 1611382784 | bytes 12583168 | tf_op jit(solution)/shard_map/yu,byx->bux/dot_general | solution.py:48
  238.2 110.0 %while.14 = (s32[]{:T(128)}, f32[2,256,512]{2,1,0:T(8,128)S(1)}, s32[16]{0:T(128)S(1)}, s32[16]{0:T(128)S(1)}, f32[16,2,64,128]{3,2,0,1:T(8,128)S(1)}, /*index=5*/s32[]{:T(128)}, s32[]{:T(128)}, s32[]{:T(128)}, s32[]{:T(128)}) while((s32[]{:T(128)}, f32[2,256,512]{2,1,0:T(8,128)S(1)}, s32[16]{0:T(128)S(1)}, s32[16]{0:T(128)S(1)}, ...), condition=%wide.region_8.9_spmd, body=%wide.region_7.8_spmd.sunk | while | flops 16392 | bytes 327889 | solution.py:117
  349.2 35.2 %all-reduce.2.cloned.1.call-done = f32[2,256,512]{2,1,0:T(8,128)} async-done(((f32[2,256,512]{2,1,0:T(8,128)}), f32[2,256,512]{2,1,0:T(8,128)}) %all-reduce.2.cloned.1.call-update) | async-done | bytes 1048592 | tf_op jit(solution)/shard_map/psum | solution.py:181
  390.8 4.9 %fusion.25 = f32[256,512]{1,0:T(8,128)S(1)} fusion(f32[256,512]{1,0:T(8,128)S(1)} %convolution_subtract_fusion.3, s32[512]{0:T(512)S(1)} %iota_add_fusion), kind=kOutput, calls=%fused_computation.59 | convolution fusion | flops 809238528 | bytes 1050624 | tf_op jit(solution)/shard_map/yv,xv->yx/dot_general | solution.py:48
  395.8 5.3 %fusion.24 = f32[256,512]{1,0:T(8,128)S(1)} fusion(f32[256,512]{1,0:T(8,128)S(1)} %convolution_subtract_fusion.3, s32[512]{0:T(512)S(1)} %iota_add_fusion), kind=kOutput, calls=%fused_computation.58 | convolution fusion | flops 809238528 | bytes 1050624 | tf_op jit(solution)/shard_map/yv,xv->yx/dot_general | solution.py:48
  402.7 4.9 %fusion.9 = f32[1,256,512]{2,1,0:T(8,128)S(1)} fusion(f32[256,512]{1,0:T(8,128)S(1)} %fusion.25, f32[256,512]{1,0:T(8,128)S(1)} %convolution_add_fusion.3, s32[512]{0:T(512)S(1)} %iota_add_fusion), kind=kOutput, calls=%fused_computation.39 | convolution fusion | flops 809369600 | bytes 1574912 | tf_op jit(solution)/shard_map/yv,xv->yx/dot_general | solution.py:48
  407.6 5.1 %fusion.10 = f32[1,256,512]{2,1,0:T(8,128)S(1)} fusion(f32[256,512]{1,0:T(8,128)S(1)} %fusion.24, f32[256,512]{1,0:T(8,128)S(1)} %convolution_add_fusion.3, s32[512]{0:T(512)S(1)} %iota_add_fusion), kind=kOutput, calls=%fused_computation.41 | convolution fusion | flops 809369600 | bytes 1574912 | tf_op jit(solution)/shard_map/yv,xv->yx/dot_general | solution.py:48
  412.9 3.4 collective-permute-start.2
  416.3 6.9 %collective-permute-done.2 = f32[2,256,16]{2,1,0:T(8,128)S(1)} collective-permute-done((f32[2,256,16]{2,1,0:T(8,128)S(1)}, f32[2,256,16]{2,1,0:T(8,128)S(1)}, u32[]{:S(2)}, u32[]{:S(2)}) %collective-permute-start.2) | collective-permute-done | bytes 32800 | tf_op jit(solution)/shard_map/ppermute | solution.py:26
  426.2 5.7 %collective-permute-done.3 = f32[2,256,16]{2,1,0:T(8,128)S(1)} collective-permute-done((f32[2,256,16]{2,1,0:T(8,128)S(1)}, f32[2,256,16]{2,1,0:T(8,128)S(1)}, u32[]{:S(2)}, u32[]{:S(2)}) %collective-permute-start.3) | collective-permute-done | bytes 32800 | tf_op jit(solution)/shard_map/ppermute | solution.py:29
  (190 shorter events, 135.6 us)
Async XLA Ops:
  7.2 22.8 %copy-start = (s32[16,4]{0,1:T(4,128)S(1)}, s32[16,4]{0,1:T(4,128)}, u32[]{:S(2)}) copy-start(s32[16,4]{0,1:T(4,128)} %param.15) | copy-start | bytes 772
  21.0 9.2 %copy-start.9 = (f32[2,64,128]{2,1,0:T(8,128)S(1)}, f32[2,64,128]{2,1,0:T(8,128)}, u32[]{:S(2)}) copy-start(f32[2,64,128]{2,1,0:T(8,128)} %param.14) | copy-start | bytes 196612
  21.1 9.2 %copy-start.10 = (s32[32]{0:T(128)S(1)}, s32[32]{0:T(128)}, u32[]{:S(2)}) copy-start(s32[32]{0:T(128)} %param.17) | copy-start | bytes 388
  21.1 9.2 %copy-start.11 = (s32[32]{0:T(128)S(1)}, s32[32]{0:T(128)}, u32[]{:S(2)}) copy-start(s32[32]{0:T(128)} %param.16) | copy-start | bytes 388
  22.5 114.6 %all-to-all-start = ((bf16[4,32,8,480]{3,1,0,2:T(8,128)(2,1)}), bf16[4,32,8,480]{3,1,0,2:T(8,128)(2,1)S(1)}, u32[]{:S(2)}, u32[]{:S(2)}) async-start(bf16[4,32,8,480]{3,1,0,2:T(8,128)(2,1)} %copy.49), calls=%async_computation | async-start | bytes 2097152 | tf_op jit(solution)/shard_map/all_to_all | solution.py:169
  28.5 355.9 %all-reduce.2.cloned.1.call-start = ((), (), s32[]{:S(2)}) async-start(), calls=%async_computation.1 | async-start | bytes 2097152 | tf_op jit(solution)/shard_map/psum | solution.py:181
  86.0 4.1 copy-start.7
  102.9 4.9 %copy-start.4 = (f32[16,64,512]{2,1,0:T(8,128)S(1)}, f32[16,64,512]{2,1,0:T(8,128)}, u32[]{:S(2)}) copy-start(f32[16,64,512]{2,1,0:T(8,128)} %convolution_subtract_fusion.1) | copy-start | bytes 6291460
  145.7 23.6 %collective-permute-start = (bf16[4,256,16]{1,2,0:T(8,128)(2,1)S(1)}, bf16[4,256,16]{1,2,0:T(8,128)(2,1)S(1)}, u32[]{:S(2)}, u32[]{:S(2)}) collective-permute-start(bf16[4,256,16]{1,2,0:T(8,128)(2,1)S(1)} %get-tuple-element.163), channel_id=1, source_target_pairs={{0,1},{1,2},{2,3},{3,4},{4,5},{5,6},{6,7},{8,9},{9,10},{10,11},{11... | collective-permute-start | bytes 98312 | tf_op jit(solution)/shard_map/ppermute | solution.py:26
  149.1 20.2 %collective-permute-start.1 = (bf16[4,256,16]{1,2,0:T(8,128)(2,1)S(1)}, bf16[4,256,16]{1,2,0:T(8,128)(2,1)S(1)}, u32[]{:S(2)}, u32[]{:S(2)}) collective-permute-start(bf16[4,256,16]{1,2,0:T(8,128)(2,1)S(1)} %get-tuple-element.164), channel_id=1, source_target_pairs={{1,0},{2,1},{3,2},{4,3},{5,4},{6,5},{7,6},{9,8},{10,9},{11,10},{12... | collective-permute-start | bytes 98312 | tf_op jit(solution)/shard_map/ppermute | solution.py:29
  189.2 11.6 %copy-start.2 = (f32[16,256,512]{1,2,0:T(8,128)S(1)}, f32[16,256,512]{1,2,0:T(8,128)}, u32[]{:S(2)}) copy-start(f32[16,256,512]{1,2,0:T(8,128)} %get-tuple-element.158) | copy-start | bytes 25165828
  200.9 8.5 %copy-start.3 = (f32[16,256,512]{1,2,0:T(8,128)S(1)}, f32[16,256,512]{1,2,0:T(8,128)}, u32[]{:S(2)}) copy-start(f32[16,256,512]{1,2,0:T(8,128)} %get-tuple-element.157) | copy-start | bytes 25165828
  238.0 146.4 %copy-start.8 = (f32[2,256,512]{2,1,0:T(8,128)S(1)}, f32[2,256,512]{2,1,0:T(8,128)}, u32[]{:S(2)}) copy-start(f32[2,256,512]{2,1,0:T(8,128)} %get-tuple-element.283) | copy-start | bytes 3145732
  348.2 1.0 copy-start.5
  385.9 15.1 %copy-start.6 = (f32[2,256,512]{2,1,0:T(8,128)}, f32[2,256,512]{2,1,0:T(8,128)S(1)}, u32[]{:S(2)}) copy-start(f32[2,256,512]{2,1,0:T(8,128)S(1)} %multiply_subtract_fusion) | copy-start | bytes 3145732
  412.9 10.4 %collective-permute-start.2 = (f32[2,256,16]{2,1,0:T(8,128)S(1)}, f32[2,256,16]{2,1,0:T(8,128)S(1)}, u32[]{:S(2)}, u32[]{:S(2)}) collective-permute-start(f32[2,256,16]{2,1,0:T(8,128)S(1)} %fusion.50), channel_id=1, source_target_pairs={{0,1},{1,2},{2,3},{3,4},{4,5},{5,6},{6,7},{8,9},{9,10},{10,11},{11... | collective-permute-start | bytes 98312 | tf_op jit(solution)/shard_map/ppermute | solution.py:26
  423.4 8.6 %collective-permute-start.3 = (f32[2,256,16]{2,1,0:T(8,128)S(1)}, f32[2,256,16]{2,1,0:T(8,128)S(1)}, u32[]{:S(2)}, u32[]{:S(2)}) collective-permute-start(f32[2,256,16]{2,1,0:T(8,128)S(1)} %get-tuple-element.162), channel_id=1, source_target_pairs={{1,0},{2,1},{3,2},{4,3},{5,4},{6,5},{7,6},{9,8},{10,9},{11,10},{12... | collective-permute-start | bytes 98312 | tf_op jit(solution)/shard_map/ppermute | solution.py:29
  432.1 1.7 copy-start.1
Sparse Core Ops, SparseCore 0:
  349.3 35.1 all-reduce.1
where the time goes:
time: 447 us; the launch traced here: 441 us
  matrix products  140 us (31%)
  local copies, waits for them, and re-layouts  124 us (28%)
  loops' own time  63.2 us (14%)
  waiting for transfers between devices  48 us (11%)
  other arithmetic  31.4 us (7%)
  starting transfers between devices  18.7 us (4%)
  between operations  16.1 us (4%)
    dot_general x24, matrix products, einsum_pair(): return jnp.einsum(form, first, second, precision=highest)  140 us
    another operation x1, loops' own time, place_boxes(): lax.fori_loop(0, grads.shape[0], add_box, jnp.zeros((2, height, width), j...  62.9 us
    gather x48, local copies, waits for them, and re-layouts  55.2 us
    psum x1, waiting for transfers between devices, body(): total = lax.psum(local_total, 'grp')  35.2 us
    dynamic_update_slice x16, local copies, waits for them, and re-layouts, add_box(): return lax.dynamic_update_slice(total, current + grads[number], corner)  26.8 us
    dynamic_slice x32, local copies, waits for them, and re-layouts, add_box(): corner = (anchor, row_starts[number], col_starts[number])  18.8 us
    mul x1, other arithmetic, box_gradients(): misfit[:, None] * field_im  18.1 us
  transfers between devices with their start and end apart: 6, of which 3 were waited for; matrix products, arithmetic and copies ran while one was open for 28% of the time, Pallas kernels for 0%

commit v1 on v0

v1 whole, which is shorter than its diff:
```python
import functools
import math

import jax
import jax.numpy as jnp
import ml_dtypes
import numpy as np
from jax import lax
from jax.experimental import pallas as pl
from jax.experimental.pallas import tpu as pltpu
from jax.sharding import PartitionSpec as P

OV = 32
BC = 32
STEP = 0.02
F32 = jnp.float32
BF16 = jnp.bfloat16
VMEM = pltpu.VMEM
SMEM = pltpu.SMEM
MIB = 1 << 20


def two_parts(table):
    table = np.asarray(table, np.float64)
    high = table.astype(ml_dtypes.bfloat16)
    low = (table - high.astype(np.float64)).astype(ml_dtypes.bfloat16)
    return high, low


def wave(places, freqs, length, norm):
    turns = np.outer(places, freqs) % length
    angle = turns * (2.0 * math.pi / length)
    return np.cos(angle) / math.sqrt(norm), np.sin(angle) / math.sqrt(norm)


def low_pass(length, band):
    places = 2 * np.arange(length // 2)[:, None] - np.arange(length)[None, :]
    total = np.ones(places.shape)
    for freq in range(1, band):
        total += 2.0 * np.cos(2.0 * math.pi * ((freq * places) % length) / length)
    return total / length


def stacked_tables(height, width, band_rows, band_cols):
    row_re, row_im = wave(
        2 * np.arange(height // 2), np.arange(band_rows) - band_rows // 2, height, band_rows
    )
    rows = np.block([[row_re, -row_im], [row_im, row_re]])
    col_re, col_im = wave(
        np.arange(band_cols) - band_cols // 2, 2 * np.arange(width // 2), width, band_cols
    )
    cols = np.block([[col_re, col_im], [-col_im, col_re]])
    return rows, cols


def split(values):
    high = values.astype(BF16)
    return high, (values - high.astype(F32)).astype(BF16)


def mm(left, right):
    return jnp.dot(left, right, preferred_element_type=F32)


def vmem_spec(count):
    return [pl.BlockSpec(memory_space=VMEM)] * count


def dequant_kernel(raw_ref, scales_ref, out_ref, *, rows_here, core, margin):
    lines, strip = raw_ref.shape
    coarse_rows, coarse_cols = scales_ref.shape
    tiles, _, width = out_ref.shape
    ratio = lines // coarse_rows
    row = lax.broadcasted_iota(jnp.int32, (lines, coarse_rows), 0)
    pick = lax.broadcasted_iota(jnp.int32, (lines, coarse_rows), 1)
    spread_rows = (row // ratio == pick).astype(F32).astype(BF16)
    factors = mm(spread_rows, scales_ref[...]).astype(BF16)
    block = lax.broadcasted_iota(jnp.int32, (coarse_cols, width), 0)
    place = lax.broadcasted_iota(jnp.int32, (coarse_cols, width), 1)
    for tile in range(tiles):
        start = tile * core - margin
        column = place + start
        inside = (column >= block * BC) & (column < (block + 1) * BC)
        scale = mm(factors, inside.astype(F32).astype(BF16))
        base = max(start, 0) // 128 * 128
        span = min(width + 128, strip - base)
        codes = raw_ref[:, base : base + span].astype(F32)
        turn = (base - start) % span
        if turn:
            codes = pltpu.roll(codes, turn, 1)
        out_ref[tile] = (codes[:, :width] * scale).astype(BF16)


def dequantize(raw, scales, tiles, core, margin, width):
    frames, rows_here, strip = raw.shape
    return pl.pallas_call(
        functools.partial(dequant_kernel, rows_here=rows_here, core=core, margin=margin),
        out_shape=jax.ShapeDtypeStruct((tiles, frames * rows_here, width), BF16),
        in_specs=vmem_spec(2),
        out_specs=pl.BlockSpec(memory_space=VMEM),
        compiler_params=pltpu.CompilerParams(vmem_limit_bytes=40 * MIB),
        name="dequantize",
    )(raw.reshape(frames * rows_here, strip), scales.reshape(-1, scales.shape[-1]))


def box_area(top, left, band_rows, band_cols):
    row = top // 8 * 8
    col = left // 128 * 128
    area = (
        pl.ds(pl.multiple_of(row, 8), band_rows + 8),
        pl.ds(pl.multiple_of(col, 128), band_cols + 128),
    )
    return area, top - row, left - col


def field_kernel(
    led_row, led_col, patterns, spec_ref, pupil_ref, cols_hi, cols_lo, rows_hi, rows_lo,
    field_ref, estimate_ref, wide, bright,
):
    step = pl.program_id(0)
    group = field_ref.shape[0]
    band_rows, band_cols = pupil_ref.shape[1:]
    width = spec_ref.shape[2]
    half_h = field_ref.shape[1] // 2
    half_w = field_ref.shape[2]

    @pl.when(step == 0)
    def _():
        wide[...] = jnp.zeros_like(wide)
        wide[:, : spec_ref.shape[1], :width] = spec_ref[...]

    boxes = []
    for place in range(group):
        led = step * group + place
        top = led_row[led]
        left = led_col[led]
        area, down, right = box_area(top, left, band_rows, band_cols)
        parts = []
        for part in range(2):
            strip = pltpu.roll(wide[(part, *area)], lax.rem(2 * band_cols - right, 2 * band_cols), 1)
            strip = pltpu.roll(strip[:, :band_cols], lax.rem(band_rows + 8 - down, band_rows + 8), 0)
            parts.append(strip[:band_rows])
        lit_re = pupil_ref[0] * parts[0] - pupil_ref[1] * parts[1]
        lit_im = pupil_ref[0] * parts[1] + pupil_ref[1] * parts[0]
        boxes.append(jnp.concatenate([lit_re, lit_im], axis=1))
    high, low = split(jnp.concatenate(boxes, axis=0))
    spread = mm(high, cols_hi[...]) + mm(high, cols_lo[...]) + mm(low, cols_hi[...])
    left_rows = jnp.concatenate([rows_hi[...], rows_hi[...], rows_lo[...]], axis=1)
    for place in range(group):
        one = spread[place * band_rows : (place + 1) * band_rows]
        high, low = split(jnp.concatenate([one[:, :half_w], one[:, half_w:]], axis=0))
        field = mm(left_rows, jnp.concatenate([high, low, high], axis=0))
        field_ref[place] = field
        bright[step * group + place] = field[:half_h] ** 2 + field[half_h:] ** 2

    @pl.when(step == pl.num_programs(0) - 1)
    def _():
        def one_frame(frame, carry):
            total = bright[patterns[frame, 0]]
            for lit in range(1, patterns.shape[1]):
                total += bright[patterns[frame, lit]]
            estimate_ref[frame] = total
            return carry

        lax.fori_loop(0, patterns.shape[0], one_frame, 0)


def all_fields(spectrum, pupil, patterns, led_row, led_col, tables, group=4):
    rows, cols = tables
    leds = led_row.shape[0]
    _, height, width = spectrum.shape
    half_h, half_w = height // 2, width // 2
    whole = lambda shape: pl.BlockSpec(shape, lambda i: (0,) * len(shape))
    scalar = pl.BlockSpec(memory_space=SMEM)
    constants = [*two_parts(cols), *two_parts(rows)]
    return pl.pallas_call(
        field_kernel,
        grid=(leds // group,),
        out_shape=(
            jax.ShapeDtypeStruct((leds, 2 * half_h, half_w), F32),
            jax.ShapeDtypeStruct((patterns.shape[0], half_h, half_w), F32),
        ),
        in_specs=[scalar] * 3
        + [whole(spectrum.shape), whole(pupil.shape)]
        + [whole(c.shape) for c in constants],
        out_specs=(
            pl.BlockSpec((group, 2 * half_h, half_w), lambda i: (i, 0, 0)),
            whole((patterns.shape[0], half_h, half_w)),
        ),
        scratch_shapes=[
            pltpu.VMEM((2, height + 8, width + 128), F32),
            pltpu.VMEM((leds, half_h, half_w), F32),
        ],
        compiler_params=pltpu.CompilerParams(vmem_limit_bytes=40 * MIB),
        cost_estimate=pl.CostEstimate(
            flops=8_000_000_000, bytes_accessed=16_000_000, transcendentals=0
        ),
        name="fields",
    )(led_row, led_col, patterns, spectrum, pupil, *constants)


def window_kernel(
    dq_ref, flat_ref, part_a, part_b, odd, lc_hi, lc_lo, lr_hi, lr_lo, shapes_ref,
    window_ref, slopes_ref, *, margin, core,
):
    slabs, lines, width = dq_ref.shape
    frames, half_h, half_w = window_ref.shape
    rows_here = lines // frames
    height = slabs * rows_here
    is_odd = odd[0] == 1
    first, second = part_a[...], part_b[...]
    from_left = jnp.where(is_odd, first, second)
    from_right = jnp.where(is_odd, second, first)
    gains = jnp.concatenate([from_left, flat_ref[...], from_right], axis=1)
    yc = lax.broadcasted_iota(jnp.int32, (height, 1), 0).astype(F32) - (height - 1) / 2.0
    place = lax.broadcasted_iota(jnp.int32, (1, width), 1)
    in_core = ((place >= margin) & (place < margin + core)).astype(F32)
    xc = (place.astype(F32) - margin - (core - 1) / 2.0) * in_core
    over_y = 1.0 / (core * (height * (height * height - 1) / 12.0))
    over_x = 1.0 / (height * (core * (core * core - 1) / 12.0))
    values = [dq_ref[slab].astype(F32) for slab in range(slabs)]
    lane = lax.broadcasted_iota(jnp.int32, (1, 128), 1)
    flats = []
    for frame in range(frames):
        cut = slice(frame * rows_here, (frame + 1) * rows_here)
        flats.append(jnp.concatenate([v[cut] for v in values], axis=0) * gains)
    flattened = jnp.concatenate(flats, axis=0)
    high, low = split(flattened)
    narrow = mm(high, lc_hi[...]) + mm(high, lc_lo[...]) + mm(low, lc_hi[...])
    left_rows = jnp.concatenate([lr_hi[...], lr_hi[...], lr_lo[...]], axis=1)
    slopes_ref[...] = jnp.zeros_like(slopes_ref)
    for frame in range(frames):
        cut = slice(frame * height, (frame + 1) * height)
        slope_y = jnp.sum(jnp.sum(flats[frame] * yc, axis=0, keepdims=True) * in_core) * over_y
        slope_x = jnp.sum(jnp.sum(flats[frame], axis=0, keepdims=True) * xc) * over_x
        high, low = split(narrow[cut])
        window = mm(left_rows, jnp.concatenate([high, low, high], axis=0))
        window = window - shapes_ref[0] * slope_y - shapes_ref[1] * slope_x
        mean = jnp.sum(window) * (1.0 / (half_h * half_w))
        window_ref[frame] = (window - mean).astype(BF16)
        slopes_ref[frame : frame + 1] = jnp.where(
            lane == 0, slope_y, jnp.where(lane == 1, slope_x, jnp.where(lane == 2, mean, 0.0))
        )


def tilt_shapes(height, width, margin, core, lr, lc):
    rows_y = lr @ (np.arange(height) - (height - 1) / 2.0)
    local = np.arange(width) - margin
    shapes = []
    for begin, end, shift in ((0, core, 0), (-margin, 0, core), (core, core + margin, -core)):
        on = (local >= begin) & (local < end)
        xc = (local + shift - (core - 1) / 2.0) * on
        flat_line = on.astype(np.float64) @ lc
        xc_line = xc @ lc
        shapes.append(np.outer(rows_y, flat_line))
        shapes.append(np.outer(np.ones(len(rows_y)), xc_line))
    return np.stack(shapes).astype(np.float32)


def windows(arrived, flat, part_a, part_b, odd, frames, passes, shapes, margin, core):
    lr, lc = passes
    constants = [*two_parts(lc), *two_parts(lr)]
    half_h, half_w = lr.shape[0], lc.shape[1]
    return pl.pallas_call(
        functools.partial(window_kernel, margin=margin, core=core),
        out_shape=(
            jax.ShapeDtypeStruct((frames, half_h, half_w), BF16),
            jax.ShapeDtypeStruct((8, 128), F32),
        ),
        in_specs=vmem_spec(4) + [pl.BlockSpec(memory_space=SMEM)] + vmem_spec(5),
        out_specs=tuple(vmem_spec(2)),
        compiler_params=pltpu.CompilerParams(vmem_limit_bytes=40 * MIB),
        name="windows",
    )(arrived, flat, part_a, part_b, odd, *constants, shapes[:2])


def update_kernel(
    led_row, led_col, patterns, where, field_ref, estimate_ref, w0, w1, w2, w3,
    s0, s1, s2, s3, spec_ref, pupil_ref, shapes_ref, rt_hi, rt_lo, ct_hi, ct_lo,
    fr_hi, fr_lo, fc_hi, fc_lo,
    fresh_ref, high_ref, low_ref, first_ref, second_ref, misfit, weight, grads,
):
    step = pl.program_id(0)
    group = field_ref.shape[0]
    band_rows, band_cols = pupil_ref.shape[1:]
    height, width = spec_ref.shape[1:]
    half_h, half_w = misfit.shape[1:]
    frames_here = w0.shape[0]
    my_group = where[0]
    is_odd = where[1] == 1

    @pl.when(step == 0)
    def _():
        grads[...] = jnp.zeros_like(grads)
        weight[...] = jnp.zeros_like(weight)
        for slot, (window, slopes) in enumerate(((w0, s0), (w1, s1), (w2, s2), (w3, s3))):
            owner = jnp.bitwise_xor(my_group, slot)
            for place in range(frames_here):
                frame = owner * frames_here + place
                own = slopes[place : place + 1]
                first = slopes[8 + place : 9 + place]
                second = slopes[16 + place : 17 + place]
                left = jnp.where(is_odd, first, second)
                right = jnp.where(is_odd, second, first)
                value = estimate_ref[frame] - window[place].astype(F32) - own[:, 2:3]
                value += shapes_ref[0] * left[:, 0:1] + shapes_ref[1] * left[:, 1:2]
                value += shapes_ref[2] * right[:, 0:1] + shapes_ref[3] * right[:, 1:2]
                for lit in range(patterns.shape[1]):
                    weight[patterns[frame, lit]] += value

    left_rows = jnp.concatenate([rt_hi[...], rt_lo[...]], axis=0)
    backs = []
    for place in range(group):
        q = weight[step * group + place]
        field = field_ref[place]
        high, low = split(jnp.concatenate([field[:half_h] * q, field[half_h:] * q], axis=0))
        both = mm(left_rows, high)
        back = both[: 2 * band_rows] + both[2 * band_rows :] + mm(rt_hi[...], low)
        backs.append(jnp.concatenate([back[:band_rows], back[band_rows:]], axis=1))
    high, low = split(jnp.concatenate(backs, axis=0))
    boxes = mm(high, ct_hi[...]) + mm(high, ct_lo[...]) + mm(low, ct_hi[...])
    for place in range(group):
        led = step * group + place
        one = boxes[place * band_rows : (place + 1) * band_rows]
        back_re, back_im = one[:, :band_cols], one[:, band_cols:]
        parts = (
            pupil_ref[0] * back_re + pupil_ref[1] * back_im,
            pupil_ref[0] * back_im - pupil_ref[1] * back_re,
        )
        top = led_row[led]
        left = led_col[led]
        area, down, right = box_area(top, left, band_rows, band_cols)
        for part in range(2):
            filled = jnp.concatenate([parts[part], jnp.zeros((8, band_cols), F32)], axis=0)
            filled = pltpu.roll(filled, down, 0)
            filled = jnp.concatenate([filled, jnp.zeros((band_rows + 8, 128), F32)], axis=1)
            grads[(part, *area)] += pltpu.roll(filled, right, 1)

    @pl.when(step == pl.num_programs(0) - 1)
    def _():
        fresh_re = spec_ref[0] - (4.0 * STEP) * grads[0, :height, :width]
        fresh_im = spec_ref[1] - (4.0 * STEP) * grads[1, :height, :width]
        fresh_ref[0] = fresh_re
        fresh_ref[1] = fresh_im
        re_hi, re_lo = split(fresh_re)
        im_hi, im_lo = split(fresh_im)
        high = jnp.concatenate([re_hi, im_hi], axis=0)
        low = jnp.concatenate([re_lo, im_lo], axis=0)
        spread = mm(fr_hi[...], high) + mm(fr_lo[...], high) + mm(fr_hi[...], low)
        high, low = split(jnp.concatenate([spread[:height], spread[height:]], axis=1))
        high_ref[...] = high
        low_ref[...] = low
        contract = functools.partial(
            lax.dot_general,
            dimension_numbers=(((1,), (1,)), ((), ())),
            preferred_element_type=F32,
        )
        sides = (
            contract(fc_hi[...], high) + contract(fc_lo[...], high) + contract(fc_hi[...], low)
        )
        half = sides.shape[0] // 2
        to_left, to_right = sides[:half], sides[half:]
        first_ref[...] = jnp.where(is_odd, to_left, to_right)
        second_ref[...] = jnp.where(is_odd, to_right, to_left)


def update(
    field, estimate, window_parts, slope_parts, spectrum, pupil, patterns, led_row, led_col,
    where, tables, shapes, margin, group=4,
):
    rows, cols = tables
    leds = led_row.shape[0]
    _, height, width = spectrum.shape
    half_h, half_w = height // 2, width // 2
    fr_re, fr_im = wave(np.arange(height), np.arange(height) - height // 2, height, height)
    full_rows = np.block([[fr_re, -fr_im], [fr_im, fr_re]])
    side_places = np.concatenate([np.arange(margin), width - margin + np.arange(margin)])
    fc_re, fc_im = wave(side_places, np.arange(width) - width // 2, width, width)
    sides = np.concatenate(
        [
            np.concatenate([fc_re[:margin], -fc_im[:margin]], axis=1),
            np.concatenate([fc_im[:margin], fc_re[:margin]], axis=1),
            np.concatenate([fc_re[margin:], -fc_im[margin:]], axis=1),
            np.concatenate([fc_im[margin:], fc_re[margin:]], axis=1),
        ]
    )
    constants = [
        shapes[2:],
        *two_parts(rows.T),
        *two_parts(cols.T),
        *two_parts(full_rows),
        *two_parts(sides),
    ]
    whole = lambda shape: pl.BlockSpec(shape, lambda i: (0,) * len(shape))
    scalar = pl.BlockSpec(memory_space=SMEM)
    operands = [estimate, *window_parts, *slope_parts, spectrum, pupil, *constants]
    out_shape = (
        jax.ShapeDtypeStruct(spectrum.shape, F32),
        jax.ShapeDtypeStruct((height, 2 * width), BF16),
        jax.ShapeDtypeStruct((height, 2 * width), BF16),
        jax.ShapeDtypeStruct((2 * margin, height), F32),
        jax.ShapeDtypeStruct((2 * margin, height), F32),
    )
    return pl.pallas_call(
        update_kernel,
        grid=(leds // group,),
        out_shape=out_shape,
        in_specs=[scalar] * 4
        + [pl.BlockSpec((group, 2 * half_h, half_w), lambda i: (i, 0, 0))]
        + [whole(o.shape) for o in operands],
        out_specs=tuple(whole(o.shape) for o in out_shape),
        scratch_shapes=[
            pltpu.VMEM((8, half_h, half_w), F32),
            pltpu.VMEM((leds, half_h, half_w), F32),
            pltpu.VMEM((2, height + 8, width + 128), F32),
        ],
        compiler_params=pltpu.CompilerParams(vmem_limit_bytes=48 * MIB),
        name="update",
    )(led_row, led_col, patterns, where, field, *operands)


def object_kernel(high_ref, low_ref, re_hi, re_lo, im_hi, im_lo, out_ref):
    width = re_hi.shape[0]
    core = out_ref.shape[2]
    zre_hi, zim_hi = high_ref[:, :width], high_ref[:, width:]
    zre_lo, zim_lo = low_ref[:, :width], low_ref[:, width:]
    z_re = jnp.concatenate([zre_hi, zre_hi, zre_lo], axis=1)
    z_im = jnp.concatenate([zim_hi, zim_hi, zim_lo], axis=1)
    c_re = jnp.concatenate([re_hi[...], re_lo[...], re_hi[...]], axis=0)
    c_im = jnp.concatenate([im_hi[...], im_lo[...], im_hi[...]], axis=0)
    out_ref[0] = (mm(z_re, c_re) - mm(z_im, c_im))[:, :core]
    out_ref[1] = (mm(z_re, c_im) + mm(z_im, c_re))[:, :core]


def object_core(high, low, margin, core):
    height, width = high.shape[0], high.shape[1] // 2
    places = (margin + np.arange(width)) % width
    col_re, col_im = wave(np.arange(width) - width // 2, places, width, width)
    constants = [*two_parts(col_re), *two_parts(col_im)]
    return pl.pallas_call(
        object_kernel,
        out_shape=jax.ShapeDtypeStruct((2, height, core), F32),
        in_specs=vmem_spec(6),
        out_specs=pl.BlockSpec(memory_space=VMEM),
        compiler_params=pltpu.CompilerParams(vmem_limit_bytes=40 * MIB),
        cost_estimate=pl.CostEstimate(
            flops=3_000_000_000, bytes_accessed=5_000_000, transcendentals=0
        ),
        name="object",
    )(high, low, *constants)


def blend_kernel(where, first_ref, second_ref, in_ref, out_ref, *, margin, last):
    side = pl.program_id(0)
    tile = where[2]
    is_odd = where[1] == 1
    height = out_ref.shape[1]
    lanes = out_ref.shape[2]
    lane = lax.broadcasted_iota(jnp.int32, (1, lanes), 1).astype(F32)
    span = 2.0 * margin

    def other_of(incoming):
        wide = jnp.concatenate([incoming, jnp.zeros((lanes - margin, height), F32)], axis=0)
        return jnp.transpose(wide, (1, 0))

    @pl.when(side == 0)
    def _():
        on = (lane < margin) & (tile > 0)
        own_w = jnp.where(on, (lane + margin + 0.5) / span, 1.0)
        other_w = jnp.where(on, (margin - lane - 0.5) / span, 0.0)
        incoming = jnp.where(is_odd, first_ref[...], second_ref[...])
        for part in range(2):
            other = other_of(incoming[part * margin : (part + 1) * margin])
            out_ref[part] = in_ref[part] * own_w + other * other_w

    @pl.when(side == 1)
    def _():
        q = lane - last
        on = (q >= 0.0) & (q < margin) & (tile < where[3] - 1)
        own_w = jnp.where(on, (span - q - 0.5) / span, 1.0)
        other_w = jnp.where(on, (q + 0.5) / span, 0.0)
        incoming = jnp.where(is_odd, second_ref[...], first_ref[...])
        for part in range(2):
            other = other_of(incoming[part * margin : (part + 1) * margin])
            out_ref[part] = in_ref[part] * own_w + pltpu.roll(other, last, 1) * other_w


def blend(core_part, first, second, where, margin):
    _, height, core = core_part.shape
    lanes = 128
    steps = pl.cdiv(core, lanes) - 1
    last = core - margin - steps * lanes
    block = pl.BlockSpec((2, height, lanes), lambda i: (0, 0, i * steps))
    whole = pl.BlockSpec(first.shape, lambda i: (0, 0))
    return pl.pallas_call(
        functools.partial(blend_kernel, margin=margin, last=last),
        grid=(2,),
        out_shape=jax.ShapeDtypeStruct(core_part.shape, F32),
        in_specs=[pl.BlockSpec(memory_space=SMEM), whole, whole, block],
        out_specs=block,
        input_output_aliases={3: 0},
        name="blend",
    )(where, first, second, core_part)


def body(raw, scales, flat, spectrum, pupil, patterns, led_row, led_col):
    height, core = flat.shape
    margin = OV // 2
    width = core + OV
    tiles = lax.axis_size("tile")
    tile = lax.axis_index("tile")
    grp = lax.axis_index("grp")
    frames_here = raw.shape[0]
    band_rows, band_cols = pupil.shape[1:]
    spectrum_tile = spectrum[0]
    odd = lax.rem(tile, 2)
    where = jnp.stack([grp, odd, tile, jnp.int32(tiles)]).astype(jnp.int32)

    swap_a = [(i, i ^ 1) for i in range(tiles)]
    swap_b = [(i, ((i + 1) ^ 1) - 1) for i in range(1, tiles - 1)]

    def neighbours(for_a, for_b):
        return lax.ppermute(for_a, "tile", swap_a), lax.ppermute(for_b, "tile", swap_b)

    tables = stacked_tables(height, width, band_rows, band_cols)
    passes = (low_pass(height, band_rows), low_pass(width, band_cols).T)
    shapes = tilt_shapes(height, width, margin, core, *passes)

    codes = dequantize(raw, scales, tiles, core, margin, width)
    arrived = lax.all_to_all(codes, "tile", split_axis=0, concat_axis=0, tiled=True)
    flat_left, flat_right = flat[:, :margin], flat[:, core - margin :]
    is_odd = odd == 1
    flat_a, flat_b = neighbours(
        jnp.where(is_odd, flat_left, flat_right), jnp.where(is_odd, flat_right, flat_left)
    )
    field, estimate = all_fields(spectrum_tile, pupil, patterns, led_row, led_col, tables)
    window, slopes = windows(
        arrived, flat, flat_a, flat_b, where[1:2], frames_here, passes, shapes, margin, core
    )

    swap_core = [(i, i ^ 1) for i in range(4)]
    swap_chip = [(i, i ^ 2) for i in range(4)]
    other = functools.partial(lax.ppermute, axis_name="grp")
    window_2 = other(window, perm=swap_chip)
    window_1 = other(window, perm=swap_core)
    window_3 = other(window_2, perm=swap_core)
    slopes_a, slopes_b = neighbours(slopes, slopes)
    slopes_0 = jnp.concatenate([slopes, slopes_a, slopes_b], axis=0)
    slopes_2 = other(slopes_0, perm=swap_chip)
    slopes_1 = other(slopes_0, perm=swap_core)
    slopes_3 = other(slopes_2, perm=swap_core)

    fresh, high, low, for_a, for_b = update(
        field, estimate, (window, window_1, window_2, window_3),
        (slopes_0, slopes_1, slopes_2, slopes_3), spectrum_tile, pupil, patterns,
        led_row, led_col, where, tables, shapes, margin,
    )
    side_a, side_b = neighbours(for_a, for_b)
    core_part = object_core(high, low, margin, core)
    stitched = blend(core_part, side_a, side_b, where, margin)
    return fresh[None], stitched


def solution(mesh):
    return jax.shard_map(
        body,
        mesh=mesh,
        in_specs=(
            P("grp", "tile", None),
            P("grp", "tile", None),
            P(None, "tile"),
            P("tile", None, None, None),
            P(),
            P(),
            P(),
            P(),
        ),
        out_specs=(P("tile", None, None, None), P(None, None, "tile")),
        check_vma=False,
    )
```

time: 447 us -> 110 us (0.25)
  the two profiles are of different devices: /device:TPU:24 before, /device:TPU:12 now
where the time goes in v1:
time: 110 us; the launch traced here: 109 us
  Pallas kernels  33.5 us (30%)
  local copies, waits for them, and re-layouts  27.6 us (25%)
  waiting for transfers between devices  25.3 us (23%)
  starting transfers between devices  21.5 us (20%)
    unnamed x77, local copies, waits for them, and re-layouts  27 us
    ppermute x3, waiting for transfers between devices, neighbours(): lax.ppermute(for_b, 'tile', swap_b)  23.9 us
    pallas_call x1, Pallas kernels, update(): pl.pallas_call(update_kernel, grid=(leds // group,), out_shape=out_shape,...  16.5 us
    ppermute x3, starting transfers between devices, neighbours(): lax.ppermute(for_b, 'tile', swap_b)  9.99 us
    pallas_call x1, Pallas kernels, all_fields(): pl.pallas_call(field_kernel, grid=(leds // group,), out_shape=(jax.ShapeD...  9.14 us
    all_to_all x1, starting transfers between devices, body(): lax.all_to_all(codes, 'tile', split_axis=0, concat_axis=0, tiled=True)  6.22 us
    ppermute x3, starting transfers between devices, neighbours(): lax.ppermute(for_a, 'tile', swap_a)  2.64 us
  transfers between devices with their start and end apart: 13, of which 5 were waited for; matrix products, arithmetic and copies ran while one was open for 4% of the time, Pallas kernels for 10%

profile of v1, /device:TPU:12, one launch (start us, length us, event | category | flops | bytes accessed | tf_op | source)
XLA Modules:
  0.0 109.0 jit_solution(1629115180080192733)
XLA Ops:
  0.7 1.3 %copy-done.4 = bf16[4,32,3840]{2,1,0:T(8,128)(2,1)S(1)} copy-done((bf16[4,32,3840]{2,1,0:T(8,128)(2,1)S(1)}, bf16[4,32,3840]{2,1,0:T(8,128)(2,1)}, u32[]{:S(2)}) %copy-start.4) | copy-done | bytes 983064
  2.6 1.9 %dequantize.1 = bf16[8,128,512]{2,1,0:T(8,128)(2,1)} custom-call(bf16[128,3840]{1,0:T(8,128)(2,1)S(1)} %bitcast.9, bf16[32,120]{1,0:T(8,128)(2,1)S(1)} %bitcast.10), custom_call_target="tpu_custom_call" | custom-call | tf_op jit(solution)/shard_map/dequantize/pallas_call | solution.py:96
  4.5 6.2 %all-to-all-start = ((bf16[8,128,512]{2,1,0:T(8,128)(2,1)}), bf16[8,128,512]{2,1,0:T(8,128)(2,1)S(1)}, u32[]{:S(2)}, u32[]{:S(2)}) async-start(bf16[8,128,512]{2,1,0:T(8,128)(2,1)} %dequantize.1), calls=%async_computation | async-start | bytes 2097152 | tf_op jit(solution)/shard_map/all_to_all | solution.py:530
  10.7 1.2 %copy.36.flat_ref = f32[256,480]{1,0:T(8,128)S(1)} copy(f32[256,480]{0,1:T(8,128)} %param.32) | data formatting | bytes 983040 | tf_op args[2]
  12.1 3.4 %collective-permute-start.1 = (f32[256,16]{1,0:T(8,128)S(1)}, f32[256,16]{1,0:T(8,128)S(1)}, u32[]{:S(2)}, u32[]{:S(2)}) collective-permute-start(f32[256,16]{1,0:T(8,128)S(1)} %get-tuple-element.22), channel_id=1, source_target_pairs={{1,2},{2,1},{3,4},{4,3},{5,6},{6,5},{9,10},{10,9},{11,12},{12,11},... | collective-permute-start | bytes 49160 | tf_op jit(solution)/shard_map/ppermute | solution.py:523
  16.8 21.0 %collective-permute-done.1.part_b = f32[256,16]{1,0:T(8,128)S(1)} collective-permute-done((f32[256,16]{1,0:T(8,128)S(1)}, f32[256,16]{1,0:T(8,128)S(1)}, u32[]{:S(2)}, u32[]{:S(2)}) %collective-permute-start.1) | collective-permute-done | bytes 16416 | tf_op jit(solution)/shard_map/ppermute | solution.py:523
  37.8 0.9 copy-done.10
  38.8 0.9 copy-done.11
  39.7 0.9 copy-done.12
  40.7 0.8 copy-done.19
  41.5 0.8 copy-done.20
  42.4 2.1 %windows.1 = (bf16[4,128,256]{2,1,0:T(8,128)(2,1)S(1)}, f32[8,128]{1,0:T(8,128)S(1)}) custom-call(bf16[8,128,512]{2,1,0:T(8,128)(2,1)S(1)} %all-to-all-done.dq_ref, f32[256,480]{1,0:T(8,128)S(1)} %copy.36.flat_ref, f32[256,16]{1,0:T(8,128)S(1)} %collective-permute-done.part_a, f32[256,16]{1,0:T(8,128)S(1)} %collective-permute-done.1.part_b, s32[1]{0:T(128)} %bitcast.1.odd, ...), custom_call_target="tpu_custom_call" | custom-call | tf_op jit(solution)/shard_map/windows/pallas_call | solution.py:264
  44.6 1.6 %collective-permute-start.3 = (bf16[4,128,256]{2,1,0:T(8,128)(2,1)S(1)}, bf16[4,128,256]{2,1,0:T(8,128)(2,1)}, u32[]{:S(2)}, u32[]{:S(2)}) collective-permute-start(bf16[4,128,256]{2,1,0:T(8,128)(2,1)S(1)} %get-tuple-element.13.w0), channel_id=1, source_target_pairs={{0,16},{8,24},{16,0},{24,8},{1,17},{9,25},{17,1},{25,9},{2,18},{10... | collective-permute-start | bytes 786440 | tf_op jit(solution)/shard_map/ppermute | solution.py:544
  46.7 3.3 %collective-permute-start.6 = (f32[8,128]{1,0:T(8,128)S(1)}, f32[8,128]{1,0:T(8,128)S(1)}, u32[]{:S(2)}, u32[]{:S(2)}) collective-permute-start(f32[8,128]{1,0:T(8,128)S(1)} %get-tuple-element.14), channel_id=1, source_target_pairs={{1,2},{2,1},{3,4},{4,3},{5,6},{6,5},{9,10},{10,9},{11,12},{12,11},... | collective-permute-start | bytes 12296 | tf_op jit(solution)/shard_map/ppermute | solution.py:523
  50.7 2.4 %collective-permute-done.6 = f32[8,128]{1,0:T(8,128)S(1)} collective-permute-done((f32[8,128]{1,0:T(8,128)S(1)}, f32[8,128]{1,0:T(8,128)S(1)}, u32[]{:S(2)}, u32[]{:S(2)}) %collective-permute-start.6) | collective-permute-done | bytes 4128 | tf_op jit(solution)/shard_map/ppermute | solution.py:523
  55.1 0.9 copy-done.30
  56.0 0.9 copy-done.31
  57.0 0.8 copy-done.32
  57.8 0.8 copy-done.33
  58.7 9.1 %fields.1 = (f32[32,256,256]{2,1,0:T(8,128)S(1)}, f32[16,128,256]{2,1,0:T(8,128)S(1)}) custom-call(s32[32]{0:T(128)S(1)} %copy-done.23, s32[32]{0:T(128)S(1)} %copy-done.24, s32[16,4]{1,0:T(8,128)S(1)} %copy.37.patterns, f32[2,256,512]{2,1,0:T(8,128)S(1)} %bitcast.7, f32[2,64,128]{2,1,0:T(8,128)S(1)} %copy-done.15, bf16[256,512]{1,0:T(8,128)(2,1)S(1)} %copy-done.31, ...), custom_call_target="tpu_custom_call" | custom-call | flops 8000000000 | bytes 16000000 | tf_op jit(solution)/shard_map/fields/pallas_call | solution.py:176
  67.9 3.3 %copy-done = f32[32,256,256]{2,1,0:T(8,128)} copy-done((f32[32,256,256]{2,1,0:T(8,128)}, f32[32,256,256]{2,1,0:T(8,128)S(1)}, u32[]{:S(2)}) %copy-start) | copy-done | bytes 8388632
  71.2 1.3 %copy-done.2 = f32[16,128,256]{2,1,0:T(8,128)} copy-done((f32[16,128,256]{2,1,0:T(8,128)}, f32[16,128,256]{2,1,0:T(8,128)S(1)}, u32[]{:S(2)}) %copy-start.2) | copy-done | bytes 2097176
  73.1 1.0 collective-permute-done.7.s1
  74.5 0.9 copy-done.14
  75.4 0.8 copy-done.16
  78.5 16.5 %update.1 = (f32[2,256,512]{2,1,0:T(8,128)}, bf16[256,1024]{1,0:T(8,128)(2,1)S(1)}, bf16[256,1024]{1,0:T(8,128)(2,1)S(1)}, f32[32,256]{1,0:T(8,128)S(1)}, f32[32,256]{1,0:T(8,128)S(1)}) custom-call(s32[32]{0:T(128)S(1)} %copy-done.23, s32[32]{0:T(128)S(1)} %copy-done.25, s32[16,4]{1,0:T(8,128)S(1)} %copy.37.patterns, s32[4]{0:T(128)S(1)} %pad_add_fusion.where, ...), custom_call_target="tpu_custom_call" | custom-call | tf_op jit(solution)/shard_map/update/pallas_call | solution.py:404
  95.0 1.9 %collective-permute-start.10 = (f32[32,256]{1,0:T(8,128)S(1)}, f32[32,256]{1,0:T(8,128)S(1)}, u32[]{:S(2)}, u32[]{:S(2)}) collective-permute-start(f32[32,256]{1,0:T(8,128)S(1)} %get-tuple-element.16), channel_id=1, source_target_pairs={{0,1},{1,0},{2,3},{3,2},{4,5},{5,4},{6,7},{7,6},{8,9},{9,8},{10,11... | collective-permute-start | bytes 98312 | tf_op jit(solution)/shard_map/ppermute | solution.py:523
  97.0 3.3 %collective-permute-start.11 = (f32[32,256]{1,0:T(8,128)S(1)}, f32[32,256]{1,0:T(8,128)S(1)}, u32[]{:S(2)}, u32[]{:S(2)}) collective-permute-start(f32[32,256]{1,0:T(8,128)S(1)} %get-tuple-element.17), channel_id=1, source_target_pairs={{1,2},{2,1},{3,4},{4,3},{5,6},{6,5},{9,10},{10,9},{11,12},{12,11},... | collective-permute-start | bytes 98312 | tf_op jit(solution)/shard_map/ppermute | solution.py:523
  100.4 1.8 %object.1.in_ref = f32[2,256,480]{2,1,0:T(8,128)S(1)} custom-call(bf16[256,1024]{1,0:T(8,128)(2,1)S(1)} %get-tuple-element.18.high_ref, bf16[256,1024]{1,0:T(8,128)(2,1)S(1)} %get-tuple-element.19.low_ref, bf16[512,512]{1,0:T(8,128)(2,1)S(1)} %copy-done.29, bf16[512,512]{1,0:T(8,128)(2,1)S(1)} %copy-done.28, bf16[512,512]{1,0:T(8,128)(2,1)S(1)} %copy-done.27, ...), custom_call_target="tpu_custom_call" | custom-call | flops 3000000000 | bytes 5000000 | tf_op jit(solution)/shard_map/object/pallas_call | solution.py:440
  102.2 1.0 copy-done.1
  104.4 2.1 %blend.1 = f32[2,256,480]{2,1,0:T(8,128)} custom-call(s32[4]{0:T(128)} %copy-done.22, f32[32,256]{1,0:T(8,128)} %copy-done.34, f32[32,256]{1,0:T(8,128)} %copy-done.35, f32[2,256,480]{2,1,0:T(8,128)} %copy-done.1), custom_call_target="tpu_custom_call", output_to_operand_aliasing={{}: (3, {})} | custom-call | tf_op jit(solution)/shard_map/blend/pallas_call | solution.py:495
  106.5 2.5 %copy.38 = f32[2,256,480]{1,2,0:T(8,128)} copy(f32[2,256,480]{2,1,0:T(8,128)} %blend.1) | data formatting | bytes 1966080
  (80 shorter events, 10.1 us)
Async XLA Ops:
  0.6 53.6 %copy-start.3 = (f32[1,2,256,512]{3,2,1,0:T(8,128)S(1)}, f32[1,2,256,512]{3,2,1,0:T(8,128)}, u32[]{:S(2)}) copy-start(f32[1,2,256,512]{3,2,1,0:T(8,128)} %param.33) | copy-start | bytes 3145732
  0.6 1.3 %copy-start.4 = (bf16[4,32,3840]{2,1,0:T(8,128)(2,1)S(1)}, bf16[4,32,3840]{2,1,0:T(8,128)(2,1)}, u32[]{:S(2)}) copy-start(bf16[4,32,3840]{2,1,0:T(8,128)(2,1)} %param.30) | copy-start | bytes 2949124
  2.6 51.6 %copy-start.23 = (s32[32]{0:T(128)S(1)}, s32[32]{0:T(128)}, u32[]{:S(2)}) copy-start(s32[32]{0:T(128)} %led_row.3) | copy-start | bytes 388
  2.6 51.6 %copy-start.24 = (s32[32]{0:T(128)S(1)}, s32[32]{0:T(128)}, u32[]{:S(2)}) copy-start(s32[32]{0:T(128)} %led_col.3) | copy-start | bytes 388
  4.5 33.3 %all-to-all-start = ((bf16[8,128,512]{2,1,0:T(8,128)(2,1)}), bf16[8,128,512]{2,1,0:T(8,128)(2,1)S(1)}, u32[]{:S(2)}, u32[]{:S(2)}) async-start(bf16[8,128,512]{2,1,0:T(8,128)(2,1)} %dequantize.1), calls=%async_computation | async-start | bytes 2097152 | tf_op jit(solution)/shard_map/all_to_all | solution.py:530
  12.1 25.8 %collective-permute-start.1 = (f32[256,16]{1,0:T(8,128)S(1)}, f32[256,16]{1,0:T(8,128)S(1)}, u32[]{:S(2)}, u32[]{:S(2)}) collective-permute-start(f32[256,16]{1,0:T(8,128)S(1)} %get-tuple-element.22), channel_id=1, source_target_pairs={{1,2},{2,1},{3,4},{4,3},{5,6},{6,5},{9,10},{10,9},{11,12},{12,11},... | collective-permute-start | bytes 49160 | tf_op jit(solution)/shard_map/ppermute | solution.py:523
  15.4 22.4 %collective-permute-start = (f32[256,16]{1,0:T(8,128)S(1)}, f32[256,16]{1,0:T(8,128)S(1)}, u32[]{:S(2)}, u32[]{:S(2)}) collective-permute-start(f32[256,16]{1,0:T(8,128)S(1)} %get-tuple-element.23), channel_id=1, source_target_pairs={{0,1},{1,0},{2,3},{3,2},{4,5},{5,4},{6,7},{7,6},{8,9},{9,8},{10,11... | collective-permute-start | bytes 49160 | tf_op jit(solution)/shard_map/ppermute | solution.py:523
  37.8 1.0 copy-start.10
  44.5 5.6 %collective-permute-start.5 = (f32[8,128]{1,0:T(8,128)S(1)}, f32[8,128]{1,0:T(8,128)S(1)}, u32[]{:S(2)}, u32[]{:S(2)}) collective-permute-start(f32[8,128]{1,0:T(8,128)S(1)} %get-tuple-element.14), channel_id=1, source_target_pairs={{0,1},{1,0},{2,3},{3,2},{4,5},{5,4},{6,7},{7,6},{8,9},{9,8},{10,11... | collective-permute-start | bytes 12296 | tf_op jit(solution)/shard_map/ppermute | solution.py:523
  44.6 9.7 %collective-permute-start.3 = (bf16[4,128,256]{2,1,0:T(8,128)(2,1)S(1)}, bf16[4,128,256]{2,1,0:T(8,128)(2,1)}, u32[]{:S(2)}, u32[]{:S(2)}) collective-permute-start(bf16[4,128,256]{2,1,0:T(8,128)(2,1)S(1)} %get-tuple-element.13.w0), channel_id=1, source_target_pairs={{0,16},{8,24},{16,0},{24,8},{1,17},{9,25},{17,1},{25,9},{2,18},{10... | collective-permute-start | bytes 786440 | tf_op jit(solution)/shard_map/ppermute | solution.py:544
  46.7 6.4 %collective-permute-start.6 = (f32[8,128]{1,0:T(8,128)S(1)}, f32[8,128]{1,0:T(8,128)S(1)}, u32[]{:S(2)}, u32[]{:S(2)}) collective-permute-start(f32[8,128]{1,0:T(8,128)S(1)} %get-tuple-element.14), channel_id=1, source_target_pairs={{1,2},{2,1},{3,4},{4,3},{5,6},{6,5},{9,10},{10,9},{11,12},{12,11},... | collective-permute-start | bytes 12296 | tf_op jit(solution)/shard_map/ppermute | solution.py:523
  50.0 24.4 %collective-permute-start.2 = (bf16[4,128,256]{2,1,0:T(8,128)(2,1)S(1)}, bf16[4,128,256]{2,1,0:T(8,128)(2,1)}, u32[]{:S(2)}, u32[]{:S(2)}) collective-permute-start(bf16[4,128,256]{2,1,0:T(8,128)(2,1)S(1)} %get-tuple-element.13.w0), channel_id=1, source_target_pairs={{0,8},{8,0},{16,24},{24,16},{1,9},{9,1},{17,25},{25,17},{2,10},{10... | collective-permute-start | bytes 786440 | tf_op jit(solution)/shard_map/ppermute | solution.py:545
  53.7 19.3 %collective-permute-start.8 = (f32[24,128]{1,0:T(8,128)}, f32[24,128]{1,0:T(8,128)}, u32[]{:S(2)}, u32[]{:S(2)}) collective-permute-start(f32[24,128]{1,0:T(8,128)} %constant_dynamic-update-slice_fusion.s0), channel_id=1, source_target_pairs={{0,16},{8,24},{16,0},{24,8},{1,17},{9,25},{17,1},{25,9},{2,18},{10... | collective-permute-start | bytes 36872 | tf_op jit(solution)/shard_map/ppermute | solution.py:549
  54.2 20.2 %collective-permute-start.4 = (bf16[4,128,256]{2,1,0:T(8,128)(2,1)}, bf16[4,128,256]{2,1,0:T(8,128)(2,1)}, u32[]{:S(2)}, u32[]{:S(2)}) collective-permute-start(bf16[4,128,256]{2,1,0:T(8,128)(2,1)} %collective-permute-done.3.w2), channel_id=1, source_target_pairs={{0,8},{8,0},{16,24},{24,16},{1,9},{9,1},{17,25},{25,17},{2,10},{10... | collective-permute-start | bytes 786440 | tf_op jit(solution)/shard_map/ppermute | solution.py:546
  58.7 15.7 %copy-start.5 = (bf16[512,512]{1,0:T(8,128)(2,1)S(1)}, bf16[512,512]{1,0:T(8,128)(2,1)}, u32[]{:S(2)}) copy-start(bf16[512,512]{1,0:T(8,128)(2,1)} %constant.75.clone.fr_lo) | copy-start | bytes 1572868
  58.7 15.7 %copy-start.6 = (bf16[512,512]{1,0:T(8,128)(2,1)S(1)}, bf16[512,512]{1,0:T(8,128)(2,1)}, u32[]{:S(2)}) copy-start(bf16[512,512]{1,0:T(8,128)(2,1)} %constant.74.clone.fr_hi) | copy-start | bytes 1572868
  58.7 15.7 %copy-start.7 = (f32[4,128,256]{2,1,0:T(8,128)S(1)}, f32[4,128,256]{2,1,0:T(8,128)}, u32[]{:S(2)}) copy-start(f32[4,128,256]{2,1,0:T(8,128)} %constant.69.clone.shapes_ref) | copy-start | bytes 1572868
  58.7 15.7 %copy-start.8 = (bf16[512,256]{1,0:T(8,128)(2,1)S(1)}, bf16[512,256]{1,0:T(8,128)(2,1)}, u32[]{:S(2)}) copy-start(bf16[512,256]{1,0:T(8,128)(2,1)} %constant.73.clone.ct_lo) | copy-start | bytes 786436
  58.7 15.7 %copy-start.9 = (bf16[512,256]{1,0:T(8,128)(2,1)S(1)}, bf16[512,256]{1,0:T(8,128)(2,1)}, u32[]{:S(2)}) copy-start(bf16[512,256]{1,0:T(8,128)(2,1)} %constant.72.clone.ct_hi) | copy-start | bytes 786436
  58.7 15.7 %copy-start.13 = (bf16[64,1024]{1,0:T(8,128)(2,1)S(1)}, bf16[64,1024]{1,0:T(8,128)(2,1)}, u32[]{:S(2)}) copy-start(bf16[64,1024]{1,0:T(8,128)(2,1)} %constant.77.clone.fc_lo) | copy-start | bytes 393220
  67.9 3.3 %copy-start = (f32[32,256,256]{2,1,0:T(8,128)}, f32[32,256,256]{2,1,0:T(8,128)S(1)}, u32[]{:S(2)}) copy-start(f32[32,256,256]{2,1,0:T(8,128)S(1)} %get-tuple-element.11.field_ref) | copy-start | bytes 25165828
  71.2 1.3 %copy-start.2 = (f32[16,128,256]{2,1,0:T(8,128)}, f32[16,128,256]{2,1,0:T(8,128)S(1)}, u32[]{:S(2)}) copy-start(f32[16,128,256]{2,1,0:T(8,128)S(1)} %get-tuple-element.12.estimate_ref) | copy-start | bytes 6291460
  72.5 1.5 %collective-permute-start.7 = (f32[24,128]{1,0:T(8,128)}, f32[24,128]{1,0:T(8,128)S(1)}, u32[]{:S(2)}, u32[]{:S(2)}) collective-permute-start(f32[24,128]{1,0:T(8,128)} %constant_dynamic-update-slice_fusion.s0), channel_id=1, source_target_pairs={{0,8},{8,0},{16,24},{24,16},{1,9},{9,1},{17,25},{25,17},{2,10},{10... | collective-permute-start | bytes 36872 | tf_op jit(solution)/shard_map/ppermute | solution.py:550
  73.0 1.4 %collective-permute-start.9 = (f32[24,128]{1,0:T(8,128)}, f32[24,128]{1,0:T(8,128)S(1)}, u32[]{:S(2)}, u32[]{:S(2)}) collective-permute-start(f32[24,128]{1,0:T(8,128)} %collective-permute-done.8.s2), channel_id=1, source_target_pairs={{0,8},{8,0},{16,24},{24,16},{1,9},{9,1},{17,25},{25,17},{2,10},{10... | collective-permute-start | bytes 36872 | tf_op jit(solution)/shard_map/ppermute | solution.py:551
  73.1 29.1 %copy-start.22 = (s32[4]{0:T(128)}, s32[4]{0:T(128)S(1)}, u32[]{:S(2)}) copy-start(s32[4]{0:T(128)S(1)} %pad_add_fusion.where) | copy-start | bytes 52
  78.5 21.8 %copy-start.26 = (bf16[512,512]{1,0:T(8,128)(2,1)S(1)}, bf16[512,512]{1,0:T(8,128)(2,1)}, u32[]{:S(2)}) copy-start(bf16[512,512]{1,0:T(8,128)(2,1)} %constant.81.clone.im_lo) | copy-start | bytes 1572868
  78.5 21.8 %copy-start.27 = (bf16[512,512]{1,0:T(8,128)(2,1)S(1)}, bf16[512,512]{1,0:T(8,128)(2,1)}, u32[]{:S(2)}) copy-start(bf16[512,512]{1,0:T(8,128)(2,1)} %constant.80.clone.im_hi) | copy-start | bytes 1572868
  78.5 21.8 %copy-start.28 = (bf16[512,512]{1,0:T(8,128)(2,1)S(1)}, bf16[512,512]{1,0:T(8,128)(2,1)}, u32[]{:S(2)}) copy-start(bf16[512,512]{1,0:T(8,128)(2,1)} %constant.79.clone.re_lo) | copy-start | bytes 1572868
  78.5 21.8 %copy-start.29 = (bf16[512,512]{1,0:T(8,128)(2,1)S(1)}, bf16[512,512]{1,0:T(8,128)(2,1)}, u32[]{:S(2)}) copy-start(bf16[512,512]{1,0:T(8,128)(2,1)} %constant.78.clone.re_hi) | copy-start | bytes 1572868
  95.0 8.1 %collective-permute-start.10 = (f32[32,256]{1,0:T(8,128)S(1)}, f32[32,256]{1,0:T(8,128)S(1)}, u32[]{:S(2)}, u32[]{:S(2)}) collective-permute-start(f32[32,256]{1,0:T(8,128)S(1)} %get-tuple-element.16), channel_id=1, source_target_pairs={{0,1},{1,0},{2,3},{3,2},{4,5},{5,4},{6,7},{7,6},{8,9},{9,8},{10,11... | collective-permute-start | bytes 98312 | tf_op jit(solution)/shard_map/ppermute | solution.py:523
  97.0 6.7 %collective-permute-start.11 = (f32[32,256]{1,0:T(8,128)S(1)}, f32[32,256]{1,0:T(8,128)S(1)}, u32[]{:S(2)}, u32[]{:S(2)}) collective-permute-start(f32[32,256]{1,0:T(8,128)S(1)} %get-tuple-element.17), channel_id=1, source_target_pairs={{1,2},{2,1},{3,4},{4,3},{5,6},{6,5},{9,10},{10,9},{11,12},{12,11},... | collective-permute-start | bytes 98312 | tf_op jit(solution)/shard_map/ppermute | solution.py:523
  102.2 1.0 copy-start.1
  (17 other events, 14.0 us)

commit v2 on v1

--- a/solution.py
+++ b/solution.py
@@ -17,7 +17,7 @@
 BF16 = jnp.bfloat16
 VMEM = pltpu.VMEM
 SMEM = pltpu.SMEM
-MIB = 1 << 20
+LIMIT = 58 << 20
 
 
 def two_parts(table):
@@ -66,10 +66,32 @@
     return [pl.BlockSpec(memory_space=VMEM)] * count
 
 
-def dequant_kernel(raw_ref, scales_ref, out_ref, *, rows_here, core, margin):
+def parts_rows(values, columns):
+    high = values.astype(BF16).astype(F32)
+    rest = values - high
+    middle = rest.astype(BF16).astype(F32)
+    last = rest - middle
+    top = jnp.concatenate([high, middle], axis=1)
+    bottom = jnp.concatenate([last, jnp.zeros_like(last)], axis=1)
+    rows = jnp.concatenate([top, bottom], axis=0)
+    if columns > 256:
+        rows = jnp.concatenate([rows, jnp.zeros((16, columns - 256), F32)], axis=1)
+    return rows.astype(BF16)
+
+
+def rows_value(rows):
+    rows = rows.astype(F32)
+    return rows[:8, :128] + rows[:8, 128:256] + rows[8:, :128]
+
+
+def strips_kernel(
+    where, raw_ref, scales_ref, gains_ref, lc_hi, lc_lo, out_ref, *, frames, core, margin
+):
     lines, strip = raw_ref.shape
     coarse_rows, coarse_cols = scales_ref.shape
-    tiles, _, width = out_ref.shape
+    tiles = out_ref.shape[0]
+    width, half_w = lc_hi.shape
+    rows_here = lines // frames
     ratio = lines // coarse_rows
     row = lax.broadcasted_iota(jnp.int32, (lines, coarse_rows), 0)
     pick = lax.broadcasted_iota(jnp.int32, (lines, coarse_rows), 1)
@@ -77,6 +99,16 @@
     factors = mm(spread_rows, scales_ref[...]).astype(BF16)
     block = lax.broadcasted_iota(jnp.int32, (coarse_cols, width), 0)
     place = lax.broadcasted_iota(jnp.int32, (coarse_cols, width), 1)
+    line = lax.broadcasted_iota(jnp.int32, (1, width), 1)
+    in_core = ((line >= margin) & (line < margin + core)).astype(F32)
+    xc = (line.astype(F32) - margin - (core - 1) / 2.0) * in_core
+    first_row = (where[2] * rows_here).astype(F32)
+    height = rows_here * tiles
+    yc = lax.broadcasted_iota(jnp.int32, (rows_here, 1), 0).astype(F32)
+    yc = yc + (first_row - (height - 1) / 2.0)
+    lane = lax.broadcasted_iota(jnp.int32, (8, 128), 1)
+    narrow_lane = lax.broadcasted_iota(jnp.int32, (1, 128), 1)
+    own, means = [], []
     for tile in range(tiles):
         start = tile * core - margin
         column = place + start
@@ -88,19 +120,60 @@
         turn = (base - start) % span
         if turn:
             codes = pltpu.roll(codes, turn, 1)
-        out_ref[tile] = (codes[:, :width] * scale).astype(BF16)
-
-
-def dequantize(raw, scales, tiles, core, margin, width):
+        gains = pltpu.roll(gains_ref[tile].astype(F32), margin, 1)
+        if tile > 0:
+            end = gains_ref[tile - 1][:, width - 128 :].astype(F32)
+            end = pltpu.roll(end, (2 * margin) + margin, 1)
+            end = jnp.where(narrow_lane < margin, end, 0.0)
+            gains = jnp.concatenate([gains[:, :128] + end, gains[:, 128:]], axis=1)
+        if tile < tiles - 1:
+            end = gains_ref[tile + 1][:, :128].astype(F32)
+            end = pltpu.roll(end, 128 - margin, 1)
+            end = jnp.where(narrow_lane >= 128 - margin, end, 0.0)
+            gains = jnp.concatenate(
+                [gains[:, : width - 128], gains[:, width - 128 :] + end], axis=1
+            )
+        gains = jnp.concatenate([gains + 1.0] * frames, axis=0)
+        flattened = codes[:, :width] * scale * gains
+        high, low = split(flattened)
+        narrow = mm(high, lc_hi[...]) + mm(high, lc_lo[...]) + mm(low, lc_hi[...])
+        sums, lines_y, flat_means, centred = [], [], [], []
+        for frame in range(frames):
+            cut = slice(frame * rows_here, (frame + 1) * rows_here)
+            sums.append(jnp.sum(flattened[cut], axis=0, keepdims=True))
+            lines_y.append(jnp.sum(flattened[cut] * yc, axis=0, keepdims=True))
+            mean = jnp.sum(narrow[cut]) * (1.0 / (rows_here * half_w))
+            flat_means.append(jnp.full((1, 1), mean, F32))
+            centred.append(narrow[cut] - mean)
+        out_ref[tile, :lines] = jnp.concatenate(centred, axis=0).astype(BF16)
+        blank = [jnp.zeros((8 - frames, width), F32)]
+        slope_y = jnp.sum(jnp.concatenate(lines_y + blank, axis=0) * in_core, axis=1, keepdims=True)
+        slope_x = jnp.sum(jnp.concatenate(sums + blank, axis=0) * xc, axis=1, keepdims=True)
+        own.append(jnp.where(lane == 0, slope_y, jnp.where(lane == 1, slope_x, 0.0)))
+        mean = jnp.concatenate(flat_means + [jnp.zeros((8 - frames, 1), F32)], axis=0)
+        means.append(jnp.where(lane == 6, mean, 0.0))
+    for tile in range(tiles):
+        packed = own[tile] + means[tile]
+        if tile > 0:
+            packed += pltpu.roll(own[tile - 1], 2, 1)
+        if tile < tiles - 1:
+            packed += pltpu.roll(own[tile + 1], 4, 1)
+        out_ref[tile, lines:] = parts_rows(packed, half_w)
+
+
+def strips(raw, scales, gains, where, lc, tiles, core, margin):
     frames, rows_here, strip = raw.shape
     return pl.pallas_call(
-        functools.partial(dequant_kernel, rows_here=rows_here, core=core, margin=margin),
-        out_shape=jax.ShapeDtypeStruct((tiles, frames * rows_here, width), BF16),
-        in_specs=vmem_spec(2),
+        functools.partial(strips_kernel, frames=frames, core=core, margin=margin),
+        out_shape=jax.ShapeDtypeStruct((tiles, frames * rows_here + 16, lc.shape[1]), BF16),
+        in_specs=[pl.BlockSpec(memory_space=SMEM)] + vmem_spec(5),
         out_specs=pl.BlockSpec(memory_space=VMEM),
-        compiler_params=pltpu.CompilerParams(vmem_limit_bytes=40 * MIB),
-        name="dequantize",
-    )(raw.reshape(frames * rows_here, strip), scales.reshape(-1, scales.shape[-1]))
+        compiler_params=pltpu.CompilerParams(vmem_limit_bytes=LIMIT),
+        name="strips",
+    )(
+        where, raw.reshape(frames * rows_here, strip), scales.reshape(-1, scales.shape[-1]), gains,
+        *two_parts(lc),
+    )
 
 
 def box_area(top, left, band_rows, band_cols):
@@ -191,7 +264,7 @@
             pltpu.VMEM((2, height + 8, width + 128), F32),
             pltpu.VMEM((leds, half_h, half_w), F32),
         ],
-        compiler_params=pltpu.CompilerParams(vmem_limit_bytes=40 * MIB),
+        compiler_params=pltpu.CompilerParams(vmem_limit_bytes=LIMIT),
         cost_estimate=pl.CostEstimate(
             flops=8_000_000_000, bytes_accessed=16_000_000, transcendentals=0
         ),
@@ -199,48 +272,40 @@
     )(led_row, led_col, patterns, spectrum, pupil, *constants)
 
 
-def window_kernel(
-    dq_ref, flat_ref, part_a, part_b, odd, lc_hi, lc_lo, lr_hi, lr_lo, shapes_ref,
-    window_ref, slopes_ref, *, margin, core,
-):
-    slabs, lines, width = dq_ref.shape
-    frames, half_h, half_w = window_ref.shape
+def window_kernel(dq_ref, after, lr_hi, lr_lo, lr_sum, shapes_ref, window_ref, *, frames, core):
+    slabs, lines, half_w = dq_ref.shape
+    lines -= 16
+    half_h = lr_hi.shape[0]
     rows_here = lines // frames
     height = slabs * rows_here
-    is_odd = odd[0] == 1
-    first, second = part_a[...], part_b[...]
-    from_left = jnp.where(is_odd, first, second)
-    from_right = jnp.where(is_odd, second, first)
-    gains = jnp.concatenate([from_left, flat_ref[...], from_right], axis=1)
-    yc = lax.broadcasted_iota(jnp.int32, (height, 1), 0).astype(F32) - (height - 1) / 2.0
-    place = lax.broadcasted_iota(jnp.int32, (1, width), 1)
-    in_core = ((place >= margin) & (place < margin + core)).astype(F32)
-    xc = (place.astype(F32) - margin - (core - 1) / 2.0) * in_core
     over_y = 1.0 / (core * (height * (height * height - 1) / 12.0))
     over_x = 1.0 / (height * (core * (core * core - 1) / 12.0))
-    values = [dq_ref[slab].astype(F32) for slab in range(slabs)]
-    lane = lax.broadcasted_iota(jnp.int32, (1, 128), 1)
-    flats = []
+    lane = lax.broadcasted_iota(jnp.int32, (8, 128), 1)
+    notes = [rows_value(dq_ref[slab, lines:]) for slab in range(slabs)]
+    slopes = functools.reduce(jnp.add, notes)
+    slopes = slopes * jnp.where(lane % 2 == 0, over_y, over_x)
+    slab_means = jnp.zeros((8, 128), F32)
+    for slab in range(slabs):
+        slab_means = jnp.where(lane == slab, notes[slab][:, 6:7], slab_means)
+    left_rows = jnp.concatenate([lr_hi[...], lr_lo[...]], axis=1)
+    if rows_here % 16:
+        values = [dq_ref[slab, :lines].astype(F32) for slab in range(slabs)]
+    else:
+        values = [dq_ref[slab, :lines] for slab in range(slabs)]
+    means = []
     for frame in range(frames):
         cut = slice(frame * rows_here, (frame + 1) * rows_here)
-        flats.append(jnp.concatenate([v[cut] for v in values], axis=0) * gains)
-    flattened = jnp.concatenate(flats, axis=0)
-    high, low = split(flattened)
-    narrow = mm(high, lc_hi[...]) + mm(high, lc_lo[...]) + mm(low, lc_hi[...])
-    left_rows = jnp.concatenate([lr_hi[...], lr_hi[...], lr_lo[...]], axis=1)
-    slopes_ref[...] = jnp.zeros_like(slopes_ref)
-    for frame in range(frames):
-        cut = slice(frame * height, (frame + 1) * height)
-        slope_y = jnp.sum(jnp.sum(flats[frame] * yc, axis=0, keepdims=True) * in_core) * over_y
-        slope_x = jnp.sum(jnp.sum(flats[frame], axis=0, keepdims=True) * xc) * over_x
-        high, low = split(narrow[cut])
-        window = mm(left_rows, jnp.concatenate([high, low, high], axis=0))
-        window = window - shapes_ref[0] * slope_y - shapes_ref[1] * slope_x
+        whole = jnp.concatenate([v[cut] for v in values], axis=0).astype(BF16)
+        window = mm(left_rows, jnp.concatenate([whole, whole], axis=0))
+        level = jnp.sum(lr_sum[...] * slab_means[frame : frame + 1], axis=1, keepdims=True)
+        window = window + level
+        for shape in range(6):
+            window = window - shapes_ref[shape] * slopes[frame : frame + 1, shape : shape + 1]
         mean = jnp.sum(window) * (1.0 / (half_h * half_w))
-        window_ref[frame] = (window - mean).astype(BF16)
-        slopes_ref[frame : frame + 1] = jnp.where(
-            lane == 0, slope_y, jnp.where(lane == 1, slope_x, jnp.where(lane == 2, mean, 0.0))
-        )
+        means.append(jnp.full((1, 128), mean, F32))
+        window_ref[frame * half_h : (frame + 1) * half_h] = (window - mean).astype(BF16)
+    means = jnp.concatenate(means + [jnp.zeros((8 - frames, 128), F32)], axis=0)
+    window_ref[frames * half_h :] = parts_rows(means, half_w)
 
 
 def tilt_shapes(height, width, margin, core, lr, lc):
@@ -257,26 +322,24 @@
     return np.stack(shapes).astype(np.float32)
 
 
-def windows(arrived, flat, part_a, part_b, odd, frames, passes, shapes, margin, core):
-    lr, lc = passes
-    constants = [*two_parts(lc), *two_parts(lr)]
-    half_h, half_w = lr.shape[0], lc.shape[1]
+def windows(arrived, after, frames, lr, shapes, core):
+    slabs, _, half_w = arrived.shape
+    half_h, height = lr.shape
+    sums = np.zeros((half_h, 128), np.float32)
+    sums[:, :slabs] = lr.reshape(half_h, slabs, height // slabs).sum(axis=2)
     return pl.pallas_call(
-        functools.partial(window_kernel, margin=margin, core=core),
-        out_shape=(
-            jax.ShapeDtypeStruct((frames, half_h, half_w), BF16),
-            jax.ShapeDtypeStruct((8, 128), F32),
-        ),
-        in_specs=vmem_spec(4) + [pl.BlockSpec(memory_space=SMEM)] + vmem_spec(5),
-        out_specs=tuple(vmem_spec(2)),
-        compiler_params=pltpu.CompilerParams(vmem_limit_bytes=40 * MIB),
+        functools.partial(window_kernel, frames=frames, core=core),
+        out_shape=jax.ShapeDtypeStruct((frames * half_h + 16, half_w), BF16),
+        in_specs=vmem_spec(1) + [pl.BlockSpec(memory_space=pl.ANY)] + vmem_spec(4),
+        out_specs=pl.BlockSpec(memory_space=VMEM),
+        compiler_params=pltpu.CompilerParams(vmem_limit_bytes=LIMIT),
         name="windows",
-    )(arrived, flat, part_a, part_b, odd, *constants, shapes[:2])
+    )(arrived, after, *two_parts(lr), sums, shapes)
 
 
 def update_kernel(
     led_row, led_col, patterns, where, field_ref, estimate_ref, w0, w1, w2, w3,
-    s0, s1, s2, s3, spec_ref, pupil_ref, shapes_ref, rt_hi, rt_lo, ct_hi, ct_lo,
+    spec_ref, pupil_ref, rt_hi, rt_lo, ct_hi, ct_lo,
     fr_hi, fr_lo, fc_hi, fc_lo,
     fresh_ref, high_ref, low_ref, first_ref, second_ref, misfit, weight, grads,
 ):
@@ -285,7 +348,7 @@
     band_rows, band_cols = pupil_ref.shape[1:]
     height, width = spec_ref.shape[1:]
     half_h, half_w = misfit.shape[1:]
-    frames_here = w0.shape[0]
+    frames_here = w0.shape[0] // half_h
     my_group = where[0]
     is_odd = where[1] == 1
 
@@ -293,18 +356,13 @@
     def _():
         grads[...] = jnp.zeros_like(grads)
         weight[...] = jnp.zeros_like(weight)
-        for slot, (window, slopes) in enumerate(((w0, s0), (w1, s1), (w2, s2), (w3, s3))):
+        for slot, window in enumerate((w0, w1, w2, w3)):
             owner = jnp.bitwise_xor(my_group, slot)
+            means = rows_value(window[frames_here * half_h :])
             for place in range(frames_here):
                 frame = owner * frames_here + place
-                own = slopes[place : place + 1]
-                first = slopes[8 + place : 9 + place]
-                second = slopes[16 + place : 17 + place]
-                left = jnp.where(is_odd, first, second)
-                right = jnp.where(is_odd, second, first)
-                value = estimate_ref[frame] - window[place].astype(F32) - own[:, 2:3]
-                value += shapes_ref[0] * left[:, 0:1] + shapes_ref[1] * left[:, 1:2]
-                value += shapes_ref[2] * right[:, 0:1] + shapes_ref[3] * right[:, 1:2]
+                value = estimate_ref[frame] - means[place : place + 1, 0:1]
+                value -= window[place * half_h : (place + 1) * half_h].astype(F32)
                 for lit in range(patterns.shape[1]):
                     weight[patterns[frame, lit]] += value
 
@@ -365,8 +423,8 @@
 
 
 def update(
-    field, estimate, window_parts, slope_parts, spectrum, pupil, patterns, led_row, led_col,
-    where, tables, shapes, margin, group=4,
+    field, estimate, window_parts, spectrum, pupil, patterns, led_row, led_col, where, tables,
+    margin, group=4,
 ):
     rows, cols = tables
     leds = led_row.shape[0]
@@ -385,7 +443,6 @@
         ]
     )
     constants = [
-        shapes[2:],
         *two_parts(rows.T),
         *two_parts(cols.T),
         *two_parts(full_rows),
@@ -393,7 +450,7 @@
     ]
     whole = lambda shape: pl.BlockSpec(shape, lambda i: (0,) * len(shape))
     scalar = pl.BlockSpec(memory_space=SMEM)
-    operands = [estimate, *window_parts, *slope_parts, spectrum, pupil, *constants]
+    operands = [estimate, *window_parts, spectrum, pupil, *constants]
     out_shape = (
         jax.ShapeDtypeStruct(spectrum.shape, F32),
         jax.ShapeDtypeStruct((height, 2 * width), BF16),
@@ -414,7 +471,7 @@
             pltpu.VMEM((leds, half_h, half_w), F32),
             pltpu.VMEM((2, height + 8, width + 128), F32),
         ],
-        compiler_params=pltpu.CompilerParams(vmem_limit_bytes=48 * MIB),
+        compiler_params=pltpu.CompilerParams(vmem_limit_bytes=LIMIT),
         name="update",
     )(led_row, led_col, patterns, where, field, *operands)
 
@@ -442,7 +499,7 @@
         out_shape=jax.ShapeDtypeStruct((2, height, core), F32),
         in_specs=vmem_spec(6),
         out_specs=pl.BlockSpec(memory_space=VMEM),
-        compiler_params=pltpu.CompilerParams(vmem_limit_bytes=40 * MIB),
+        compiler_params=pltpu.CompilerParams(vmem_limit_bytes=LIMIT),
         cost_estimate=pl.CostEstimate(
             flops=3_000_000_000, bytes_accessed=5_000_000, transcendentals=0
         ),
@@ -526,17 +583,13 @@
     passes = (low_pass(height, band_rows), low_pass(width, band_cols).T)
     shapes = tilt_shapes(height, width, margin, core, *passes)
 
-    codes = dequantize(raw, scales, tiles, core, margin, width)
-    arrived = lax.all_to_all(codes, "tile", split_axis=0, concat_axis=0, tiled=True)
-    flat_left, flat_right = flat[:, :margin], flat[:, core - margin :]
-    is_odd = odd == 1
-    flat_a, flat_b = neighbours(
-        jnp.where(is_odd, flat_left, flat_right), jnp.where(is_odd, flat_right, flat_left)
-    )
+    gains = (flat - 1.0).astype(BF16).reshape(tiles, height // tiles, core)
+    gains = jnp.pad(gains, ((0, 0), (0, 0), (0, OV)))
+    gains = lax.all_to_all(gains, "tile", split_axis=0, concat_axis=0, tiled=True)
+    narrow = strips(raw, scales, gains, where, passes[1], tiles, core, margin)
+    arrived = lax.all_to_all(narrow, "tile", split_axis=0, concat_axis=0, tiled=True)
     field, estimate = all_fields(spectrum_tile, pupil, patterns, led_row, led_col, tables)
-    window, slopes = windows(
-        arrived, flat, flat_a, flat_b, where[1:2], frames_here, passes, shapes, margin, core
-    )
+    window = windows(arrived, estimate, frames_here, passes[0], shapes, core)
 
     swap_core = [(i, i ^ 1) for i in range(4)]
     swap_chip = [(i, i ^ 2) for i in range(4)]
@@ -544,16 +597,10 @@
     window_2 = other(window, perm=swap_chip)
     window_1 = other(window, perm=swap_core)
     window_3 = other(window_2, perm=swap_core)
-    slopes_a, slopes_b = neighbours(slopes, slopes)
-    slopes_0 = jnp.concatenate([slopes, slopes_a, slopes_b], axis=0)
-    slopes_2 = other(slopes_0, perm=swap_chip)
-    slopes_1 = other(slopes_0, perm=swap_core)
-    slopes_3 = other(slopes_2, perm=swap_core)
 
     fresh, high, low, for_a, for_b = update(
-        field, estimate, (window, window_1, window_2, window_3),
-        (slopes_0, slopes_1, slopes_2, slopes_3), spectrum_tile, pupil, patterns,
-        led_row, led_col, where, tables, shapes, margin,
+        field, estimate, (window, window_1, window_2, window_3), spectrum_tile, pupil, patterns,
+        led_row, led_col, where, tables, margin,
     )
     side_a, side_b = neighbours(for_a, for_b)
     core_part = object_core(high, low, margin, core)

time: 110 us -> 87.5 us (0.80)
  the two profiles are of different devices: /device:TPU:12 before, /device:TPU:22 now
where the time goes in v2:
time: 87.5 us; the launch traced here: 86.8 us
  Pallas kernels  43.3 us (49%)
  starting transfers between devices  19.4 us (22%)
  waiting for transfers between devices  13.6 us (16%)
  local copies, waits for them, and re-layouts  8.14 us (9%)
  other arithmetic  1.62 us (2%)
    pallas_call x1, Pallas kernels, update(): pl.pallas_call(update_kernel, grid=(leds // group,), out_shape=out_shape,...  17 us
    pallas_call x1, Pallas kernels, all_fields(): pl.pallas_call(field_kernel, grid=(leds // group,), out_shape=(jax.ShapeD...  11.8 us
    unnamed x16, local copies, waits for them, and re-layouts  7.27 us
    ppermute x1, waiting for transfers between devices, body(): window_2 = other(window, perm=swap_chip)  7 us
    all_to_all x1, starting transfers between devices, body(): lax.all_to_all(narrow, 'tile', split_axis=0, concat_axis=0, tiled=True)  6.87 us
    all_to_all x1, starting transfers between devices, body(): lax.all_to_all(gains, 'tile', split_axis=0, concat_axis=0, tiled=True)  6.11 us
    all_to_all x1, waiting for transfers between devices, body(): lax.all_to_all(gains, 'tile', split_axis=0, concat_axis=0, tiled=True)  5.08 us
    ppermute x1, starting transfers between devices, neighbours(): lax.ppermute(for_b, 'tile', swap_b)  4.94 us
  transfers between devices with their start and end apart: 7, of which 3 were waited for; matrix products, arithmetic and copies ran while one was open for 2% of the time, Pallas kernels for 19%

profile of v2, /device:TPU:22, one launch (start us, length us, event | category | flops | bytes accessed | tf_op | source)
XLA Modules:
  0.0 86.8 jit_solution(2554752778259948327)
XLA Ops:
  0.6 1.1 %add_convert_fusion = bf16[256,480]{0,1:T(8,128)(2,1)S(1)} fusion(f32[256,480]{0,1:T(8,128)} %param.32), kind=kLoop, calls=%fused_computation | loop fusion | flops 245760 | bytes 737280 | tf_op jit(solution)/shard_map/convert_element_type | solution.py:586
  1.7 0.1 copy.34
  1.8 0.7 pad.4
  2.6 6.1 %all-to-all-start = ((bf16[8,32,512]{2,1,0:T(8,128)(2,1)}), bf16[8,32,512]{2,1,0:T(8,128)(2,1)S(1)}, u32[]{:S(2)}, u32[]{:S(2)}) async-start(bf16[8,32,512]{2,1,0:T(8,128)(2,1)} %pad.4), calls=%async_computation | async-start | bytes 524288 | tf_op jit(solution)/shard_map/all_to_all | solution.py:588
  8.7 0.6 pad_add_fusion.where
  9.2 5.1 %all-to-all-done.gains_ref = bf16[8,32,512]{2,1,0:T(8,128)(2,1)S(1)} async-done(((bf16[8,32,512]{2,1,0:T(8,128)(2,1)}), bf16[8,32,512]{2,1,0:T(8,128)(2,1)S(1)}, u32[]{:S(2)}, u32[]{:S(2)}) %all-to-all-start) | async-done | bytes 262176 | tf_op jit(solution)/shard_map/all_to_all | solution.py:588
  14.3 0.7 copy-done.1
  15.0 4.8 %strips.1 = bf16[8,144,256]{2,1,0:T(8,128)(2,1)} custom-call(s32[4]{0:T(128)} %pad_add_fusion.where, bf16[128,3840]{1,0:T(8,128)(2,1)} %bitcast.11, bf16[32,120]{1,0:T(8,128)(2,1)} %bitcast.12, bf16[8,32,512]{2,1,0:T(8,128)(2,1)} %copy-done.1, bf16[512,256]{1,0:T(8,128)(2,1)} %constant.65.clone.lc_hi, bf16[512,256]{1,0:T(8,128)(2,1)} %constant.66.clone.lc_lo), custom_call_target="tpu_custom_call" | custom-call | tf_op jit(solution)/shard_map/strips/pallas_call | solution.py:166
  19.8 6.9 %all-to-all-start.1 = ((bf16[8,144,256]{2,1,0:T(8,128)(2,1)}), bf16[8,144,256]{2,1,0:T(8,128)(2,1)S(1)}, u32[]{:S(2)}, u32[]{:S(2)}) async-start(bf16[8,144,256]{2,1,0:T(8,128)(2,1)} %strips.1), calls=%async_computation.1 | async-start | bytes 1179648 | tf_op jit(solution)/shard_map/all_to_all | solution.py:590
  26.7 1.4 %copy.35.patterns = s32[16,4]{1,0:T(8,128)} copy(s32[16,4]{0,1:T(4,128)} %param.35) | data formatting | bytes 512 | tf_op args[5]
  28.0 11.8 %fields.1 = (f32[32,256,256]{2,1,0:T(8,128)}, f32[16,128,256]{2,1,0:T(8,128)}) custom-call(s32[32]{0:T(128)} %led_row.3, s32[32]{0:T(128)} %led_col.3, s32[16,4]{1,0:T(8,128)} %copy.35.patterns, f32[2,256,512]{2,1,0:T(8,128)} %bitcast.9, f32[2,64,128]{2,1,0:T(8,128)} %pupil_ref.3, bf16[256,512]{1,0:T(8,128)(2,1)} %constant.67.clone.cols_hi, ...), custom_call_target="tpu_custom_call" | custom-call | flops 8000000000 | bytes 16000000 | tf_op jit(solution)/shard_map/fields/pallas_call | solution.py:249
  39.8 0.0 all-to-all-done.1.dq_ref
  39.8 0.0 copy-start
  39.8 0.8 copy-done
  40.7 3.1 %windows.1.w0 = bf16[528,256]{1,0:T(8,128)(2,1)} custom-call(bf16[8,144,256]{2,1,0:T(8,128)(2,1)} %copy-done, f32[16,128,256]{2,1,0:T(8,128)} %get-tuple-element.10.after.estimate_ref, bf16[128,256]{1,0:T(8,128)(2,1)} %constant.71.clone.lr_hi, bf16[128,256]{1,0:T(8,128)(2,1)} %constant.72.clone.lr_lo, f32[128,128]{1,0:T(8,128)} %constant.73.clone.lr_sum, ...), custom_call_target="tpu_custom_call" | custom-call | tf_op jit(solution)/shard_map/windows/pallas_call | solution.py:330
  43.7 0.5 collective-permute-start.1
  44.2 0.0 collective-permute-start
  44.3 7.0 %collective-permute-done.1.w2 = bf16[528,256]{1,0:T(8,128)(2,1)S(1)} collective-permute-done((bf16[528,256]{1,0:T(8,128)(2,1)}, bf16[528,256]{1,0:T(8,128)(2,1)S(1)}, u32[]{:S(2)}, u32[]{:S(2)}) %collective-permute-start.1) | collective-permute-done | bytes 270368 | tf_op jit(solution)/shard_map/ppermute | solution.py:597
  51.3 0.0 collective-permute-start.2
  51.3 0.0 collective-permute-done.w1
  51.3 1.5 %collective-permute-done.2.w3 = bf16[528,256]{1,0:T(8,128)(2,1)S(1)} collective-permute-done((bf16[528,256]{1,0:T(8,128)(2,1)S(1)}, bf16[528,256]{1,0:T(8,128)(2,1)S(1)}, u32[]{:S(2)}, u32[]{:S(2)}) %collective-permute-start.2) | collective-permute-done | bytes 270368 | tf_op jit(solution)/shard_map/ppermute | solution.py:599
  52.8 0.7 copy-done.4
  53.5 17.0 %update.1 = (f32[2,256,512]{2,1,0:T(8,128)}, bf16[256,1024]{1,0:T(8,128)(2,1)}, bf16[256,1024]{1,0:T(8,128)(2,1)}, f32[32,256]{1,0:T(8,128)}, f32[32,256]{1,0:T(8,128)}) custom-call(s32[32]{0:T(128)} %led_row.3, s32[32]{0:T(128)} %led_col.3, s32[16,4]{1,0:T(8,128)} %copy.35.patterns, s32[4]{0:T(128)} %pad_add_fusion.where, ...), custom_call_target="tpu_custom_call" | custom-call | tf_op jit(solution)/shard_map/update/pallas_call | solution.py:461
  70.5 1.0 %collective-permute-start.3 = (f32[32,256]{1,0:T(8,128)}, f32[32,256]{1,0:T(8,128)S(1)}, u32[]{:S(2)}, u32[]{:S(2)}) collective-permute-start(f32[32,256]{1,0:T(8,128)} %get-tuple-element.12), channel_id=1, source_target_pairs={{0,1},{1,0},{2,3},{3,2},{4,5},{5,4},{6,7},{7,6},{8,9},{9,8},{10,11... | collective-permute-start | bytes 98312 | tf_op jit(solution)/shard_map/ppermute | solution.py:580
  71.4 4.9 %collective-permute-start.4 = (f32[32,256]{1,0:T(8,128)}, f32[32,256]{1,0:T(8,128)S(1)}, u32[]{:S(2)}, u32[]{:S(2)}) collective-permute-start(f32[32,256]{1,0:T(8,128)} %get-tuple-element.13), channel_id=1, source_target_pairs={{1,2},{2,1},{3,4},{4,3},{5,6},{6,5},{9,10},{10,9},{11,12},{12,11},... | collective-permute-start | bytes 98312 | tf_op jit(solution)/shard_map/ppermute | solution.py:580
  76.4 4.6 %object.1.in_ref = f32[2,256,480]{2,1,0:T(8,128)} custom-call(bf16[256,1024]{1,0:T(8,128)(2,1)} %get-tuple-element.14.high_ref, bf16[256,1024]{1,0:T(8,128)(2,1)} %get-tuple-element.15.low_ref, bf16[512,512]{1,0:T(8,128)(2,1)} %constant.83.clone.re_hi, bf16[512,512]{1,0:T(8,128)(2,1)} %constant.84.clone.re_lo, bf16[512,512]{1,0:T(8,128)(2,1)} %constant.85.clone.im_hi, ...), custom_call_target="tpu_custom_call" | custom-call | flops 3000000000 | bytes 5000000 | tf_op jit(solution)/shard_map/object/pallas_call | solution.py:497
  81.0 0.0 collective-permute-done.3.first_ref
  81.0 0.0 collective-permute-done.4.second_ref
  81.0 0.6 copy-done.5
  81.6 0.6 copy-done.6
  82.2 2.1 %blend.1 = f32[2,256,480]{2,1,0:T(8,128)} custom-call(s32[4]{0:T(128)} %pad_add_fusion.where, f32[32,256]{1,0:T(8,128)} %copy-done.5, f32[32,256]{1,0:T(8,128)} %copy-done.6, f32[2,256,480]{2,1,0:T(8,128)} %object.1.in_ref), custom_call_target="tpu_custom_call", output_to_operand_aliasing={{}: (3, {})} | custom-call | tf_op jit(solution)/shard_map/blend/pallas_call | solution.py:552
  84.3 2.5 %copy.36 = f32[2,256,480]{1,2,0:T(8,128)} copy(f32[2,256,480]{2,1,0:T(8,128)} %blend.1) | data formatting | bytes 1966080
  (8 shorter events, 0.0 us)
Async XLA Ops:
  2.6 11.7 %all-to-all-start = ((bf16[8,32,512]{2,1,0:T(8,128)(2,1)}), bf16[8,32,512]{2,1,0:T(8,128)(2,1)S(1)}, u32[]{:S(2)}, u32[]{:S(2)}) async-start(bf16[8,32,512]{2,1,0:T(8,128)(2,1)} %pad.4), calls=%async_computation | async-start | bytes 524288 | tf_op jit(solution)/shard_map/all_to_all | solution.py:588
  14.3 0.7 copy-start.1
  19.8 20.0 %all-to-all-start.1 = ((bf16[8,144,256]{2,1,0:T(8,128)(2,1)}), bf16[8,144,256]{2,1,0:T(8,128)(2,1)S(1)}, u32[]{:S(2)}, u32[]{:S(2)}) async-start(bf16[8,144,256]{2,1,0:T(8,128)(2,1)} %strips.1), calls=%async_computation.1 | async-start | bytes 1179648 | tf_op jit(solution)/shard_map/all_to_all | solution.py:590
  39.8 0.8 copy-start
  43.7 7.5 %collective-permute-start.1 = (bf16[528,256]{1,0:T(8,128)(2,1)}, bf16[528,256]{1,0:T(8,128)(2,1)S(1)}, u32[]{:S(2)}, u32[]{:S(2)}) collective-permute-start(bf16[528,256]{1,0:T(8,128)(2,1)} %windows.1.w0), channel_id=1, source_target_pairs={{0,16},{8,24},{16,0},{24,8},{1,17},{9,25},{17,1},{25,9},{2,18},{10... | collective-permute-start | bytes 811016 | tf_op jit(solution)/shard_map/ppermute | solution.py:597
  44.2 7.0 %collective-permute-start = (bf16[528,256]{1,0:T(8,128)(2,1)}, bf16[528,256]{1,0:T(8,128)(2,1)S(1)}, u32[]{:S(2)}, u32[]{:S(2)}) collective-permute-start(bf16[528,256]{1,0:T(8,128)(2,1)} %windows.1.w0), channel_id=1, source_target_pairs={{0,8},{8,0},{16,24},{24,16},{1,9},{9,1},{17,25},{25,17},{2,10},{10... | collective-permute-start | bytes 811016 | tf_op jit(solution)/shard_map/ppermute | solution.py:598
  51.2 1.6 %copy-start.2 = (bf16[528,256]{1,0:T(8,128)(2,1)}, bf16[528,256]{1,0:T(8,128)(2,1)S(1)}, u32[]{:S(2)}) copy-start(bf16[528,256]{1,0:T(8,128)(2,1)S(1)} %collective-permute-done.1.w2) | copy-start | bytes 811012
  51.3 1.5 %collective-permute-start.2 = (bf16[528,256]{1,0:T(8,128)(2,1)S(1)}, bf16[528,256]{1,0:T(8,128)(2,1)S(1)}, u32[]{:S(2)}, u32[]{:S(2)}) collective-permute-start(bf16[528,256]{1,0:T(8,128)(2,1)S(1)} %collective-permute-done.1.w2), channel_id=1, source_target_pairs={{0,8},{8,0},{16,24},{24,16},{1,9},{9,1},{17,25},{25,17},{2,10},{10... | collective-permute-start | bytes 811016 | tf_op jit(solution)/shard_map/ppermute | solution.py:599
  51.3 1.5 %copy-start.3 = (bf16[528,256]{1,0:T(8,128)(2,1)}, bf16[528,256]{1,0:T(8,128)(2,1)S(1)}, u32[]{:S(2)}) copy-start(bf16[528,256]{1,0:T(8,128)(2,1)S(1)} %collective-permute-done.w1) | copy-start | bytes 811012
  52.8 0.7 copy-start.4
  70.5 10.5 %collective-permute-start.3 = (f32[32,256]{1,0:T(8,128)}, f32[32,256]{1,0:T(8,128)S(1)}, u32[]{:S(2)}, u32[]{:S(2)}) collective-permute-start(f32[32,256]{1,0:T(8,128)} %get-tuple-element.12), channel_id=1, source_target_pairs={{0,1},{1,0},{2,3},{3,2},{4,5},{5,4},{6,7},{7,6},{8,9},{9,8},{10,11... | collective-permute-start | bytes 98312 | tf_op jit(solution)/shard_map/ppermute | solution.py:580
  71.4 9.6 %collective-permute-start.4 = (f32[32,256]{1,0:T(8,128)}, f32[32,256]{1,0:T(8,128)S(1)}, u32[]{:S(2)}, u32[]{:S(2)}) collective-permute-start(f32[32,256]{1,0:T(8,128)} %get-tuple-element.13), channel_id=1, source_target_pairs={{1,2},{2,1},{3,4},{4,3},{5,6},{6,5},{9,10},{10,9},{11,12},{12,11},... | collective-permute-start | bytes 98312 | tf_op jit(solution)/shard_map/ppermute | solution.py:580
  81.0 0.6 copy-start.5
  81.6 0.6 copy-start.6

commit v3 on v2

v3 whole, which is shorter than its diff:
```python
import functools
import math

import jax
import jax.numpy as jnp
import ml_dtypes
import numpy as np
from jax import lax
from jax.experimental import pallas as pl
from jax.experimental.pallas import tpu as pltpu
from jax.sharding import PartitionSpec as P

OV = 32
BC = 32
STEP = 0.02
F32 = jnp.float32
BF16 = jnp.bfloat16
VMEM = pltpu.VMEM
SMEM = pltpu.SMEM
LIMIT = 30 << 20


def two_parts(table):
    table = np.asarray(table, np.float64)
    high = table.astype(ml_dtypes.bfloat16)
    low = (table - high.astype(np.float64)).astype(ml_dtypes.bfloat16)
    return high, low


def wave(places, freqs, length, norm):
    turns = np.outer(places, freqs) % length
    angle = turns * (2.0 * math.pi / length)
    return np.cos(angle) / math.sqrt(norm), np.sin(angle) / math.sqrt(norm)


def low_pass(length, band):
    places = 2 * np.arange(length // 2)[:, None] - np.arange(length)[None, :]
    total = np.ones(places.shape)
    for freq in range(1, band):
        total += 2.0 * np.cos(2.0 * math.pi * ((freq * places) % length) / length)
    return total / length


def stacked_tables(height, width, band_rows, band_cols):
    row_re, row_im = wave(
        2 * np.arange(height // 2), np.arange(band_rows) - band_rows // 2, height, band_rows
    )
    rows = np.block([[row_re, -row_im], [row_im, row_re]])
    col_re, col_im = wave(
        np.arange(band_cols) - band_cols // 2, 2 * np.arange(width // 2), width, band_cols
    )
    cols = np.block([[col_re, col_im], [-col_im, col_re]])
    return rows, cols


def split(values):
    high = values.astype(BF16)
    return high, (values - high.astype(F32)).astype(BF16)


def mm(left, right):
    return jnp.dot(left, right, preferred_element_type=F32)


def vmem_spec(count):
    return [pl.BlockSpec(memory_space=VMEM)] * count


def parts_rows(values, columns):
    high = values.astype(BF16).astype(F32)
    rest = values - high
    middle = rest.astype(BF16).astype(F32)
    last = rest - middle
    top = jnp.concatenate([high, middle], axis=1)
    bottom = jnp.concatenate([last, jnp.zeros_like(last)], axis=1)
    rows = jnp.concatenate([top, bottom], axis=0)
    if columns > 256:
        rows = jnp.concatenate([rows, jnp.zeros((16, columns - 256), F32)], axis=1)
    return rows.astype(BF16)


def rows_value(rows):
    rows = rows.astype(F32)
    return rows[:8, :128] + rows[:8, 128:256] + rows[8:, :128]


def gains_kernel(flat_hbm, out_ref, flat, sems):
    core, height = flat_hbm.shape
    tiles, rows_here, width = out_ref.shape
    spans = [(begin, min(128, core - begin)) for begin in range(0, core, 128)]
    loads = []
    for number, (begin, length) in enumerate(spans):
        part = pl.ds(begin, length)
        load = pltpu.make_async_copy(flat_hbm.at[part], flat.at[part], sems.at[number])
        load.start()
        loads.append(load)
    for load, (begin, length) in zip(loads, spans):
        load.wait()
        gains = flat[begin : begin + length] - 1.0
        if length < 128:
            gains = jnp.concatenate([gains, jnp.zeros((128 - length, height), F32)], axis=0)
        by_rows = jnp.transpose(gains, (1, 0)).reshape(tiles, rows_here, 128)
        out_ref[:, :, begin : begin + 128] = by_rows.astype(BF16)


def gains_by_rows(flat, tiles, width):
    core, height = flat.shape
    return pl.pallas_call(
        gains_kernel,
        out_shape=jax.ShapeDtypeStruct((tiles, height // tiles, width), BF16),
        in_specs=[pl.BlockSpec(memory_space=pltpu.HBM)],
        out_specs=pl.BlockSpec(memory_space=VMEM),
        scratch_shapes=[pltpu.VMEM((core, height), F32), pltpu.SemaphoreType.DMA((-(-core // 128),))],
        compiler_params=pltpu.CompilerParams(vmem_limit_bytes=LIMIT),
        name="gains",
    )(pltpu.with_memory_space_constraint(flat, pltpu.HBM))


def dequantize_kernel(raw_ref, scales_ref, after, out_ref, *, core, margin):
    lines, strip = raw_ref.shape
    coarse_rows, coarse_cols = scales_ref.shape
    tiles, _, width = out_ref.shape
    ratio = lines // coarse_rows
    row = lax.broadcasted_iota(jnp.int32, (lines, coarse_rows), 0)
    pick = lax.broadcasted_iota(jnp.int32, (lines, coarse_rows), 1)
    spread_rows = (row // ratio == pick).astype(F32).astype(BF16)
    factors = mm(spread_rows, scales_ref[...])
    wide = (coarse_cols // 128 + 1) * 128
    factors = jnp.concatenate([factors, jnp.zeros((lines, wide - coarse_cols), F32)], axis=1)

    blocks = []
    for tile in range(tiles):
        begin = (tile * core - margin) // BC
        blocks.append(pltpu.roll(factors, -begin % wide, 1)[:, :128].astype(BF16))
    block = lax.broadcasted_iota(jnp.int32, (128, width), 0)
    place = lax.broadcasted_iota(jnp.int32, (128, width), 1) + (-margin) % BC
    inside = (place >= block * BC) & (place < (block + 1) * BC)
    scales = mm(jnp.concatenate(blocks, axis=0), inside.astype(F32).astype(BF16))
    for tile in range(tiles):
        start = tile * core - margin
        base = max(start, 0) // 128 * 128
        span = min(width + 128, strip - base)
        codes = raw_ref[:, base : base + span].astype(F32)
        turn = (base - start) % span
        if turn:
            codes = pltpu.roll(codes, turn, 1)
        out_ref[tile] = codes[:, :width] * scales[tile * lines : (tile + 1) * lines]


def dequantize(raw, scales, after, tiles, core, margin):
    frames, rows_here, strip = raw.shape
    return pl.pallas_call(
        functools.partial(dequantize_kernel, core=core, margin=margin),
        out_shape=jax.ShapeDtypeStruct((tiles, frames * rows_here, core + 2 * margin), F32),
        in_specs=vmem_spec(2) + [pl.BlockSpec(memory_space=pl.ANY)],
        out_specs=pl.BlockSpec(memory_space=VMEM),
        compiler_params=pltpu.CompilerParams(vmem_limit_bytes=LIMIT),
        cost_estimate=pl.CostEstimate(
            flops=2_000_000_000, bytes_accessed=4_000_000, transcendentals=0
        ),
        name="dequantize",
    )(raw.reshape(frames * rows_here, strip), scales.reshape(-1, scales.shape[-1]), after)


def strips_kernel(where, dq_ref, gains_ref, lc_ref, out_ref, *, frames, core, margin):
    tiles, lines, width = dq_ref.shape
    half_w = lc_ref.shape[1]
    rows_here = lines // frames
    line = lax.broadcasted_iota(jnp.int32, (1, width), 1)
    in_core = ((line >= margin) & (line < margin + core)).astype(F32)
    xc = (line.astype(F32) - margin - (core - 1) / 2.0) * in_core
    first_row = (where[2] * rows_here).astype(F32)
    height = rows_here * tiles
    yc = lax.broadcasted_iota(jnp.int32, (rows_here, 1), 0).astype(F32)
    yc = yc + (first_row - (height - 1) / 2.0)
    lane = lax.broadcasted_iota(jnp.int32, (8, 128), 1)
    narrow_lane = lax.broadcasted_iota(jnp.int32, (1, 128), 1)

    own, highs, lows = [], [], []
    for tile in range(tiles):
        gains = pltpu.roll(gains_ref[tile].astype(F32), margin, 1)
        if tile > 0:
            end = gains_ref[tile - 1][:, width - 128 :].astype(F32)
            end = pltpu.roll(end, (2 * margin) + margin, 1)
            end = jnp.where(narrow_lane < margin, end, 0.0)
            gains = jnp.concatenate([gains[:, :128] + end, gains[:, 128:]], axis=1)
        if tile < tiles - 1:
            end = gains_ref[tile + 1][:, :128].astype(F32)
            end = pltpu.roll(end, 128 - margin, 1)
            end = jnp.where(narrow_lane >= 128 - margin, end, 0.0)
            gains = jnp.concatenate(
                [gains[:, : width - 128], gains[:, width - 128 :] + end], axis=1
            )
        gains = jnp.concatenate([gains + 1.0] * frames, axis=0)
        flattened = dq_ref[tile] * gains
        high, low = split(flattened)
        highs.append(high)
        lows.append(low)
        sums, lines_y = [], []
        for frame in range(frames):
            cut = slice(frame * rows_here, (frame + 1) * rows_here)
            sums.append(jnp.sum(flattened[cut], axis=0, keepdims=True))
            lines_y.append(jnp.sum(flattened[cut] * yc, axis=0, keepdims=True))
        blank = [jnp.zeros((8 - frames, width), F32)]
        slope_y = jnp.sum(jnp.concatenate(lines_y + blank, axis=0) * in_core, axis=1, keepdims=True)
        slope_x = jnp.sum(jnp.concatenate(sums + blank, axis=0) * xc, axis=1, keepdims=True)
        own.append(jnp.where(lane == 0, slope_y, jnp.where(lane == 1, slope_x, 0.0)))
    high, low = jnp.concatenate(highs, axis=0), jnp.concatenate(lows, axis=0)
    lc_hi, lc_lo = lc_ref[:width], lc_ref[width:]
    narrow = mm(high, lc_hi) + mm(high, lc_lo) + mm(low, lc_hi)
    for tile in range(tiles):
        one = narrow[tile * lines : (tile + 1) * lines]
        means, centred = [], []
        for frame in range(frames):
            cut = slice(frame * rows_here, (frame + 1) * rows_here)
            mean = jnp.sum(one[cut], axis=0, keepdims=True)
            mean = jnp.sum(mean, axis=1, keepdims=True) * (1.0 / (rows_here * half_w))
            means.append(mean)
            centred.append(one[cut] - mean)
        out_ref[tile, :lines] = jnp.concatenate(centred, axis=0).astype(BF16)
        mean = jnp.concatenate(means + [jnp.zeros((8 - frames, 1), F32)], axis=0)
        packed = own[tile] + jnp.where(lane == 6, mean, 0.0)
        if tile > 0:
            packed += pltpu.roll(own[tile - 1], 2, 1)
        if tile < tiles - 1:
            packed += pltpu.roll(own[tile + 1], 4, 1)
        out_ref[tile, lines:] = parts_rows(packed, half_w)


def strips(dequantized, gains, where, lc, frames, core, margin):
    tiles, lines, _ = dequantized.shape
    return pl.pallas_call(
        functools.partial(strips_kernel, frames=frames, core=core, margin=margin),
        out_shape=jax.ShapeDtypeStruct((tiles, lines + 16, lc.shape[1]), BF16),
        in_specs=[pl.BlockSpec(memory_space=SMEM)] + vmem_spec(3),
        out_specs=pl.BlockSpec(memory_space=VMEM),
        compiler_params=pltpu.CompilerParams(vmem_limit_bytes=LIMIT),
        name="strips",
    )(where, dequantized, gains, np.concatenate(two_parts(lc)))


def box_area(top, left, band_rows, band_cols):
    row = top // 8 * 8
    col = left // 128 * 128
    area = (
        pl.ds(pl.multiple_of(row, 8), band_rows + 8),
        pl.ds(pl.multiple_of(col, 128), band_cols + 128),
    )
    return area, top - row, left - col


def field_kernel(
    led_row, led_col, patterns, spec_ref, pupil_ref, cols_ref, rows_ref,
    rows_hbm, small_hbm, field_ref, estimate_ref, rows_out, small_out, wide, bright, sems, *, group,
):
    leds, half_h, half_w = bright.shape
    loads = [
        pltpu.make_async_copy(rows_hbm, rows_out, sems.at[0]),
        pltpu.make_async_copy(small_hbm, small_out, sems.at[1]),
    ]
    for load in loads:
        load.start()
    band_rows, band_cols = pupil_ref.shape[1:]
    width = spec_ref.shape[2]
    depth = 2 * band_cols
    wide[...] = jnp.zeros_like(wide)
    wide[:, : spec_ref.shape[1], :width] = spec_ref[...]

    def some(step, carry):
        boxes = []
        for place in range(group):
            led = step * group + place
            area, down, right = box_area(led_row[led], led_col[led], band_rows, band_cols)
            back = lax.rem(2 * band_cols - right, 2 * band_cols)
            up = lax.rem(band_rows + 8 - down, band_rows + 8)
            parts = []
            for part in range(2):
                strip = pltpu.roll(wide[(part, *area)], back, 1)
                parts.append(pltpu.roll(strip[:, :band_cols], up, 0)[:band_rows])
            lit_re = pupil_ref[0] * parts[0] - pupil_ref[1] * parts[1]
            lit_im = pupil_ref[0] * parts[1] + pupil_ref[1] * parts[0]
            boxes.append(jnp.concatenate([lit_re, lit_im], axis=1))
        high, low = split(jnp.concatenate(boxes, axis=0))
        cols_hi, cols_lo = cols_ref[:depth], cols_ref[depth:]
        spread = mm(high, cols_hi) + mm(high, cols_lo) + mm(low, cols_hi)
        for place in range(group):
            one = spread[place * band_rows : (place + 1) * band_rows]
            high, low = split(jnp.concatenate([one[:, :half_w], one[:, half_w:]], axis=0))
            field = mm(rows_ref[...], jnp.concatenate([high, low, high], axis=0))
            field_ref[step * group + place] = field
            bright[step * group + place] = field[:half_h] ** 2 + field[half_h:] ** 2
        return carry

    lax.fori_loop(0, leds // group, some, 0)

    def one_frame(frame, carry):
        total = bright[patterns[0, frame]]
        for lit in range(1, patterns.shape[0]):
            total += bright[patterns[lit, frame]]
        estimate_ref[frame] = total
        return carry

    lax.fori_loop(0, patterns.shape[1], one_frame, 0)
    for load in loads:
        load.wait()


def all_fields(spectrum, pupil, patterns, led_row, led_col, tables, handed, group=8):
    rows, cols = tables
    leds = led_row.shape[0]
    _, height, width = spectrum.shape
    half_h, half_w = height // 2, width // 2
    high, low = two_parts(rows)
    return pl.pallas_call(
        functools.partial(field_kernel, group=group),
        out_shape=(
            jax.ShapeDtypeStruct((leds, 2 * half_h, half_w), F32),
            jax.ShapeDtypeStruct((patterns.shape[1], half_h, half_w), F32),
            *(jax.ShapeDtypeStruct(table.shape, table.dtype) for table in handed),
        ),
        in_specs=[pl.BlockSpec(memory_space=SMEM)] * 3
        + vmem_spec(4)
        + [pl.BlockSpec(memory_space=pltpu.HBM)] * 2,
        out_specs=tuple(vmem_spec(4)),
        scratch_shapes=[
            pltpu.VMEM((2, height + 8, width + 128), F32),
            pltpu.VMEM((leds, half_h, half_w), F32),
            pltpu.SemaphoreType.DMA((2,)),
        ],
        compiler_params=pltpu.CompilerParams(vmem_limit_bytes=LIMIT),
        cost_estimate=pl.CostEstimate(
            flops=8_000_000_000, bytes_accessed=16_000_000, transcendentals=0
        ),
        name="fields",
    )(
        led_row, led_col, patterns, spectrum, pupil, np.concatenate(two_parts(cols)),
        np.concatenate([high, high, low], axis=1),
        *(pltpu.with_memory_space_constraint(jnp.asarray(t), pltpu.HBM) for t in handed),
    )


def window_kernel(dq_ref, rows_ref, small_ref, window_ref, *, frames, core):
    slabs, lines, half_w = dq_ref.shape
    lines -= 16
    half_h = rows_ref.shape[0]
    lr_sum, line = small_ref[:half_h, :128], small_ref[half_h:]
    rows_here = lines // frames
    height = slabs * rows_here
    over_y = 1.0 / (core * (height * (height * height - 1) / 12.0))
    over_x = 1.0 / (height * (core * (core * core - 1) / 12.0))
    lane = lax.broadcasted_iota(jnp.int32, (8, 128), 1)
    notes = [rows_value(dq_ref[slab, lines:]) for slab in range(slabs)]
    slopes = functools.reduce(jnp.add, notes)
    slopes = slopes * jnp.where(lane % 2 == 0, over_y, over_x)
    slab_means = jnp.zeros((8, 128), F32)
    for slab in range(slabs):
        slab_means = jnp.where(lane == slab, notes[slab][:, 6:7], slab_means)
    if rows_here % 16:
        values = [dq_ref[slab, :lines].astype(F32) for slab in range(slabs)]
    else:
        values = [dq_ref[slab, :lines] for slab in range(slabs)]
    means = []
    for frame in range(frames):
        cut = slice(frame * rows_here, (frame + 1) * rows_here)
        whole = jnp.concatenate([v[cut] for v in values], axis=0).astype(BF16)
        window = mm(rows_ref[...], jnp.concatenate([whole, whole], axis=0))
        level = jnp.sum(lr_sum * slab_means[frame : frame + 1], axis=1, keepdims=True)
        window = window + level
        tilt_y, tilt_x = 0.0, 0.0
        for side in range(3):
            tilt_y += line[2 * side : 2 * side + 1] * slopes[frame : frame + 1, 2 * side : 2 * side + 1]
            tilt_x += line[2 * side + 1 : 2 * side + 2] * slopes[frame : frame + 1, 2 * side + 1 : 2 * side + 2]
        window = window - lr_sum[:, 127:128] * tilt_y - tilt_x
        mean = jnp.sum(window, axis=0, keepdims=True)
        mean = jnp.sum(mean, axis=1, keepdims=True) * (1.0 / (half_h * half_w))
        means.append(jnp.broadcast_to(mean, (1, 128)))
        window_ref[frame * half_h : (frame + 1) * half_h] = (window - mean).astype(BF16)
    means = jnp.concatenate(means + [jnp.zeros((8 - frames, 128), F32)], axis=0)
    window_ref[frames * half_h :] = parts_rows(means, half_w)


def tilt_lines(width, margin, core, lc):
    local = np.arange(width) - margin
    lines = []
    for begin, end, shift in ((0, core, 0), (-margin, 0, core), (core, core + margin, -core)):
        on = (local >= begin) & (local < end)
        lines.append(on.astype(np.float64) @ lc)
        lines.append(((local + shift - (core - 1) / 2.0) * on) @ lc)
    return np.stack(lines + lines[:2])


def window_tables(tiles, passes, margin, core):
    lr, lc = passes
    half_h, height = lr.shape
    sums = np.zeros((half_h, lc.shape[1]))
    sums[:, :tiles] = lr.reshape(half_h, tiles, height // tiles).sum(axis=2)
    sums[:, 127] = lr @ (np.arange(height) - (height - 1) / 2.0)
    small = np.concatenate([sums, tilt_lines(lc.shape[0], margin, core, lc)])
    return np.concatenate(two_parts(lr), axis=1), small.astype(np.float32)


def windows(arrived, rows, small, frames, core):
    half_h, half_w = rows.shape[0], arrived.shape[2]
    return pl.pallas_call(
        functools.partial(window_kernel, frames=frames, core=core),
        out_shape=jax.ShapeDtypeStruct((frames * half_h + 16, half_w), BF16),
        in_specs=vmem_spec(3),
        out_specs=pl.BlockSpec(memory_space=VMEM),
        compiler_params=pltpu.CompilerParams(vmem_limit_bytes=LIMIT),
        name="windows",
    )(arrived, rows, small)


def fetch_kernel(after, field_hbm, field_ref, sem):
    load = pltpu.make_async_copy(field_hbm, field_ref, sem)
    load.start()
    load.wait()


def fetch(field, after):
    return pl.pallas_call(
        fetch_kernel,
        out_shape=jax.ShapeDtypeStruct(field.shape, F32),
        in_specs=[pl.BlockSpec(memory_space=pl.ANY), pl.BlockSpec(memory_space=pltpu.HBM)],
        out_specs=pl.BlockSpec(memory_space=VMEM),
        scratch_shapes=[pltpu.SemaphoreType.DMA],
        compiler_params=pltpu.CompilerParams(vmem_limit_bytes=LIMIT),
        cost_estimate=pl.CostEstimate(flops=0, bytes_accessed=16_000_000, transcendentals=0),
        name="fetch",
    )(after, pltpu.with_memory_space_constraint(field, pltpu.HBM))


def across(left, right):
    dims = (((1,), (1,)), ((), ()))
    return lax.dot_general(left, right, dims, preferred_element_type=F32)


def update_kernel(
    led_row, led_col, patterns, where, field_ref, estimate_ref, w0, w1, w2, w3,
    spec_ref, pupil_ref, small_ref, big_hbm,
    fresh_ref, high_ref, low_ref, first_ref, second_ref,
    weight, grads, big, big_sem, *, group,
):
    leds, half_h, half_w = weight.shape
    band_rows, band_cols = pupil_ref.shape[1:]
    height, width = spec_ref.shape[1:]
    frames_here = w0.shape[0] // half_h
    is_odd = where[1] == 1
    big_load = pltpu.make_async_copy(big_hbm, big, big_sem)
    big_load.start()
    grads[...] = jnp.zeros_like(grads)
    weight[...] = jnp.zeros_like(weight)
    for slot, window in enumerate((w0, w1, w2, w3)):
        owner = jnp.bitwise_xor(where[0], slot)
        means = rows_value(window[frames_here * half_h :])
        for place in range(frames_here):
            frame = owner * frames_here + place
            value = estimate_ref[frame] - means[place : place + 1, 0:1]
            value -= window[place * half_h : (place + 1) * half_h].astype(F32)
            for lit in range(patterns.shape[0]):
                weight[patterns[lit, frame]] += value

    table_rows = 2 * band_rows

    def some(step, carry):
        left_rows = small_ref[: 2 * table_rows]
        cols_hi = small_ref[2 * table_rows : 2 * table_rows + 2 * half_w]
        cols_lo = small_ref[2 * table_rows + 2 * half_w :]
        backs = []
        for place in range(group):
            q = weight[step * group + place]
            field = field_ref[step * group + place]
            high, low = split(jnp.concatenate([field[:half_h] * q, field[half_h:] * q], axis=0))
            both = mm(left_rows, high)
            back = both[:table_rows] + both[table_rows:] + mm(left_rows[:table_rows], low)
            backs.append(jnp.concatenate([back[:band_rows], back[band_rows:]], axis=1))
        high, low = split(jnp.concatenate(backs, axis=0))
        boxes = mm(high, cols_hi) + mm(high, cols_lo) + mm(low, cols_hi)
        for place in range(group):
            led = step * group + place
            one = boxes[place * band_rows : (place + 1) * band_rows]
            back_re, back_im = one[:, :band_cols], one[:, band_cols:]
            parts = (
                pupil_ref[0] * back_re + pupil_ref[1] * back_im,
                pupil_ref[0] * back_im - pupil_ref[1] * back_re,
            )
            area, down, right = box_area(led_row[led], led_col[led], band_rows, band_cols)
            for part in range(2):
                filled = jnp.concatenate([parts[part], jnp.zeros((8, band_cols), F32)], axis=0)
                filled = pltpu.roll(filled, down, 0)
                filled = jnp.concatenate([filled, jnp.zeros((band_rows + 8, 128), F32)], axis=1)
                grads[(part, *area)] += pltpu.roll(filled, right, 1)
        return carry

    lax.fori_loop(0, leds // group, some, 0)
    fresh_re = spec_ref[0] - (4.0 * STEP) * grads[0, :height, :width]
    fresh_im = spec_ref[1] - (4.0 * STEP) * grads[1, :height, :width]
    fresh_ref[0] = fresh_re
    fresh_ref[1] = fresh_im
    re_hi, re_lo = split(fresh_re)
    im_hi, im_lo = split(fresh_im)
    high = jnp.concatenate([re_hi, im_hi], axis=0)
    low = jnp.concatenate([re_lo, im_lo], axis=0)
    big_load.wait()
    full = 2 * height
    rows_hi, rows_lo = big[:full], big[full : 2 * full]
    spread = mm(rows_hi, high) + mm(rows_lo, high) + mm(rows_hi, low)
    high, low = split(jnp.concatenate([spread[:height], spread[height:]], axis=1))
    high_ref[...] = high
    low_ref[...] = low
    side_rows = 2 * first_ref.shape[0]
    side = big[2 * full :]
    side_hi = jnp.concatenate([side[:side_rows], side[side_rows : 2 * side_rows]], axis=1)
    side_lo = jnp.concatenate([side[2 * side_rows : 3 * side_rows], side[3 * side_rows :]], axis=1)
    sides = across(side_hi, high) + across(side_lo, high) + across(side_hi, low)
    half = side_rows // 2
    to_left, to_right = sides[:half], sides[half:]
    first_ref[...] = jnp.where(is_odd, to_left, to_right)
    second_ref[...] = jnp.where(is_odd, to_right, to_left)


def update(
    field, estimate, window_parts, spectrum, pupil, patterns, led_row, led_col, where, tables,
    margin, group=8,
):
    rows, cols = tables
    leds = led_row.shape[0]
    _, height, width = spectrum.shape
    half_h, half_w = height // 2, width // 2
    fr_re, fr_im = wave(np.arange(height), np.arange(height) - height // 2, height, height)
    full_rows = np.block([[fr_re, -fr_im], [fr_im, fr_re]])
    side_places = np.concatenate([np.arange(margin), width - margin + np.arange(margin)])
    fc_re, fc_im = wave(side_places, np.arange(width) - width // 2, width, width)
    from_re = np.concatenate([fc_re[:margin], fc_im[:margin], fc_re[margin:], fc_im[margin:]])
    from_im = np.concatenate([-fc_im[:margin], fc_re[:margin], -fc_im[margin:], fc_re[margin:]])
    sides = [two_parts(from_re), two_parts(from_im)]
    big = np.concatenate(
        [*two_parts(full_rows), sides[0][0], sides[1][0], sides[0][1], sides[1][1]]
    )
    small = np.concatenate([*two_parts(rows.T), *two_parts(cols.T)])
    out_shape = (
        jax.ShapeDtypeStruct(spectrum.shape, F32),
        jax.ShapeDtypeStruct((height, 2 * width), BF16),
        jax.ShapeDtypeStruct((height, 2 * width), BF16),
        jax.ShapeDtypeStruct((2 * margin, height), F32),
        jax.ShapeDtypeStruct((2 * margin, height), F32),
    )
    return pl.pallas_call(
        functools.partial(update_kernel, group=group),
        out_shape=out_shape,
        in_specs=[pl.BlockSpec(memory_space=SMEM)] * 4
        + vmem_spec(9)
        + [pl.BlockSpec(memory_space=pltpu.HBM)],
        out_specs=tuple(vmem_spec(5)),
        scratch_shapes=[
            pltpu.VMEM((leds, half_h, half_w), F32),
            pltpu.VMEM((2, height + 8, width + 128), F32),
            pltpu.VMEM(big.shape, BF16),
            pltpu.SemaphoreType.DMA,
        ],
        compiler_params=pltpu.CompilerParams(vmem_limit_bytes=LIMIT),
        name="update",
    )(
        led_row, led_col, patterns, where, field, estimate, *window_parts, spectrum, pupil, small,
        pltpu.with_memory_space_constraint(jnp.asarray(big), pltpu.HBM),
    )


def object_kernel(high_ref, low_ref, table_ref, out_ref):
    core = out_ref.shape[1]
    width = high_ref.shape[1] // 2
    re_im_hi, re_im_lo = table_ref[: 2 * core], table_ref[2 * core :]
    parts = []
    for part in range(2):
        cut = slice(part * width, (part + 1) * width)
        z_hi, z_lo = high_ref[:, cut], low_ref[:, cut]
        parts.append(across(re_im_hi, z_hi) + across(re_im_lo, z_hi) + across(re_im_hi, z_lo))
    out_ref[0] = parts[0][:core] - parts[1][core:]
    out_ref[1] = parts[0][core:] + parts[1][:core]


def object_core(high, low, margin, core):
    height, width = high.shape[0], high.shape[1] // 2
    col_re, col_im = wave(margin + np.arange(core), np.arange(width) - width // 2, width, width)
    table = np.concatenate(two_parts(np.concatenate([col_re, col_im])))
    return pl.pallas_call(
        object_kernel,
        out_shape=jax.ShapeDtypeStruct((2, core, height), F32),
        in_specs=vmem_spec(3),
        out_specs=pl.BlockSpec(memory_space=VMEM),
        compiler_params=pltpu.CompilerParams(vmem_limit_bytes=LIMIT),
        cost_estimate=pl.CostEstimate(
            flops=3_000_000_000, bytes_accessed=5_000_000, transcendentals=0
        ),
        name="object",
    )(high, low, table)


def blend_kernel(where, first_ref, second_ref, in_ref, out_ref):
    side = pl.program_id(0)
    tile = where[2]
    is_odd = where[1] == 1
    margin = out_ref.shape[1]
    k = lax.broadcasted_iota(jnp.int32, (margin, 1), 0).astype(F32)
    span = 2.0 * margin
    at_left = side == 0
    own_w = jnp.where(at_left, k + margin + 0.5, span - k - 0.5) / span
    other_w = jnp.where(at_left, margin - k - 0.5, k + 0.5) / span
    has_other = jnp.where(at_left, tile > 0, tile < where[3] - 1)
    own_w = jnp.where(has_other, own_w, 1.0)
    other_w = jnp.where(has_other, other_w, 0.0)
    use_first = jnp.where(at_left, is_odd, jnp.logical_not(is_odd))
    other = jnp.where(use_first, first_ref[...], second_ref[...])
    for part in range(2):
        cut = slice(part * margin, (part + 1) * margin)
        out_ref[part] = in_ref[part] * own_w + other[cut] * other_w


def blend(core_part, first, second, where, margin):
    _, core, height = core_part.shape
    last = core // margin - 1
    block = pl.BlockSpec((2, margin, height), lambda i: (0, i * last, 0))
    whole = pl.BlockSpec(first.shape, lambda i: (0, 0))
    return pl.pallas_call(
        blend_kernel,
        grid=(2,),
        out_shape=jax.ShapeDtypeStruct(core_part.shape, F32),
        in_specs=[pl.BlockSpec(memory_space=SMEM), whole, whole, block],
        out_specs=block,
        input_output_aliases={3: 0},
        compiler_params=pltpu.CompilerParams(vmem_limit_bytes=LIMIT),
        name="blend",
    )(where, first, second, core_part)


def body(raw, scales, flat, spectrum, pupil, patterns, led_row, led_col):
    height, core = flat.shape
    margin = OV // 2
    width = core + OV
    tiles = lax.axis_size("tile")
    tile = lax.axis_index("tile")
    grp = lax.axis_index("grp")
    frames_here = raw.shape[0]
    band_rows, band_cols = pupil.shape[1:]
    spectrum_tile = spectrum[0]
    patterns = patterns.T
    odd = lax.rem(tile, 2)
    where = jnp.stack([grp, odd, tile, jnp.int32(tiles)]).astype(jnp.int32)

    swap_a = [(i, i ^ 1) for i in range(tiles)]
    swap_b = [(i, ((i + 1) ^ 1) - 1) for i in range(1, tiles - 1)]

    def neighbours(for_a, for_b):
        return lax.ppermute(for_a, "tile", swap_a), lax.ppermute(for_b, "tile", swap_b)

    tables = stacked_tables(height, width, band_rows, band_cols)
    passes = (low_pass(height, band_rows), low_pass(width, band_cols).T)

    by_rows = gains_by_rows(flat.T, tiles, width)
    dequantized = dequantize(raw, scales, by_rows, tiles, core, margin)
    gains = lax.all_to_all(by_rows, "tile", split_axis=0, concat_axis=0, tiled=True)
    narrow = strips(dequantized, gains, where, passes[1], frames_here, core, margin)
    arrived = lax.all_to_all(narrow, "tile", split_axis=0, concat_axis=0, tiled=True)
    handed = window_tables(tiles, passes, margin, core)
    field, estimate, rows, small = all_fields(
        spectrum_tile, pupil, patterns, led_row, led_col, tables, handed
    )
    window = windows(arrived, rows, small, frames_here, core)
    field = fetch(field, window)

    swap_core = [(i, i ^ 1) for i in range(4)]
    swap_chip = [(i, i ^ 2) for i in range(4)]
    other = functools.partial(lax.ppermute, axis_name="grp")
    window_2 = other(window, perm=swap_chip)
    window_1 = other(window, perm=swap_core)
    window_2, field = lax.optimization_barrier((window_2, field))
    window_3 = other(window_2, perm=swap_core)

    fresh, high, low, for_a, for_b = update(
        field, estimate, (window, window_1, window_2, window_3), spectrum_tile, pupil, patterns,
        led_row, led_col, where, tables, margin,
    )
    side_a, side_b = neighbours(for_a, for_b)
    core_part = object_core(high, low, margin, core)
    stitched = blend(core_part, side_a, side_b, where, margin)
    return fresh[None], jnp.transpose(stitched, (0, 2, 1))


def solution(mesh):
    return jax.shard_map(
        body,
        mesh=mesh,
        in_specs=(
            P("grp", "tile", None),
            P("grp", "tile", None),
            P(None, "tile"),
            P("tile", None, None, None),
            P(),
            P(),
            P(),
            P(),
        ),
        out_specs=(P("tile", None, None, None), P(None, None, "tile")),
        check_vma=False,
    )
```

time: 87.5 us -> 68.2 us (0.78)
  the two profiles are of different devices: /device:TPU:22 before, /device:TPU:24 now
where the time goes in v3:
time: 68.2 us; the launch traced here: 67.6 us
  Pallas kernels  31.2 us (46%)
  starting transfers between devices  18.6 us (27%)
  waiting for transfers between devices  9.44 us (14%)
  local copies, waits for them, and re-layouts  7.45 us (11%)
  between operations  0.79 us (1%)
    pallas_call x1, Pallas kernels, update(): pl.pallas_call(functools.partial(update_kernel, group=group), out_shape=o...  9.95 us
    unnamed x28, local copies, waits for them, and re-layouts  7.45 us
    pallas_call x1, Pallas kernels, all_fields(): pl.pallas_call(functools.partial(field_kernel, group=group), out_shape=(j...  7.3 us
    all_to_all x1, starting transfers between devices, body(): lax.all_to_all(narrow, 'tile', split_axis=0, concat_axis=0, tiled=True)  6.28 us
    all_to_all x1, starting transfers between devices, body(): lax.all_to_all(by_rows, 'tile', split_axis=0, concat_axis=0, tiled=True)  6.07 us
    pallas_call x1, Pallas kernels, fetch(): pl.pallas_call(fetch_kernel, out_shape=jax.ShapeDtypeStruct(field.shape,...  3.52 us
    all_to_all x1, waiting for transfers between devices, body(): lax.all_to_all(by_rows, 'tile', split_axis=0, concat_axis=0, tiled=True)  3.49 us
    pallas_call x1, Pallas kernels, strips(): pl.pallas_call(functools.partial(strips_kernel, frames=frames, core=core,...  3.1 us
  transfers between devices with their start and end apart: 7, of which 4 were waited for; matrix products, arithmetic and copies ran while one was open for 0% of the time, Pallas kernels for 21%

profile of v3, /device:TPU:24, one launch (start us, length us, event | category | flops | bytes accessed | tf_op | source)
XLA Modules:
  0.0 67.6 jit_solution(3812862796734655491)
XLA Ops:
  0.6 2.1 %gains.1.after = bf16[8,32,512]{2,1,0:T(8,128)(2,1)} custom-call(f32[480,256]{1,0:T(8,128)} %bitcast.17), custom_call_target="tpu_custom_call" | custom-call | tf_op jit(solution)/shard_map/gains/pallas_call | solution.py:108
  2.7 6.1 %all-to-all-start = ((bf16[8,32,512]{2,1,0:T(8,128)(2,1)}), bf16[8,32,512]{2,1,0:T(8,128)(2,1)S(1)}, u32[]{:S(2)}, u32[]{:S(2)}) async-start(bf16[8,32,512]{2,1,0:T(8,128)(2,1)} %gains.1.after), calls=%async_computation | async-start | bytes 524288 | tf_op jit(solution)/shard_map/all_to_all | solution.py:661
  8.8 0.1 pad_add_fusion.where
  8.8 1.2 %copy-done.9 = bf16[4,32,3840]{2,1,0:T(8,128)(2,1)S(1)} copy-done((bf16[4,32,3840]{2,1,0:T(8,128)(2,1)S(1)}, bf16[4,32,3840]{2,1,0:T(8,128)(2,1)}, u32[]{:S(2)}) %copy-start.9) | copy-done | bytes 983064
  10.0 0.7 %copy-done.10 = bf16[4,8,120]{2,1,0:T(8,128)(2,1)S(1)} copy-done((bf16[4,8,120]{2,1,0:T(8,128)(2,1)S(1)}, bf16[4,8,120]{2,1,0:T(8,128)(2,1)}, u32[]{:S(2)}) %copy-start.10) | copy-done | bytes 7704
  10.7 0.7 %dequantize.1.dq_ref = f32[8,128,512]{2,1,0:T(8,128)S(1)} custom-call(bf16[128,3840]{1,0:T(8,128)(2,1)S(1)} %bitcast.14, bf16[32,120]{1,0:T(8,128)(2,1)S(1)} %bitcast.15, bf16[8,32,512]{2,1,0:T(8,128)(2,1)} %gains.1.after), custom_call_target="tpu_custom_call" | custom-call | flops 2000000000 | bytes 4000000 | tf_op jit(solution)/shard_map/dequantize/pallas_call | solution.py:152
  11.4 0.0 copy-start.5
  11.5 0.0 copy-start.6
  11.5 0.0 copy-start.7
  11.5 0.0 copy-start.8
  11.5 0.0 copy-start.13
  11.5 3.5 %all-to-all-done.gains_ref = bf16[8,32,512]{2,1,0:T(8,128)(2,1)S(1)} async-done(((bf16[8,32,512]{2,1,0:T(8,128)(2,1)}), bf16[8,32,512]{2,1,0:T(8,128)(2,1)S(1)}, u32[]{:S(2)}, u32[]{:S(2)}) %all-to-all-start) | async-done | bytes 262176 | tf_op jit(solution)/shard_map/all_to_all | solution.py:661
  15.0 3.1 %strips.1 = bf16[8,144,256]{2,1,0:T(8,128)(2,1)} custom-call(s32[4]{0:T(128)S(1)} %pad_add_fusion.where, f32[8,128,512]{2,1,0:T(8,128)S(1)} %dequantize.1.dq_ref, bf16[8,32,512]{2,1,0:T(8,128)(2,1)S(1)} %all-to-all-done.gains_ref, bf16[1024,256]{1,0:T(8,128)(2,1)S(1)} %copy-done.4), custom_call_target="tpu_custom_call" | custom-call | tf_op jit(solution)/shard_map/strips/pallas_call | solution.py:232
  18.1 6.3 %all-to-all-start.1 = ((bf16[8,144,256]{2,1,0:T(8,128)(2,1)}), bf16[8,144,256]{2,1,0:T(8,128)(2,1)S(1)}, u32[]{:S(2)}, u32[]{:S(2)}) async-start(bf16[8,144,256]{2,1,0:T(8,128)(2,1)} %strips.1), calls=%async_computation.1 | async-start | bytes 1179648 | tf_op jit(solution)/shard_map/all_to_all | solution.py:663
  24.4 0.0 copy-start.1
  24.4 1.2 %copy-done.1 = f32[1,2,256,512]{3,2,1,0:T(8,128)S(1)} copy-done((f32[1,2,256,512]{3,2,1,0:T(8,128)S(1)}, f32[1,2,256,512]{3,2,1,0:T(8,128)}, u32[]{:S(2)}) %copy-start.1) | copy-done | bytes 1048600
  25.6 1.0 %copy-done.12 = bf16[512,512]{1,0:T(8,128)(2,1)S(1)} copy-done((bf16[512,512]{1,0:T(8,128)(2,1)S(1)}, bf16[512,512]{1,0:T(8,128)(2,1)}, u32[]{:S(2)}) %copy-start.12) | copy-done | bytes 524312
  26.7 7.3 %fields.1 = (f32[32,256,256]{2,1,0:T(8,128)S(1)}, f32[16,128,256]{2,1,0:T(8,128)S(1)}, bf16[128,512]{1,0:T(8,128)(2,1)S(1)}, f32[136,256]{1,0:T(8,128)S(1)}) custom-call(s32[32]{0:T(128)S(1)} %copy-done.7, s32[32]{0:T(128)S(1)} %copy-done.8, s32[4,16]{1,0:T(4,128)S(1)} %bitcast.12, f32[2,256,512]{2,1,0:T(8,128)S(1)} %bitcast.10, ...), custom_call_target="tpu_custom_call" | custom-call | flops 8000000000 | bytes 16000000 | tf_op jit(solution)/shard_map/fields/pallas_call | solution.py:314
  34.0 3.2 %copy-done = f32[32,256,256]{2,1,0:T(8,128)} copy-done((f32[32,256,256]{2,1,0:T(8,128)}, f32[32,256,256]{2,1,0:T(8,128)S(1)}, u32[]{:S(2)}) %copy-start) | copy-done | bytes 8388632
  37.2 0.0 all-to-all-done.1.dq_ref
  37.3 0.5 windows.1.after.w0
  37.8 1.6 %collective-permute-start = (bf16[528,256]{1,0:T(8,128)(2,1)S(1)}, bf16[528,256]{1,0:T(8,128)(2,1)S(1)}, u32[]{:S(2)}, u32[]{:S(2)}) collective-permute-start(bf16[528,256]{1,0:T(8,128)(2,1)S(1)} %windows.1.after.w0), channel_id=1, source_target_pairs={{0,16},{8,24},{16,0},{24,8},{1,17},{9,25},{17,1},{25,9},{2,18},{10... | collective-permute-start | bytes 811016 | tf_op jit(solution)/shard_map/ppermute | solution.py:674
  39.3 0.0 collective-permute-start.1
  39.3 3.5 %fetch.1.field_ref = f32[32,256,256]{2,1,0:T(8,128)S(1)} custom-call(bf16[528,256]{1,0:T(8,128)(2,1)S(1)} %windows.1.after.w0, f32[32,256,256]{2,1,0:T(8,128)} %copy-done), custom_call_target="tpu_custom_call" | custom-call | bytes 16000000 | tf_op jit(solution)/shard_map/fetch/pallas_call | solution.py:421
  42.8 2.3 %collective-permute-done.w2 = bf16[528,256]{1,0:T(8,128)(2,1)S(1)} collective-permute-done((bf16[528,256]{1,0:T(8,128)(2,1)S(1)}, bf16[528,256]{1,0:T(8,128)(2,1)S(1)}, u32[]{:S(2)}, u32[]{:S(2)}) %collective-permute-start) | collective-permute-done | bytes 270368 | tf_op jit(solution)/shard_map/ppermute | solution.py:674
  45.1 1.5 %collective-permute-done.2.w3 = bf16[528,256]{1,0:T(8,128)(2,1)S(1)} collective-permute-done((bf16[528,256]{1,0:T(8,128)(2,1)S(1)}, bf16[528,256]{1,0:T(8,128)(2,1)S(1)}, u32[]{:S(2)}, u32[]{:S(2)}) %collective-permute-start.2) | collective-permute-done | bytes 270368 | tf_op jit(solution)/shard_map/ppermute | solution.py:677
  46.7 9.9 %update.1 = (f32[2,256,512]{2,1,0:T(8,128)}, bf16[256,1024]{1,0:T(8,128)(2,1)S(1)}, bf16[256,1024]{1,0:T(8,128)(2,1)S(1)}, f32[32,256]{1,0:T(8,128)S(1)}, f32[32,256]{1,0:T(8,128)S(1)}) custom-call(s32[32]{0:T(128)S(1)} %copy-done.7, s32[32]{0:T(128)S(1)} %copy-done.8, s32[4,16]{1,0:T(4,128)S(1)} %bitcast.13, s32[4]{0:T(128)S(1)} %pad_add_fusion.where, ...), custom_call_target="tpu_custom_call" | custom-call | tf_op jit(solution)/shard_map/update/pallas_call | solution.py:548
  56.6 2.8 %collective-permute-start.3 = (f32[32,256]{1,0:T(8,128)S(1)}, f32[32,256]{1,0:T(8,128)S(1)}, u32[]{:S(2)}, u32[]{:S(2)}) collective-permute-start(f32[32,256]{1,0:T(8,128)S(1)} %get-tuple-element.20), channel_id=1, source_target_pairs={{0,1},{1,0},{2,3},{3,2},{4,5},{5,4},{6,7},{7,6},{8,9},{9,8},{10,11... | collective-permute-start | bytes 98312 | tf_op jit(solution)/shard_map/ppermute | solution.py:654
  59.5 1.9 %collective-permute-start.4 = (f32[32,256]{1,0:T(8,128)S(1)}, f32[32,256]{1,0:T(8,128)S(1)}, u32[]{:S(2)}, u32[]{:S(2)}) collective-permute-start(f32[32,256]{1,0:T(8,128)S(1)} %get-tuple-element.21), channel_id=1, source_target_pairs={{1,2},{2,1},{3,4},{4,3},{5,6},{6,5},{9,10},{10,9},{11,12},{12,11},... | collective-permute-start | bytes 98312 | tf_op jit(solution)/shard_map/ppermute | solution.py:654
  61.4 2.7 %object.1.in_ref = f32[2,480,256]{2,1,0:T(8,128)} custom-call(bf16[256,1024]{1,0:T(8,128)(2,1)S(1)} %get-tuple-element.22.high_ref, bf16[256,1024]{1,0:T(8,128)(2,1)S(1)} %get-tuple-element.23.low_ref, bf16[1920,512]{1,0:T(8,128)(2,1)S(1)} %copy-done.11), custom_call_target="tpu_custom_call" | custom-call | flops 3000000000 | bytes 5000000 | tf_op jit(solution)/shard_map/object/pallas_call | solution.py:586
  64.1 2.1 %collective-permute-done.4.second_ref = f32[32,256]{1,0:T(8,128)S(1)} collective-permute-done((f32[32,256]{1,0:T(8,128)S(1)}, f32[32,256]{1,0:T(8,128)S(1)}, u32[]{:S(2)}, u32[]{:S(2)}) %collective-permute-start.4) | collective-permute-done | bytes 32800 | tf_op jit(solution)/shard_map/ppermute | solution.py:654
  66.2 1.5 %blend.1 = f32[2,480,256]{2,1,0:T(8,128)} custom-call(s32[4]{0:T(128)S(1)} %pad_add_fusion.where, f32[32,256]{1,0:T(8,128)S(1)} %collective-permute-done.3.first_ref, f32[32,256]{1,0:T(8,128)S(1)} %collective-permute-done.4.second_ref, f32[2,480,256]{2,1,0:T(8,128)} %object.1.in_ref), custom_call_target="tpu_custom_call", output_to_operand_aliasing={{}: (3, {})} | custom-call | tf_op jit(solution)/shard_map/blend/pallas_call | solution.py:624
  (20 shorter events, 0.0 us)
Async XLA Ops:
  2.7 12.3 %all-to-all-start = ((bf16[8,32,512]{2,1,0:T(8,128)(2,1)}), bf16[8,32,512]{2,1,0:T(8,128)(2,1)S(1)}, u32[]{:S(2)}, u32[]{:S(2)}) async-start(bf16[8,32,512]{2,1,0:T(8,128)(2,1)} %gains.1.after), calls=%async_computation | async-start | bytes 524288 | tf_op jit(solution)/shard_map/all_to_all | solution.py:661
  8.8 1.2 %copy-start.9 = (bf16[4,32,3840]{2,1,0:T(8,128)(2,1)S(1)}, bf16[4,32,3840]{2,1,0:T(8,128)(2,1)}, u32[]{:S(2)}) copy-start(bf16[4,32,3840]{2,1,0:T(8,128)(2,1)} %param.16) | copy-start | bytes 2949124
  10.0 0.7 %copy-start.10 = (bf16[4,8,120]{2,1,0:T(8,128)(2,1)S(1)}, bf16[4,8,120]{2,1,0:T(8,128)(2,1)}, u32[]{:S(2)}) copy-start(bf16[4,8,120]{2,1,0:T(8,128)(2,1)} %param.17) | copy-start | bytes 23044
  10.7 4.3 %copy-start.4 = (bf16[1024,256]{1,0:T(8,128)(2,1)S(1)}, bf16[1024,256]{1,0:T(8,128)(2,1)}, u32[]{:S(2)}) copy-start(bf16[1024,256]{1,0:T(8,128)(2,1)} %constant.31.clone.lc_ref) | copy-start | bytes 1572868
  11.4 12.9 %copy-start.5 = (f32[2,64,128]{2,1,0:T(8,128)S(1)}, f32[2,64,128]{2,1,0:T(8,128)}, u32[]{:S(2)}) copy-start(f32[2,64,128]{2,1,0:T(8,128)} %pupil_ref.3) | copy-start | bytes 196612
  11.5 12.9 %copy-start.6 = (s32[16,4]{0,1:T(4,128)S(1)}, s32[16,4]{0,1:T(4,128)}, u32[]{:S(2)}) copy-start(s32[16,4]{0,1:T(4,128)} %param.21) | copy-start | bytes 772
  11.5 12.9 %copy-start.7 = (s32[32]{0:T(128)S(1)}, s32[32]{0:T(128)}, u32[]{:S(2)}) copy-start(s32[32]{0:T(128)} %led_row.3) | copy-start | bytes 388
  11.5 12.9 %copy-start.8 = (s32[32]{0:T(128)S(1)}, s32[32]{0:T(128)}, u32[]{:S(2)}) copy-start(s32[32]{0:T(128)} %led_col.3) | copy-start | bytes 388
  11.5 12.9 %copy-start.13 = (bf16[256,384]{1,0:T(8,128)(2,1)S(1)}, bf16[256,384]{1,0:T(8,128)(2,1)}, u32[]{:S(2)}) copy-start(bf16[256,384]{1,0:T(8,128)(2,1)} %constant.35.clone.rows_ref) | copy-start | bytes 589828
  18.1 19.2 %all-to-all-start.1 = ((bf16[8,144,256]{2,1,0:T(8,128)(2,1)}), bf16[8,144,256]{2,1,0:T(8,128)(2,1)S(1)}, u32[]{:S(2)}, u32[]{:S(2)}) async-start(bf16[8,144,256]{2,1,0:T(8,128)(2,1)} %strips.1), calls=%async_computation.1 | async-start | bytes 1179648 | tf_op jit(solution)/shard_map/all_to_all | solution.py:663
  24.4 1.2 %copy-start.1 = (f32[1,2,256,512]{3,2,1,0:T(8,128)S(1)}, f32[1,2,256,512]{3,2,1,0:T(8,128)}, u32[]{:S(2)}) copy-start(f32[1,2,256,512]{3,2,1,0:T(8,128)} %param.19) | copy-start | bytes 3145732
  25.6 1.0 %copy-start.12 = (bf16[512,512]{1,0:T(8,128)(2,1)S(1)}, bf16[512,512]{1,0:T(8,128)(2,1)}, u32[]{:S(2)}) copy-start(bf16[512,512]{1,0:T(8,128)(2,1)} %constant.34.clone.cols_ref) | copy-start | bytes 1572868
  34.0 3.2 %copy-start = (f32[32,256,256]{2,1,0:T(8,128)}, f32[32,256,256]{2,1,0:T(8,128)S(1)}, u32[]{:S(2)}) copy-start(f32[32,256,256]{2,1,0:T(8,128)S(1)} %get-tuple-element.15.field_hbm) | copy-start | bytes 25165828
  37.8 7.4 %collective-permute-start = (bf16[528,256]{1,0:T(8,128)(2,1)S(1)}, bf16[528,256]{1,0:T(8,128)(2,1)S(1)}, u32[]{:S(2)}, u32[]{:S(2)}) collective-permute-start(bf16[528,256]{1,0:T(8,128)(2,1)S(1)} %windows.1.after.w0), channel_id=1, source_target_pairs={{0,16},{8,24},{16,0},{24,8},{1,17},{9,25},{17,1},{25,9},{2,18},{10... | collective-permute-start | bytes 811016 | tf_op jit(solution)/shard_map/ppermute | solution.py:674
  39.3 5.8 %collective-permute-start.1 = (bf16[528,256]{1,0:T(8,128)(2,1)S(1)}, bf16[528,256]{1,0:T(8,128)(2,1)S(1)}, u32[]{:S(2)}, u32[]{:S(2)}) collective-permute-start(bf16[528,256]{1,0:T(8,128)(2,1)S(1)} %windows.1.after.w0), channel_id=1, source_target_pairs={{0,8},{8,0},{16,24},{24,16},{1,9},{9,1},{17,25},{25,17},{2,10},{10... | collective-permute-start | bytes 811016 | tf_op jit(solution)/shard_map/ppermute | solution.py:675
  39.3 7.3 %copy-start.2 = (f32[1,2,256,512]{3,2,1,0:T(8,128)S(1)}, f32[1,2,256,512]{3,2,1,0:T(8,128)}, u32[]{:S(2)}) copy-start(f32[1,2,256,512]{3,2,1,0:T(8,128)} %param.19) | copy-start | bytes 3145732
  39.3 7.3 %copy-start.3 = (bf16[1280,256]{1,0:T(8,128)(2,1)S(1)}, bf16[1280,256]{1,0:T(8,128)(2,1)}, u32[]{:S(2)}) copy-start(bf16[1280,256]{1,0:T(8,128)(2,1)} %constant.37.clone.small_ref) | copy-start | bytes 1966084
  45.1 1.5 %collective-permute-start.2 = (bf16[528,256]{1,0:T(8,128)(2,1)S(1)}, bf16[528,256]{1,0:T(8,128)(2,1)S(1)}, u32[]{:S(2)}, u32[]{:S(2)}) collective-permute-start(bf16[528,256]{1,0:T(8,128)(2,1)S(1)} %collective-permute-done.w2), channel_id=1, source_target_pairs={{0,8},{8,0},{16,24},{24,16},{1,9},{9,1},{17,25},{25,17},{2,10},{10... | collective-permute-start | bytes 811016 | tf_op jit(solution)/shard_map/ppermute | solution.py:677
  46.7 14.7 %copy-start.11 = (bf16[1920,512]{1,0:T(8,128)(2,1)S(1)}, bf16[1920,512]{1,0:T(8,128)(2,1)}, u32[]{:S(2)}) copy-start(bf16[1920,512]{1,0:T(8,128)(2,1)} %constant.38.clone.table_ref) | copy-start | bytes 5898244
  56.6 7.4 %collective-permute-start.3 = (f32[32,256]{1,0:T(8,128)S(1)}, f32[32,256]{1,0:T(8,128)S(1)}, u32[]{:S(2)}, u32[]{:S(2)}) collective-permute-start(f32[32,256]{1,0:T(8,128)S(1)} %get-tuple-element.20), channel_id=1, source_target_pairs={{0,1},{1,0},{2,3},{3,2},{4,5},{5,4},{6,7},{7,6},{8,9},{9,8},{10,11... | collective-permute-start | bytes 98312 | tf_op jit(solution)/shard_map/ppermute | solution.py:654
  59.5 6.7 %collective-permute-start.4 = (f32[32,256]{1,0:T(8,128)S(1)}, f32[32,256]{1,0:T(8,128)S(1)}, u32[]{:S(2)}, u32[]{:S(2)}) collective-permute-start(f32[32,256]{1,0:T(8,128)S(1)} %get-tuple-element.21), channel_id=1, source_target_pairs={{1,2},{2,1},{3,4},{4,3},{5,6},{6,5},{9,10},{10,9},{11,12},{12,11},... | collective-permute-start | bytes 98312 | tf_op jit(solution)/shard_map/ppermute | solution.py:654

commit v4 on v3

--- a/solution.py
+++ b/solution.py
@@ -66,27 +66,19 @@
     return [pl.BlockSpec(memory_space=VMEM)] * count
 
 
-def parts_rows(values, columns):
+def parts_rows(values):
     high = values.astype(BF16).astype(F32)
-    rest = values - high
-    middle = rest.astype(BF16).astype(F32)
-    last = rest - middle
-    top = jnp.concatenate([high, middle], axis=1)
-    bottom = jnp.concatenate([last, jnp.zeros_like(last)], axis=1)
-    rows = jnp.concatenate([top, bottom], axis=0)
-    if columns > 256:
-        rows = jnp.concatenate([rows, jnp.zeros((16, columns - 256), F32)], axis=1)
-    return rows.astype(BF16)
+    return jnp.concatenate([high, values - high], axis=0).astype(BF16)
 
 
 def rows_value(rows):
     rows = rows.astype(F32)
-    return rows[:8, :128] + rows[:8, 128:256] + rows[8:, :128]
-
-
-def gains_kernel(flat_hbm, out_ref, flat, sems):
+    return rows[:8, :128] + rows[8:, :128]
+
+
+def gains_kernel(flat_hbm, out_hbm, flat, out, sems, out_sems):
     core, height = flat_hbm.shape
-    tiles, rows_here, width = out_ref.shape
+    tiles, rows_here, width = out_hbm.shape
     spans = [(begin, min(128, core - begin)) for begin in range(0, core, 128)]
     loads = []
     for number, (begin, length) in enumerate(spans):
@@ -94,13 +86,20 @@
         load = pltpu.make_async_copy(flat_hbm.at[part], flat.at[part], sems.at[number])
         load.start()
         loads.append(load)
-    for load, (begin, length) in zip(loads, spans):
+    stores = []
+    for number, (load, (begin, length)) in enumerate(zip(loads, spans)):
         load.wait()
         gains = flat[begin : begin + length] - 1.0
         if length < 128:
             gains = jnp.concatenate([gains, jnp.zeros((128 - length, height), F32)], axis=0)
         by_rows = jnp.transpose(gains, (1, 0)).reshape(tiles, rows_here, 128)
-        out_ref[:, :, begin : begin + 128] = by_rows.astype(BF16)
+        out[:, :, begin : begin + 128] = by_rows.astype(BF16)
+        part = (slice(None), slice(None), pl.ds(begin, 128))
+        store = pltpu.make_async_copy(out.at[part], out_hbm.at[part], out_sems.at[number])
+        store.start()
+        stores.append(store)
+    for store in stores:
+        store.wait()
 
 
 def gains_by_rows(flat, tiles, width):
@@ -109,8 +108,13 @@
         gains_kernel,
         out_shape=jax.ShapeDtypeStruct((tiles, height // tiles, width), BF16),
         in_specs=[pl.BlockSpec(memory_space=pltpu.HBM)],
-        out_specs=pl.BlockSpec(memory_space=VMEM),
-        scratch_shapes=[pltpu.VMEM((core, height), F32), pltpu.SemaphoreType.DMA((-(-core // 128),))],
+        out_specs=pl.BlockSpec(memory_space=pltpu.HBM),
+        scratch_shapes=[
+            pltpu.VMEM((core, height), F32),
+            pltpu.VMEM((tiles, height // tiles, width), BF16),
+            pltpu.SemaphoreType.DMA((-(-core // 128),)),
+            pltpu.SemaphoreType.DMA((-(-core // 128),)),
+        ],
         compiler_params=pltpu.CompilerParams(vmem_limit_bytes=LIMIT),
         name="gains",
     )(pltpu.with_memory_space_constraint(flat, pltpu.HBM))
@@ -162,7 +166,7 @@
     )(raw.reshape(frames * rows_here, strip), scales.reshape(-1, scales.shape[-1]), after)
 
 
-def strips_kernel(where, dq_ref, gains_ref, lc_ref, out_ref, *, frames, core, margin):
+def strips_kernel(where, dq_ref, gains_ref, lc_ref, out_hbm, out_ref, sems, *, frames, core, margin):
     tiles, lines, width = dq_ref.shape
     half_w = lc_ref.shape[1]
     rows_here = lines // frames
@@ -176,8 +180,10 @@
     lane = lax.broadcasted_iota(jnp.int32, (8, 128), 1)
     narrow_lane = lax.broadcasted_iota(jnp.int32, (1, 128), 1)
 
-    own, highs, lows = [], [], []
-    for tile in range(tiles):
+    lc_hi, lc_lo = lc_ref[:width], lc_ref[width:]
+    own, stores = [], []
+
+    def windowed(tile):
         gains = pltpu.roll(gains_ref[tile].astype(F32), margin, 1)
         if tile > 0:
             end = gains_ref[tile - 1][:, width - 128 :].astype(F32)
@@ -193,9 +199,6 @@
             )
         gains = jnp.concatenate([gains + 1.0] * frames, axis=0)
         flattened = dq_ref[tile] * gains
-        high, low = split(flattened)
-        highs.append(high)
-        lows.append(low)
         sums, lines_y = [], []
         for frame in range(frames):
             cut = slice(frame * rows_here, (frame + 1) * rows_here)
@@ -205,11 +208,9 @@
         slope_y = jnp.sum(jnp.concatenate(lines_y + blank, axis=0) * in_core, axis=1, keepdims=True)
         slope_x = jnp.sum(jnp.concatenate(sums + blank, axis=0) * xc, axis=1, keepdims=True)
         own.append(jnp.where(lane == 0, slope_y, jnp.where(lane == 1, slope_x, 0.0)))
-    high, low = jnp.concatenate(highs, axis=0), jnp.concatenate(lows, axis=0)
-    lc_hi, lc_lo = lc_ref[:width], lc_ref[width:]
-    narrow = mm(high, lc_hi) + mm(high, lc_lo) + mm(low, lc_hi)
-    for tile in range(tiles):
-        one = narrow[tile * lines : (tile + 1) * lines]
+        return split(flattened)
+
+    def finish(tile, one):
         means, centred = [], []
         for frame in range(frames):
             cut = slice(frame * rows_here, (frame + 1) * rows_here)
@@ -217,23 +218,52 @@
             mean = jnp.sum(mean, axis=1, keepdims=True) * (1.0 / (rows_here * half_w))
             means.append(mean)
             centred.append(one[cut] - mean)
-        out_ref[tile, :lines] = jnp.concatenate(centred, axis=0).astype(BF16)
+        centred = jnp.concatenate(centred, axis=0)
+        for part in range(half_w // 128):
+            columns = centred[:, part * 128 : (part + 1) * 128]
+            out_ref[tile, part * lines : (part + 1) * lines] = columns.astype(BF16)
         mean = jnp.concatenate(means + [jnp.zeros((8 - frames, 1), F32)], axis=0)
         packed = own[tile] + jnp.where(lane == 6, mean, 0.0)
         if tile > 0:
             packed += pltpu.roll(own[tile - 1], 2, 1)
         if tile < tiles - 1:
             packed += pltpu.roll(own[tile + 1], 4, 1)
-        out_ref[tile, lines:] = parts_rows(packed, half_w)
+        out_ref[tile, half_w // 128 * lines :] = parts_rows(packed)
+
+    part_tiles = max(tiles // 2, 1)
+    waiting = None
+    for begin in range(0, tiles, part_tiles):
+        both = [windowed(tile) for tile in range(begin, begin + part_tiles)]
+        high = jnp.concatenate([pair[0] for pair in both], axis=0)
+        low = jnp.concatenate([pair[1] for pair in both], axis=0)
+        if waiting is not None:
+            finish(*waiting)
+        narrow = mm(high, lc_hi) + mm(high, lc_lo) + mm(low, lc_hi)
+        for number in range(part_tiles):
+            one = (begin + number, narrow[number * lines : (number + 1) * lines])
+            if number == part_tiles - 1 and begin + part_tiles < tiles:
+                waiting = one
+            else:
+                finish(*one)
+        done = begin + part_tiles - (1 if begin + part_tiles < tiles else 0)
+        first = max(begin - 1, 0)
+        span = pl.ds(first, done - first)
+        store = pltpu.make_async_copy(out_ref.at[span], out_hbm.at[span], sems.at[begin // part_tiles])
+        store.start()
+        stores.append(store)
+    for store in stores:
+        store.wait()
 
 
 def strips(dequantized, gains, where, lc, frames, core, margin):
     tiles, lines, _ = dequantized.shape
+    shape = (tiles, lines * (lc.shape[1] // 128) + 16, 128)
     return pl.pallas_call(
         functools.partial(strips_kernel, frames=frames, core=core, margin=margin),
-        out_shape=jax.ShapeDtypeStruct((tiles, lines + 16, lc.shape[1]), BF16),
+        out_shape=jax.ShapeDtypeStruct(shape, BF16),
         in_specs=[pl.BlockSpec(memory_space=SMEM)] + vmem_spec(3),
-        out_specs=pl.BlockSpec(memory_space=VMEM),
+        out_specs=pl.BlockSpec(memory_space=pltpu.HBM),
+        scratch_shapes=[pltpu.VMEM(shape, BF16), pltpu.SemaphoreType.DMA((2,))],
         compiler_params=pltpu.CompilerParams(vmem_limit_bytes=LIMIT),
         name="strips",
     )(where, dequantized, gains, np.concatenate(two_parts(lc)))
@@ -340,25 +370,28 @@
 
 
 def window_kernel(dq_ref, rows_ref, small_ref, window_ref, *, frames, core):
-    slabs, lines, half_w = dq_ref.shape
-    lines -= 16
-    half_h = rows_ref.shape[0]
+    slabs, lines, _ = dq_ref.shape
+    half_h, half_w = rows_ref.shape[0], window_ref.shape[1]
+    halves = half_w // 128
+    lines = (lines - 16) // halves
     lr_sum, line = small_ref[:half_h, :128], small_ref[half_h:]
     rows_here = lines // frames
     height = slabs * rows_here
     over_y = 1.0 / (core * (height * (height * height - 1) / 12.0))
     over_x = 1.0 / (height * (core * (core * core - 1) / 12.0))
     lane = lax.broadcasted_iota(jnp.int32, (8, 128), 1)
-    notes = [rows_value(dq_ref[slab, lines:]) for slab in range(slabs)]
+    notes = [rows_value(dq_ref[slab, halves * lines :]) for slab in range(slabs)]
     slopes = functools.reduce(jnp.add, notes)
     slopes = slopes * jnp.where(lane % 2 == 0, over_y, over_x)
     slab_means = jnp.zeros((8, 128), F32)
     for slab in range(slabs):
         slab_means = jnp.where(lane == slab, notes[slab][:, 6:7], slab_means)
+    values = []
+    for slab in range(slabs):
+        parts = [dq_ref[slab, part * lines : (part + 1) * lines] for part in range(halves)]
+        values.append(jnp.concatenate(parts, axis=1))
     if rows_here % 16:
-        values = [dq_ref[slab, :lines].astype(F32) for slab in range(slabs)]
-    else:
-        values = [dq_ref[slab, :lines] for slab in range(slabs)]
+        values = [value.astype(F32) for value in values]
     means = []
     for frame in range(frames):
         cut = slice(frame * rows_here, (frame + 1) * rows_here)
@@ -376,7 +409,8 @@
         means.append(jnp.broadcast_to(mean, (1, 128)))
         window_ref[frame * half_h : (frame + 1) * half_h] = (window - mean).astype(BF16)
     means = jnp.concatenate(means + [jnp.zeros((8 - frames, 128), F32)], axis=0)
-    window_ref[frames * half_h :] = parts_rows(means, half_w)
+    notes = parts_rows(means)
+    window_ref[frames * half_h :] = jnp.concatenate([notes] * halves, axis=1)
 
 
 def tilt_lines(width, margin, core, lc):
@@ -400,7 +434,7 @@
 
 
 def windows(arrived, rows, small, frames, core):
-    half_h, half_w = rows.shape[0], arrived.shape[2]
+    half_h, half_w = rows.shape[0], small.shape[1]
     return pl.pallas_call(
         functools.partial(window_kernel, frames=frames, core=core),
         out_shape=jax.ShapeDtypeStruct((frames * half_h + 16, half_w), BF16),
@@ -411,23 +445,48 @@
     )(arrived, rows, small)
 
 
-def fetch_kernel(after, field_hbm, field_ref, sem):
+def add_frame(weight, patterns, frame, value):
+    for lit in range(patterns.shape[0]):
+        weight[patterns[lit, frame]] += value
+
+
+def fetch_kernel(patterns, where, estimate_ref, window, field_hbm, field_ref, weight, sem):
     load = pltpu.make_async_copy(field_hbm, field_ref, sem)
     load.start()
+    weight[...] = jnp.zeros_like(weight)
+    frames, half_h, _ = estimate_ref.shape
+    frames_here = window.shape[0] // half_h
+
+    def one_frame(frame, carry):
+        add_frame(weight, patterns, frame, estimate_ref[frame])
+        return carry
+
+    lax.fori_loop(0, frames, one_frame, 0)
+    means = rows_value(window[frames_here * half_h :])
+    for place in range(frames_here):
+        value = window[place * half_h : (place + 1) * half_h].astype(F32)
+        value = -means[place : place + 1, 0:1] - value
+        add_frame(weight, patterns, where[0] * frames_here + place, value)
     load.wait()
 
 
-def fetch(field, after):
+def fetch(field, estimate, window, patterns, where):
+    leds = field.shape[0]
     return pl.pallas_call(
         fetch_kernel,
-        out_shape=jax.ShapeDtypeStruct(field.shape, F32),
-        in_specs=[pl.BlockSpec(memory_space=pl.ANY), pl.BlockSpec(memory_space=pltpu.HBM)],
-        out_specs=pl.BlockSpec(memory_space=VMEM),
+        out_shape=(
+            jax.ShapeDtypeStruct(field.shape, F32),
+            jax.ShapeDtypeStruct((leds, *estimate.shape[1:]), F32),
+        ),
+        in_specs=[pl.BlockSpec(memory_space=SMEM)] * 2
+        + vmem_spec(2)
+        + [pl.BlockSpec(memory_space=pltpu.HBM)],
+        out_specs=tuple(vmem_spec(2)),
         scratch_shapes=[pltpu.SemaphoreType.DMA],
         compiler_params=pltpu.CompilerParams(vmem_limit_bytes=LIMIT),
         cost_estimate=pl.CostEstimate(flops=0, bytes_accessed=16_000_000, transcendentals=0),
         name="fetch",
-    )(after, pltpu.with_memory_space_constraint(field, pltpu.HBM))
+    )(patterns, where, estimate, window, pltpu.with_memory_space_constraint(field, pltpu.HBM))
 
 
 def across(left, right):
@@ -436,29 +495,26 @@
 
 
 def update_kernel(
-    led_row, led_col, patterns, where, field_ref, estimate_ref, w0, w1, w2, w3,
+    led_row, led_col, patterns, where, field_ref, weight_in, w1, w2, w3,
     spec_ref, pupil_ref, small_ref, big_hbm,
-    fresh_ref, high_ref, low_ref, first_ref, second_ref,
-    weight, grads, big, big_sem, *, group,
+    fresh_hbm, high_ref, low_ref, first_ref, second_ref, weight,
+    grads, fresh_ref, big, big_sem, fresh_sem, *, group,
 ):
     leds, half_h, half_w = weight.shape
     band_rows, band_cols = pupil_ref.shape[1:]
     height, width = spec_ref.shape[1:]
-    frames_here = w0.shape[0] // half_h
+    frames_here = w1.shape[0] // half_h
     is_odd = where[1] == 1
     big_load = pltpu.make_async_copy(big_hbm, big, big_sem)
     big_load.start()
     grads[...] = jnp.zeros_like(grads)
-    weight[...] = jnp.zeros_like(weight)
-    for slot, window in enumerate((w0, w1, w2, w3)):
-        owner = jnp.bitwise_xor(where[0], slot)
+    for slot, window in enumerate((w1, w2, w3)):
+        owner = jnp.bitwise_xor(where[0], slot + 1)
         means = rows_value(window[frames_here * half_h :])
         for place in range(frames_here):
-            frame = owner * frames_here + place
-            value = estimate_ref[frame] - means[place : place + 1, 0:1]
-            value -= window[place * half_h : (place + 1) * half_h].astype(F32)
-            for lit in range(patterns.shape[0]):
-                weight[patterns[lit, frame]] += value
+            value = window[place * half_h : (place + 1) * half_h].astype(F32)
+            value = -means[place : place + 1, 0:1] - value
+            add_frame(weight, patterns, owner * frames_here + place, value)
 
     table_rows = 2 * band_rows
 
@@ -497,6 +553,8 @@
     fresh_im = spec_ref[1] - (4.0 * STEP) * grads[1, :height, :width]
     fresh_ref[0] = fresh_re
     fresh_ref[1] = fresh_im
+    store = pltpu.make_async_copy(fresh_ref, fresh_hbm, fresh_sem)
+    store.start()
     re_hi, re_lo = split(fresh_re)
     im_hi, im_lo = split(fresh_im)
     high = jnp.concatenate([re_hi, im_hi], axis=0)
@@ -517,10 +575,11 @@
     to_left, to_right = sides[:half], sides[half:]
     first_ref[...] = jnp.where(is_odd, to_left, to_right)
     second_ref[...] = jnp.where(is_odd, to_right, to_left)
+    store.wait()
 
 
 def update(
-    field, estimate, window_parts, spectrum, pupil, patterns, led_row, led_col, where, tables,
+    field, weight, window_parts, spectrum, pupil, patterns, led_row, led_col, where, tables,
     margin, group=8,
 ):
     rows, cols = tables
@@ -544,39 +603,57 @@
         jax.ShapeDtypeStruct((height, 2 * width), BF16),
         jax.ShapeDtypeStruct((2 * margin, height), F32),
         jax.ShapeDtypeStruct((2 * margin, height), F32),
+        jax.ShapeDtypeStruct(weight.shape, F32),
     )
     return pl.pallas_call(
         functools.partial(update_kernel, group=group),
         out_shape=out_shape,
         in_specs=[pl.BlockSpec(memory_space=SMEM)] * 4
-        + vmem_spec(9)
+        + vmem_spec(8)
         + [pl.BlockSpec(memory_space=pltpu.HBM)],
-        out_specs=tuple(vmem_spec(5)),
+        out_specs=(pl.BlockSpec(memory_space=pltpu.HBM), *vmem_spec(5)),
+        input_output_aliases={5: 5},
         scratch_shapes=[
-            pltpu.VMEM((leds, half_h, half_w), F32),
             pltpu.VMEM((2, height + 8, width + 128), F32),
+            pltpu.VMEM(spectrum.shape, F32),
             pltpu.VMEM(big.shape, BF16),
             pltpu.SemaphoreType.DMA,
+            pltpu.SemaphoreType.DMA,
         ],
         compiler_params=pltpu.CompilerParams(vmem_limit_bytes=LIMIT),
         name="update",
     )(
-        led_row, led_col, patterns, where, field, estimate, *window_parts, spectrum, pupil, small,
+        led_row, led_col, patterns, where, field, weight, *window_parts, spectrum, pupil, small,
         pltpu.with_memory_space_constraint(jnp.asarray(big), pltpu.HBM),
-    )
-
-
-def object_kernel(high_ref, low_ref, table_ref, out_ref):
-    core = out_ref.shape[1]
+    )[:5]
+
+
+def object_kernel(high_ref, low_ref, table_ref, out_hbm, edges_ref, out, sems):
+    core = out.shape[1]
+    margin = edges_ref.shape[2]
     width = high_ref.shape[1] // 2
-    re_im_hi, re_im_lo = table_ref[: 2 * core], table_ref[2 * core :]
-    parts = []
+    stores = []
     for part in range(2):
-        cut = slice(part * width, (part + 1) * width)
-        z_hi, z_lo = high_ref[:, cut], low_ref[:, cut]
-        parts.append(across(re_im_hi, z_hi) + across(re_im_lo, z_hi) + across(re_im_hi, z_lo))
-    out_ref[0] = parts[0][:core] - parts[1][core:]
-    out_ref[1] = parts[0][core:] + parts[1][:core]
+        total = None
+        for other in range(2):
+            rows = slice((part ^ other) * core, (part ^ other) * core + core)
+            more = slice(rows.start + 2 * core, rows.stop + 2 * core)
+            cut = slice(other * width, (other + 1) * width)
+            z_hi, z_lo = high_ref[:, cut], low_ref[:, cut]
+            one = across(table_ref[rows], z_hi) + across(table_ref[more], z_hi)
+            one = one + across(table_ref[rows], z_lo)
+            if total is None:
+                total = one
+            else:
+                total = total + one if part else total - one
+        out[part] = total
+        edges_ref[part, 0] = total[:margin]
+        edges_ref[part, 1] = total[core - margin :]
+        store = pltpu.make_async_copy(out.at[part], out_hbm.at[part], sems.at[part])
+        store.start()
+        stores.append(store)
+    for store in stores:
+        store.wait()
 
 
 def object_core(high, low, margin, core):
@@ -585,9 +662,13 @@
     table = np.concatenate(two_parts(np.concatenate([col_re, col_im])))
     return pl.pallas_call(
         object_kernel,
-        out_shape=jax.ShapeDtypeStruct((2, core, height), F32),
+        out_shape=(
+            jax.ShapeDtypeStruct((2, core, height), F32),
+            jax.ShapeDtypeStruct((2, 2, margin, height), F32),
+        ),
         in_specs=vmem_spec(3),
-        out_specs=pl.BlockSpec(memory_space=VMEM),
+        out_specs=(pl.BlockSpec(memory_space=pltpu.HBM), pl.BlockSpec(memory_space=VMEM)),
+        scratch_shapes=[pltpu.VMEM((2, core, height), F32), pltpu.SemaphoreType.DMA((2,))],
         compiler_params=pltpu.CompilerParams(vmem_limit_bytes=LIMIT),
         cost_estimate=pl.CostEstimate(
             flops=3_000_000_000, bytes_accessed=5_000_000, transcendentals=0
@@ -596,41 +677,51 @@
     )(high, low, table)
 
 
-def blend_kernel(where, first_ref, second_ref, in_ref, out_ref):
-    side = pl.program_id(0)
+def blend_kernel(where, first_ref, second_ref, edges_ref, core_hbm, out_hbm, mixed, sems):
     tile = where[2]
     is_odd = where[1] == 1
-    margin = out_ref.shape[1]
+    margin, core = edges_ref.shape[2], out_hbm.shape[1]
     k = lax.broadcasted_iota(jnp.int32, (margin, 1), 0).astype(F32)
     span = 2.0 * margin
-    at_left = side == 0
-    own_w = jnp.where(at_left, k + margin + 0.5, span - k - 0.5) / span
-    other_w = jnp.where(at_left, margin - k - 0.5, k + 0.5) / span
-    has_other = jnp.where(at_left, tile > 0, tile < where[3] - 1)
-    own_w = jnp.where(has_other, own_w, 1.0)
-    other_w = jnp.where(has_other, other_w, 0.0)
-    use_first = jnp.where(at_left, is_odd, jnp.logical_not(is_odd))
-    other = jnp.where(use_first, first_ref[...], second_ref[...])
-    for part in range(2):
-        cut = slice(part * margin, (part + 1) * margin)
-        out_ref[part] = in_ref[part] * own_w + other[cut] * other_w
-
-
-def blend(core_part, first, second, where, margin):
-    _, core, height = core_part.shape
-    last = core // margin - 1
-    block = pl.BlockSpec((2, margin, height), lambda i: (0, i * last, 0))
-    whole = pl.BlockSpec(first.shape, lambda i: (0, 0))
+    from_left = jnp.where(is_odd, first_ref[...], second_ref[...])
+    from_right = jnp.where(is_odd, second_ref[...], first_ref[...])
+    sides = (
+        ((k + margin + 0.5) / span, (margin - k - 0.5) / span, tile > 0, from_left, 0),
+        (
+            (span - k - 0.5) / span, (k + 0.5) / span, tile < where[3] - 1, from_right,
+            core - margin,
+        ),
+    )
+    stores = []
+    for side, (own_w, other_w, has_other, other, begin) in enumerate(sides):
+        own_w = jnp.where(has_other, own_w, 1.0)
+        other_w = jnp.where(has_other, other_w, 0.0)
+        for part in range(2):
+            cut = slice(part * margin, (part + 1) * margin)
+            mixed[part, side] = edges_ref[part, side] * own_w + other[cut] * other_w
+            store = pltpu.make_async_copy(
+                mixed.at[part, side], out_hbm.at[part, pl.ds(begin, margin)],
+                sems.at[2 * side + part],
+            )
+            store.start()
+            stores.append(store)
+    for store in stores:
+        store.wait()
+
+
+def blend(core_part, edges, first, second, where):
     return pl.pallas_call(
         blend_kernel,
-        grid=(2,),
         out_shape=jax.ShapeDtypeStruct(core_part.shape, F32),
-        in_specs=[pl.BlockSpec(memory_space=SMEM), whole, whole, block],
-        out_specs=block,
-        input_output_aliases={3: 0},
+        in_specs=[pl.BlockSpec(memory_space=SMEM)]
+        + vmem_spec(3)
+        + [pl.BlockSpec(memory_space=pltpu.HBM)],
+        out_specs=pl.BlockSpec(memory_space=pltpu.HBM),
+        input_output_aliases={4: 0},
+        scratch_shapes=[pltpu.VMEM(edges.shape, F32), pltpu.SemaphoreType.DMA((4,))],
         compiler_params=pltpu.CompilerParams(vmem_limit_bytes=LIMIT),
         name="blend",
-    )(where, first, second, core_part)
+    )(where, first, second, edges, core_part)
 
 
 def body(raw, scales, flat, spectrum, pupil, patterns, led_row, led_col):
@@ -666,23 +757,23 @@
         spectrum_tile, pupil, patterns, led_row, led_col, tables, handed
     )
     window = windows(arrived, rows, small, frames_here, core)
-    field = fetch(field, window)
+    field, weight = fetch(field, estimate, window, patterns, where)
 
     swap_core = [(i, i ^ 1) for i in range(4)]
     swap_chip = [(i, i ^ 2) for i in range(4)]
     other = functools.partial(lax.ppermute, axis_name="grp")
     window_2 = other(window, perm=swap_chip)
     window_1 = other(window, perm=swap_core)
-    window_2, field = lax.optimization_barrier((window_2, field))
+    window_2, field, weight = lax.optimization_barrier((window_2, field, weight))
     window_3 = other(window_2, perm=swap_core)
 
     fresh, high, low, for_a, for_b = update(
-        field, estimate, (window, window_1, window_2, window_3), spectrum_tile, pupil, patterns,
+        field, weight, (window_1, window_2, window_3), spectrum_tile, pupil, patterns,
         led_row, led_col, where, tables, margin,
     )
     side_a, side_b = neighbours(for_a, for_b)
-    core_part = object_core(high, low, margin, core)
-    stitched = blend(core_part, side_a, side_b, where, margin)
+    core_part, edges = object_core(high, low, margin, core)
+    stitched = blend(core_part, edges, side_a, side_b, where)
     return fresh[None], jnp.transpose(stitched, (0, 2, 1))
 
 

time: 68.2 us -> 66.4 us (0.974)
  transfers between devices with their start and end apart: 7 -> 7, of which waited for: 4 -> 4; matrix products, arithmetic and copies ran while one was open for 0% -> 0% of each run, Pallas kernels for 21% -> 22%
where the time goes in v4:
time: 66.4 us; the launch traced here: 65.9 us
  Pallas kernels  30.7 us (46%)
  starting transfers between devices  18 us (27%)
  waiting for transfers between devices  9 us (14%)
  local copies, waits for them, and re-layouts  7.35 us (11%)
  between operations  0.8 us (1%)
    pallas_call x1, Pallas kernels, update(): pl.pallas_call(functools.partial(update_kernel, group=group), out_shape=o...  9.28 us
    unnamed x28, local copies, waits for them, and re-layouts  7.35 us
    pallas_call x1, Pallas kernels, all_fields(): pl.pallas_call(functools.partial(field_kernel, group=group), out_shape=(j...  7.29 us
    all_to_all x1, starting transfers between devices, body(): lax.all_to_all(narrow, 'tile', split_axis=0, concat_axis=0, tiled=True)  6.3 us
    all_to_all x1, starting transfers between devices, body(): lax.all_to_all(by_rows, 'tile', split_axis=0, concat_axis=0, tiled=True)  6.07 us
    pallas_call x1, Pallas kernels, fetch(): pl.pallas_call(fetch_kernel, out_shape=(jax.ShapeDtypeStruct(field.shape,...  3.96 us
    all_to_all x1, waiting for transfers between devices, body(): lax.all_to_all(by_rows, 'tile', split_axis=0, concat_axis=0, tiled=True)  3.53 us
    pallas_call x1, Pallas kernels, strips(): pl.pallas_call(functools.partial(strips_kernel, frames=frames, core=core,...  3.05 us
  transfers between devices with their start and end apart: 7, of which 4 were waited for; matrix products, arithmetic and copies ran while one was open for 0% of the time, Pallas kernels for 22%

profile of v4, /device:TPU:24, one launch (start us, length us, event | category | flops | bytes accessed | tf_op | source)
XLA Modules:
  0.0 65.9 jit_solution(257014426323363022)
XLA Ops:
  0.6 0.0 copy-start.4
  0.6 2.1 %gains.1.after = bf16[8,32,512]{2,1,0:T(8,128)(2,1)} custom-call(f32[480,256]{1,0:T(8,128)} %bitcast.18), custom_call_target="tpu_custom_call" | custom-call | tf_op jit(solution)/shard_map/gains/pallas_call | solution.py:107
  2.7 6.1 %all-to-all-start = ((bf16[8,32,512]{2,1,0:T(8,128)(2,1)}), bf16[8,32,512]{2,1,0:T(8,128)(2,1)S(1)}, u32[]{:S(2)}, u32[]{:S(2)}) async-start(bf16[8,32,512]{2,1,0:T(8,128)(2,1)} %gains.1.after), calls=%async_computation | async-start | bytes 524288 | tf_op jit(solution)/shard_map/all_to_all | solution.py:752
  8.8 0.1 pad_add_fusion.where
  8.9 1.2 %copy-done.9 = bf16[4,32,3840]{2,1,0:T(8,128)(2,1)S(1)} copy-done((bf16[4,32,3840]{2,1,0:T(8,128)(2,1)S(1)}, bf16[4,32,3840]{2,1,0:T(8,128)(2,1)}, u32[]{:S(2)}) %copy-start.9) | copy-done | bytes 983064
  10.1 0.7 %copy-done.10 = bf16[4,8,120]{2,1,0:T(8,128)(2,1)S(1)} copy-done((bf16[4,8,120]{2,1,0:T(8,128)(2,1)S(1)}, bf16[4,8,120]{2,1,0:T(8,128)(2,1)}, u32[]{:S(2)}) %copy-start.10) | copy-done | bytes 7704
  10.8 0.0 copy-start.12
  10.8 0.7 %dequantize.1.dq_ref = f32[8,128,512]{2,1,0:T(8,128)S(1)} custom-call(bf16[128,3840]{1,0:T(8,128)(2,1)S(1)} %bitcast.15, bf16[32,120]{1,0:T(8,128)(2,1)S(1)} %bitcast.16, bf16[8,32,512]{2,1,0:T(8,128)(2,1)} %gains.1.after), custom_call_target="tpu_custom_call" | custom-call | flops 2000000000 | bytes 4000000 | tf_op jit(solution)/shard_map/dequantize/pallas_call | solution.py:156
  11.5 3.5 %all-to-all-done.gains_ref = bf16[8,32,512]{2,1,0:T(8,128)(2,1)S(1)} async-done(((bf16[8,32,512]{2,1,0:T(8,128)(2,1)}), bf16[8,32,512]{2,1,0:T(8,128)(2,1)S(1)}, u32[]{:S(2)}, u32[]{:S(2)}) %all-to-all-start) | async-done | bytes 262176 | tf_op jit(solution)/shard_map/all_to_all | solution.py:752
  15.0 3.1 %strips.1 = bf16[8,272,128]{2,1,0:T(8,128)(2,1)} custom-call(s32[4]{0:T(128)S(1)} %pad_add_fusion.where, f32[8,128,512]{2,1,0:T(8,128)S(1)} %dequantize.1.dq_ref, bf16[8,32,512]{2,1,0:T(8,128)(2,1)S(1)} %all-to-all-done.gains_ref, bf16[1024,256]{1,0:T(8,128)(2,1)S(1)} %copy-done.4), custom_call_target="tpu_custom_call" | custom-call | tf_op jit(solution)/shard_map/strips/pallas_call | solution.py:261
  18.1 6.3 %all-to-all-start.1 = ((bf16[8,272,128]{2,1,0:T(8,128)(2,1)}), bf16[8,272,128]{2,1,0:T(8,128)(2,1)S(1)}, u32[]{:S(2)}, u32[]{:S(2)}) async-start(bf16[8,272,128]{2,1,0:T(8,128)(2,1)} %strips.1), calls=%async_computation.1 | async-start | bytes 1114112 | tf_op jit(solution)/shard_map/all_to_all | solution.py:754
  24.4 0.0 copy-start.1
  24.4 1.2 %copy-done.1 = f32[1,2,256,512]{3,2,1,0:T(8,128)S(1)} copy-done((f32[1,2,256,512]{3,2,1,0:T(8,128)S(1)}, f32[1,2,256,512]{3,2,1,0:T(8,128)}, u32[]{:S(2)}) %copy-start.1) | copy-done | bytes 1048600
  25.7 0.9 %copy-done.13 = bf16[256,384]{1,0:T(8,128)(2,1)S(1)} copy-done((bf16[256,384]{1,0:T(8,128)(2,1)S(1)}, bf16[256,384]{1,0:T(8,128)(2,1)}, u32[]{:S(2)}) %copy-start.13) | copy-done | bytes 196632
  26.6 7.3 %fields.1 = (f32[32,256,256]{2,1,0:T(8,128)S(1)}, f32[16,128,256]{2,1,0:T(8,128)S(1)}, bf16[128,512]{1,0:T(8,128)(2,1)S(1)}, f32[136,256]{1,0:T(8,128)S(1)}) custom-call(s32[32]{0:T(128)S(1)} %copy-done.7, s32[32]{0:T(128)S(1)} %copy-done.8, s32[4,16]{1,0:T(4,128)S(1)} %bitcast.12, f32[2,256,512]{2,1,0:T(8,128)S(1)} %bitcast.10, ...), custom_call_target="tpu_custom_call" | custom-call | flops 8000000000 | bytes 16000000 | tf_op jit(solution)/shard_map/fields/pallas_call | solution.py:344
  33.9 3.3 %copy-done = f32[32,256,256]{2,1,0:T(8,128)} copy-done((f32[32,256,256]{2,1,0:T(8,128)}, f32[32,256,256]{2,1,0:T(8,128)S(1)}, u32[]{:S(2)}) %copy-start) | copy-done | bytes 8388632
  37.2 0.0 all-to-all-done.1.dq_ref
  37.2 0.5 windows.1.window
  37.6 1.6 %collective-permute-start = (bf16[528,256]{1,0:T(8,128)(2,1)S(1)}, bf16[528,256]{1,0:T(8,128)(2,1)S(1)}, u32[]{:S(2)}, u32[]{:S(2)}) collective-permute-start(bf16[528,256]{1,0:T(8,128)(2,1)S(1)} %windows.1.window), channel_id=1, source_target_pairs={{0,16},{8,24},{16,0},{24,8},{1,17},{9,25},{17,1},{25,9},{2,18},{10... | collective-permute-start | bytes 811016 | tf_op jit(solution)/shard_map/ppermute | solution.py:765
  39.2 0.0 collective-permute-start.1
  39.2 4.0 %fetch.1 = (f32[32,256,256]{2,1,0:T(8,128)S(1)}, f32[32,128,256]{2,1,0:T(8,128)S(1)}) custom-call(s32[4,16]{1,0:T(4,128)S(1)} %bitcast.13, s32[4]{0:T(128)S(1)} %pad_add_fusion.where, f32[16,128,256]{2,1,0:T(8,128)S(1)} %get-tuple-element.20.estimate_ref, bf16[528,256]{1,0:T(8,128)(2,1)S(1)} %windows.1.window, f32[32,256,256]{2,1,0:T(8,128)} %copy-done), custom_call_target="tpu_custom_call" | custom-call | bytes 16000000 | tf_op jit(solution)/shard_map/fetch/pallas_call | solution.py:475
  43.2 1.9 %collective-permute-done.w2 = bf16[528,256]{1,0:T(8,128)(2,1)S(1)} collective-permute-done((bf16[528,256]{1,0:T(8,128)(2,1)S(1)}, bf16[528,256]{1,0:T(8,128)(2,1)S(1)}, u32[]{:S(2)}, u32[]{:S(2)}) %collective-permute-start) | collective-permute-done | bytes 270368 | tf_op jit(solution)/shard_map/ppermute | solution.py:765
  45.0 0.0 collective-permute-start.2
  45.0 0.0 collective-permute-done.1.w1
  45.0 1.5 %collective-permute-done.2.w3 = bf16[528,256]{1,0:T(8,128)(2,1)S(1)} collective-permute-done((bf16[528,256]{1,0:T(8,128)(2,1)S(1)}, bf16[528,256]{1,0:T(8,128)(2,1)S(1)}, u32[]{:S(2)}, u32[]{:S(2)}) %collective-permute-start.2) | collective-permute-done | bytes 270368 | tf_op jit(solution)/shard_map/ppermute | solution.py:768
  46.6 9.3 %update.1 = (f32[2,256,512]{2,1,0:T(8,128)}, bf16[256,1024]{1,0:T(8,128)(2,1)S(1)}, bf16[256,1024]{1,0:T(8,128)(2,1)S(1)}, f32[32,256]{1,0:T(8,128)S(1)}, f32[32...) custom-call(s32[32]{0:T(128)S(1)} %copy-done.7, s32[32]{0:T(128)S(1)} %copy-done.8, ...), custom_call_target="tpu_custom_call", output_to_operand_aliasing={{5}: (5, {})} | custom-call | tf_op jit(solution)/shard_map/update/pallas_call | solution.py:608
  55.9 2.2 %collective-permute-start.3 = (f32[32,256]{1,0:T(8,128)S(1)}, f32[32,256]{1,0:T(8,128)S(1)}, u32[]{:S(2)}, u32[]{:S(2)}) collective-permute-start(f32[32,256]{1,0:T(8,128)S(1)} %get-tuple-element.28), channel_id=1, source_target_pairs={{0,1},{1,0},{2,3},{3,2},{4,5},{5,4},{6,7},{7,6},{8,9},{9,8},{10,11... | collective-permute-start | bytes 98312 | tf_op jit(solution)/shard_map/ppermute | solution.py:745
  58.0 1.9 %collective-permute-start.4 = (f32[32,256]{1,0:T(8,128)S(1)}, f32[32,256]{1,0:T(8,128)S(1)}, u32[]{:S(2)}, u32[]{:S(2)}) collective-permute-start(f32[32,256]{1,0:T(8,128)S(1)} %get-tuple-element.29), channel_id=1, source_target_pairs={{1,2},{2,1},{3,4},{4,3},{5,6},{6,5},{9,10},{10,9},{11,12},{12,11},... | collective-permute-start | bytes 98312 | tf_op jit(solution)/shard_map/ppermute | solution.py:745
  60.0 2.7 %object.1 = (f32[2,480,256]{2,1,0:T(8,128)}, f32[2,2,16,256]{3,2,1,0:T(8,128)S(1)}) custom-call(bf16[256,1024]{1,0:T(8,128)(2,1)S(1)} %get-tuple-element.30.high_ref, bf16[256,1024]{1,0:T(8,128)(2,1)S(1)} %get-tuple-element.31.low_ref, bf16[1920,512]{1,0:T(8,128)(2,1)S(1)} %copy-done.11), custom_call_target="tpu_custom_call" | custom-call | flops 3000000000 | bytes 5000000 | tf_op jit(solution)/shard_map/object/pallas_call | solution.py:663
  62.6 0.0 collective-permute-done.3.first_ref
  62.7 2.1 %collective-permute-done.4.second_ref = f32[32,256]{1,0:T(8,128)S(1)} collective-permute-done((f32[32,256]{1,0:T(8,128)S(1)}, f32[32,256]{1,0:T(8,128)S(1)}, u32[]{:S(2)}, u32[]{:S(2)}) %collective-permute-start.4) | collective-permute-done | bytes 32800 | tf_op jit(solution)/shard_map/ppermute | solution.py:745
  64.7 1.2 %blend.1 = f32[2,480,256]{2,1,0:T(8,128)} custom-call(s32[4]{0:T(128)S(1)} %pad_add_fusion.where, f32[32,256]{1,0:T(8,128)S(1)} %collective-permute-done.3.first_ref, f32[32,256]{1,0:T(8,128)S(1)} %collective-permute-done.4.second_ref, f32[2,2,16,256]{3,2,1,0:T(8,128)S(1)} %get-tuple-element.32.edges_ref, ...), custom_call_target="tpu_custom_call", output_to_operand_aliasing={{}: (4, {})} | custom-call | tf_op jit(solution)/shard_map/blend/pallas_call | solution.py:713
  (20 shorter events, 0.0 us)
Async XLA Ops:
  0.6 14.4 %copy-start.4 = (bf16[1024,256]{1,0:T(8,128)(2,1)S(1)}, bf16[1024,256]{1,0:T(8,128)(2,1)}, u32[]{:S(2)}) copy-start(bf16[1024,256]{1,0:T(8,128)(2,1)} %constant.31.clone.lc_ref) | copy-start | bytes 1572868
  2.7 12.3 %all-to-all-start = ((bf16[8,32,512]{2,1,0:T(8,128)(2,1)}), bf16[8,32,512]{2,1,0:T(8,128)(2,1)S(1)}, u32[]{:S(2)}, u32[]{:S(2)}) async-start(bf16[8,32,512]{2,1,0:T(8,128)(2,1)} %gains.1.after), calls=%async_computation | async-start | bytes 524288 | tf_op jit(solution)/shard_map/all_to_all | solution.py:752
  8.9 1.2 %copy-start.9 = (bf16[4,32,3840]{2,1,0:T(8,128)(2,1)S(1)}, bf16[4,32,3840]{2,1,0:T(8,128)(2,1)}, u32[]{:S(2)}) copy-start(bf16[4,32,3840]{2,1,0:T(8,128)(2,1)} %param.16) | copy-start | bytes 2949124
  10.1 0.7 %copy-start.10 = (bf16[4,8,120]{2,1,0:T(8,128)(2,1)S(1)}, bf16[4,8,120]{2,1,0:T(8,128)(2,1)}, u32[]{:S(2)}) copy-start(bf16[4,8,120]{2,1,0:T(8,128)(2,1)} %param.17) | copy-start | bytes 23044
  10.8 13.6 %copy-start.5 = (f32[2,64,128]{2,1,0:T(8,128)S(1)}, f32[2,64,128]{2,1,0:T(8,128)}, u32[]{:S(2)}) copy-start(f32[2,64,128]{2,1,0:T(8,128)} %pupil_ref.3) | copy-start | bytes 196612
  10.8 13.6 %copy-start.6 = (s32[16,4]{0,1:T(4,128)S(1)}, s32[16,4]{0,1:T(4,128)}, u32[]{:S(2)}) copy-start(s32[16,4]{0,1:T(4,128)} %param.21) | copy-start | bytes 772
  10.8 13.6 %copy-start.7 = (s32[32]{0:T(128)S(1)}, s32[32]{0:T(128)}, u32[]{:S(2)}) copy-start(s32[32]{0:T(128)} %led_row.3) | copy-start | bytes 388
  10.8 13.6 %copy-start.8 = (s32[32]{0:T(128)S(1)}, s32[32]{0:T(128)}, u32[]{:S(2)}) copy-start(s32[32]{0:T(128)} %led_col.3) | copy-start | bytes 388
  10.8 13.6 %copy-start.12 = (bf16[512,512]{1,0:T(8,128)(2,1)S(1)}, bf16[512,512]{1,0:T(8,128)(2,1)}, u32[]{:S(2)}) copy-start(bf16[512,512]{1,0:T(8,128)(2,1)} %constant.34.clone.cols_ref) | copy-start | bytes 1572868
  18.1 19.1 %all-to-all-start.1 = ((bf16[8,272,128]{2,1,0:T(8,128)(2,1)}), bf16[8,272,128]{2,1,0:T(8,128)(2,1)S(1)}, u32[]{:S(2)}, u32[]{:S(2)}) async-start(bf16[8,272,128]{2,1,0:T(8,128)(2,1)} %strips.1), calls=%async_computation.1 | async-start | bytes 1114112 | tf_op jit(solution)/shard_map/all_to_all | solution.py:754
  24.4 1.2 %copy-start.1 = (f32[1,2,256,512]{3,2,1,0:T(8,128)S(1)}, f32[1,2,256,512]{3,2,1,0:T(8,128)}, u32[]{:S(2)}) copy-start(f32[1,2,256,512]{3,2,1,0:T(8,128)} %param.19) | copy-start | bytes 3145732
  25.7 0.9 %copy-start.13 = (bf16[256,384]{1,0:T(8,128)(2,1)S(1)}, bf16[256,384]{1,0:T(8,128)(2,1)}, u32[]{:S(2)}) copy-start(bf16[256,384]{1,0:T(8,128)(2,1)} %constant.35.clone.rows_ref) | copy-start | bytes 589828
  33.9 3.3 %copy-start = (f32[32,256,256]{2,1,0:T(8,128)}, f32[32,256,256]{2,1,0:T(8,128)S(1)}, u32[]{:S(2)}) copy-start(f32[32,256,256]{2,1,0:T(8,128)S(1)} %get-tuple-element.21.field_hbm) | copy-start | bytes 25165828
  37.6 7.4 %collective-permute-start = (bf16[528,256]{1,0:T(8,128)(2,1)S(1)}, bf16[528,256]{1,0:T(8,128)(2,1)S(1)}, u32[]{:S(2)}, u32[]{:S(2)}) collective-permute-start(bf16[528,256]{1,0:T(8,128)(2,1)S(1)} %windows.1.window), channel_id=1, source_target_pairs={{0,16},{8,24},{16,0},{24,8},{1,17},{9,25},{17,1},{25,9},{2,18},{10... | collective-permute-start | bytes 811016 | tf_op jit(solution)/shard_map/ppermute | solution.py:765
  39.2 5.8 %collective-permute-start.1 = (bf16[528,256]{1,0:T(8,128)(2,1)S(1)}, bf16[528,256]{1,0:T(8,128)(2,1)S(1)}, u32[]{:S(2)}, u32[]{:S(2)}) collective-permute-start(bf16[528,256]{1,0:T(8,128)(2,1)S(1)} %windows.1.window), channel_id=1, source_target_pairs={{0,8},{8,0},{16,24},{24,16},{1,9},{9,1},{17,25},{25,17},{2,10},{10... | collective-permute-start | bytes 811016 | tf_op jit(solution)/shard_map/ppermute | solution.py:766
  39.2 7.4 %copy-start.2 = (f32[1,2,256,512]{3,2,1,0:T(8,128)S(1)}, f32[1,2,256,512]{3,2,1,0:T(8,128)}, u32[]{:S(2)}) copy-start(f32[1,2,256,512]{3,2,1,0:T(8,128)} %param.19) | copy-start | bytes 3145732
  39.2 7.4 %copy-start.3 = (bf16[1280,256]{1,0:T(8,128)(2,1)S(1)}, bf16[1280,256]{1,0:T(8,128)(2,1)}, u32[]{:S(2)}) copy-start(bf16[1280,256]{1,0:T(8,128)(2,1)} %constant.37.clone.small_ref) | copy-start | bytes 1966084
  45.0 14.9 %copy-start.11 = (bf16[1920,512]{1,0:T(8,128)(2,1)S(1)}, bf16[1920,512]{1,0:T(8,128)(2,1)}, u32[]{:S(2)}) copy-start(bf16[1920,512]{1,0:T(8,128)(2,1)} %constant.38.clone.table_ref) | copy-start | bytes 5898244
  45.0 1.5 %collective-permute-start.2 = (bf16[528,256]{1,0:T(8,128)(2,1)S(1)}, bf16[528,256]{1,0:T(8,128)(2,1)S(1)}, u32[]{:S(2)}, u32[]{:S(2)}) collective-permute-start(bf16[528,256]{1,0:T(8,128)(2,1)S(1)} %collective-permute-done.w2), channel_id=1, source_target_pairs={{0,8},{8,0},{16,24},{24,16},{1,9},{9,1},{17,25},{25,17},{2,10},{10... | collective-permute-start | bytes 811016 | tf_op jit(solution)/shard_map/ppermute | solution.py:768
  55.9 6.8 %collective-permute-start.3 = (f32[32,256]{1,0:T(8,128)S(1)}, f32[32,256]{1,0:T(8,128)S(1)}, u32[]{:S(2)}, u32[]{:S(2)}) collective-permute-start(f32[32,256]{1,0:T(8,128)S(1)} %get-tuple-element.28), channel_id=1, source_target_pairs={{0,1},{1,0},{2,3},{3,2},{4,5},{5,4},{6,7},{7,6},{8,9},{9,8},{10,11... | collective-permute-start | bytes 98312 | tf_op jit(solution)/shard_map/ppermute | solution.py:745
  58.0 6.7 %collective-permute-start.4 = (f32[32,256]{1,0:T(8,128)S(1)}, f32[32,256]{1,0:T(8,128)S(1)}, u32[]{:S(2)}, u32[]{:S(2)}) collective-permute-start(f32[32,256]{1,0:T(8,128)S(1)} %get-tuple-element.29), channel_id=1, source_target_pairs={{1,2},{2,1},{3,4},{4,3},{5,6},{6,5},{9,10},{10,9},{11,12},{12,11},... | collective-permute-start | bytes 98312 | tf_op jit(solution)/shard_map/ppermute | solution.py:745

commit v5 on v4

--- a/solution.py
+++ b/solution.py
@@ -33,8 +33,13 @@
     return np.cos(angle) / math.sqrt(norm), np.sin(angle) / math.sqrt(norm)
 
 
+def pairs(length):
+    first = np.arange(1, length // 2, 2)
+    return np.concatenate([first, length - first])
+
+
 def low_pass(length, band):
-    places = 2 * np.arange(length // 2)[:, None] - np.arange(length)[None, :]
+    places = pairs(length)[:, None] - np.arange(length)[None, :]
     total = np.ones(places.shape)
     for freq in range(1, band):
         total += 2.0 * np.cos(2.0 * math.pi * ((freq * places) % length) / length)
@@ -43,14 +48,20 @@
 
 def stacked_tables(height, width, band_rows, band_cols):
     row_re, row_im = wave(
-        2 * np.arange(height // 2), np.arange(band_rows) - band_rows // 2, height, band_rows
+        pairs(height), np.arange(band_rows) - band_rows // 2, height, band_rows
     )
     rows = np.block([[row_re, -row_im], [row_im, row_re]])
     col_re, col_im = wave(
-        np.arange(band_cols) - band_cols // 2, 2 * np.arange(width // 2), width, band_cols
+        np.arange(band_cols) - band_cols // 2, pairs(width), width, band_cols
     )
     cols = np.block([[col_re, col_im], [-col_im, col_re]])
-    return rows, cols
+    half_rows, half_cols = height // 4, width // 4
+    high, low = two_parts(np.concatenate([row_re[:half_rows], row_im[:half_rows]]).T)
+    back_rows = np.block([[high, high], [low, np.zeros_like(low)]])
+    back_cols = np.concatenate(
+        two_parts(np.concatenate([col_re[:, :half_cols], col_im[:, :half_cols]], axis=1).T), axis=1
+    )
+    return rows, cols, back_rows, back_cols
 
 
 def split(values):
@@ -64,6 +75,10 @@
 
 def vmem_spec(count):
     return [pl.BlockSpec(memory_space=VMEM)] * count
+
+
+def lane_blocks(values):
+    return [values[:, begin : begin + 128] for begin in range(0, values.shape[1], 128)]
 
 
 def parts_rows(values):
@@ -336,7 +351,7 @@
 
 
 def all_fields(spectrum, pupil, patterns, led_row, led_col, tables, handed, group=8):
-    rows, cols = tables
+    rows, cols, _, _ = tables
     leds = led_row.shape[0]
     _, height, width = spectrum.shape
     half_h, half_w = height // 2, width // 2
@@ -496,9 +511,9 @@
 
 def update_kernel(
     led_row, led_col, patterns, where, field_ref, weight_in, w1, w2, w3,
-    spec_ref, pupil_ref, small_ref, big_hbm,
+    spec_ref, pupil_ref, back_ref, big_hbm,
     fresh_hbm, high_ref, low_ref, first_ref, second_ref, weight,
-    grads, fresh_ref, big, big_sem, fresh_sem, *, group,
+    grads, fresh_ref, big, sides_ref, big_sem, fresh_sems, *, group,
 ):
     leds, half_h, half_w = weight.shape
     band_rows, band_cols = pupil_ref.shape[1:]
@@ -516,26 +531,35 @@
             value = -means[place : place + 1, 0:1] - value
             add_frame(weight, patterns, owner * frames_here + place, value)
 
-    table_rows = 2 * band_rows
+    left_rows = 2 * band_rows
+    pair_rows, pair_cols = half_h // 2, half_w // 2
 
     def some(step, carry):
-        left_rows = small_ref[: 2 * table_rows]
-        cols_hi = small_ref[2 * table_rows : 2 * table_rows + 2 * half_w]
-        cols_lo = small_ref[2 * table_rows + 2 * half_w :]
         backs = []
         for place in range(group):
             q = weight[step * group + place]
             field = field_ref[step * group + place]
-            high, low = split(jnp.concatenate([field[:half_h] * q, field[half_h:] * q], axis=0))
-            both = mm(left_rows, high)
-            back = both[:table_rows] + both[table_rows:] + mm(left_rows[:table_rows], low)
-            backs.append(jnp.concatenate([back[:band_rows], back[band_rows:]], axis=1))
+            g_re, g_im = field[:half_h] * q, field[half_h:] * q
+            re_a, re_b = g_re[:pair_rows], g_re[pair_rows:]
+            im_a, im_b = g_im[:pair_rows], g_im[pair_rows:]
+            to_re = jnp.concatenate([re_a + re_b, im_a - im_b], axis=0)
+            to_im = jnp.concatenate([im_a + im_b, re_b - re_a], axis=0)
+            high, low = split(jnp.concatenate([to_re, to_im], axis=1))
+            both = mm(back_ref[:left_rows], jnp.concatenate([high, low], axis=0))
+            back = both[:band_rows] + both[band_rows:]
+            re_a, re_b = back[:, :pair_cols], back[:, pair_cols : 2 * pair_cols]
+            im_a, im_b = back[:, 2 * pair_cols : 3 * pair_cols], back[:, 3 * pair_cols :]
+            backs.append(jnp.concatenate([re_a + re_b, im_a - im_b], axis=1))
+            backs.append(jnp.concatenate([im_a + im_b, re_b - re_a], axis=1))
         high, low = split(jnp.concatenate(backs, axis=0))
-        boxes = mm(high, cols_hi) + mm(high, cols_lo) + mm(low, cols_hi)
+        cols = back_ref[left_rows:]
+        both = mm(jnp.concatenate([high, low], axis=1), jnp.concatenate([cols, cols], axis=0))
+        boxes = both[:, :band_cols] + both[:, band_cols:]
         for place in range(group):
             led = step * group + place
-            one = boxes[place * band_rows : (place + 1) * band_rows]
-            back_re, back_im = one[:, :band_cols], one[:, band_cols:]
+            begin = 2 * place * band_rows
+            back_re = boxes[begin : begin + band_rows]
+            back_im = boxes[begin + band_rows : begin + 2 * band_rows]
             parts = (
                 pupil_ref[0] * back_re + pupil_ref[1] * back_im,
                 pupil_ref[0] * back_im - pupil_ref[1] * back_re,
@@ -551,52 +575,85 @@
     lax.fori_loop(0, leds // group, some, 0)
     fresh_re = spec_ref[0] - (4.0 * STEP) * grads[0, :height, :width]
     fresh_im = spec_ref[1] - (4.0 * STEP) * grads[1, :height, :width]
-    fresh_ref[0] = fresh_re
-    fresh_ref[1] = fresh_im
-    store = pltpu.make_async_copy(fresh_ref, fresh_hbm, fresh_sem)
-    store.start()
-    re_hi, re_lo = split(fresh_re)
-    im_hi, im_lo = split(fresh_im)
-    high = jnp.concatenate([re_hi, im_hi], axis=0)
-    low = jnp.concatenate([re_lo, im_lo], axis=0)
+    for part, fresh in enumerate((fresh_re, fresh_im)):
+        for number, block in enumerate(lane_blocks(fresh)):
+            fresh_ref[part, number] = block
+    stores = []
+    for number in range(width // 128):
+        store = pltpu.make_async_copy(
+            fresh_ref.at[:, number], fresh_hbm.at[:, :, pl.ds(number * 128, 128)],
+            fresh_sems.at[number],
+        )
+        store.start()
+        stores.append(store)
     big_load.wait()
-    full = 2 * height
-    rows_hi, rows_lo = big[:full], big[full : 2 * full]
-    spread = mm(rows_hi, high) + mm(rows_lo, high) + mm(rows_hi, low)
-    high, low = split(jnp.concatenate([spread[:height], spread[height:]], axis=1))
+
+    def spread(parity, table):
+        rows = pl.ds(parity, height // 2, stride=2)
+        parts = [
+            jnp.concatenate([fresh_ref[part, n, rows] for n in range(width // 128)], axis=1)
+            for part in range(2)
+        ]
+        high, low = split(jnp.concatenate(parts, axis=0))
+        table_hi, table_lo = big[table : table + height], big[table + height : table + 2 * height]
+        left = jnp.concatenate([table_hi, table_lo, table_hi], axis=1)
+        return mm(left, jnp.concatenate([high, high, low], axis=0))
+
+    even, odd = spread(0, 0), spread(1, 2 * height)
+    upper, lower = even + odd, even - odd
+    half = height // 2
+    z_re = jnp.concatenate([upper[:half], lower[:half]], axis=0)
+    z_im = jnp.concatenate([upper[half:], lower[half:]], axis=0)
+
+    near = [z[:, : width // 2] for z in (z_re, z_im)]
+    far = [z[:, width // 2 :] for z in (z_re, z_im)]
+    mixed = [a + b for a, b in zip(near, far)] + [a - b for a, b in zip(near, far)]
+    high, low = split(jnp.concatenate(mixed, axis=1))
     high_ref[...] = high
     low_ref[...] = low
-    side_rows = 2 * first_ref.shape[0]
-    side = big[2 * full :]
-    side_hi = jnp.concatenate([side[:side_rows], side[side_rows : 2 * side_rows]], axis=1)
-    side_lo = jnp.concatenate([side[2 * side_rows : 3 * side_rows], side[3 * side_rows :]], axis=1)
-    sides = across(side_hi, high) + across(side_lo, high) + across(side_hi, low)
-    half = side_rows // 2
-    to_left, to_right = sides[:half], sides[half:]
+    count = sides_ref.shape[1] // 2
+    for parity in range(2):
+        table = 4 * height + 4 * count * parity
+        cut = slice(parity * width, (parity + 1) * width)
+        side_hi = jnp.concatenate([big[table : table + count], big[table + count : table + 2 * count]], axis=1)
+        side_lo = jnp.concatenate(
+            [big[table + 2 * count : table + 3 * count], big[table + 3 * count : table + 4 * count]], axis=1
+        )
+        one = across(side_hi, high[:, cut]) + across(side_lo, high[:, cut])
+        one = one + across(side_hi, low[:, cut])
+        for number, block in enumerate(lane_blocks(one)):
+            sides_ref[number, pl.ds(parity, count, stride=2)] = block
+    sides = jnp.concatenate([sides_ref[n] for n in range(height // 128)], axis=1)
+    to_left, to_right = sides[:count], sides[count:]
     first_ref[...] = jnp.where(is_odd, to_left, to_right)
     second_ref[...] = jnp.where(is_odd, to_right, to_left)
-    store.wait()
+    for store in stores:
+        store.wait()
 
 
 def update(
     field, weight, window_parts, spectrum, pupil, patterns, led_row, led_col, where, tables,
     margin, group=8,
 ):
-    rows, cols = tables
+    _, _, back_rows, back_cols = tables
     leds = led_row.shape[0]
     _, height, width = spectrum.shape
     half_h, half_w = height // 2, width // 2
-    fr_re, fr_im = wave(np.arange(height), np.arange(height) - height // 2, height, height)
-    full_rows = np.block([[fr_re, -fr_im], [fr_im, fr_re]])
-    side_places = np.concatenate([np.arange(margin), width - margin + np.arange(margin)])
-    fc_re, fc_im = wave(side_places, np.arange(width) - width // 2, width, width)
-    from_re = np.concatenate([fc_re[:margin], fc_im[:margin], fc_re[margin:], fc_im[margin:]])
-    from_im = np.concatenate([-fc_im[:margin], fc_re[:margin], -fc_im[margin:], fc_re[margin:]])
-    sides = [two_parts(from_re), two_parts(from_im)]
-    big = np.concatenate(
-        [*two_parts(full_rows), sides[0][0], sides[1][0], sides[0][1], sides[1][1]]
-    )
-    small = np.concatenate([*two_parts(rows.T), *two_parts(cols.T)])
+    big = []
+    for parity in range(2):
+        freqs = np.arange(parity, height, 2) - height // 2
+        re, im = wave(np.arange(height // 2), freqs, height, height)
+        big += two_parts(np.block([[re, -im], [im, re]]))
+    for parity in range(2):
+        left = np.arange(parity, margin, 2)
+        freqs = np.arange(width // 2) - width // 2
+        l_re, l_im = wave(left, freqs, width, width)
+        r_re, r_im = wave(left + width - margin, freqs, width, width)
+        from_re = two_parts(np.concatenate([l_re, l_im, r_re, r_im]))
+        from_im = two_parts(np.concatenate([-l_im, l_re, -r_im, r_re]))
+        big += [from_re[0], from_im[0], from_re[1], from_im[1]]
+    big = np.concatenate(big)
+    back = np.concatenate([back_rows, back_cols])
     out_shape = (
         jax.ShapeDtypeStruct(spectrum.shape, F32),
         jax.ShapeDtypeStruct((height, 2 * width), BF16),
@@ -615,51 +672,72 @@
         input_output_aliases={5: 5},
         scratch_shapes=[
             pltpu.VMEM((2, height + 8, width + 128), F32),
-            pltpu.VMEM(spectrum.shape, F32),
+            pltpu.VMEM((2, width // 128, height, 128), F32),
             pltpu.VMEM(big.shape, BF16),
+            pltpu.VMEM((height // 128, 4 * margin, 128), F32),
             pltpu.SemaphoreType.DMA,
-            pltpu.SemaphoreType.DMA,
+            pltpu.SemaphoreType.DMA((width // 128,)),
         ],
         compiler_params=pltpu.CompilerParams(vmem_limit_bytes=LIMIT),
         name="update",
     )(
-        led_row, led_col, patterns, where, field, weight, *window_parts, spectrum, pupil, small,
+        led_row, led_col, patterns, where, field, weight, *window_parts, spectrum, pupil, back,
         pltpu.with_memory_space_constraint(jnp.asarray(big), pltpu.HBM),
     )[:5]
 
 
 def object_kernel(high_ref, low_ref, table_ref, out_hbm, edges_ref, out, sems):
-    core = out.shape[1]
+    core = out.shape[2]
     margin = edges_ref.shape[2]
-    width = high_ref.shape[1] // 2
+    half = core // 2
+    depth = high_ref.shape[1] // 4
+    cuts = (slice(0, half // 2 // 16 * 16 + 16), slice(half // 2 // 16 * 16 + 16, half))
     stores = []
+    for number, cut in enumerate(cuts):
+        for parity in range(2):
+            lefts = []
+            for begin in (4 * parity * half, (4 * parity + 1) * half):
+                rows = slice(begin + cut.start, begin + cut.stop)
+                more = slice(rows.start + 2 * half, rows.stop + 2 * half)
+                lefts.append(jnp.concatenate([table_ref[rows], table_ref[more], table_ref[rows]], axis=1))
+            left = jnp.concatenate(lefts, axis=0)
+            products = []
+            for part in range(2):
+                lanes = slice((2 * parity + part) * depth, (2 * parity + part + 1) * depth)
+                z_hi, z_lo = high_ref[:, lanes], low_ref[:, lanes]
+                products.append(across(left, jnp.concatenate([z_hi, z_hi, z_lo], axis=1)))
+            count = cut.stop - cut.start
+            rows = pl.ds(2 * cut.start + parity, count, stride=2)
+            real = products[0][:count] - products[1][count:]
+            imaginary = products[0][count:] + products[1][:count]
+            for part, values in enumerate((real, imaginary)):
+                for lanes, block in enumerate(lane_blocks(values)):
+                    out[part, lanes, rows] = block
+        span = pl.ds(2 * cut.start, 2 * (cut.stop - cut.start))
+        for lanes in range(out.shape[1]):
+            store = pltpu.make_async_copy(
+                out.at[:, lanes, span], out_hbm.at[:, span, pl.ds(lanes * 128, 128)],
+                sems.at[number, lanes],
+            )
+            store.start()
+            stores.append(store)
     for part in range(2):
-        total = None
-        for other in range(2):
-            rows = slice((part ^ other) * core, (part ^ other) * core + core)
-            more = slice(rows.start + 2 * core, rows.stop + 2 * core)
-            cut = slice(other * width, (other + 1) * width)
-            z_hi, z_lo = high_ref[:, cut], low_ref[:, cut]
-            one = across(table_ref[rows], z_hi) + across(table_ref[more], z_hi)
-            one = one + across(table_ref[rows], z_lo)
-            if total is None:
-                total = one
-            else:
-                total = total + one if part else total - one
-        out[part] = total
-        edges_ref[part, 0] = total[:margin]
-        edges_ref[part, 1] = total[core - margin :]
-        store = pltpu.make_async_copy(out.at[part], out_hbm.at[part], sems.at[part])
-        store.start()
-        stores.append(store)
+        for side, begin in enumerate((0, core - margin)):
+            edge = [out[part, n, begin : begin + margin] for n in range(out.shape[1])]
+            edges_ref[part, side] = jnp.concatenate(edge, axis=1)
     for store in stores:
         store.wait()
 
 
 def object_core(high, low, margin, core):
     height, width = high.shape[0], high.shape[1] // 2
-    col_re, col_im = wave(margin + np.arange(core), np.arange(width) - width // 2, width, width)
-    table = np.concatenate(two_parts(np.concatenate([col_re, col_im])))
+    table = []
+    for parity in range(2):
+        places = margin + np.arange(parity, core, 2)
+        table += two_parts(
+            np.concatenate(wave(places, np.arange(width // 2) - width // 2, width, width))
+        )
+    table = np.concatenate(table)
     return pl.pallas_call(
         object_kernel,
         out_shape=(
@@ -668,7 +746,10 @@
         ),
         in_specs=vmem_spec(3),
         out_specs=(pl.BlockSpec(memory_space=pltpu.HBM), pl.BlockSpec(memory_space=VMEM)),
-        scratch_shapes=[pltpu.VMEM((2, core, height), F32), pltpu.SemaphoreType.DMA((2,))],
+        scratch_shapes=[
+            pltpu.VMEM((2, height // 128, core, 128), F32),
+            pltpu.SemaphoreType.DMA((2, height // 128)),
+        ],
         compiler_params=pltpu.CompilerParams(vmem_limit_bytes=LIMIT),
         cost_estimate=pl.CostEstimate(
             flops=3_000_000_000, bytes_accessed=5_000_000, transcendentals=0

time: 66.4 us -> 64.5 us (0.971)
  Pallas kernels: 30.7 us -> 28.2 us
    pallas_call x1, Pallas kernels: 9.28 us -> 7.34 us  [update(): pl.pallas_call(functools.partial(update_kernel, group=group), out_shape=o...]
where the time goes in v5:
time: 64.5 us; the launch traced here: 64 us
  Pallas kernels  28.2 us (44%)
  starting transfers between devices  18 us (28%)
  waiting for transfers between devices  9.6 us (15%)
  local copies, waits for them, and re-layouts  7.35 us (11%)
  between operations  0.8 us (1%)
    unnamed x28, local copies, waits for them, and re-layouts  7.35 us
    pallas_call x1, Pallas kernels, update(): pl.pallas_call(functools.partial(update_kernel, group=group), out_shape=o...  7.34 us
    pallas_call x1, Pallas kernels, all_fields(): pl.pallas_call(functools.partial(field_kernel, group=group), out_shape=(j...  7.29 us
    all_to_all x1, starting transfers between devices, body(): lax.all_to_all(narrow, 'tile', split_axis=0, concat_axis=0, tiled=True)  6.3 us
    all_to_all x1, starting transfers between devices, body(): lax.all_to_all(by_rows, 'tile', split_axis=0, concat_axis=0, tiled=True)  6.07 us
    pallas_call x1, Pallas kernels, fetch(): pl.pallas_call(fetch_kernel, out_shape=(jax.ShapeDtypeStruct(field.shape,...  3.96 us
    all_to_all x1, waiting for transfers between devices, body(): lax.all_to_all(by_rows, 'tile', split_axis=0, concat_axis=0, tiled=True)  3.53 us
    pallas_call x1, Pallas kernels, strips(): pl.pallas_call(functools.partial(strips_kernel, frames=frames, core=core,...  3.05 us
  transfers between devices with their start and end apart: 7, of which 4 were waited for; matrix products, arithmetic and copies ran while one was open for 0% of the time, Pallas kernels for 22%

profile of v5, /device:TPU:24, one launch (start us, length us, event | category | flops | bytes accessed | tf_op | source)
XLA Modules:
  0.0 64.0 jit_solution(8803803011092820841)
XLA Ops:
  0.6 0.0 copy-start.3
  0.6 2.1 %gains.1.after = bf16[8,32,512]{2,1,0:T(8,128)(2,1)} custom-call(f32[480,256]{1,0:T(8,128)} %bitcast.18), custom_call_target="tpu_custom_call" | custom-call | tf_op jit(solution)/shard_map/gains/pallas_call | solution.py:122
  2.7 6.1 %all-to-all-start = ((bf16[8,32,512]{2,1,0:T(8,128)(2,1)}), bf16[8,32,512]{2,1,0:T(8,128)(2,1)S(1)}, u32[]{:S(2)}, u32[]{:S(2)}) async-start(bf16[8,32,512]{2,1,0:T(8,128)(2,1)} %gains.1.after), calls=%async_computation | async-start | bytes 524288 | tf_op jit(solution)/shard_map/all_to_all | solution.py:833
  8.8 0.1 pad_add_fusion.where
  8.9 1.2 %copy-done.9 = bf16[4,32,3840]{2,1,0:T(8,128)(2,1)S(1)} copy-done((bf16[4,32,3840]{2,1,0:T(8,128)(2,1)S(1)}, bf16[4,32,3840]{2,1,0:T(8,128)(2,1)}, u32[]{:S(2)}) %copy-start.9) | copy-done | bytes 983064
  10.1 0.7 %copy-done.10 = bf16[4,8,120]{2,1,0:T(8,128)(2,1)S(1)} copy-done((bf16[4,8,120]{2,1,0:T(8,128)(2,1)S(1)}, bf16[4,8,120]{2,1,0:T(8,128)(2,1)}, u32[]{:S(2)}) %copy-start.10) | copy-done | bytes 7704
  10.8 0.0 copy-start.12
  10.8 0.7 %dequantize.1.dq_ref = f32[8,128,512]{2,1,0:T(8,128)S(1)} custom-call(bf16[128,3840]{1,0:T(8,128)(2,1)S(1)} %bitcast.15, bf16[32,120]{1,0:T(8,128)(2,1)S(1)} %bitcast.16, bf16[8,32,512]{2,1,0:T(8,128)(2,1)} %gains.1.after), custom_call_target="tpu_custom_call" | custom-call | flops 2000000000 | bytes 4000000 | tf_op jit(solution)/shard_map/dequantize/pallas_call | solution.py:171
  11.5 3.5 %all-to-all-done.gains_ref = bf16[8,32,512]{2,1,0:T(8,128)(2,1)S(1)} async-done(((bf16[8,32,512]{2,1,0:T(8,128)(2,1)}), bf16[8,32,512]{2,1,0:T(8,128)(2,1)S(1)}, u32[]{:S(2)}, u32[]{:S(2)}) %all-to-all-start) | async-done | bytes 262176 | tf_op jit(solution)/shard_map/all_to_all | solution.py:833
  15.0 3.1 %strips.1 = bf16[8,272,128]{2,1,0:T(8,128)(2,1)} custom-call(s32[4]{0:T(128)S(1)} %pad_add_fusion.where, f32[8,128,512]{2,1,0:T(8,128)S(1)} %dequantize.1.dq_ref, bf16[8,32,512]{2,1,0:T(8,128)(2,1)S(1)} %all-to-all-done.gains_ref, bf16[1024,256]{1,0:T(8,128)(2,1)S(1)} %copy-done.3), custom_call_target="tpu_custom_call" | custom-call | tf_op jit(solution)/shard_map/strips/pallas_call | solution.py:276
  18.1 6.3 %all-to-all-start.1 = ((bf16[8,272,128]{2,1,0:T(8,128)(2,1)}), bf16[8,272,128]{2,1,0:T(8,128)(2,1)S(1)}, u32[]{:S(2)}, u32[]{:S(2)}) async-start(bf16[8,272,128]{2,1,0:T(8,128)(2,1)} %strips.1), calls=%async_computation.1 | async-start | bytes 1114112 | tf_op jit(solution)/shard_map/all_to_all | solution.py:835
  24.4 0.0 copy-start.1
  24.4 1.2 %copy-done.1 = f32[1,2,256,512]{3,2,1,0:T(8,128)S(1)} copy-done((f32[1,2,256,512]{3,2,1,0:T(8,128)S(1)}, f32[1,2,256,512]{3,2,1,0:T(8,128)}, u32[]{:S(2)}) %copy-start.1) | copy-done | bytes 1048600
  25.7 0.9 %copy-done.13 = bf16[256,384]{1,0:T(8,128)(2,1)S(1)} copy-done((bf16[256,384]{1,0:T(8,128)(2,1)S(1)}, bf16[256,384]{1,0:T(8,128)(2,1)}, u32[]{:S(2)}) %copy-start.13) | copy-done | bytes 196632
  26.6 7.3 %fields.1 = (f32[32,256,256]{2,1,0:T(8,128)S(1)}, f32[16,128,256]{2,1,0:T(8,128)S(1)}, bf16[128,512]{1,0:T(8,128)(2,1)S(1)}, f32[136,256]{1,0:T(8,128)S(1)}) custom-call(s32[32]{0:T(128)S(1)} %copy-done.7, s32[32]{0:T(128)S(1)} %copy-done.8, s32[4,16]{1,0:T(4,128)S(1)} %bitcast.12, f32[2,256,512]{2,1,0:T(8,128)S(1)} %bitcast.10, ...), custom_call_target="tpu_custom_call" | custom-call | flops 8000000000 | bytes 16000000 | tf_op jit(solution)/shard_map/fields/pallas_call | solution.py:359
  33.9 3.3 %copy-done = f32[32,256,256]{2,1,0:T(8,128)} copy-done((f32[32,256,256]{2,1,0:T(8,128)}, f32[32,256,256]{2,1,0:T(8,128)S(1)}, u32[]{:S(2)}) %copy-start) | copy-done | bytes 8388632
  37.2 0.0 all-to-all-done.1.dq_ref
  37.2 0.5 windows.1.window
  37.6 1.6 %collective-permute-start = (bf16[528,256]{1,0:T(8,128)(2,1)S(1)}, bf16[528,256]{1,0:T(8,128)(2,1)S(1)}, u32[]{:S(2)}, u32[]{:S(2)}) collective-permute-start(bf16[528,256]{1,0:T(8,128)(2,1)S(1)} %windows.1.window), channel_id=1, source_target_pairs={{0,16},{8,24},{16,0},{24,8},{1,17},{9,25},{17,1},{25,9},{2,18},{10... | collective-permute-start | bytes 811016 | tf_op jit(solution)/shard_map/ppermute | solution.py:846
  39.2 0.0 collective-permute-start.1
  39.2 4.0 %fetch.1 = (f32[32,256,256]{2,1,0:T(8,128)S(1)}, f32[32,128,256]{2,1,0:T(8,128)S(1)}) custom-call(s32[4,16]{1,0:T(4,128)S(1)} %bitcast.13, s32[4]{0:T(128)S(1)} %pad_add_fusion.where, f32[16,128,256]{2,1,0:T(8,128)S(1)} %get-tuple-element.20.estimate_ref, bf16[528,256]{1,0:T(8,128)(2,1)S(1)} %windows.1.window, f32[32,256,256]{2,1,0:T(8,128)} %copy-done), custom_call_target="tpu_custom_call" | custom-call | bytes 16000000 | tf_op jit(solution)/shard_map/fetch/pallas_call | solution.py:490
  43.2 1.8 %collective-permute-done.w2 = bf16[528,256]{1,0:T(8,128)(2,1)S(1)} collective-permute-done((bf16[528,256]{1,0:T(8,128)(2,1)S(1)}, bf16[528,256]{1,0:T(8,128)(2,1)S(1)}, u32[]{:S(2)}, u32[]{:S(2)}) %collective-permute-start) | collective-permute-done | bytes 270368 | tf_op jit(solution)/shard_map/ppermute | solution.py:846
  45.0 0.0 collective-permute-start.2
  45.0 0.0 collective-permute-done.1.w1
  45.0 1.5 %collective-permute-done.2.w3 = bf16[528,256]{1,0:T(8,128)(2,1)S(1)} collective-permute-done((bf16[528,256]{1,0:T(8,128)(2,1)S(1)}, bf16[528,256]{1,0:T(8,128)(2,1)S(1)}, u32[]{:S(2)}, u32[]{:S(2)}) %collective-permute-start.2) | collective-permute-done | bytes 270368 | tf_op jit(solution)/shard_map/ppermute | solution.py:849
  46.6 7.3 %update.1 = (f32[2,256,512]{2,1,0:T(8,128)}, bf16[256,1024]{1,0:T(8,128)(2,1)S(1)}, bf16[256,1024]{1,0:T(8,128)(2,1)S(1)}, f32[32,256]{1,0:T(8,128)S(1)}, f32[32...) custom-call(s32[32]{0:T(128)S(1)} %copy-done.7, s32[32]{0:T(128)S(1)} %copy-done.8, ...), custom_call_target="tpu_custom_call", output_to_operand_aliasing={{5}: (5, {})} | custom-call | tf_op jit(solution)/shard_map/update/pallas_call | solution.py:665
  53.9 2.2 %collective-permute-start.3 = (f32[32,256]{1,0:T(8,128)S(1)}, f32[32,256]{1,0:T(8,128)S(1)}, u32[]{:S(2)}, u32[]{:S(2)}) collective-permute-start(f32[32,256]{1,0:T(8,128)S(1)} %get-tuple-element.28), channel_id=1, source_target_pairs={{0,1},{1,0},{2,3},{3,2},{4,5},{5,4},{6,7},{7,6},{8,9},{9,8},{10,11... | collective-permute-start | bytes 98312 | tf_op jit(solution)/shard_map/ppermute | solution.py:826
  56.1 1.9 %collective-permute-start.4 = (f32[32,256]{1,0:T(8,128)S(1)}, f32[32,256]{1,0:T(8,128)S(1)}, u32[]{:S(2)}, u32[]{:S(2)}) collective-permute-start(f32[32,256]{1,0:T(8,128)S(1)} %get-tuple-element.29), channel_id=1, source_target_pairs={{1,2},{2,1},{3,4},{4,3},{5,6},{6,5},{9,10},{10,9},{11,12},{12,11},... | collective-permute-start | bytes 98312 | tf_op jit(solution)/shard_map/ppermute | solution.py:826
  58.0 2.1 %object.1 = (f32[2,480,256]{2,1,0:T(8,128)}, f32[2,2,16,256]{3,2,1,0:T(8,128)S(1)}) custom-call(bf16[256,1024]{1,0:T(8,128)(2,1)S(1)} %get-tuple-element.30.high_ref, bf16[256,1024]{1,0:T(8,128)(2,1)S(1)} %get-tuple-element.31.low_ref, bf16[1920,256]{1,0:T(8,128)(2,1)S(1)} %copy-done.11), custom_call_target="tpu_custom_call" | custom-call | flops 3000000000 | bytes 5000000 | tf_op jit(solution)/shard_map/object/pallas_call | solution.py:741
  60.1 0.0 collective-permute-done.3.first_ref
  60.1 2.7 %collective-permute-done.4.second_ref = f32[32,256]{1,0:T(8,128)S(1)} collective-permute-done((f32[32,256]{1,0:T(8,128)S(1)}, f32[32,256]{1,0:T(8,128)S(1)}, u32[]{:S(2)}, u32[]{:S(2)}) %collective-permute-start.4) | collective-permute-done | bytes 32800 | tf_op jit(solution)/shard_map/ppermute | solution.py:826
  62.8 1.2 %blend.1 = f32[2,480,256]{2,1,0:T(8,128)} custom-call(s32[4]{0:T(128)S(1)} %pad_add_fusion.where, f32[32,256]{1,0:T(8,128)S(1)} %collective-permute-done.3.first_ref, f32[32,256]{1,0:T(8,128)S(1)} %collective-permute-done.4.second_ref, f32[2,2,16,256]{3,2,1,0:T(8,128)S(1)} %get-tuple-element.32.edges_ref, ...), custom_call_target="tpu_custom_call", output_to_operand_aliasing={{}: (4, {})} | custom-call | tf_op jit(solution)/shard_map/blend/pallas_call | solution.py:794
  (20 shorter events, 0.0 us)
Async XLA Ops:
  0.6 14.4 %copy-start.3 = (bf16[1024,256]{1,0:T(8,128)(2,1)S(1)}, bf16[1024,256]{1,0:T(8,128)(2,1)}, u32[]{:S(2)}) copy-start(bf16[1024,256]{1,0:T(8,128)(2,1)} %constant.31.clone.lc_ref) | copy-start | bytes 1572868
  2.7 12.3 %all-to-all-start = ((bf16[8,32,512]{2,1,0:T(8,128)(2,1)}), bf16[8,32,512]{2,1,0:T(8,128)(2,1)S(1)}, u32[]{:S(2)}, u32[]{:S(2)}) async-start(bf16[8,32,512]{2,1,0:T(8,128)(2,1)} %gains.1.after), calls=%async_computation | async-start | bytes 524288 | tf_op jit(solution)/shard_map/all_to_all | solution.py:833
  8.9 1.2 %copy-start.9 = (bf16[4,32,3840]{2,1,0:T(8,128)(2,1)S(1)}, bf16[4,32,3840]{2,1,0:T(8,128)(2,1)}, u32[]{:S(2)}) copy-start(bf16[4,32,3840]{2,1,0:T(8,128)(2,1)} %param.16) | copy-start | bytes 2949124
  10.1 0.7 %copy-start.10 = (bf16[4,8,120]{2,1,0:T(8,128)(2,1)S(1)}, bf16[4,8,120]{2,1,0:T(8,128)(2,1)}, u32[]{:S(2)}) copy-start(bf16[4,8,120]{2,1,0:T(8,128)(2,1)} %param.17) | copy-start | bytes 23044
  10.8 13.6 %copy-start.5 = (f32[2,64,128]{2,1,0:T(8,128)S(1)}, f32[2,64,128]{2,1,0:T(8,128)}, u32[]{:S(2)}) copy-start(f32[2,64,128]{2,1,0:T(8,128)} %pupil_ref.3) | copy-start | bytes 196612
  10.8 13.6 %copy-start.6 = (s32[16,4]{0,1:T(4,128)S(1)}, s32[16,4]{0,1:T(4,128)}, u32[]{:S(2)}) copy-start(s32[16,4]{0,1:T(4,128)} %param.21) | copy-start | bytes 772
  10.8 13.6 %copy-start.7 = (s32[32]{0:T(128)S(1)}, s32[32]{0:T(128)}, u32[]{:S(2)}) copy-start(s32[32]{0:T(128)} %led_row.3) | copy-start | bytes 388
  10.8 13.6 %copy-start.8 = (s32[32]{0:T(128)S(1)}, s32[32]{0:T(128)}, u32[]{:S(2)}) copy-start(s32[32]{0:T(128)} %led_col.3) | copy-start | bytes 388
  10.8 13.6 %copy-start.12 = (bf16[512,512]{1,0:T(8,128)(2,1)S(1)}, bf16[512,512]{1,0:T(8,128)(2,1)}, u32[]{:S(2)}) copy-start(bf16[512,512]{1,0:T(8,128)(2,1)} %constant.34.clone.cols_ref) | copy-start | bytes 1572868
  18.1 19.1 %all-to-all-start.1 = ((bf16[8,272,128]{2,1,0:T(8,128)(2,1)}), bf16[8,272,128]{2,1,0:T(8,128)(2,1)S(1)}, u32[]{:S(2)}, u32[]{:S(2)}) async-start(bf16[8,272,128]{2,1,0:T(8,128)(2,1)} %strips.1), calls=%async_computation.1 | async-start | bytes 1114112 | tf_op jit(solution)/shard_map/all_to_all | solution.py:835
  24.4 1.2 %copy-start.1 = (f32[1,2,256,512]{3,2,1,0:T(8,128)S(1)}, f32[1,2,256,512]{3,2,1,0:T(8,128)}, u32[]{:S(2)}) copy-start(f32[1,2,256,512]{3,2,1,0:T(8,128)} %param.19) | copy-start | bytes 3145732
  25.7 0.9 %copy-start.13 = (bf16[256,384]{1,0:T(8,128)(2,1)S(1)}, bf16[256,384]{1,0:T(8,128)(2,1)}, u32[]{:S(2)}) copy-start(bf16[256,384]{1,0:T(8,128)(2,1)} %constant.35.clone.rows_ref) | copy-start | bytes 589828
  33.9 3.3 %copy-start = (f32[32,256,256]{2,1,0:T(8,128)}, f32[32,256,256]{2,1,0:T(8,128)S(1)}, u32[]{:S(2)}) copy-start(f32[32,256,256]{2,1,0:T(8,128)S(1)} %get-tuple-element.21.field_hbm) | copy-start | bytes 25165828
  37.6 7.4 %collective-permute-start = (bf16[528,256]{1,0:T(8,128)(2,1)S(1)}, bf16[528,256]{1,0:T(8,128)(2,1)S(1)}, u32[]{:S(2)}, u32[]{:S(2)}) collective-permute-start(bf16[528,256]{1,0:T(8,128)(2,1)S(1)} %windows.1.window), channel_id=1, source_target_pairs={{0,16},{8,24},{16,0},{24,8},{1,17},{9,25},{17,1},{25,9},{2,18},{10... | collective-permute-start | bytes 811016 | tf_op jit(solution)/shard_map/ppermute | solution.py:846
  39.2 5.8 %collective-permute-start.1 = (bf16[528,256]{1,0:T(8,128)(2,1)S(1)}, bf16[528,256]{1,0:T(8,128)(2,1)S(1)}, u32[]{:S(2)}, u32[]{:S(2)}) collective-permute-start(bf16[528,256]{1,0:T(8,128)(2,1)S(1)} %windows.1.window), channel_id=1, source_target_pairs={{0,8},{8,0},{16,24},{24,16},{1,9},{9,1},{17,25},{25,17},{2,10},{10... | collective-permute-start | bytes 811016 | tf_op jit(solution)/shard_map/ppermute | solution.py:847
  39.2 7.4 %copy-start.2 = (f32[1,2,256,512]{3,2,1,0:T(8,128)S(1)}, f32[1,2,256,512]{3,2,1,0:T(8,128)}, u32[]{:S(2)}) copy-start(f32[1,2,256,512]{3,2,1,0:T(8,128)} %param.19) | copy-start | bytes 3145732
  39.2 7.4 %copy-start.4 = (bf16[384,256]{1,0:T(8,128)(2,1)S(1)}, bf16[384,256]{1,0:T(8,128)(2,1)}, u32[]{:S(2)}) copy-start(bf16[384,256]{1,0:T(8,128)(2,1)} %constant.37.clone.back_ref) | copy-start | bytes 589828
  45.0 13.0 %copy-start.11 = (bf16[1920,256]{1,0:T(8,128)(2,1)S(1)}, bf16[1920,256]{1,0:T(8,128)(2,1)}, u32[]{:S(2)}) copy-start(bf16[1920,256]{1,0:T(8,128)(2,1)} %constant.38.clone.table_ref) | copy-start | bytes 2949124
  45.0 1.5 %collective-permute-start.2 = (bf16[528,256]{1,0:T(8,128)(2,1)S(1)}, bf16[528,256]{1,0:T(8,128)(2,1)S(1)}, u32[]{:S(2)}, u32[]{:S(2)}) collective-permute-start(bf16[528,256]{1,0:T(8,128)(2,1)S(1)} %collective-permute-done.w2), channel_id=1, source_target_pairs={{0,8},{8,0},{16,24},{24,16},{1,9},{9,1},{17,25},{25,17},{2,10},{10... | collective-permute-start | bytes 811016 | tf_op jit(solution)/shard_map/ppermute | solution.py:849
  53.9 6.2 %collective-permute-start.3 = (f32[32,256]{1,0:T(8,128)S(1)}, f32[32,256]{1,0:T(8,128)S(1)}, u32[]{:S(2)}, u32[]{:S(2)}) collective-permute-start(f32[32,256]{1,0:T(8,128)S(1)} %get-tuple-element.28), channel_id=1, source_target_pairs={{0,1},{1,0},{2,3},{3,2},{4,5},{5,4},{6,7},{7,6},{8,9},{9,8},{10,11... | collective-permute-start | bytes 98312 | tf_op jit(solution)/shard_map/ppermute | solution.py:826
  56.1 6.7 %collective-permute-start.4 = (f32[32,256]{1,0:T(8,128)S(1)}, f32[32,256]{1,0:T(8,128)S(1)}, u32[]{:S(2)}, u32[]{:S(2)}) collective-permute-start(f32[32,256]{1,0:T(8,128)S(1)} %get-tuple-element.29), channel_id=1, source_target_pairs={{1,2},{2,1},{3,4},{4,3},{5,6},{6,5},{9,10},{10,9},{11,12},{12,11},... | collective-permute-start | bytes 98312 | tf_op jit(solution)/shard_map/ppermute | solution.py:826

commit v6 on v5

--- a/solution.py
+++ b/solution.py
@@ -91,26 +91,19 @@
     return rows[:8, :128] + rows[8:, :128]
 
 
-def gains_kernel(flat_hbm, out_hbm, flat, out, sems, out_sems):
-    core, height = flat_hbm.shape
+def gains_kernel(flat_ref, out_hbm, out, sems):
+    core, height = flat_ref.shape
     tiles, rows_here, width = out_hbm.shape
-    spans = [(begin, min(128, core - begin)) for begin in range(0, core, 128)]
-    loads = []
-    for number, (begin, length) in enumerate(spans):
-        part = pl.ds(begin, length)
-        load = pltpu.make_async_copy(flat_hbm.at[part], flat.at[part], sems.at[number])
-        load.start()
-        loads.append(load)
     stores = []
-    for number, (load, (begin, length)) in enumerate(zip(loads, spans)):
-        load.wait()
-        gains = flat[begin : begin + length] - 1.0
+    for number, begin in enumerate(range(0, width, 128)):
+        length = min(128, core - begin)
+        gains = flat_ref[begin : begin + length] - 1.0
         if length < 128:
             gains = jnp.concatenate([gains, jnp.zeros((128 - length, height), F32)], axis=0)
         by_rows = jnp.transpose(gains, (1, 0)).reshape(tiles, rows_here, 128)
         out[:, :, begin : begin + 128] = by_rows.astype(BF16)
         part = (slice(None), slice(None), pl.ds(begin, 128))
-        store = pltpu.make_async_copy(out.at[part], out_hbm.at[part], out_sems.at[number])
+        store = pltpu.make_async_copy(out.at[part], out_hbm.at[part], sems.at[number])
         store.start()
         stores.append(store)
     for store in stores:
@@ -119,20 +112,16 @@
 
 def gains_by_rows(flat, tiles, width):
     core, height = flat.shape
+    shape = (tiles, height // tiles, width)
     return pl.pallas_call(
         gains_kernel,
-        out_shape=jax.ShapeDtypeStruct((tiles, height // tiles, width), BF16),
-        in_specs=[pl.BlockSpec(memory_space=pltpu.HBM)],
+        out_shape=jax.ShapeDtypeStruct(shape, BF16),
+        in_specs=vmem_spec(1),
         out_specs=pl.BlockSpec(memory_space=pltpu.HBM),
-        scratch_shapes=[
-            pltpu.VMEM((core, height), F32),
-            pltpu.VMEM((tiles, height // tiles, width), BF16),
-            pltpu.SemaphoreType.DMA((-(-core // 128),)),
-            pltpu.SemaphoreType.DMA((-(-core // 128),)),
-        ],
+        scratch_shapes=[pltpu.VMEM(shape, BF16), pltpu.SemaphoreType.DMA((width // 128,))],
         compiler_params=pltpu.CompilerParams(vmem_limit_bytes=LIMIT),
         name="gains",
-    )(pltpu.with_memory_space_constraint(flat, pltpu.HBM))
+    )(flat)
 
 
 def dequantize_kernel(raw_ref, scales_ref, after, out_ref, *, core, margin):
@@ -181,14 +170,14 @@
     )(raw.reshape(frames * rows_here, strip), scales.reshape(-1, scales.shape[-1]), after)
 
 
-def strips_kernel(where, dq_ref, gains_ref, lc_ref, out_hbm, out_ref, sems, *, frames, core, margin):
+def strips_kernel(dq_ref, gains_ref, lc_ref, out_hbm, out_ref, sems, *, frames, core, margin):
     tiles, lines, width = dq_ref.shape
     half_w = lc_ref.shape[1]
     rows_here = lines // frames
     line = lax.broadcasted_iota(jnp.int32, (1, width), 1)
     in_core = ((line >= margin) & (line < margin + core)).astype(F32)
     xc = (line.astype(F32) - margin - (core - 1) / 2.0) * in_core
-    first_row = (where[2] * rows_here).astype(F32)
+    first_row = (lax.axis_index("tile") * rows_here).astype(F32)
     height = rows_here * tiles
     yc = lax.broadcasted_iota(jnp.int32, (rows_here, 1), 0).astype(F32)
     yc = yc + (first_row - (height - 1) / 2.0)
@@ -223,7 +212,7 @@
         slope_y = jnp.sum(jnp.concatenate(lines_y + blank, axis=0) * in_core, axis=1, keepdims=True)
         slope_x = jnp.sum(jnp.concatenate(sums + blank, axis=0) * xc, axis=1, keepdims=True)
         own.append(jnp.where(lane == 0, slope_y, jnp.where(lane == 1, slope_x, 0.0)))
-        return split(flattened)
+        return flattened.astype(BF16)
 
     def finish(tile, one):
         means, centred = [], []
@@ -248,12 +237,10 @@
     part_tiles = max(tiles // 2, 1)
     waiting = None
     for begin in range(0, tiles, part_tiles):
-        both = [windowed(tile) for tile in range(begin, begin + part_tiles)]
-        high = jnp.concatenate([pair[0] for pair in both], axis=0)
-        low = jnp.concatenate([pair[1] for pair in both], axis=0)
+        pixels = jnp.concatenate([windowed(t) for t in range(begin, begin + part_tiles)], axis=0)
         if waiting is not None:
             finish(*waiting)
-        narrow = mm(high, lc_hi) + mm(high, lc_lo) + mm(low, lc_hi)
+        narrow = mm(pixels, lc_hi) + mm(pixels, lc_lo)
         for number in range(part_tiles):
             one = (begin + number, narrow[number * lines : (number + 1) * lines])
             if number == part_tiles - 1 and begin + part_tiles < tiles:
@@ -270,18 +257,18 @@
         store.wait()
 
 
-def strips(dequantized, gains, where, lc, frames, core, margin):
+def strips(dequantized, gains, lc, frames, core, margin):
     tiles, lines, _ = dequantized.shape
     shape = (tiles, lines * (lc.shape[1] // 128) + 16, 128)
     return pl.pallas_call(
         functools.partial(strips_kernel, frames=frames, core=core, margin=margin),
         out_shape=jax.ShapeDtypeStruct(shape, BF16),
-        in_specs=[pl.BlockSpec(memory_space=SMEM)] + vmem_spec(3),
+        in_specs=vmem_spec(3),
         out_specs=pl.BlockSpec(memory_space=pltpu.HBM),
         scratch_shapes=[pltpu.VMEM(shape, BF16), pltpu.SemaphoreType.DMA((2,))],
         compiler_params=pltpu.CompilerParams(vmem_limit_bytes=LIMIT),
         name="strips",
-    )(where, dequantized, gains, np.concatenate(two_parts(lc)))
+    )(dequantized, gains, np.concatenate(two_parts(lc)))
 
 
 def box_area(top, left, band_rows, band_cols):
@@ -465,7 +452,7 @@
         weight[patterns[lit, frame]] += value
 
 
-def fetch_kernel(patterns, where, estimate_ref, window, field_hbm, field_ref, weight, sem):
+def fetch_kernel(patterns, estimate_ref, window, field_hbm, field_ref, weight, sem):
     load = pltpu.make_async_copy(field_hbm, field_ref, sem)
     load.start()
     weight[...] = jnp.zeros_like(weight)
@@ -481,11 +468,11 @@
     for place in range(frames_here):
         value = window[place * half_h : (place + 1) * half_h].astype(F32)
         value = -means[place : place + 1, 0:1] - value
-        add_frame(weight, patterns, where[0] * frames_here + place, value)
+        add_frame(weight, patterns, lax.axis_index("grp") * frames_here + place, value)
     load.wait()
 
 
-def fetch(field, estimate, window, patterns, where):
+def fetch(field, estimate, window, patterns):
     leds = field.shape[0]
     return pl.pallas_call(
         fetch_kernel,
@@ -493,7 +480,7 @@
             jax.ShapeDtypeStruct(field.shape, F32),
             jax.ShapeDtypeStruct((leds, *estimate.shape[1:]), F32),
         ),
-        in_specs=[pl.BlockSpec(memory_space=SMEM)] * 2
+        in_specs=[pl.BlockSpec(memory_space=SMEM)]
         + vmem_spec(2)
         + [pl.BlockSpec(memory_space=pltpu.HBM)],
         out_specs=tuple(vmem_spec(2)),
@@ -501,7 +488,7 @@
         compiler_params=pltpu.CompilerParams(vmem_limit_bytes=LIMIT),
         cost_estimate=pl.CostEstimate(flops=0, bytes_accessed=16_000_000, transcendentals=0),
         name="fetch",
-    )(patterns, where, estimate, window, pltpu.with_memory_space_constraint(field, pltpu.HBM))
+    )(patterns, estimate, window, pltpu.with_memory_space_constraint(field, pltpu.HBM))
 
 
 def across(left, right):
@@ -510,7 +497,7 @@
 
 
 def update_kernel(
-    led_row, led_col, patterns, where, field_ref, weight_in, w1, w2, w3,
+    led_row, led_col, patterns, field_ref, weight_in, w1, w2, w3,
     spec_ref, pupil_ref, back_ref, big_hbm,
     fresh_hbm, high_ref, low_ref, first_ref, second_ref, weight,
     grads, fresh_ref, big, sides_ref, big_sem, fresh_sems, *, group,
@@ -519,12 +506,12 @@
     band_rows, band_cols = pupil_ref.shape[1:]
     height, width = spec_ref.shape[1:]
     frames_here = w1.shape[0] // half_h
-    is_odd = where[1] == 1
+    is_odd = lax.rem(lax.axis_index("tile"), 2) == 1
     big_load = pltpu.make_async_copy(big_hbm, big, big_sem)
     big_load.start()
     grads[...] = jnp.zeros_like(grads)
     for slot, window in enumerate((w1, w2, w3)):
-        owner = jnp.bitwise_xor(where[0], slot + 1)
+        owner = jnp.bitwise_xor(lax.axis_index("grp"), slot + 1)
         means = rows_value(window[frames_here * half_h :])
         for place in range(frames_here):
             value = window[place * half_h : (place + 1) * half_h].astype(F32)
@@ -632,7 +619,7 @@
 
 
 def update(
-    field, weight, window_parts, spectrum, pupil, patterns, led_row, led_col, where, tables,
+    field, weight, window_parts, spectrum, pupil, patterns, led_row, led_col, tables,
     margin, group=8,
 ):
     _, _, back_rows, back_cols = tables
@@ -665,11 +652,11 @@
     return pl.pallas_call(
         functools.partial(update_kernel, group=group),
         out_shape=out_shape,
-        in_specs=[pl.BlockSpec(memory_space=SMEM)] * 4
+        in_specs=[pl.BlockSpec(memory_space=SMEM)] * 3
         + vmem_spec(8)
         + [pl.BlockSpec(memory_space=pltpu.HBM)],
         out_specs=(pl.BlockSpec(memory_space=pltpu.HBM), *vmem_spec(5)),
-        input_output_aliases={5: 5},
+        input_output_aliases={4: 5},
         scratch_shapes=[
             pltpu.VMEM((2, height + 8, width + 128), F32),
             pltpu.VMEM((2, width // 128, height, 128), F32),
@@ -681,7 +668,7 @@
         compiler_params=pltpu.CompilerParams(vmem_limit_bytes=LIMIT),
         name="update",
     )(
-        led_row, led_col, patterns, where, field, weight, *window_parts, spectrum, pupil, back,
+        led_row, led_col, patterns, field, weight, *window_parts, spectrum, pupil, back,
         pltpu.with_memory_space_constraint(jnp.asarray(big), pltpu.HBM),
     )[:5]
 
@@ -758,9 +745,9 @@
     )(high, low, table)
 
 
-def blend_kernel(where, first_ref, second_ref, edges_ref, core_hbm, out_hbm, mixed, sems):
-    tile = where[2]
-    is_odd = where[1] == 1
+def blend_kernel(first_ref, second_ref, edges_ref, core_hbm, out_hbm, mixed, sems):
+    tile = lax.axis_index("tile")
+    is_odd = lax.rem(tile, 2) == 1
     margin, core = edges_ref.shape[2], out_hbm.shape[1]
     k = lax.broadcasted_iota(jnp.int32, (margin, 1), 0).astype(F32)
     span = 2.0 * margin
@@ -769,7 +756,7 @@
     sides = (
         ((k + margin + 0.5) / span, (margin - k - 0.5) / span, tile > 0, from_left, 0),
         (
-            (span - k - 0.5) / span, (k + 0.5) / span, tile < where[3] - 1, from_right,
+            (span - k - 0.5) / span, (k + 0.5) / span, tile < lax.axis_size("tile") - 1, from_right,
             core - margin,
         ),
     )
@@ -779,30 +766,27 @@
         other_w = jnp.where(has_other, other_w, 0.0)
         for part in range(2):
             cut = slice(part * margin, (part + 1) * margin)
-            mixed[part, side] = edges_ref[part, side] * own_w + other[cut] * other_w
-            store = pltpu.make_async_copy(
-                mixed.at[part, side], out_hbm.at[part, pl.ds(begin, margin)],
-                sems.at[2 * side + part],
-            )
-            store.start()
-            stores.append(store)
+            mixed[side, part] = edges_ref[part, side] * own_w + other[cut] * other_w
+        store = pltpu.make_async_copy(
+            mixed.at[side], out_hbm.at[:, pl.ds(begin, margin)], sems.at[side]
+        )
+        store.start()
+        stores.append(store)
     for store in stores:
         store.wait()
 
 
-def blend(core_part, edges, first, second, where):
+def blend(core_part, edges, first, second):
     return pl.pallas_call(
         blend_kernel,
         out_shape=jax.ShapeDtypeStruct(core_part.shape, F32),
-        in_specs=[pl.BlockSpec(memory_space=SMEM)]
-        + vmem_spec(3)
-        + [pl.BlockSpec(memory_space=pltpu.HBM)],
+        in_specs=vmem_spec(3) + [pl.BlockSpec(memory_space=pltpu.HBM)],
         out_specs=pl.BlockSpec(memory_space=pltpu.HBM),
-        input_output_aliases={4: 0},
-        scratch_shapes=[pltpu.VMEM(edges.shape, F32), pltpu.SemaphoreType.DMA((4,))],
+        input_output_aliases={3: 0},
+        scratch_shapes=[pltpu.VMEM(edges.shape, F32), pltpu.SemaphoreType.DMA((2,))],
         compiler_params=pltpu.CompilerParams(vmem_limit_bytes=LIMIT),
         name="blend",
-    )(where, first, second, edges, core_part)
+    )(first, second, edges, core_part)
 
 
 def body(raw, scales, flat, spectrum, pupil, patterns, led_row, led_col):
@@ -810,14 +794,10 @@
     margin = OV // 2
     width = core + OV
     tiles = lax.axis_size("tile")
-    tile = lax.axis_index("tile")
-    grp = lax.axis_index("grp")
     frames_here = raw.shape[0]
     band_rows, band_cols = pupil.shape[1:]
     spectrum_tile = spectrum[0]
     patterns = patterns.T
-    odd = lax.rem(tile, 2)
-    where = jnp.stack([grp, odd, tile, jnp.int32(tiles)]).astype(jnp.int32)
 
     swap_a = [(i, i ^ 1) for i in range(tiles)]
     swap_b = [(i, ((i + 1) ^ 1) - 1) for i in range(1, tiles - 1)]
@@ -831,14 +811,14 @@
     by_rows = gains_by_rows(flat.T, tiles, width)
     dequantized = dequantize(raw, scales, by_rows, tiles, core, margin)
     gains = lax.all_to_all(by_rows, "tile", split_axis=0, concat_axis=0, tiled=True)
-    narrow = strips(dequantized, gains, where, passes[1], frames_here, core, margin)
+    narrow = strips(dequantized, gains, passes[1], frames_here, core, margin)
     arrived = lax.all_to_all(narrow, "tile", split_axis=0, concat_axis=0, tiled=True)
     handed = window_tables(tiles, passes, margin, core)
     field, estimate, rows, small = all_fields(
         spectrum_tile, pupil, patterns, led_row, led_col, tables, handed
     )
     window = windows(arrived, rows, small, frames_here, core)
-    field, weight = fetch(field, estimate, window, patterns, where)
+    field, weight = fetch(field, estimate, window, patterns)
 
     swap_core = [(i, i ^ 1) for i in range(4)]
     swap_chip = [(i, i ^ 2) for i in range(4)]
@@ -850,11 +830,11 @@
 
     fresh, high, low, for_a, for_b = update(
         field, weight, (window_1, window_2, window_3), spectrum_tile, pupil, patterns,
-        led_row, led_col, where, tables, margin,
+        led_row, led_col, tables, margin,
     )
     side_a, side_b = neighbours(for_a, for_b)
     core_part, edges = object_core(high, low, margin, core)
-    stitched = blend(core_part, edges, side_a, side_b, where)
+    stitched = blend(core_part, edges, side_a, side_b)
     return fresh[None], jnp.transpose(stitched, (0, 2, 1))
 
 

time: 64.5 us -> 63 us (0.977)
  Pallas kernels: 28.2 us -> 25.6 us
  local copies, waits for them, and re-layouts: 7.35 us -> 8.37 us
    pallas_call x1, Pallas kernels: 2.08 us -> 0.83 us  [gains_by_rows(): pl.pallas_call(gains_kernel, out_shape=jax.ShapeDtypeStruct(shape, BF16),...]
    unnamed x28 -> x30, local copies, waits for them, and re-layouts: 7.35 us -> 8.37 us
    pallas_call x1, Pallas kernels: 3.05 us -> 2.24 us  [strips(): pl.pallas_call(functools.partial(strips_kernel, frames=frames, core=core,...]
where the time goes in v6:
time: 63 us; the launch traced here: 62.5 us
  Pallas kernels  25.6 us (41%)
  starting transfers between devices  18 us (29%)
  waiting for transfers between devices  9.67 us (15%)
  local copies, waits for them, and re-layouts  8.37 us (13%)
  between operations  0.8 us (1%)
    unnamed x30, local copies, waits for them, and re-layouts  8.37 us
    pallas_call x1, Pallas kernels, update(): pl.pallas_call(functools.partial(update_kernel, group=group), out_shape=o...  7.4 us
    pallas_call x1, Pallas kernels, all_fields(): pl.pallas_call(functools.partial(field_kernel, group=group), out_shape=(j...  7.3 us
    all_to_all x1, starting transfers between devices, body(): lax.all_to_all(narrow, 'tile', split_axis=0, concat_axis=0, tiled=True)  6.29 us
    all_to_all x1, starting transfers between devices, body(): lax.all_to_all(by_rows, 'tile', split_axis=0, concat_axis=0, tiled=True)  6.07 us
    pallas_call x1, Pallas kernels, fetch(): pl.pallas_call(fetch_kernel, out_shape=(jax.ShapeDtypeStruct(field.shape,...  3.95 us
    all_to_all x1, waiting for transfers between devices, body(): lax.all_to_all(by_rows, 'tile', split_axis=0, concat_axis=0, tiled=True)  3.61 us
    ppermute x1, waiting for transfers between devices, neighbours(): lax.ppermute(for_b, 'tile', swap_b)  2.69 us
  transfers between devices with their start and end apart: 7, of which 4 were waited for; matrix products, arithmetic and copies ran while one was open for 0% of the time, Pallas kernels for 22%

profile of v6, /device:TPU:24, one launch (start us, length us, event | category | flops | bytes accessed | tf_op | source)
XLA Modules:
  0.0 62.5 jit_solution(459884406217992227)
XLA Ops:
  0.6 0.0 copy-start.4
  0.6 1.0 %copy-done.4 = f32[256,480]{0,1:T(8,128)S(1)} copy-done((f32[256,480]{0,1:T(8,128)S(1)}, f32[256,480]{0,1:T(8,128)}, u32[]{:S(2)}) %copy-start.4) | copy-done | bytes 491544
  1.7 0.8 %gains.1.after = bf16[8,32,512]{2,1,0:T(8,128)(2,1)} custom-call(f32[480,256]{1,0:T(8,128)S(1)} %bitcast.9), custom_call_target="tpu_custom_call" | custom-call | tf_op jit(solution)/shard_map/gains/pallas_call | solution.py:116
  2.5 6.1 %all-to-all-start = ((bf16[8,32,512]{2,1,0:T(8,128)(2,1)}), bf16[8,32,512]{2,1,0:T(8,128)(2,1)S(1)}, u32[]{:S(2)}, u32[]{:S(2)}) async-start(bf16[8,32,512]{2,1,0:T(8,128)(2,1)} %gains.1.after), calls=%async_computation | async-start | bytes 524288 | tf_op jit(solution)/shard_map/all_to_all | solution.py:813
  8.6 1.2 %copy-done.10 = bf16[4,32,3840]{2,1,0:T(8,128)(2,1)S(1)} copy-done((bf16[4,32,3840]{2,1,0:T(8,128)(2,1)S(1)}, bf16[4,32,3840]{2,1,0:T(8,128)(2,1)}, u32[]{:S(2)}) %copy-start.10) | copy-done | bytes 983064
  9.8 0.7 %copy-done.11 = bf16[4,8,120]{2,1,0:T(8,128)(2,1)S(1)} copy-done((bf16[4,8,120]{2,1,0:T(8,128)(2,1)S(1)}, bf16[4,8,120]{2,1,0:T(8,128)(2,1)}, u32[]{:S(2)}) %copy-start.11) | copy-done | bytes 7704
  10.5 0.0 copy-start.13
  10.5 0.7 %dequantize.1.dq_ref = f32[8,128,512]{2,1,0:T(8,128)S(1)} custom-call(bf16[128,3840]{1,0:T(8,128)(2,1)S(1)} %bitcast.13, bf16[32,120]{1,0:T(8,128)(2,1)S(1)} %bitcast.14, bf16[8,32,512]{2,1,0:T(8,128)(2,1)} %gains.1.after), custom_call_target="tpu_custom_call" | custom-call | flops 2000000000 | bytes 4000000 | tf_op jit(solution)/shard_map/dequantize/pallas_call | solution.py:160
  11.2 3.6 %all-to-all-done.gains_ref = bf16[8,32,512]{2,1,0:T(8,128)(2,1)S(1)} async-done(((bf16[8,32,512]{2,1,0:T(8,128)(2,1)}), bf16[8,32,512]{2,1,0:T(8,128)(2,1)S(1)}, u32[]{:S(2)}, u32[]{:S(2)}) %all-to-all-start) | async-done | bytes 262176 | tf_op jit(solution)/shard_map/all_to_all | solution.py:813
  14.8 2.2 %strips.1 = bf16[8,272,128]{2,1,0:T(8,128)(2,1)} custom-call(f32[8,128,512]{2,1,0:T(8,128)S(1)} %dequantize.1.dq_ref, bf16[8,32,512]{2,1,0:T(8,128)(2,1)S(1)} %all-to-all-done.gains_ref, bf16[1024,256]{1,0:T(8,128)(2,1)S(1)} %copy-done.3), custom_call_target="tpu_custom_call" | custom-call | tf_op jit(solution)/shard_map/strips/pallas_call | solution.py:263
  17.1 6.3 %all-to-all-start.1 = ((bf16[8,272,128]{2,1,0:T(8,128)(2,1)}), bf16[8,272,128]{2,1,0:T(8,128)(2,1)S(1)}, u32[]{:S(2)}, u32[]{:S(2)}) async-start(bf16[8,272,128]{2,1,0:T(8,128)(2,1)} %strips.1), calls=%async_computation.1 | async-start | bytes 1114112 | tf_op jit(solution)/shard_map/all_to_all | solution.py:815
  23.4 0.0 copy-start.1
  23.4 1.2 %copy-done.1 = f32[1,2,256,512]{3,2,1,0:T(8,128)S(1)} copy-done((f32[1,2,256,512]{3,2,1,0:T(8,128)S(1)}, f32[1,2,256,512]{3,2,1,0:T(8,128)}, u32[]{:S(2)}) %copy-start.1) | copy-done | bytes 1048600
  24.6 0.9 %copy-done.14 = bf16[256,384]{1,0:T(8,128)(2,1)S(1)} copy-done((bf16[256,384]{1,0:T(8,128)(2,1)S(1)}, bf16[256,384]{1,0:T(8,128)(2,1)}, u32[]{:S(2)}) %copy-start.14) | copy-done | bytes 196632
  25.5 7.3 %fields.1 = (f32[32,256,256]{2,1,0:T(8,128)S(1)}, f32[16,128,256]{2,1,0:T(8,128)S(1)}, bf16[128,512]{1,0:T(8,128)(2,1)S(1)}, f32[136,256]{1,0:T(8,128)S(1)}) custom-call(s32[32]{0:T(128)S(1)} %copy-done.8, s32[32]{0:T(128)S(1)} %copy-done.9, s32[4,16]{1,0:T(4,128)S(1)} %bitcast.10, f32[2,256,512]{2,1,0:T(8,128)S(1)} %bitcast.7, f32[2,64,128]{2,1,0:T(8,128)S(1)} %copy-done.6, ...), custom_call_target="tpu_custom_call" | custom-call | flops 8000000000 | bytes 16000000 | tf_op jit(solution)/shard_map/fields/pallas_call | solution.py:346
  32.9 3.3 %copy-done = f32[32,256,256]{2,1,0:T(8,128)} copy-done((f32[32,256,256]{2,1,0:T(8,128)}, f32[32,256,256]{2,1,0:T(8,128)S(1)}, u32[]{:S(2)}) %copy-start) | copy-done | bytes 8388632
  36.1 0.0 all-to-all-done.1.dq_ref
  36.1 0.5 windows.1.window
  36.6 1.6 %collective-permute-start = (bf16[528,256]{1,0:T(8,128)(2,1)S(1)}, bf16[528,256]{1,0:T(8,128)(2,1)S(1)}, u32[]{:S(2)}, u32[]{:S(2)}) collective-permute-start(bf16[528,256]{1,0:T(8,128)(2,1)S(1)} %windows.1.window), channel_id=1, source_target_pairs={{0,16},{8,24},{16,0},{24,8},{1,17},{9,25},{17,1},{25,9},{2,18},{10... | collective-permute-start | bytes 811016 | tf_op jit(solution)/shard_map/ppermute | solution.py:826
  38.2 0.0 collective-permute-start.1
  38.2 4.0 %fetch.1 = (f32[32,256,256]{2,1,0:T(8,128)S(1)}, f32[32,128,256]{2,1,0:T(8,128)S(1)}) custom-call(s32[4,16]{1,0:T(4,128)S(1)} %bitcast.11, f32[16,128,256]{2,1,0:T(8,128)S(1)} %get-tuple-element.20.estimate_ref, bf16[528,256]{1,0:T(8,128)(2,1)S(1)} %windows.1.window, f32[32,256,256]{2,1,0:T(8,128)} %copy-done), custom_call_target="tpu_custom_call" | custom-call | bytes 16000000 | tf_op jit(solution)/shard_map/fetch/pallas_call | solution.py:477
  42.1 1.8 %collective-permute-done.w2 = bf16[528,256]{1,0:T(8,128)(2,1)S(1)} collective-permute-done((bf16[528,256]{1,0:T(8,128)(2,1)S(1)}, bf16[528,256]{1,0:T(8,128)(2,1)S(1)}, u32[]{:S(2)}, u32[]{:S(2)}) %collective-permute-start) | collective-permute-done | bytes 270368 | tf_op jit(solution)/shard_map/ppermute | solution.py:826
  44.0 0.0 collective-permute-start.2
  44.0 0.0 collective-permute-done.1.w1
  44.0 1.5 %collective-permute-done.2.w3 = bf16[528,256]{1,0:T(8,128)(2,1)S(1)} collective-permute-done((bf16[528,256]{1,0:T(8,128)(2,1)S(1)}, bf16[528,256]{1,0:T(8,128)(2,1)S(1)}, u32[]{:S(2)}, u32[]{:S(2)}) %collective-permute-start.2) | collective-permute-done | bytes 270368 | tf_op jit(solution)/shard_map/ppermute | solution.py:829
  45.5 7.4 %update.1 = (f32[2,256,512]{2,1,0:T(8,128)}, bf16[256,1024]{1,0:T(8,128)(2,1)S(1)}, bf16[256,1024]{1,0:T(8,128)(2,1)S(1)}, f32[32,256]{1,0:T(8,128)S(1)}, f32[32...) custom-call(s32[32]{0:T(128)S(1)} %copy-done.8, s32[32]{0:T(128)S(1)} %copy-done.9, ...), custom_call_target="tpu_custom_call", output_to_operand_aliasing={{5}: (4, {})} | custom-call | tf_op jit(solution)/shard_map/update/pallas_call | solution.py:652
  52.9 2.2 %collective-permute-start.3 = (f32[32,256]{1,0:T(8,128)S(1)}, f32[32,256]{1,0:T(8,128)S(1)}, u32[]{:S(2)}, u32[]{:S(2)}) collective-permute-start(f32[32,256]{1,0:T(8,128)S(1)} %get-tuple-element.28), channel_id=1, source_target_pairs={{0,1},{1,0},{2,3},{3,2},{4,5},{5,4},{6,7},{7,6},{8,9},{9,8},{10,11... | collective-permute-start | bytes 98312 | tf_op jit(solution)/shard_map/ppermute | solution.py:806
  55.1 1.9 %collective-permute-start.4 = (f32[32,256]{1,0:T(8,128)S(1)}, f32[32,256]{1,0:T(8,128)S(1)}, u32[]{:S(2)}, u32[]{:S(2)}) collective-permute-start(f32[32,256]{1,0:T(8,128)S(1)} %get-tuple-element.29), channel_id=1, source_target_pairs={{1,2},{2,1},{3,4},{4,3},{5,6},{6,5},{9,10},{10,9},{11,12},{12,11},... | collective-permute-start | bytes 98312 | tf_op jit(solution)/shard_map/ppermute | solution.py:806
  57.1 2.1 %object.1 = (f32[2,480,256]{2,1,0:T(8,128)}, f32[2,2,16,256]{3,2,1,0:T(8,128)S(1)}) custom-call(bf16[256,1024]{1,0:T(8,128)(2,1)S(1)} %get-tuple-element.30.high_ref, bf16[256,1024]{1,0:T(8,128)(2,1)S(1)} %get-tuple-element.31.low_ref, bf16[1920,256]{1,0:T(8,128)(2,1)S(1)} %copy-done.12), custom_call_target="tpu_custom_call" | custom-call | flops 3000000000 | bytes 5000000 | tf_op jit(solution)/shard_map/object/pallas_call | solution.py:728
  59.1 0.0 collective-permute-done.3.first_ref
  59.1 2.7 %collective-permute-done.4.second_ref = f32[32,256]{1,0:T(8,128)S(1)} collective-permute-done((f32[32,256]{1,0:T(8,128)S(1)}, f32[32,256]{1,0:T(8,128)S(1)}, u32[]{:S(2)}, u32[]{:S(2)}) %collective-permute-start.4) | collective-permute-done | bytes 32800 | tf_op jit(solution)/shard_map/ppermute | solution.py:806
  61.8 0.7 %blend.1 = f32[2,480,256]{2,1,0:T(8,128)} custom-call(f32[32,256]{1,0:T(8,128)S(1)} %collective-permute-done.3.first_ref, f32[32,256]{1,0:T(8,128)S(1)} %collective-permute-done.4.second_ref, f32[2,2,16,256]{3,2,1,0:T(8,128)S(1)} %get-tuple-element.32.edges_ref, f32[2,480,256]{2,1,0:T(8,128)} %get-tuple-element.33.core_hbm), custom_call_target="tpu_custom_call", output_to_operand_aliasing={{}: (3, {})} | custom-call | tf_op jit(solution)/shard_map/blend/pallas_call | solution.py:780
  (21 shorter events, 0.0 us)
Async XLA Ops:
  0.6 1.0 %copy-start.4 = (f32[256,480]{0,1:T(8,128)S(1)}, f32[256,480]{0,1:T(8,128)}, u32[]{:S(2)}) copy-start(f32[256,480]{0,1:T(8,128)} %param.18) | copy-start | bytes 1474564
  1.7 13.1 %copy-start.3 = (bf16[1024,256]{1,0:T(8,128)(2,1)S(1)}, bf16[1024,256]{1,0:T(8,128)(2,1)}, u32[]{:S(2)}) copy-start(bf16[1024,256]{1,0:T(8,128)(2,1)} %constant.16.clone.lc_ref) | copy-start | bytes 1572868
  2.5 12.3 %all-to-all-start = ((bf16[8,32,512]{2,1,0:T(8,128)(2,1)}), bf16[8,32,512]{2,1,0:T(8,128)(2,1)S(1)}, u32[]{:S(2)}, u32[]{:S(2)}) async-start(bf16[8,32,512]{2,1,0:T(8,128)(2,1)} %gains.1.after), calls=%async_computation | async-start | bytes 524288 | tf_op jit(solution)/shard_map/all_to_all | solution.py:813
  8.6 1.2 %copy-start.10 = (bf16[4,32,3840]{2,1,0:T(8,128)(2,1)S(1)}, bf16[4,32,3840]{2,1,0:T(8,128)(2,1)}, u32[]{:S(2)}) copy-start(bf16[4,32,3840]{2,1,0:T(8,128)(2,1)} %param.16) | copy-start | bytes 2949124
  9.8 0.7 %copy-start.11 = (bf16[4,8,120]{2,1,0:T(8,128)(2,1)S(1)}, bf16[4,8,120]{2,1,0:T(8,128)(2,1)}, u32[]{:S(2)}) copy-start(bf16[4,8,120]{2,1,0:T(8,128)(2,1)} %param.17) | copy-start | bytes 23044
  10.5 12.9 %copy-start.6 = (f32[2,64,128]{2,1,0:T(8,128)S(1)}, f32[2,64,128]{2,1,0:T(8,128)}, u32[]{:S(2)}) copy-start(f32[2,64,128]{2,1,0:T(8,128)} %pupil_ref.3) | copy-start | bytes 196612
  10.5 12.9 %copy-start.7 = (s32[16,4]{0,1:T(4,128)S(1)}, s32[16,4]{0,1:T(4,128)}, u32[]{:S(2)}) copy-start(s32[16,4]{0,1:T(4,128)} %param.21) | copy-start | bytes 772
  10.5 12.9 %copy-start.8 = (s32[32]{0:T(128)S(1)}, s32[32]{0:T(128)}, u32[]{:S(2)}) copy-start(s32[32]{0:T(128)} %led_row.3) | copy-start | bytes 388
  10.5 12.9 %copy-start.9 = (s32[32]{0:T(128)S(1)}, s32[32]{0:T(128)}, u32[]{:S(2)}) copy-start(s32[32]{0:T(128)} %led_col.3) | copy-start | bytes 388
  10.5 12.9 %copy-start.13 = (bf16[512,512]{1,0:T(8,128)(2,1)S(1)}, bf16[512,512]{1,0:T(8,128)(2,1)}, u32[]{:S(2)}) copy-start(bf16[512,512]{1,0:T(8,128)(2,1)} %constant.19.clone.cols_ref) | copy-start | bytes 1572868
  17.1 19.1 %all-to-all-start.1 = ((bf16[8,272,128]{2,1,0:T(8,128)(2,1)}), bf16[8,272,128]{2,1,0:T(8,128)(2,1)S(1)}, u32[]{:S(2)}, u32[]{:S(2)}) async-start(bf16[8,272,128]{2,1,0:T(8,128)(2,1)} %strips.1), calls=%async_computation.1 | async-start | bytes 1114112 | tf_op jit(solution)/shard_map/all_to_all | solution.py:815
  23.4 1.2 %copy-start.1 = (f32[1,2,256,512]{3,2,1,0:T(8,128)S(1)}, f32[1,2,256,512]{3,2,1,0:T(8,128)}, u32[]{:S(2)}) copy-start(f32[1,2,256,512]{3,2,1,0:T(8,128)} %param.19) | copy-start | bytes 3145732
  24.6 0.9 %copy-start.14 = (bf16[256,384]{1,0:T(8,128)(2,1)S(1)}, bf16[256,384]{1,0:T(8,128)(2,1)}, u32[]{:S(2)}) copy-start(bf16[256,384]{1,0:T(8,128)(2,1)} %constant.20.clone.rows_ref) | copy-start | bytes 589828
  32.8 3.3 %copy-start = (f32[32,256,256]{2,1,0:T(8,128)}, f32[32,256,256]{2,1,0:T(8,128)S(1)}, u32[]{:S(2)}) copy-start(f32[32,256,256]{2,1,0:T(8,128)S(1)} %get-tuple-element.21.field_hbm) | copy-start | bytes 25165828
  36.6 7.4 %collective-permute-start = (bf16[528,256]{1,0:T(8,128)(2,1)S(1)}, bf16[528,256]{1,0:T(8,128)(2,1)S(1)}, u32[]{:S(2)}, u32[]{:S(2)}) collective-permute-start(bf16[528,256]{1,0:T(8,128)(2,1)S(1)} %windows.1.window), channel_id=1, source_target_pairs={{0,16},{8,24},{16,0},{24,8},{1,17},{9,25},{17,1},{25,9},{2,18},{10... | collective-permute-start | bytes 811016 | tf_op jit(solution)/shard_map/ppermute | solution.py:826
  38.2 5.8 %collective-permute-start.1 = (bf16[528,256]{1,0:T(8,128)(2,1)S(1)}, bf16[528,256]{1,0:T(8,128)(2,1)S(1)}, u32[]{:S(2)}, u32[]{:S(2)}) collective-permute-start(bf16[528,256]{1,0:T(8,128)(2,1)S(1)} %windows.1.window), channel_id=1, source_target_pairs={{0,8},{8,0},{16,24},{24,16},{1,9},{9,1},{17,25},{25,17},{2,10},{10... | collective-permute-start | bytes 811016 | tf_op jit(solution)/shard_map/ppermute | solution.py:827
  38.2 7.4 %copy-start.2 = (f32[1,2,256,512]{3,2,1,0:T(8,128)S(1)}, f32[1,2,256,512]{3,2,1,0:T(8,128)}, u32[]{:S(2)}) copy-start(f32[1,2,256,512]{3,2,1,0:T(8,128)} %param.19) | copy-start | bytes 3145732
  38.2 7.4 %copy-start.5 = (bf16[384,256]{1,0:T(8,128)(2,1)S(1)}, bf16[384,256]{1,0:T(8,128)(2,1)}, u32[]{:S(2)}) copy-start(bf16[384,256]{1,0:T(8,128)(2,1)} %constant.22.clone.back_ref) | copy-start | bytes 589828
  44.0 13.1 %copy-start.12 = (bf16[1920,256]{1,0:T(8,128)(2,1)S(1)}, bf16[1920,256]{1,0:T(8,128)(2,1)}, u32[]{:S(2)}) copy-start(bf16[1920,256]{1,0:T(8,128)(2,1)} %constant.23.clone.table_ref) | copy-start | bytes 2949124
  44.0 1.5 %collective-permute-start.2 = (bf16[528,256]{1,0:T(8,128)(2,1)S(1)}, bf16[528,256]{1,0:T(8,128)(2,1)S(1)}, u32[]{:S(2)}, u32[]{:S(2)}) collective-permute-start(bf16[528,256]{1,0:T(8,128)(2,1)S(1)} %collective-permute-done.w2), channel_id=1, source_target_pairs={{0,8},{8,0},{16,24},{24,16},{1,9},{9,1},{17,25},{25,17},{2,10},{10... | collective-permute-start | bytes 811016 | tf_op jit(solution)/shard_map/ppermute | solution.py:829
  52.9 6.2 %collective-permute-start.3 = (f32[32,256]{1,0:T(8,128)S(1)}, f32[32,256]{1,0:T(8,128)S(1)}, u32[]{:S(2)}, u32[]{:S(2)}) collective-permute-start(f32[32,256]{1,0:T(8,128)S(1)} %get-tuple-element.28), channel_id=1, source_target_pairs={{0,1},{1,0},{2,3},{3,2},{4,5},{5,4},{6,7},{7,6},{8,9},{9,8},{10,11... | collective-permute-start | bytes 98312 | tf_op jit(solution)/shard_map/ppermute | solution.py:806
  55.1 6.7 %collective-permute-start.4 = (f32[32,256]{1,0:T(8,128)S(1)}, f32[32,256]{1,0:T(8,128)S(1)}, u32[]{:S(2)}, u32[]{:S(2)}) collective-permute-start(f32[32,256]{1,0:T(8,128)S(1)} %get-tuple-element.29), channel_id=1, source_target_pairs={{1,2},{2,1},{3,4},{4,3},{5,6},{6,5},{9,10},{10,9},{11,12},{12,11},... | collective-permute-start | bytes 98312 | tf_op jit(solution)/shard_map/ppermute | solution.py:806

commit v7 on v6

--- a/solution.py
+++ b/solution.py
@@ -187,6 +187,22 @@
     lc_hi, lc_lo = lc_ref[:width], lc_ref[width:]
     own, stores = [], []
 
+    all_yc = jnp.concatenate([yc] * frames, axis=0)
+
+    def by_frame(values, weights):
+        sums = []
+        for frame in range(frames):
+            one = values[frame * rows_here : (frame + 1) * rows_here]
+            one = functools.reduce(
+                jnp.add, [one[row : row + 8] for row in range(0, rows_here, 8)]
+            )
+            if weights is not None:
+                one = one * weights
+            one = functools.reduce(jnp.add, lane_blocks(one))
+            one = jnp.sum(one, axis=1, keepdims=True)
+            sums.append(jnp.sum(one, axis=0, keepdims=True))
+        return jnp.concatenate(sums + [jnp.zeros((8 - frames, 1), F32)], axis=0)
+
     def windowed(tile):
         gains = pltpu.roll(gains_ref[tile].astype(F32), margin, 1)
         if tile > 0:
@@ -203,30 +219,21 @@
             )
         gains = jnp.concatenate([gains + 1.0] * frames, axis=0)
         flattened = dq_ref[tile] * gains
-        sums, lines_y = [], []
+        slope_y = by_frame(flattened * all_yc, in_core)
+        slope_x = by_frame(flattened, xc)
+        own.append(jnp.where(lane == 0, slope_y, jnp.where(lane == 1, slope_x, 0.0)))
+        return flattened.astype(BF16)
+
+    def finish(tile, one):
+        mean = by_frame(one, None) * (1.0 / (rows_here * half_w))
+        centred = []
         for frame in range(frames):
             cut = slice(frame * rows_here, (frame + 1) * rows_here)
-            sums.append(jnp.sum(flattened[cut], axis=0, keepdims=True))
-            lines_y.append(jnp.sum(flattened[cut] * yc, axis=0, keepdims=True))
-        blank = [jnp.zeros((8 - frames, width), F32)]
-        slope_y = jnp.sum(jnp.concatenate(lines_y + blank, axis=0) * in_core, axis=1, keepdims=True)
-        slope_x = jnp.sum(jnp.concatenate(sums + blank, axis=0) * xc, axis=1, keepdims=True)
-        own.append(jnp.where(lane == 0, slope_y, jnp.where(lane == 1, slope_x, 0.0)))
-        return flattened.astype(BF16)
-
-    def finish(tile, one):
-        means, centred = [], []
-        for frame in range(frames):
-            cut = slice(frame * rows_here, (frame + 1) * rows_here)
-            mean = jnp.sum(one[cut], axis=0, keepdims=True)
-            mean = jnp.sum(mean, axis=1, keepdims=True) * (1.0 / (rows_here * half_w))
-            means.append(mean)
-            centred.append(one[cut] - mean)
+            centred.append(one[cut] - mean[frame : frame + 1])
         centred = jnp.concatenate(centred, axis=0)
         for part in range(half_w // 128):
             columns = centred[:, part * 128 : (part + 1) * 128]
             out_ref[tile, part * lines : (part + 1) * lines] = columns.astype(BF16)
-        mean = jnp.concatenate(means + [jnp.zeros((8 - frames, 1), F32)], axis=0)
         packed = own[tile] + jnp.where(lane == 6, mean, 0.0)
         if tile > 0:
             packed += pltpu.roll(own[tile - 1], 2, 1)
@@ -452,23 +459,29 @@
         weight[patterns[lit, frame]] += value
 
 
+def take_windows(weight, patterns, windows_here, slots, half_h):
+    for window, slot in zip(windows_here, slots):
+        frames_here = window.shape[0] // half_h
+        owner = jnp.bitwise_xor(lax.axis_index("grp"), slot)
+        means = rows_value(window[frames_here * half_h :])
+        for place in range(frames_here):
+            value = window[place * half_h : (place + 1) * half_h].astype(F32)
+            value = -means[place : place + 1, 0:1] - value
+            add_frame(weight, patterns, owner * frames_here + place, value)
+
+
 def fetch_kernel(patterns, estimate_ref, window, field_hbm, field_ref, weight, sem):
     load = pltpu.make_async_copy(field_hbm, field_ref, sem)
     load.start()
     weight[...] = jnp.zeros_like(weight)
     frames, half_h, _ = estimate_ref.shape
-    frames_here = window.shape[0] // half_h
 
     def one_frame(frame, carry):
         add_frame(weight, patterns, frame, estimate_ref[frame])
         return carry
 
     lax.fori_loop(0, frames, one_frame, 0)
-    means = rows_value(window[frames_here * half_h :])
-    for place in range(frames_here):
-        value = window[place * half_h : (place + 1) * half_h].astype(F32)
-        value = -means[place : place + 1, 0:1] - value
-        add_frame(weight, patterns, lax.axis_index("grp") * frames_here + place, value)
+    take_windows(weight, patterns, (window,), (0,), half_h)
     load.wait()
 
 
@@ -491,13 +504,29 @@
     )(patterns, estimate, window, pltpu.with_memory_space_constraint(field, pltpu.HBM))
 
 
+def collect_kernel(patterns, w1, w2, weight_in, weight):
+    take_windows(weight, patterns, (w1, w2), (1, 2), weight.shape[1])
+
+
+def collect(weight, w1, w2, patterns):
+    return pl.pallas_call(
+        collect_kernel,
+        out_shape=jax.ShapeDtypeStruct(weight.shape, F32),
+        in_specs=[pl.BlockSpec(memory_space=SMEM)] + vmem_spec(3),
+        out_specs=pl.BlockSpec(memory_space=VMEM),
+        input_output_aliases={3: 0},
+        compiler_params=pltpu.CompilerParams(vmem_limit_bytes=LIMIT),
+        name="collect",
+    )(patterns, w1, w2, weight)
+
+
 def across(left, right):
     dims = (((1,), (1,)), ((), ()))
     return lax.dot_general(left, right, dims, preferred_element_type=F32)
 
 
 def update_kernel(
-    led_row, led_col, patterns, field_ref, weight_in, w1, w2, w3,
+    led_row, led_col, patterns, field_ref, weight_in, w3,
     spec_ref, pupil_ref, back_ref, big_hbm,
     fresh_hbm, high_ref, low_ref, first_ref, second_ref, weight,
     grads, fresh_ref, big, sides_ref, big_sem, fresh_sems, *, group,
@@ -505,18 +534,11 @@
     leds, half_h, half_w = weight.shape
     band_rows, band_cols = pupil_ref.shape[1:]
     height, width = spec_ref.shape[1:]
-    frames_here = w1.shape[0] // half_h
     is_odd = lax.rem(lax.axis_index("tile"), 2) == 1
     big_load = pltpu.make_async_copy(big_hbm, big, big_sem)
     big_load.start()
     grads[...] = jnp.zeros_like(grads)
-    for slot, window in enumerate((w1, w2, w3)):
-        owner = jnp.bitwise_xor(lax.axis_index("grp"), slot + 1)
-        means = rows_value(window[frames_here * half_h :])
-        for place in range(frames_here):
-            value = window[place * half_h : (place + 1) * half_h].astype(F32)
-            value = -means[place : place + 1, 0:1] - value
-            add_frame(weight, patterns, owner * frames_here + place, value)
+    take_windows(weight, patterns, (w3,), (3,), half_h)
 
     left_rows = 2 * band_rows
     pair_rows, pair_cols = half_h // 2, half_w // 2
@@ -619,7 +641,7 @@
 
 
 def update(
-    field, weight, window_parts, spectrum, pupil, patterns, led_row, led_col, tables,
+    field, weight, window, spectrum, pupil, patterns, led_row, led_col, tables,
     margin, group=8,
 ):
     _, _, back_rows, back_cols = tables
@@ -653,7 +675,7 @@
         functools.partial(update_kernel, group=group),
         out_shape=out_shape,
         in_specs=[pl.BlockSpec(memory_space=SMEM)] * 3
-        + vmem_spec(8)
+        + vmem_spec(6)
         + [pl.BlockSpec(memory_space=pltpu.HBM)],
         out_specs=(pl.BlockSpec(memory_space=pltpu.HBM), *vmem_spec(5)),
         input_output_aliases={4: 5},
@@ -668,7 +690,7 @@
         compiler_params=pltpu.CompilerParams(vmem_limit_bytes=LIMIT),
         name="update",
     )(
-        led_row, led_col, patterns, field, weight, *window_parts, spectrum, pupil, back,
+        led_row, led_col, patterns, field, weight, window, spectrum, pupil, back,
         pltpu.with_memory_space_constraint(jnp.asarray(big), pltpu.HBM),
     )[:5]
 
@@ -827,9 +849,10 @@
     window_1 = other(window, perm=swap_core)
     window_2, field, weight = lax.optimization_barrier((window_2, field, weight))
     window_3 = other(window_2, perm=swap_core)
+    weight = collect(weight, window_1, window_2, patterns)
 
     fresh, high, low, for_a, for_b = update(
-        field, weight, (window_1, window_2, window_3), spectrum_tile, pupil, patterns,
+        field, weight, window_3, spectrum_tile, pupil, patterns,
         led_row, led_col, tables, margin,
     )
     side_a, side_b = neighbours(for_a, for_b)

time: 63 us -> 62.3 us (0.989)
  waiting for transfers between devices: 9.67 us -> 8.68 us
    ppermute x1, waiting for transfers between devices: 1.54 us -> 0.52 us  [body(): window_3 = other(window_2, perm=swap_core)]
    pallas_call x0 -> x1, Pallas kernels: none -> 1 us  [collect(): pl.pallas_call(collect_kernel, out_shape=jax.ShapeDtypeStruct(weight.shap...]
  transfers between devices with their start and end apart: 7 -> 7, of which waited for: 4 -> 4; matrix products, arithmetic and copies ran while one was open for 0% -> 0% of each run, Pallas kernels for 22% -> 24%
where the time goes in v7:
time: 62.3 us; the launch traced here: 61.7 us
  Pallas kernels  25.9 us (42%)
  starting transfers between devices  18 us (29%)
  waiting for transfers between devices  8.68 us (14%)
  local copies, waits for them, and re-layouts  8.37 us (13%)
  between operations  0.81 us (1%)
    unnamed x30, local copies, waits for them, and re-layouts  8.37 us
    pallas_call x1, Pallas kernels, all_fields(): pl.pallas_call(functools.partial(field_kernel, group=group), out_shape=(j...  7.3 us
    pallas_call x1, Pallas kernels, update(): pl.pallas_call(functools.partial(update_kernel, group=group), out_shape=o...  6.91 us
    all_to_all x1, starting transfers between devices, body(): lax.all_to_all(narrow, 'tile', split_axis=0, concat_axis=0, tiled=True)  6.29 us
    all_to_all x1, starting transfers between devices, body(): lax.all_to_all(by_rows, 'tile', split_axis=0, concat_axis=0, tiled=True)  6.07 us
    pallas_call x1, Pallas kernels, fetch(): pl.pallas_call(fetch_kernel, out_shape=(jax.ShapeDtypeStruct(field.shape,...  3.95 us
    all_to_all x1, waiting for transfers between devices, body(): lax.all_to_all(by_rows, 'tile', split_axis=0, concat_axis=0, tiled=True)  3.61 us
    ppermute x1, waiting for transfers between devices, neighbours(): lax.ppermute(for_b, 'tile', swap_b)  2.69 us
  transfers between devices with their start and end apart: 7, of which 4 were waited for; matrix products, arithmetic and copies ran while one was open for 0% of the time, Pallas kernels for 24%

profile of v7, /device:TPU:24, one launch (start us, length us, event | category | flops | bytes accessed | tf_op | source)
XLA Modules:
  0.0 61.7 jit_solution(270521123525737447)
XLA Ops:
  0.6 1.0 %copy-done.4 = f32[256,480]{0,1:T(8,128)S(1)} copy-done((f32[256,480]{0,1:T(8,128)S(1)}, f32[256,480]{0,1:T(8,128)}, u32[]{:S(2)}) %copy-start.4) | copy-done | bytes 491544
  1.7 0.8 %gains.1.after = bf16[8,32,512]{2,1,0:T(8,128)(2,1)} custom-call(f32[480,256]{1,0:T(8,128)S(1)} %bitcast.9), custom_call_target="tpu_custom_call" | custom-call | tf_op jit(solution)/shard_map/gains/pallas_call | solution.py:116
  2.5 6.1 %all-to-all-start = ((bf16[8,32,512]{2,1,0:T(8,128)(2,1)}), bf16[8,32,512]{2,1,0:T(8,128)(2,1)S(1)}, u32[]{:S(2)}, u32[]{:S(2)}) async-start(bf16[8,32,512]{2,1,0:T(8,128)(2,1)} %gains.1.after), calls=%async_computation | async-start | bytes 524288 | tf_op jit(solution)/shard_map/all_to_all | solution.py:835
  8.6 1.2 %copy-done.10 = bf16[4,32,3840]{2,1,0:T(8,128)(2,1)S(1)} copy-done((bf16[4,32,3840]{2,1,0:T(8,128)(2,1)S(1)}, bf16[4,32,3840]{2,1,0:T(8,128)(2,1)}, u32[]{:S(2)}) %copy-start.10) | copy-done | bytes 983064
  9.8 0.7 %copy-done.11 = bf16[4,8,120]{2,1,0:T(8,128)(2,1)S(1)} copy-done((bf16[4,8,120]{2,1,0:T(8,128)(2,1)S(1)}, bf16[4,8,120]{2,1,0:T(8,128)(2,1)}, u32[]{:S(2)}) %copy-start.11) | copy-done | bytes 7704
  10.5 0.0 copy-start.13
  10.5 0.7 %dequantize.1.dq_ref = f32[8,128,512]{2,1,0:T(8,128)S(1)} custom-call(bf16[128,3840]{1,0:T(8,128)(2,1)S(1)} %bitcast.14, bf16[32,120]{1,0:T(8,128)(2,1)S(1)} %bitcast.15, bf16[8,32,512]{2,1,0:T(8,128)(2,1)} %gains.1.after), custom_call_target="tpu_custom_call" | custom-call | flops 2000000000 | bytes 4000000 | tf_op jit(solution)/shard_map/dequantize/pallas_call | solution.py:160
  11.2 3.6 %all-to-all-done.gains_ref = bf16[8,32,512]{2,1,0:T(8,128)(2,1)S(1)} async-done(((bf16[8,32,512]{2,1,0:T(8,128)(2,1)}), bf16[8,32,512]{2,1,0:T(8,128)(2,1)S(1)}, u32[]{:S(2)}, u32[]{:S(2)}) %all-to-all-start) | async-done | bytes 262176 | tf_op jit(solution)/shard_map/all_to_all | solution.py:835
  14.8 2.0 %strips.1 = bf16[8,272,128]{2,1,0:T(8,128)(2,1)} custom-call(f32[8,128,512]{2,1,0:T(8,128)S(1)} %dequantize.1.dq_ref, bf16[8,32,512]{2,1,0:T(8,128)(2,1)S(1)} %all-to-all-done.gains_ref, bf16[1024,256]{1,0:T(8,128)(2,1)S(1)} %copy-done.3), custom_call_target="tpu_custom_call" | custom-call | tf_op jit(solution)/shard_map/strips/pallas_call | solution.py:270
  16.8 6.3 %all-to-all-start.1 = ((bf16[8,272,128]{2,1,0:T(8,128)(2,1)}), bf16[8,272,128]{2,1,0:T(8,128)(2,1)S(1)}, u32[]{:S(2)}, u32[]{:S(2)}) async-start(bf16[8,272,128]{2,1,0:T(8,128)(2,1)} %strips.1), calls=%async_computation.1 | async-start | bytes 1114112 | tf_op jit(solution)/shard_map/all_to_all | solution.py:837
  23.1 0.0 copy-start.1
  23.1 1.2 %copy-done.1 = f32[1,2,256,512]{3,2,1,0:T(8,128)S(1)} copy-done((f32[1,2,256,512]{3,2,1,0:T(8,128)S(1)}, f32[1,2,256,512]{3,2,1,0:T(8,128)}, u32[]{:S(2)}) %copy-start.1) | copy-done | bytes 1048600
  24.3 0.9 %copy-done.14 = bf16[256,384]{1,0:T(8,128)(2,1)S(1)} copy-done((bf16[256,384]{1,0:T(8,128)(2,1)S(1)}, bf16[256,384]{1,0:T(8,128)(2,1)}, u32[]{:S(2)}) %copy-start.14) | copy-done | bytes 196632
  25.3 7.3 %fields.1 = (f32[32,256,256]{2,1,0:T(8,128)S(1)}, f32[16,128,256]{2,1,0:T(8,128)S(1)}, bf16[128,512]{1,0:T(8,128)(2,1)S(1)}, f32[136,256]{1,0:T(8,128)S(1)}) custom-call(s32[32]{0:T(128)S(1)} %copy-done.8, s32[32]{0:T(128)S(1)} %copy-done.9, s32[4,16]{1,0:T(4,128)S(1)} %bitcast.10, f32[2,256,512]{2,1,0:T(8,128)S(1)} %bitcast.7, f32[2,64,128]{2,1,0:T(8,128)S(1)} %copy-done.6, ...), custom_call_target="tpu_custom_call" | custom-call | flops 8000000000 | bytes 16000000 | tf_op jit(solution)/shard_map/fields/pallas_call | solution.py:353
  32.6 3.3 %copy-done = f32[32,256,256]{2,1,0:T(8,128)} copy-done((f32[32,256,256]{2,1,0:T(8,128)}, f32[32,256,256]{2,1,0:T(8,128)S(1)}, u32[]{:S(2)}) %copy-start) | copy-done | bytes 8388632
  35.8 0.0 all-to-all-done.1.dq_ref
  35.8 0.5 windows.1.window
  36.3 1.6 %collective-permute-start = (bf16[528,256]{1,0:T(8,128)(2,1)S(1)}, bf16[528,256]{1,0:T(8,128)(2,1)S(1)}, u32[]{:S(2)}, u32[]{:S(2)}) collective-permute-start(bf16[528,256]{1,0:T(8,128)(2,1)S(1)} %windows.1.window), channel_id=1, source_target_pairs={{0,16},{8,24},{16,0},{24,8},{1,17},{9,25},{17,1},{25,9},{2,18},{10... | collective-permute-start | bytes 811016 | tf_op jit(solution)/shard_map/ppermute | solution.py:848
  37.9 0.0 collective-permute-start.1
  37.9 4.0 %fetch.1 = (f32[32,256,256]{2,1,0:T(8,128)S(1)}, f32[32,128,256]{2,1,0:T(8,128)S(1)}) custom-call(s32[4,16]{1,0:T(4,128)S(1)} %bitcast.11, f32[16,128,256]{2,1,0:T(8,128)S(1)} %get-tuple-element.20.estimate_ref, bf16[528,256]{1,0:T(8,128)(2,1)S(1)} %windows.1.window, f32[32,256,256]{2,1,0:T(8,128)} %copy-done), custom_call_target="tpu_custom_call" | custom-call | bytes 16000000 | tf_op jit(solution)/shard_map/fetch/pallas_call | solution.py:490
  41.8 1.9 %collective-permute-done.w2 = bf16[528,256]{1,0:T(8,128)(2,1)S(1)} collective-permute-done((bf16[528,256]{1,0:T(8,128)(2,1)S(1)}, bf16[528,256]{1,0:T(8,128)(2,1)S(1)}, u32[]{:S(2)}, u32[]{:S(2)}) %collective-permute-start) | collective-permute-done | bytes 270368 | tf_op jit(solution)/shard_map/ppermute | solution.py:848
  43.7 0.0 collective-permute-start.2
  43.7 0.0 collective-permute-done.1.w1
  43.7 1.0 %collect.1.weight_in = f32[32,128,256]{2,1,0:T(8,128)S(1)} custom-call(s32[4,16]{1,0:T(4,128)S(1)} %bitcast.12, bf16[528,256]{1,0:T(8,128)(2,1)S(1)} %collective-permute-done.1.w1, bf16[528,256]{1,0:T(8,128)(2,1)S(1)} %collective-permute-done.w2, f32[32,128,256]{2,1,0:T(8,128)S(1)} %get-tuple-element.26.weight_in), custom_call_target="tpu_custom_call", output_to_operand_aliasing={{}: (3, {})} | custom-call | tf_op jit(solution)/shard_map/collect/pallas_call | solution.py:512
  44.7 0.0 copy-start.12
  44.7 0.5 collective-permute-done.2.w3
  45.3 6.9 %update.1 = (f32[2,256,512]{2,1,0:T(8,128)}, bf16[256,1024]{1,0:T(8,128)(2,1)S(1)}, bf16[256,1024]{1,0:T(8,128)(2,1)S(1)}, f32[32,256]{1,0:T(8,128)S(1)}, f32[32...) custom-call(s32[32]{0:T(128)S(1)} %copy-done.8, s32[32]{0:T(128)S(1)} %copy-done.9, ...), custom_call_target="tpu_custom_call", output_to_operand_aliasing={{5}: (4, {})} | custom-call | tf_op jit(solution)/shard_map/update/pallas_call | solution.py:674
  52.2 2.2 %collective-permute-start.3 = (f32[32,256]{1,0:T(8,128)S(1)}, f32[32,256]{1,0:T(8,128)S(1)}, u32[]{:S(2)}, u32[]{:S(2)}) collective-permute-start(f32[32,256]{1,0:T(8,128)S(1)} %get-tuple-element.28), channel_id=1, source_target_pairs={{0,1},{1,0},{2,3},{3,2},{4,5},{5,4},{6,7},{7,6},{8,9},{9,8},{10,11... | collective-permute-start | bytes 98312 | tf_op jit(solution)/shard_map/ppermute | solution.py:828
  54.4 1.9 %collective-permute-start.4 = (f32[32,256]{1,0:T(8,128)S(1)}, f32[32,256]{1,0:T(8,128)S(1)}, u32[]{:S(2)}, u32[]{:S(2)}) collective-permute-start(f32[32,256]{1,0:T(8,128)S(1)} %get-tuple-element.29), channel_id=1, source_target_pairs={{1,2},{2,1},{3,4},{4,3},{5,6},{6,5},{9,10},{10,9},{11,12},{12,11},... | collective-permute-start | bytes 98312 | tf_op jit(solution)/shard_map/ppermute | solution.py:828
  56.3 2.1 %object.1 = (f32[2,480,256]{2,1,0:T(8,128)}, f32[2,2,16,256]{3,2,1,0:T(8,128)S(1)}) custom-call(bf16[256,1024]{1,0:T(8,128)(2,1)S(1)} %get-tuple-element.30.high_ref, bf16[256,1024]{1,0:T(8,128)(2,1)S(1)} %get-tuple-element.31.low_ref, bf16[1920,256]{1,0:T(8,128)(2,1)S(1)} %copy-done.12), custom_call_target="tpu_custom_call" | custom-call | flops 3000000000 | bytes 5000000 | tf_op jit(solution)/shard_map/object/pallas_call | solution.py:750
  58.4 2.7 %collective-permute-done.4.second_ref = f32[32,256]{1,0:T(8,128)S(1)} collective-permute-done((f32[32,256]{1,0:T(8,128)S(1)}, f32[32,256]{1,0:T(8,128)S(1)}, u32[]{:S(2)}, u32[]{:S(2)}) %collective-permute-start.4) | collective-permute-done | bytes 32800 | tf_op jit(solution)/shard_map/ppermute | solution.py:828
  61.1 0.7 %blend.1 = f32[2,480,256]{2,1,0:T(8,128)} custom-call(f32[32,256]{1,0:T(8,128)S(1)} %collective-permute-done.3.first_ref, f32[32,256]{1,0:T(8,128)S(1)} %collective-permute-done.4.second_ref, f32[2,2,16,256]{3,2,1,0:T(8,128)S(1)} %get-tuple-element.32.edges_ref, f32[2,480,256]{2,1,0:T(8,128)} %get-tuple-element.33.core_hbm), custom_call_target="tpu_custom_call", output_to_operand_aliasing={{}: (3, {})} | custom-call | tf_op jit(solution)/shard_map/blend/pallas_call | solution.py:802
  (22 shorter events, 0.0 us)
Async XLA Ops:
  0.6 1.0 %copy-start.4 = (f32[256,480]{0,1:T(8,128)S(1)}, f32[256,480]{0,1:T(8,128)}, u32[]{:S(2)}) copy-start(f32[256,480]{0,1:T(8,128)} %param.18) | copy-start | bytes 1474564
  1.7 13.1 %copy-start.3 = (bf16[1024,256]{1,0:T(8,128)(2,1)S(1)}, bf16[1024,256]{1,0:T(8,128)(2,1)}, u32[]{:S(2)}) copy-start(bf16[1024,256]{1,0:T(8,128)(2,1)} %constant.16.clone.lc_ref) | copy-start | bytes 1572868
  2.5 12.3 %all-to-all-start = ((bf16[8,32,512]{2,1,0:T(8,128)(2,1)}), bf16[8,32,512]{2,1,0:T(8,128)(2,1)S(1)}, u32[]{:S(2)}, u32[]{:S(2)}) async-start(bf16[8,32,512]{2,1,0:T(8,128)(2,1)} %gains.1.after), calls=%async_computation | async-start | bytes 524288 | tf_op jit(solution)/shard_map/all_to_all | solution.py:835
  8.6 1.2 %copy-start.10 = (bf16[4,32,3840]{2,1,0:T(8,128)(2,1)S(1)}, bf16[4,32,3840]{2,1,0:T(8,128)(2,1)}, u32[]{:S(2)}) copy-start(bf16[4,32,3840]{2,1,0:T(8,128)(2,1)} %param.16) | copy-start | bytes 2949124
  9.8 0.7 %copy-start.11 = (bf16[4,8,120]{2,1,0:T(8,128)(2,1)S(1)}, bf16[4,8,120]{2,1,0:T(8,128)(2,1)}, u32[]{:S(2)}) copy-start(bf16[4,8,120]{2,1,0:T(8,128)(2,1)} %param.17) | copy-start | bytes 23044
  10.5 12.6 %copy-start.6 = (f32[2,64,128]{2,1,0:T(8,128)S(1)}, f32[2,64,128]{2,1,0:T(8,128)}, u32[]{:S(2)}) copy-start(f32[2,64,128]{2,1,0:T(8,128)} %pupil_ref.3) | copy-start | bytes 196612
  10.5 12.6 %copy-start.7 = (s32[16,4]{0,1:T(4,128)S(1)}, s32[16,4]{0,1:T(4,128)}, u32[]{:S(2)}) copy-start(s32[16,4]{0,1:T(4,128)} %param.21) | copy-start | bytes 772
  10.5 12.6 %copy-start.8 = (s32[32]{0:T(128)S(1)}, s32[32]{0:T(128)}, u32[]{:S(2)}) copy-start(s32[32]{0:T(128)} %led_row.3) | copy-start | bytes 388
  10.5 12.6 %copy-start.9 = (s32[32]{0:T(128)S(1)}, s32[32]{0:T(128)}, u32[]{:S(2)}) copy-start(s32[32]{0:T(128)} %led_col.3) | copy-start | bytes 388
  10.5 12.6 %copy-start.13 = (bf16[512,512]{1,0:T(8,128)(2,1)S(1)}, bf16[512,512]{1,0:T(8,128)(2,1)}, u32[]{:S(2)}) copy-start(bf16[512,512]{1,0:T(8,128)(2,1)} %constant.19.clone.cols_ref) | copy-start | bytes 1572868
  16.8 19.1 %all-to-all-start.1 = ((bf16[8,272,128]{2,1,0:T(8,128)(2,1)}), bf16[8,272,128]{2,1,0:T(8,128)(2,1)S(1)}, u32[]{:S(2)}, u32[]{:S(2)}) async-start(bf16[8,272,128]{2,1,0:T(8,128)(2,1)} %strips.1), calls=%async_computation.1 | async-start | bytes 1114112 | tf_op jit(solution)/shard_map/all_to_all | solution.py:837
  23.1 1.2 %copy-start.1 = (f32[1,2,256,512]{3,2,1,0:T(8,128)S(1)}, f32[1,2,256,512]{3,2,1,0:T(8,128)}, u32[]{:S(2)}) copy-start(f32[1,2,256,512]{3,2,1,0:T(8,128)} %param.19) | copy-start | bytes 3145732
  24.3 0.9 %copy-start.14 = (bf16[256,384]{1,0:T(8,128)(2,1)S(1)}, bf16[256,384]{1,0:T(8,128)(2,1)}, u32[]{:S(2)}) copy-start(bf16[256,384]{1,0:T(8,128)(2,1)} %constant.20.clone.rows_ref) | copy-start | bytes 589828
  32.6 3.3 %copy-start = (f32[32,256,256]{2,1,0:T(8,128)}, f32[32,256,256]{2,1,0:T(8,128)S(1)}, u32[]{:S(2)}) copy-start(f32[32,256,256]{2,1,0:T(8,128)S(1)} %get-tuple-element.21.field_hbm) | copy-start | bytes 25165828
  36.3 7.4 %collective-permute-start = (bf16[528,256]{1,0:T(8,128)(2,1)S(1)}, bf16[528,256]{1,0:T(8,128)(2,1)S(1)}, u32[]{:S(2)}, u32[]{:S(2)}) collective-permute-start(bf16[528,256]{1,0:T(8,128)(2,1)S(1)} %windows.1.window), channel_id=1, source_target_pairs={{0,16},{8,24},{16,0},{24,8},{1,17},{9,25},{17,1},{25,9},{2,18},{10... | collective-permute-start | bytes 811016 | tf_op jit(solution)/shard_map/ppermute | solution.py:848
  37.9 5.8 %collective-permute-start.1 = (bf16[528,256]{1,0:T(8,128)(2,1)S(1)}, bf16[528,256]{1,0:T(8,128)(2,1)S(1)}, u32[]{:S(2)}, u32[]{:S(2)}) collective-permute-start(bf16[528,256]{1,0:T(8,128)(2,1)S(1)} %windows.1.window), channel_id=1, source_target_pairs={{0,8},{8,0},{16,24},{24,16},{1,9},{9,1},{17,25},{25,17},{2,10},{10... | collective-permute-start | bytes 811016 | tf_op jit(solution)/shard_map/ppermute | solution.py:849
  43.7 1.6 %copy-start.2 = (f32[1,2,256,512]{3,2,1,0:T(8,128)S(1)}, f32[1,2,256,512]{3,2,1,0:T(8,128)}, u32[]{:S(2)}) copy-start(f32[1,2,256,512]{3,2,1,0:T(8,128)} %param.19) | copy-start | bytes 3145732
  43.7 1.6 %copy-start.5 = (bf16[384,256]{1,0:T(8,128)(2,1)S(1)}, bf16[384,256]{1,0:T(8,128)(2,1)}, u32[]{:S(2)}) copy-start(bf16[384,256]{1,0:T(8,128)(2,1)} %constant.22.clone.back_ref) | copy-start | bytes 589828
  43.7 1.5 %collective-permute-start.2 = (bf16[528,256]{1,0:T(8,128)(2,1)S(1)}, bf16[528,256]{1,0:T(8,128)(2,1)S(1)}, u32[]{:S(2)}, u32[]{:S(2)}) collective-permute-start(bf16[528,256]{1,0:T(8,128)(2,1)S(1)} %collective-permute-done.w2), channel_id=1, source_target_pairs={{0,8},{8,0},{16,24},{24,16},{1,9},{9,1},{17,25},{25,17},{2,10},{10... | collective-permute-start | bytes 811016 | tf_op jit(solution)/shard_map/ppermute | solution.py:851
  44.7 11.6 %copy-start.12 = (bf16[1920,256]{1,0:T(8,128)(2,1)S(1)}, bf16[1920,256]{1,0:T(8,128)(2,1)}, u32[]{:S(2)}) copy-start(bf16[1920,256]{1,0:T(8,128)(2,1)} %constant.23.clone.table_ref) | copy-start | bytes 2949124
  52.2 6.2 %collective-permute-start.3 = (f32[32,256]{1,0:T(8,128)S(1)}, f32[32,256]{1,0:T(8,128)S(1)}, u32[]{:S(2)}, u32[]{:S(2)}) collective-permute-start(f32[32,256]{1,0:T(8,128)S(1)} %get-tuple-element.28), channel_id=1, source_target_pairs={{0,1},{1,0},{2,3},{3,2},{4,5},{5,4},{6,7},{7,6},{8,9},{9,8},{10,11... | collective-permute-start | bytes 98312 | tf_op jit(solution)/shard_map/ppermute | solution.py:828
  54.4 6.7 %collective-permute-start.4 = (f32[32,256]{1,0:T(8,128)S(1)}, f32[32,256]{1,0:T(8,128)S(1)}, u32[]{:S(2)}, u32[]{:S(2)}) collective-permute-start(f32[32,256]{1,0:T(8,128)S(1)} %get-tuple-element.29), channel_id=1, source_target_pairs={{1,2},{2,1},{3,4},{4,3},{5,6},{6,5},{9,10},{10,9},{11,12},{12,11},... | collective-permute-start | bytes 98312 | tf_op jit(solution)/shard_map/ppermute | solution.py:828

commit v8 on v7

--- a/solution.py
+++ b/solution.py
@@ -586,11 +586,11 @@
     fresh_im = spec_ref[1] - (4.0 * STEP) * grads[1, :height, :width]
     for part, fresh in enumerate((fresh_re, fresh_im)):
         for number, block in enumerate(lane_blocks(fresh)):
-            fresh_ref[part, number] = block
+            fresh_ref[part, number, :height] = block
     stores = []
     for number in range(width // 128):
         store = pltpu.make_async_copy(
-            fresh_ref.at[:, number], fresh_hbm.at[:, :, pl.ds(number * 128, 128)],
+            fresh_ref.at[:, number, pl.ds(0, height)], fresh_hbm.at[:, :, pl.ds(number * 128, 128)],
             fresh_sems.at[number],
         )
         store.start()
@@ -620,7 +620,7 @@
     high, low = split(jnp.concatenate(mixed, axis=1))
     high_ref[...] = high
     low_ref[...] = low
-    count = sides_ref.shape[1] // 2
+    count = first_ref.shape[0]
     for parity in range(2):
         table = 4 * height + 4 * count * parity
         cut = slice(parity * width, (parity + 1) * width)
@@ -633,7 +633,7 @@
         for number, block in enumerate(lane_blocks(one)):
             sides_ref[number, pl.ds(parity, count, stride=2)] = block
     sides = jnp.concatenate([sides_ref[n] for n in range(height // 128)], axis=1)
-    to_left, to_right = sides[:count], sides[count:]
+    to_left, to_right = sides[:count], sides[count : 2 * count]
     first_ref[...] = jnp.where(is_odd, to_left, to_right)
     second_ref[...] = jnp.where(is_odd, to_right, to_left)
     for store in stores:
@@ -681,9 +681,9 @@
         input_output_aliases={4: 5},
         scratch_shapes=[
             pltpu.VMEM((2, height + 8, width + 128), F32),
-            pltpu.VMEM((2, width // 128, height, 128), F32),
+            pltpu.VMEM((2, width // 128, height + 8, 128), F32),
             pltpu.VMEM(big.shape, BF16),
-            pltpu.VMEM((height // 128, 4 * margin, 128), F32),
+            pltpu.VMEM((height // 128, 4 * margin + 8, 128), F32),
             pltpu.SemaphoreType.DMA,
             pltpu.SemaphoreType.DMA((width // 128,)),
         ],
@@ -696,7 +696,7 @@
 
 
 def object_kernel(high_ref, low_ref, table_ref, out_hbm, edges_ref, out, sems):
-    core = out.shape[2]
+    core = out_hbm.shape[1]
     margin = edges_ref.shape[2]
     half = core // 2
     depth = high_ref.shape[1] // 4
@@ -756,7 +756,7 @@
         in_specs=vmem_spec(3),
         out_specs=(pl.BlockSpec(memory_space=pltpu.HBM), pl.BlockSpec(memory_space=VMEM)),
         scratch_shapes=[
-            pltpu.VMEM((2, height // 128, core, 128), F32),
+            pltpu.VMEM((2, height // 128, core + 8, 128), F32),
             pltpu.SemaphoreType.DMA((2, height // 128)),
         ],
         compiler_params=pltpu.CompilerParams(vmem_limit_bytes=LIMIT),

time: 62.3 us -> 62.2 us (level)
  no operation moved by 1% of the time
where the time goes in v8:
time: 62.2 us; the launch traced here: 61.7 us
  Pallas kernels  25.8 us (41%)
  starting transfers between devices  18 us (29%)
  waiting for transfers between devices  8.67 us (14%)
  local copies, waits for them, and re-layouts  8.37 us (13%)
  between operations  0.81 us (1%)
    unnamed x30, local copies, waits for them, and re-layouts  8.37 us
    pallas_call x1, Pallas kernels, all_fields(): pl.pallas_call(functools.partial(field_kernel, group=group), out_shape=(j...  7.3 us
    pallas_call x1, Pallas kernels, update(): pl.pallas_call(functools.partial(update_kernel, group=group), out_shape=o...  6.89 us
    all_to_all x1, starting transfers between devices, body(): lax.all_to_all(narrow, 'tile', split_axis=0, concat_axis=0, tiled=True)  6.29 us
    all_to_all x1, starting transfers between devices, body(): lax.all_to_all(by_rows, 'tile', split_axis=0, concat_axis=0, tiled=True)  6.07 us
    pallas_call x1, Pallas kernels, fetch(): pl.pallas_call(fetch_kernel, out_shape=(jax.ShapeDtypeStruct(field.shape,...  3.95 us
    all_to_all x1, waiting for transfers between devices, body(): lax.all_to_all(by_rows, 'tile', split_axis=0, concat_axis=0, tiled=True)  3.61 us
    ppermute x1, waiting for transfers between devices, neighbours(): lax.ppermute(for_b, 'tile', swap_b)  2.68 us
  transfers between devices with their start and end apart: 7, of which 4 were waited for; matrix products, arithmetic and copies ran while one was open for 0% of the time, Pallas kernels for 24%

profile of v8, /device:TPU:24, one launch (start us, length us, event | category | flops | bytes accessed | tf_op | source)
XLA Modules:
  0.0 61.7 jit_solution(864067759760634969)
XLA Ops:
  0.6 1.0 %copy-done.4 = f32[256,480]{0,1:T(8,128)S(1)} copy-done((f32[256,480]{0,1:T(8,128)S(1)}, f32[256,480]{0,1:T(8,128)}, u32[]{:S(2)}) %copy-start.4) | copy-done | bytes 491544
  1.7 0.8 %gains.1.after = bf16[8,32,512]{2,1,0:T(8,128)(2,1)} custom-call(f32[480,256]{1,0:T(8,128)S(1)} %bitcast.9), custom_call_target="tpu_custom_call" | custom-call | tf_op jit(solution)/shard_map/gains/pallas_call | solution.py:116
  2.5 6.1 %all-to-all-start = ((bf16[8,32,512]{2,1,0:T(8,128)(2,1)}), bf16[8,32,512]{2,1,0:T(8,128)(2,1)S(1)}, u32[]{:S(2)}, u32[]{:S(2)}) async-start(bf16[8,32,512]{2,1,0:T(8,128)(2,1)} %gains.1.after), calls=%async_computation | async-start | bytes 524288 | tf_op jit(solution)/shard_map/all_to_all | solution.py:835
  8.6 1.2 %copy-done.10 = bf16[4,32,3840]{2,1,0:T(8,128)(2,1)S(1)} copy-done((bf16[4,32,3840]{2,1,0:T(8,128)(2,1)S(1)}, bf16[4,32,3840]{2,1,0:T(8,128)(2,1)}, u32[]{:S(2)}) %copy-start.10) | copy-done | bytes 983064
  9.8 0.7 %copy-done.11 = bf16[4,8,120]{2,1,0:T(8,128)(2,1)S(1)} copy-done((bf16[4,8,120]{2,1,0:T(8,128)(2,1)S(1)}, bf16[4,8,120]{2,1,0:T(8,128)(2,1)}, u32[]{:S(2)}) %copy-start.11) | copy-done | bytes 7704
  10.5 0.0 copy-start.13
  10.5 0.7 %dequantize.1.dq_ref = f32[8,128,512]{2,1,0:T(8,128)S(1)} custom-call(bf16[128,3840]{1,0:T(8,128)(2,1)S(1)} %bitcast.14, bf16[32,120]{1,0:T(8,128)(2,1)S(1)} %bitcast.15, bf16[8,32,512]{2,1,0:T(8,128)(2,1)} %gains.1.after), custom_call_target="tpu_custom_call" | custom-call | flops 2000000000 | bytes 4000000 | tf_op jit(solution)/shard_map/dequantize/pallas_call | solution.py:160
  11.2 3.6 %all-to-all-done.gains_ref = bf16[8,32,512]{2,1,0:T(8,128)(2,1)S(1)} async-done(((bf16[8,32,512]{2,1,0:T(8,128)(2,1)}), bf16[8,32,512]{2,1,0:T(8,128)(2,1)S(1)}, u32[]{:S(2)}, u32[]{:S(2)}) %all-to-all-start) | async-done | bytes 262176 | tf_op jit(solution)/shard_map/all_to_all | solution.py:835
  14.8 2.0 %strips.1 = bf16[8,272,128]{2,1,0:T(8,128)(2,1)} custom-call(f32[8,128,512]{2,1,0:T(8,128)S(1)} %dequantize.1.dq_ref, bf16[8,32,512]{2,1,0:T(8,128)(2,1)S(1)} %all-to-all-done.gains_ref, bf16[1024,256]{1,0:T(8,128)(2,1)S(1)} %copy-done.3), custom_call_target="tpu_custom_call" | custom-call | tf_op jit(solution)/shard_map/strips/pallas_call | solution.py:270
  16.8 6.3 %all-to-all-start.1 = ((bf16[8,272,128]{2,1,0:T(8,128)(2,1)}), bf16[8,272,128]{2,1,0:T(8,128)(2,1)S(1)}, u32[]{:S(2)}, u32[]{:S(2)}) async-start(bf16[8,272,128]{2,1,0:T(8,128)(2,1)} %strips.1), calls=%async_computation.1 | async-start | bytes 1114112 | tf_op jit(solution)/shard_map/all_to_all | solution.py:837
  23.1 0.0 copy-start.1
  23.1 1.2 %copy-done.1 = f32[1,2,256,512]{3,2,1,0:T(8,128)S(1)} copy-done((f32[1,2,256,512]{3,2,1,0:T(8,128)S(1)}, f32[1,2,256,512]{3,2,1,0:T(8,128)}, u32[]{:S(2)}) %copy-start.1) | copy-done | bytes 1048600
  24.3 0.9 %copy-done.14 = bf16[256,384]{1,0:T(8,128)(2,1)S(1)} copy-done((bf16[256,384]{1,0:T(8,128)(2,1)S(1)}, bf16[256,384]{1,0:T(8,128)(2,1)}, u32[]{:S(2)}) %copy-start.14) | copy-done | bytes 196632
  25.3 7.3 %fields.1 = (f32[32,256,256]{2,1,0:T(8,128)S(1)}, f32[16,128,256]{2,1,0:T(8,128)S(1)}, bf16[128,512]{1,0:T(8,128)(2,1)S(1)}, f32[136,256]{1,0:T(8,128)S(1)}) custom-call(s32[32]{0:T(128)S(1)} %copy-done.8, s32[32]{0:T(128)S(1)} %copy-done.9, s32[4,16]{1,0:T(4,128)S(1)} %bitcast.10, f32[2,256,512]{2,1,0:T(8,128)S(1)} %bitcast.7, f32[2,64,128]{2,1,0:T(8,128)S(1)} %copy-done.6, ...), custom_call_target="tpu_custom_call" | custom-call | flops 8000000000 | bytes 16000000 | tf_op jit(solution)/shard_map/fields/pallas_call | solution.py:353
  32.6 3.3 %copy-done = f32[32,256,256]{2,1,0:T(8,128)} copy-done((f32[32,256,256]{2,1,0:T(8,128)}, f32[32,256,256]{2,1,0:T(8,128)S(1)}, u32[]{:S(2)}) %copy-start) | copy-done | bytes 8388632
  35.8 0.0 all-to-all-done.1.dq_ref
  35.9 0.5 windows.1.window
  36.3 1.6 %collective-permute-start = (bf16[528,256]{1,0:T(8,128)(2,1)S(1)}, bf16[528,256]{1,0:T(8,128)(2,1)S(1)}, u32[]{:S(2)}, u32[]{:S(2)}) collective-permute-start(bf16[528,256]{1,0:T(8,128)(2,1)S(1)} %windows.1.window), channel_id=1, source_target_pairs={{0,16},{8,24},{16,0},{24,8},{1,17},{9,25},{17,1},{25,9},{2,18},{10... | collective-permute-start | bytes 811016 | tf_op jit(solution)/shard_map/ppermute | solution.py:848
  37.9 0.0 collective-permute-start.1
  37.9 4.0 %fetch.1 = (f32[32,256,256]{2,1,0:T(8,128)S(1)}, f32[32,128,256]{2,1,0:T(8,128)S(1)}) custom-call(s32[4,16]{1,0:T(4,128)S(1)} %bitcast.11, f32[16,128,256]{2,1,0:T(8,128)S(1)} %get-tuple-element.20.estimate_ref, bf16[528,256]{1,0:T(8,128)(2,1)S(1)} %windows.1.window, f32[32,256,256]{2,1,0:T(8,128)} %copy-done), custom_call_target="tpu_custom_call" | custom-call | bytes 16000000 | tf_op jit(solution)/shard_map/fetch/pallas_call | solution.py:490
  41.9 1.9 %collective-permute-done.w2 = bf16[528,256]{1,0:T(8,128)(2,1)S(1)} collective-permute-done((bf16[528,256]{1,0:T(8,128)(2,1)S(1)}, bf16[528,256]{1,0:T(8,128)(2,1)S(1)}, u32[]{:S(2)}, u32[]{:S(2)}) %collective-permute-start) | collective-permute-done | bytes 270368 | tf_op jit(solution)/shard_map/ppermute | solution.py:848
  43.7 0.0 collective-permute-start.2
  43.7 0.0 collective-permute-done.1.w1
  43.7 1.0 %collect.1.weight_in = f32[32,128,256]{2,1,0:T(8,128)S(1)} custom-call(s32[4,16]{1,0:T(4,128)S(1)} %bitcast.12, bf16[528,256]{1,0:T(8,128)(2,1)S(1)} %collective-permute-done.1.w1, bf16[528,256]{1,0:T(8,128)(2,1)S(1)} %collective-permute-done.w2, f32[32,128,256]{2,1,0:T(8,128)S(1)} %get-tuple-element.26.weight_in), custom_call_target="tpu_custom_call", output_to_operand_aliasing={{}: (3, {})} | custom-call | tf_op jit(solution)/shard_map/collect/pallas_call | solution.py:512
  44.7 0.0 copy-start.12
  44.7 0.5 collective-permute-done.2.w3
  45.3 6.9 %update.1 = (f32[2,256,512]{2,1,0:T(8,128)}, bf16[256,1024]{1,0:T(8,128)(2,1)S(1)}, bf16[256,1024]{1,0:T(8,128)(2,1)S(1)}, f32[32,256]{1,0:T(8,128)S(1)}, f32[32...) custom-call(s32[32]{0:T(128)S(1)} %copy-done.8, s32[32]{0:T(128)S(1)} %copy-done.9, ...), custom_call_target="tpu_custom_call", output_to_operand_aliasing={{5}: (4, {})} | custom-call | tf_op jit(solution)/shard_map/update/pallas_call | solution.py:674
  52.2 2.2 %collective-permute-start.3 = (f32[32,256]{1,0:T(8,128)S(1)}, f32[32,256]{1,0:T(8,128)S(1)}, u32[]{:S(2)}, u32[]{:S(2)}) collective-permute-start(f32[32,256]{1,0:T(8,128)S(1)} %get-tuple-element.28), channel_id=1, source_target_pairs={{0,1},{1,0},{2,3},{3,2},{4,5},{5,4},{6,7},{7,6},{8,9},{9,8},{10,11... | collective-permute-start | bytes 98312 | tf_op jit(solution)/shard_map/ppermute | solution.py:828
  54.3 1.9 %collective-permute-start.4 = (f32[32,256]{1,0:T(8,128)S(1)}, f32[32,256]{1,0:T(8,128)S(1)}, u32[]{:S(2)}, u32[]{:S(2)}) collective-permute-start(f32[32,256]{1,0:T(8,128)S(1)} %get-tuple-element.29), channel_id=1, source_target_pairs={{1,2},{2,1},{3,4},{4,3},{5,6},{6,5},{9,10},{10,9},{11,12},{12,11},... | collective-permute-start | bytes 98312 | tf_op jit(solution)/shard_map/ppermute | solution.py:828
  56.3 2.1 %object.1 = (f32[2,480,256]{2,1,0:T(8,128)}, f32[2,2,16,256]{3,2,1,0:T(8,128)S(1)}) custom-call(bf16[256,1024]{1,0:T(8,128)(2,1)S(1)} %get-tuple-element.30.high_ref, bf16[256,1024]{1,0:T(8,128)(2,1)S(1)} %get-tuple-element.31.low_ref, bf16[1920,256]{1,0:T(8,128)(2,1)S(1)} %copy-done.12), custom_call_target="tpu_custom_call" | custom-call | flops 3000000000 | bytes 5000000 | tf_op jit(solution)/shard_map/object/pallas_call | solution.py:750
  58.4 2.7 %collective-permute-done.4.second_ref = f32[32,256]{1,0:T(8,128)S(1)} collective-permute-done((f32[32,256]{1,0:T(8,128)S(1)}, f32[32,256]{1,0:T(8,128)S(1)}, u32[]{:S(2)}, u32[]{:S(2)}) %collective-permute-start.4) | collective-permute-done | bytes 32800 | tf_op jit(solution)/shard_map/ppermute | solution.py:828
  61.0 0.7 %blend.1 = f32[2,480,256]{2,1,0:T(8,128)} custom-call(f32[32,256]{1,0:T(8,128)S(1)} %collective-permute-done.3.first_ref, f32[32,256]{1,0:T(8,128)S(1)} %collective-permute-done.4.second_ref, f32[2,2,16,256]{3,2,1,0:T(8,128)S(1)} %get-tuple-element.32.edges_ref, f32[2,480,256]{2,1,0:T(8,128)} %get-tuple-element.33.core_hbm), custom_call_target="tpu_custom_call", output_to_operand_aliasing={{}: (3, {})} | custom-call | tf_op jit(solution)/shard_map/blend/pallas_call | solution.py:802
  (22 shorter events, 0.0 us)
Async XLA Ops:
  0.6 1.0 %copy-start.4 = (f32[256,480]{0,1:T(8,128)S(1)}, f32[256,480]{0,1:T(8,128)}, u32[]{:S(2)}) copy-start(f32[256,480]{0,1:T(8,128)} %param.18) | copy-start | bytes 1474564
  1.7 13.1 %copy-start.3 = (bf16[1024,256]{1,0:T(8,128)(2,1)S(1)}, bf16[1024,256]{1,0:T(8,128)(2,1)}, u32[]{:S(2)}) copy-start(bf16[1024,256]{1,0:T(8,128)(2,1)} %constant.16.clone.lc_ref) | copy-start | bytes 1572868
  2.5 12.3 %all-to-all-start = ((bf16[8,32,512]{2,1,0:T(8,128)(2,1)}), bf16[8,32,512]{2,1,0:T(8,128)(2,1)S(1)}, u32[]{:S(2)}, u32[]{:S(2)}) async-start(bf16[8,32,512]{2,1,0:T(8,128)(2,1)} %gains.1.after), calls=%async_computation | async-start | bytes 524288 | tf_op jit(solution)/shard_map/all_to_all | solution.py:835
  8.6 1.2 %copy-start.10 = (bf16[4,32,3840]{2,1,0:T(8,128)(2,1)S(1)}, bf16[4,32,3840]{2,1,0:T(8,128)(2,1)}, u32[]{:S(2)}) copy-start(bf16[4,32,3840]{2,1,0:T(8,128)(2,1)} %param.16) | copy-start | bytes 2949124
  9.8 0.7 %copy-start.11 = (bf16[4,8,120]{2,1,0:T(8,128)(2,1)S(1)}, bf16[4,8,120]{2,1,0:T(8,128)(2,1)}, u32[]{:S(2)}) copy-start(bf16[4,8,120]{2,1,0:T(8,128)(2,1)} %param.17) | copy-start | bytes 23044
  10.5 12.6 %copy-start.6 = (f32[2,64,128]{2,1,0:T(8,128)S(1)}, f32[2,64,128]{2,1,0:T(8,128)}, u32[]{:S(2)}) copy-start(f32[2,64,128]{2,1,0:T(8,128)} %pupil_ref.3) | copy-start | bytes 196612
  10.5 12.6 %copy-start.7 = (s32[16,4]{0,1:T(4,128)S(1)}, s32[16,4]{0,1:T(4,128)}, u32[]{:S(2)}) copy-start(s32[16,4]{0,1:T(4,128)} %param.21) | copy-start | bytes 772
  10.5 12.6 %copy-start.8 = (s32[32]{0:T(128)S(1)}, s32[32]{0:T(128)}, u32[]{:S(2)}) copy-start(s32[32]{0:T(128)} %led_row.3) | copy-start | bytes 388
  10.5 12.6 %copy-start.9 = (s32[32]{0:T(128)S(1)}, s32[32]{0:T(128)}, u32[]{:S(2)}) copy-start(s32[32]{0:T(128)} %led_col.3) | copy-start | bytes 388
  10.5 12.6 %copy-start.13 = (bf16[512,512]{1,0:T(8,128)(2,1)S(1)}, bf16[512,512]{1,0:T(8,128)(2,1)}, u32[]{:S(2)}) copy-start(bf16[512,512]{1,0:T(8,128)(2,1)} %constant.19.clone.cols_ref) | copy-start | bytes 1572868
  16.8 19.1 %all-to-all-start.1 = ((bf16[8,272,128]{2,1,0:T(8,128)(2,1)}), bf16[8,272,128]{2,1,0:T(8,128)(2,1)S(1)}, u32[]{:S(2)}, u32[]{:S(2)}) async-start(bf16[8,272,128]{2,1,0:T(8,128)(2,1)} %strips.1), calls=%async_computation.1 | async-start | bytes 1114112 | tf_op jit(solution)/shard_map/all_to_all | solution.py:837
  23.1 1.2 %copy-start.1 = (f32[1,2,256,512]{3,2,1,0:T(8,128)S(1)}, f32[1,2,256,512]{3,2,1,0:T(8,128)}, u32[]{:S(2)}) copy-start(f32[1,2,256,512]{3,2,1,0:T(8,128)} %param.19) | copy-start | bytes 3145732
  24.3 0.9 %copy-start.14 = (bf16[256,384]{1,0:T(8,128)(2,1)S(1)}, bf16[256,384]{1,0:T(8,128)(2,1)}, u32[]{:S(2)}) copy-start(bf16[256,384]{1,0:T(8,128)(2,1)} %constant.20.clone.rows_ref) | copy-start | bytes 589828
  32.6 3.3 %copy-start = (f32[32,256,256]{2,1,0:T(8,128)}, f32[32,256,256]{2,1,0:T(8,128)S(1)}, u32[]{:S(2)}) copy-start(f32[32,256,256]{2,1,0:T(8,128)S(1)} %get-tuple-element.21.field_hbm) | copy-start | bytes 25165828
  36.3 7.4 %collective-permute-start = (bf16[528,256]{1,0:T(8,128)(2,1)S(1)}, bf16[528,256]{1,0:T(8,128)(2,1)S(1)}, u32[]{:S(2)}, u32[]{:S(2)}) collective-permute-start(bf16[528,256]{1,0:T(8,128)(2,1)S(1)} %windows.1.window), channel_id=1, source_target_pairs={{0,16},{8,24},{16,0},{24,8},{1,17},{9,25},{17,1},{25,9},{2,18},{10... | collective-permute-start | bytes 811016 | tf_op jit(solution)/shard_map/ppermute | solution.py:848
  37.9 5.8 %collective-permute-start.1 = (bf16[528,256]{1,0:T(8,128)(2,1)S(1)}, bf16[528,256]{1,0:T(8,128)(2,1)S(1)}, u32[]{:S(2)}, u32[]{:S(2)}) collective-permute-start(bf16[528,256]{1,0:T(8,128)(2,1)S(1)} %windows.1.window), channel_id=1, source_target_pairs={{0,8},{8,0},{16,24},{24,16},{1,9},{9,1},{17,25},{25,17},{2,10},{10... | collective-permute-start | bytes 811016 | tf_op jit(solution)/shard_map/ppermute | solution.py:849
  43.7 1.6 %copy-start.2 = (f32[1,2,256,512]{3,2,1,0:T(8,128)S(1)}, f32[1,2,256,512]{3,2,1,0:T(8,128)}, u32[]{:S(2)}) copy-start(f32[1,2,256,512]{3,2,1,0:T(8,128)} %param.19) | copy-start | bytes 3145732
  43.7 1.6 %copy-start.5 = (bf16[384,256]{1,0:T(8,128)(2,1)S(1)}, bf16[384,256]{1,0:T(8,128)(2,1)}, u32[]{:S(2)}) copy-start(bf16[384,256]{1,0:T(8,128)(2,1)} %constant.22.clone.back_ref) | copy-start | bytes 589828
  43.7 1.5 %collective-permute-start.2 = (bf16[528,256]{1,0:T(8,128)(2,1)S(1)}, bf16[528,256]{1,0:T(8,128)(2,1)S(1)}, u32[]{:S(2)}, u32[]{:S(2)}) collective-permute-start(bf16[528,256]{1,0:T(8,128)(2,1)S(1)} %collective-permute-done.w2), channel_id=1, source_target_pairs={{0,8},{8,0},{16,24},{24,16},{1,9},{9,1},{17,25},{25,17},{2,10},{10... | collective-permute-start | bytes 811016 | tf_op jit(solution)/shard_map/ppermute | solution.py:851
  44.7 11.5 %copy-start.12 = (bf16[1920,256]{1,0:T(8,128)(2,1)S(1)}, bf16[1920,256]{1,0:T(8,128)(2,1)}, u32[]{:S(2)}) copy-start(bf16[1920,256]{1,0:T(8,128)(2,1)} %constant.23.clone.table_ref) | copy-start | bytes 2949124
  52.2 6.2 %collective-permute-start.3 = (f32[32,256]{1,0:T(8,128)S(1)}, f32[32,256]{1,0:T(8,128)S(1)}, u32[]{:S(2)}, u32[]{:S(2)}) collective-permute-start(f32[32,256]{1,0:T(8,128)S(1)} %get-tuple-element.28), channel_id=1, source_target_pairs={{0,1},{1,0},{2,3},{3,2},{4,5},{5,4},{6,7},{7,6},{8,9},{9,8},{10,11... | collective-permute-start | bytes 98312 | tf_op jit(solution)/shard_map/ppermute | solution.py:828
  54.3 6.7 %collective-permute-start.4 = (f32[32,256]{1,0:T(8,128)S(1)}, f32[32,256]{1,0:T(8,128)S(1)}, u32[]{:S(2)}, u32[]{:S(2)}) collective-permute-start(f32[32,256]{1,0:T(8,128)S(1)} %get-tuple-element.29), channel_id=1, source_target_pairs={{1,2},{2,1},{3,4},{4,3},{5,6},{6,5},{9,10},{10,9},{11,12},{12,11},... | collective-permute-start | bytes 98312 | tf_op jit(solution)/shard_map/ppermute | solution.py:828

commit v9 on v8

--- a/solution.py
+++ b/solution.py
@@ -505,6 +505,7 @@
 
 
 def collect_kernel(patterns, w1, w2, weight_in, weight):
+    weight[...] = weight_in[...]
     take_windows(weight, patterns, (w1, w2), (1, 2), weight.shape[1])
 
 
@@ -514,7 +515,6 @@
         out_shape=jax.ShapeDtypeStruct(weight.shape, F32),
         in_specs=[pl.BlockSpec(memory_space=SMEM)] + vmem_spec(3),
         out_specs=pl.BlockSpec(memory_space=VMEM),
-        input_output_aliases={3: 0},
         compiler_params=pltpu.CompilerParams(vmem_limit_bytes=LIMIT),
         name="collect",
     )(patterns, w1, w2, weight)
@@ -528,8 +528,8 @@
 def update_kernel(
     led_row, led_col, patterns, field_ref, weight_in, w3,
     spec_ref, pupil_ref, back_ref, big_hbm,
-    fresh_hbm, high_ref, low_ref, first_ref, second_ref, weight,
-    grads, fresh_ref, big, sides_ref, big_sem, fresh_sems, *, group,
+    fresh_hbm, high_ref, low_ref, first_ref, second_ref,
+    weight, grads, fresh_ref, big, sides_ref, big_sem, fresh_sems, *, group,
 ):
     leds, half_h, half_w = weight.shape
     band_rows, band_cols = pupil_ref.shape[1:]
@@ -538,6 +538,7 @@
     big_load = pltpu.make_async_copy(big_hbm, big, big_sem)
     big_load.start()
     grads[...] = jnp.zeros_like(grads)
+    weight[...] = weight_in[...]
     take_windows(weight, patterns, (w3,), (3,), half_h)
 
     left_rows = 2 * band_rows
@@ -669,7 +670,6 @@
         jax.ShapeDtypeStruct((height, 2 * width), BF16),
         jax.ShapeDtypeStruct((2 * margin, height), F32),
         jax.ShapeDtypeStruct((2 * margin, height), F32),
-        jax.ShapeDtypeStruct(weight.shape, F32),
     )
     return pl.pallas_call(
         functools.partial(update_kernel, group=group),
@@ -677,9 +677,9 @@
         in_specs=[pl.BlockSpec(memory_space=SMEM)] * 3
         + vmem_spec(6)
         + [pl.BlockSpec(memory_space=pltpu.HBM)],
-        out_specs=(pl.BlockSpec(memory_space=pltpu.HBM), *vmem_spec(5)),
-        input_output_aliases={4: 5},
+        out_specs=(pl.BlockSpec(memory_space=pltpu.HBM), *vmem_spec(4)),
         scratch_shapes=[
+            pltpu.VMEM(weight.shape, F32),
             pltpu.VMEM((2, height + 8, width + 128), F32),
             pltpu.VMEM((2, width // 128, height + 8, 128), F32),
             pltpu.VMEM(big.shape, BF16),
@@ -692,7 +692,7 @@
     )(
         led_row, led_col, patterns, field, weight, window, spectrum, pupil, back,
         pltpu.with_memory_space_constraint(jnp.asarray(big), pltpu.HBM),
-    )[:5]
+    )
 
 
 def object_kernel(high_ref, low_ref, table_ref, out_hbm, edges_ref, out, sems):

time: 62.2 us -> 62.6 us (level)
  transfers between devices with their start and end apart: 7 -> 7, of which waited for: 4 -> 4; matrix products, arithmetic and copies ran while one was open for 0% -> 0% of each run, Pallas kernels for 24% -> 25%
where the time goes in v9:
time: 62.6 us; the launch traced here: 62 us
  Pallas kernels  26.4 us (42%)
  starting transfers between devices  18 us (29%)
  waiting for transfers between devices  8.41 us (13%)
  local copies, waits for them, and re-layouts  8.37 us (13%)
  between operations  0.81 us (1%)
    unnamed x30, local copies, waits for them, and re-layouts  8.37 us
    pallas_call x1, Pallas kernels, all_fields(): pl.pallas_call(functools.partial(field_kernel, group=group), out_shape=(j...  7.3 us
    pallas_call x1, Pallas kernels, update(): pl.pallas_call(functools.partial(update_kernel, group=group), out_shape=o...  7.21 us
    all_to_all x1, starting transfers between devices, body(): lax.all_to_all(narrow, 'tile', split_axis=0, concat_axis=0, tiled=True)  6.29 us
    all_to_all x1, starting transfers between devices, body(): lax.all_to_all(by_rows, 'tile', split_axis=0, concat_axis=0, tiled=True)  6.07 us
    pallas_call x1, Pallas kernels, fetch(): pl.pallas_call(fetch_kernel, out_shape=(jax.ShapeDtypeStruct(field.shape,...  3.95 us
    all_to_all x1, waiting for transfers between devices, body(): lax.all_to_all(by_rows, 'tile', split_axis=0, concat_axis=0, tiled=True)  3.61 us
    ppermute x1, waiting for transfers between devices, neighbours(): lax.ppermute(for_b, 'tile', swap_b)  2.69 us
  transfers between devices with their start and end apart: 7, of which 4 were waited for; matrix products, arithmetic and copies ran while one was open for 0% of the time, Pallas kernels for 25%

profile of v9, /device:TPU:24, one launch (start us, length us, event | category | flops | bytes accessed | tf_op | source)
XLA Modules:
  0.0 62.0 jit_solution(1958397680486571612)
XLA Ops:
  0.6 1.0 %copy-done.4 = f32[256,480]{0,1:T(8,128)S(1)} copy-done((f32[256,480]{0,1:T(8,128)S(1)}, f32[256,480]{0,1:T(8,128)}, u32[]{:S(2)}) %copy-start.4) | copy-done | bytes 491544
  1.7 0.8 %gains.1.after = bf16[8,32,512]{2,1,0:T(8,128)(2,1)} custom-call(f32[480,256]{1,0:T(8,128)S(1)} %bitcast.9), custom_call_target="tpu_custom_call" | custom-call | tf_op jit(solution)/shard_map/gains/pallas_call | solution.py:116
  2.5 6.1 %all-to-all-start = ((bf16[8,32,512]{2,1,0:T(8,128)(2,1)}), bf16[8,32,512]{2,1,0:T(8,128)(2,1)S(1)}, u32[]{:S(2)}, u32[]{:S(2)}) async-start(bf16[8,32,512]{2,1,0:T(8,128)(2,1)} %gains.1.after), calls=%async_computation | async-start | bytes 524288 | tf_op jit(solution)/shard_map/all_to_all | solution.py:835
  8.6 1.2 %copy-done.10 = bf16[4,32,3840]{2,1,0:T(8,128)(2,1)S(1)} copy-done((bf16[4,32,3840]{2,1,0:T(8,128)(2,1)S(1)}, bf16[4,32,3840]{2,1,0:T(8,128)(2,1)}, u32[]{:S(2)}) %copy-start.10) | copy-done | bytes 983064
  9.8 0.7 %copy-done.11 = bf16[4,8,120]{2,1,0:T(8,128)(2,1)S(1)} copy-done((bf16[4,8,120]{2,1,0:T(8,128)(2,1)S(1)}, bf16[4,8,120]{2,1,0:T(8,128)(2,1)}, u32[]{:S(2)}) %copy-start.11) | copy-done | bytes 7704
  10.5 0.0 copy-start.13
  10.5 0.7 %dequantize.1.dq_ref = f32[8,128,512]{2,1,0:T(8,128)S(1)} custom-call(bf16[128,3840]{1,0:T(8,128)(2,1)S(1)} %bitcast.14, bf16[32,120]{1,0:T(8,128)(2,1)S(1)} %bitcast.15, bf16[8,32,512]{2,1,0:T(8,128)(2,1)} %gains.1.after), custom_call_target="tpu_custom_call" | custom-call | flops 2000000000 | bytes 4000000 | tf_op jit(solution)/shard_map/dequantize/pallas_call | solution.py:160
  11.2 3.6 %all-to-all-done.gains_ref = bf16[8,32,512]{2,1,0:T(8,128)(2,1)S(1)} async-done(((bf16[8,32,512]{2,1,0:T(8,128)(2,1)}), bf16[8,32,512]{2,1,0:T(8,128)(2,1)S(1)}, u32[]{:S(2)}, u32[]{:S(2)}) %all-to-all-start) | async-done | bytes 262176 | tf_op jit(solution)/shard_map/all_to_all | solution.py:835
  14.8 2.0 %strips.1 = bf16[8,272,128]{2,1,0:T(8,128)(2,1)} custom-call(f32[8,128,512]{2,1,0:T(8,128)S(1)} %dequantize.1.dq_ref, bf16[8,32,512]{2,1,0:T(8,128)(2,1)S(1)} %all-to-all-done.gains_ref, bf16[1024,256]{1,0:T(8,128)(2,1)S(1)} %copy-done.3), custom_call_target="tpu_custom_call" | custom-call | tf_op jit(solution)/shard_map/strips/pallas_call | solution.py:270
  16.8 6.3 %all-to-all-start.1 = ((bf16[8,272,128]{2,1,0:T(8,128)(2,1)}), bf16[8,272,128]{2,1,0:T(8,128)(2,1)S(1)}, u32[]{:S(2)}, u32[]{:S(2)}) async-start(bf16[8,272,128]{2,1,0:T(8,128)(2,1)} %strips.1), calls=%async_computation.1 | async-start | bytes 1114112 | tf_op jit(solution)/shard_map/all_to_all | solution.py:837
  23.1 0.0 copy-start.1
  23.1 1.2 %copy-done.1 = f32[1,2,256,512]{3,2,1,0:T(8,128)S(1)} copy-done((f32[1,2,256,512]{3,2,1,0:T(8,128)S(1)}, f32[1,2,256,512]{3,2,1,0:T(8,128)}, u32[]{:S(2)}) %copy-start.1) | copy-done | bytes 1048600
  24.3 0.9 %copy-done.14 = bf16[256,384]{1,0:T(8,128)(2,1)S(1)} copy-done((bf16[256,384]{1,0:T(8,128)(2,1)S(1)}, bf16[256,384]{1,0:T(8,128)(2,1)}, u32[]{:S(2)}) %copy-start.14) | copy-done | bytes 196632
  25.3 7.3 %fields.1 = (f32[32,256,256]{2,1,0:T(8,128)S(1)}, f32[16,128,256]{2,1,0:T(8,128)S(1)}, bf16[128,512]{1,0:T(8,128)(2,1)S(1)}, f32[136,256]{1,0:T(8,128)S(1)}) custom-call(s32[32]{0:T(128)S(1)} %copy-done.8, s32[32]{0:T(128)S(1)} %copy-done.9, s32[4,16]{1,0:T(4,128)S(1)} %bitcast.10, f32[2,256,512]{2,1,0:T(8,128)S(1)} %bitcast.7, f32[2,64,128]{2,1,0:T(8,128)S(1)} %copy-done.6, ...), custom_call_target="tpu_custom_call" | custom-call | flops 8000000000 | bytes 16000000 | tf_op jit(solution)/shard_map/fields/pallas_call | solution.py:353
  32.6 3.3 %copy-done = f32[32,256,256]{2,1,0:T(8,128)} copy-done((f32[32,256,256]{2,1,0:T(8,128)}, f32[32,256,256]{2,1,0:T(8,128)S(1)}, u32[]{:S(2)}) %copy-start) | copy-done | bytes 8388632
  35.8 0.0 all-to-all-done.1.dq_ref
  35.9 0.5 windows.1.window
  36.3 1.6 %collective-permute-start = (bf16[528,256]{1,0:T(8,128)(2,1)S(1)}, bf16[528,256]{1,0:T(8,128)(2,1)S(1)}, u32[]{:S(2)}, u32[]{:S(2)}) collective-permute-start(bf16[528,256]{1,0:T(8,128)(2,1)S(1)} %windows.1.window), channel_id=1, source_target_pairs={{0,16},{8,24},{16,0},{24,8},{1,17},{9,25},{17,1},{25,9},{2,18},{10... | collective-permute-start | bytes 811016 | tf_op jit(solution)/shard_map/ppermute | solution.py:848
  37.9 0.0 collective-permute-start.1
  37.9 4.0 %fetch.1 = (f32[32,256,256]{2,1,0:T(8,128)S(1)}, f32[32,128,256]{2,1,0:T(8,128)S(1)}) custom-call(s32[4,16]{1,0:T(4,128)S(1)} %bitcast.11, f32[16,128,256]{2,1,0:T(8,128)S(1)} %get-tuple-element.20.estimate_ref, bf16[528,256]{1,0:T(8,128)(2,1)S(1)} %windows.1.window, f32[32,256,256]{2,1,0:T(8,128)} %copy-done), custom_call_target="tpu_custom_call" | custom-call | bytes 16000000 | tf_op jit(solution)/shard_map/fetch/pallas_call | solution.py:490
  41.9 1.9 %collective-permute-done.w2 = bf16[528,256]{1,0:T(8,128)(2,1)S(1)} collective-permute-done((bf16[528,256]{1,0:T(8,128)(2,1)S(1)}, bf16[528,256]{1,0:T(8,128)(2,1)S(1)}, u32[]{:S(2)}, u32[]{:S(2)}) %collective-permute-start) | collective-permute-done | bytes 270368 | tf_op jit(solution)/shard_map/ppermute | solution.py:848
  43.7 0.0 collective-permute-start.2
  43.7 0.0 collective-permute-done.1.w1
  43.7 1.3 %collect.1.weight_in = f32[32,128,256]{2,1,0:T(8,128)S(1)} custom-call(s32[4,16]{1,0:T(4,128)S(1)} %bitcast.12, bf16[528,256]{1,0:T(8,128)(2,1)S(1)} %collective-permute-done.1.w1, bf16[528,256]{1,0:T(8,128)(2,1)S(1)} %collective-permute-done.w2, f32[32,128,256]{2,1,0:T(8,128)S(1)} %get-tuple-element.26.weight_in), custom_call_target="tpu_custom_call" | custom-call | tf_op jit(solution)/shard_map/collect/pallas_call | solution.py:513
  45.0 0.0 copy-start.12
  45.0 0.3 collective-permute-done.2.w3
  45.3 7.2 %update.1 = (f32[2,256,512]{2,1,0:T(8,128)}, bf16[256,1024]{1,0:T(8,128)(2,1)S(1)}, bf16[256,1024]{1,0:T(8,128)(2,1)S(1)}, f32[32,256]{1,0:T(8,128)S(1)}, f32[32,256]{1,0:T(8,128)S(1)}) custom-call(s32[32]{0:T(128)S(1)} %copy-done.8, s32[32]{0:T(128)S(1)} %copy-done.9, s32[4,16]{1,0:T(4,128)S(1)} %bitcast.13, ...), custom_call_target="tpu_custom_call" | custom-call | tf_op jit(solution)/shard_map/update/pallas_call | solution.py:674
  52.5 2.2 %collective-permute-start.3 = (f32[32,256]{1,0:T(8,128)S(1)}, f32[32,256]{1,0:T(8,128)S(1)}, u32[]{:S(2)}, u32[]{:S(2)}) collective-permute-start(f32[32,256]{1,0:T(8,128)S(1)} %get-tuple-element.28), channel_id=1, source_target_pairs={{0,1},{1,0},{2,3},{3,2},{4,5},{5,4},{6,7},{7,6},{8,9},{9,8},{10,11... | collective-permute-start | bytes 98312 | tf_op jit(solution)/shard_map/ppermute | solution.py:828
  54.7 1.9 %collective-permute-start.4 = (f32[32,256]{1,0:T(8,128)S(1)}, f32[32,256]{1,0:T(8,128)S(1)}, u32[]{:S(2)}, u32[]{:S(2)}) collective-permute-start(f32[32,256]{1,0:T(8,128)S(1)} %get-tuple-element.29), channel_id=1, source_target_pairs={{1,2},{2,1},{3,4},{4,3},{5,6},{6,5},{9,10},{10,9},{11,12},{12,11},... | collective-permute-start | bytes 98312 | tf_op jit(solution)/shard_map/ppermute | solution.py:828
  56.6 2.1 %object.1 = (f32[2,480,256]{2,1,0:T(8,128)}, f32[2,2,16,256]{3,2,1,0:T(8,128)S(1)}) custom-call(bf16[256,1024]{1,0:T(8,128)(2,1)S(1)} %get-tuple-element.30.high_ref, bf16[256,1024]{1,0:T(8,128)(2,1)S(1)} %get-tuple-element.31.low_ref, bf16[1920,256]{1,0:T(8,128)(2,1)S(1)} %copy-done.12), custom_call_target="tpu_custom_call" | custom-call | flops 3000000000 | bytes 5000000 | tf_op jit(solution)/shard_map/object/pallas_call | solution.py:750
  58.7 2.7 %collective-permute-done.4.second_ref = f32[32,256]{1,0:T(8,128)S(1)} collective-permute-done((f32[32,256]{1,0:T(8,128)S(1)}, f32[32,256]{1,0:T(8,128)S(1)}, u32[]{:S(2)}, u32[]{:S(2)}) %collective-permute-start.4) | collective-permute-done | bytes 32800 | tf_op jit(solution)/shard_map/ppermute | solution.py:828
  61.4 0.7 %blend.1 = f32[2,480,256]{2,1,0:T(8,128)} custom-call(f32[32,256]{1,0:T(8,128)S(1)} %collective-permute-done.3.first_ref, f32[32,256]{1,0:T(8,128)S(1)} %collective-permute-done.4.second_ref, f32[2,2,16,256]{3,2,1,0:T(8,128)S(1)} %get-tuple-element.32.edges_ref, f32[2,480,256]{2,1,0:T(8,128)} %get-tuple-element.33.core_hbm), custom_call_target="tpu_custom_call", output_to_operand_aliasing={{}: (3, {})} | custom-call | tf_op jit(solution)/shard_map/blend/pallas_call | solution.py:802
  (22 shorter events, 0.0 us)
Async XLA Ops:
  0.6 1.0 %copy-start.4 = (f32[256,480]{0,1:T(8,128)S(1)}, f32[256,480]{0,1:T(8,128)}, u32[]{:S(2)}) copy-start(f32[256,480]{0,1:T(8,128)} %param.18) | copy-start | bytes 1474564
  1.7 13.1 %copy-start.3 = (bf16[1024,256]{1,0:T(8,128)(2,1)S(1)}, bf16[1024,256]{1,0:T(8,128)(2,1)}, u32[]{:S(2)}) copy-start(bf16[1024,256]{1,0:T(8,128)(2,1)} %constant.16.clone.lc_ref) | copy-start | bytes 1572868
  2.5 12.3 %all-to-all-start = ((bf16[8,32,512]{2,1,0:T(8,128)(2,1)}), bf16[8,32,512]{2,1,0:T(8,128)(2,1)S(1)}, u32[]{:S(2)}, u32[]{:S(2)}) async-start(bf16[8,32,512]{2,1,0:T(8,128)(2,1)} %gains.1.after), calls=%async_computation | async-start | bytes 524288 | tf_op jit(solution)/shard_map/all_to_all | solution.py:835
  8.6 1.2 %copy-start.10 = (bf16[4,32,3840]{2,1,0:T(8,128)(2,1)S(1)}, bf16[4,32,3840]{2,1,0:T(8,128)(2,1)}, u32[]{:S(2)}) copy-start(bf16[4,32,3840]{2,1,0:T(8,128)(2,1)} %param.16) | copy-start | bytes 2949124
  9.8 0.7 %copy-start.11 = (bf16[4,8,120]{2,1,0:T(8,128)(2,1)S(1)}, bf16[4,8,120]{2,1,0:T(8,128)(2,1)}, u32[]{:S(2)}) copy-start(bf16[4,8,120]{2,1,0:T(8,128)(2,1)} %param.17) | copy-start | bytes 23044
  10.5 12.6 %copy-start.6 = (f32[2,64,128]{2,1,0:T(8,128)S(1)}, f32[2,64,128]{2,1,0:T(8,128)}, u32[]{:S(2)}) copy-start(f32[2,64,128]{2,1,0:T(8,128)} %pupil_ref.3) | copy-start | bytes 196612
  10.5 12.6 %copy-start.7 = (s32[16,4]{0,1:T(4,128)S(1)}, s32[16,4]{0,1:T(4,128)}, u32[]{:S(2)}) copy-start(s32[16,4]{0,1:T(4,128)} %param.21) | copy-start | bytes 772
  10.5 12.6 %copy-start.8 = (s32[32]{0:T(128)S(1)}, s32[32]{0:T(128)}, u32[]{:S(2)}) copy-start(s32[32]{0:T(128)} %led_row.3) | copy-start | bytes 388
  10.5 12.6 %copy-start.9 = (s32[32]{0:T(128)S(1)}, s32[32]{0:T(128)}, u32[]{:S(2)}) copy-start(s32[32]{0:T(128)} %led_col.3) | copy-start | bytes 388
  10.5 12.6 %copy-start.13 = (bf16[512,512]{1,0:T(8,128)(2,1)S(1)}, bf16[512,512]{1,0:T(8,128)(2,1)}, u32[]{:S(2)}) copy-start(bf16[512,512]{1,0:T(8,128)(2,1)} %constant.19.clone.cols_ref) | copy-start | bytes 1572868
  16.8 19.1 %all-to-all-start.1 = ((bf16[8,272,128]{2,1,0:T(8,128)(2,1)}), bf16[8,272,128]{2,1,0:T(8,128)(2,1)S(1)}, u32[]{:S(2)}, u32[]{:S(2)}) async-start(bf16[8,272,128]{2,1,0:T(8,128)(2,1)} %strips.1), calls=%async_computation.1 | async-start | bytes 1114112 | tf_op jit(solution)/shard_map/all_to_all | solution.py:837
  23.1 1.2 %copy-start.1 = (f32[1,2,256,512]{3,2,1,0:T(8,128)S(1)}, f32[1,2,256,512]{3,2,1,0:T(8,128)}, u32[]{:S(2)}) copy-start(f32[1,2,256,512]{3,2,1,0:T(8,128)} %param.19) | copy-start | bytes 3145732
  24.3 0.9 %copy-start.14 = (bf16[256,384]{1,0:T(8,128)(2,1)S(1)}, bf16[256,384]{1,0:T(8,128)(2,1)}, u32[]{:S(2)}) copy-start(bf16[256,384]{1,0:T(8,128)(2,1)} %constant.20.clone.rows_ref) | copy-start | bytes 589828
  32.6 3.3 %copy-start = (f32[32,256,256]{2,1,0:T(8,128)}, f32[32,256,256]{2,1,0:T(8,128)S(1)}, u32[]{:S(2)}) copy-start(f32[32,256,256]{2,1,0:T(8,128)S(1)} %get-tuple-element.21.field_hbm) | copy-start | bytes 25165828
  36.3 7.4 %collective-permute-start = (bf16[528,256]{1,0:T(8,128)(2,1)S(1)}, bf16[528,256]{1,0:T(8,128)(2,1)S(1)}, u32[]{:S(2)}, u32[]{:S(2)}) collective-permute-start(bf16[528,256]{1,0:T(8,128)(2,1)S(1)} %windows.1.window), channel_id=1, source_target_pairs={{0,16},{8,24},{16,0},{24,8},{1,17},{9,25},{17,1},{25,9},{2,18},{10... | collective-permute-start | bytes 811016 | tf_op jit(solution)/shard_map/ppermute | solution.py:848
  37.9 5.8 %collective-permute-start.1 = (bf16[528,256]{1,0:T(8,128)(2,1)S(1)}, bf16[528,256]{1,0:T(8,128)(2,1)S(1)}, u32[]{:S(2)}, u32[]{:S(2)}) collective-permute-start(bf16[528,256]{1,0:T(8,128)(2,1)S(1)} %windows.1.window), channel_id=1, source_target_pairs={{0,8},{8,0},{16,24},{24,16},{1,9},{9,1},{17,25},{25,17},{2,10},{10... | collective-permute-start | bytes 811016 | tf_op jit(solution)/shard_map/ppermute | solution.py:849
  43.7 1.6 %copy-start.2 = (f32[1,2,256,512]{3,2,1,0:T(8,128)S(1)}, f32[1,2,256,512]{3,2,1,0:T(8,128)}, u32[]{:S(2)}) copy-start(f32[1,2,256,512]{3,2,1,0:T(8,128)} %param.19) | copy-start | bytes 3145732
  43.7 1.6 %copy-start.5 = (bf16[384,256]{1,0:T(8,128)(2,1)S(1)}, bf16[384,256]{1,0:T(8,128)(2,1)}, u32[]{:S(2)}) copy-start(bf16[384,256]{1,0:T(8,128)(2,1)} %constant.22.clone.back_ref) | copy-start | bytes 589828
  43.7 1.5 %collective-permute-start.2 = (bf16[528,256]{1,0:T(8,128)(2,1)S(1)}, bf16[528,256]{1,0:T(8,128)(2,1)S(1)}, u32[]{:S(2)}, u32[]{:S(2)}) collective-permute-start(bf16[528,256]{1,0:T(8,128)(2,1)S(1)} %collective-permute-done.w2), channel_id=1, source_target_pairs={{0,8},{8,0},{16,24},{24,16},{1,9},{9,1},{17,25},{25,17},{2,10},{10... | collective-permute-start | bytes 811016 | tf_op jit(solution)/shard_map/ppermute | solution.py:851
  45.0 11.6 %copy-start.12 = (bf16[1920,256]{1,0:T(8,128)(2,1)S(1)}, bf16[1920,256]{1,0:T(8,128)(2,1)}, u32[]{:S(2)}) copy-start(bf16[1920,256]{1,0:T(8,128)(2,1)} %constant.23.clone.table_ref) | copy-start | bytes 2949124
  52.5 6.2 %collective-permute-start.3 = (f32[32,256]{1,0:T(8,128)S(1)}, f32[32,256]{1,0:T(8,128)S(1)}, u32[]{:S(2)}, u32[]{:S(2)}) collective-permute-start(f32[32,256]{1,0:T(8,128)S(1)} %get-tuple-element.28), channel_id=1, source_target_pairs={{0,1},{1,0},{2,3},{3,2},{4,5},{5,4},{6,7},{7,6},{8,9},{9,8},{10,11... | collective-permute-start | bytes 98312 | tf_op jit(solution)/shard_map/ppermute | solution.py:828
  54.7 6.7 %collective-permute-start.4 = (f32[32,256]{1,0:T(8,128)S(1)}, f32[32,256]{1,0:T(8,128)S(1)}, u32[]{:S(2)}, u32[]{:S(2)}) collective-permute-start(f32[32,256]{1,0:T(8,128)S(1)} %get-tuple-element.29), channel_id=1, source_target_pairs={{1,2},{2,1},{3,4},{4,3},{5,6},{6,5},{9,10},{10,9},{11,12},{12,11},... | collective-permute-start | bytes 98312 | tf_op jit(solution)/shard_map/ppermute | solution.py:828

commit v10 on v9

--- a/solution.py
+++ b/solution.py
@@ -378,9 +378,10 @@
     )
 
 
-def window_kernel(dq_ref, rows_ref, small_ref, window_ref, *, frames, core):
+def window_kernel(dq_ref, rows_ref, small_ref, *window_refs, frames, core):
     slabs, lines, _ = dq_ref.shape
-    half_h, half_w = rows_ref.shape[0], window_ref.shape[1]
+    half_h, half_w = rows_ref.shape[0], window_refs[0].shape[1]
+    count = frames // len(window_refs)
     halves = half_w // 128
     lines = (lines - 16) // halves
     lr_sum, line = small_ref[:half_h, :128], small_ref[half_h:]
@@ -416,10 +417,12 @@
         mean = jnp.sum(window, axis=0, keepdims=True)
         mean = jnp.sum(mean, axis=1, keepdims=True) * (1.0 / (half_h * half_w))
         means.append(jnp.broadcast_to(mean, (1, 128)))
-        window_ref[frame * half_h : (frame + 1) * half_h] = (window - mean).astype(BF16)
+        begin = frame % count * half_h
+        window_refs[frame // count][begin : begin + half_h] = (window - mean).astype(BF16)
     means = jnp.concatenate(means + [jnp.zeros((8 - frames, 128), F32)], axis=0)
-    notes = parts_rows(means)
-    window_ref[frames * half_h :] = jnp.concatenate([notes] * halves, axis=1)
+    notes = jnp.concatenate([parts_rows(means)] * halves, axis=1)
+    for window_ref in window_refs:
+        window_ref[count * half_h :] = notes
 
 
 def tilt_lines(width, margin, core, lc):
@@ -446,9 +449,9 @@
     half_h, half_w = rows.shape[0], small.shape[1]
     return pl.pallas_call(
         functools.partial(window_kernel, frames=frames, core=core),
-        out_shape=jax.ShapeDtypeStruct((frames * half_h + 16, half_w), BF16),
+        out_shape=(jax.ShapeDtypeStruct((frames // 2 * half_h + 16, half_w), BF16),) * 2,
         in_specs=vmem_spec(3),
-        out_specs=pl.BlockSpec(memory_space=VMEM),
+        out_specs=tuple(vmem_spec(2)),
         compiler_params=pltpu.CompilerParams(vmem_limit_bytes=LIMIT),
         name="windows",
     )(arrived, rows, small)
@@ -459,20 +462,26 @@
         weight[patterns[lit, frame]] += value
 
 
-def take_windows(weight, patterns, windows_here, slots, half_h):
-    for window, slot in zip(windows_here, slots):
-        frames_here = window.shape[0] // half_h
+def take_windows(weight, patterns, windows_here, places, half_h):
+    for window, (slot, part) in zip(windows_here, places):
+        count = window.shape[0] // half_h
         owner = jnp.bitwise_xor(lax.axis_index("grp"), slot)
-        means = rows_value(window[frames_here * half_h :])
-        for place in range(frames_here):
+        means = rows_value(window[count * half_h :])
+        for place in range(count):
             value = window[place * half_h : (place + 1) * half_h].astype(F32)
-            value = -means[place : place + 1, 0:1] - value
-            add_frame(weight, patterns, owner * frames_here + place, value)
-
-
-def fetch_kernel(patterns, estimate_ref, window, field_hbm, field_ref, weight, sem):
-    load = pltpu.make_async_copy(field_hbm, field_ref, sem)
-    load.start()
+            own = part * count + place
+            value = -means[own : own + 1, 0:1] - value
+            add_frame(weight, patterns, owner * (2 * count) + own, value)
+
+
+def fetch_kernel(patterns, estimate_ref, part_a, part_b, field_hbm, field_ref, weight, sem):
+    quarter = field_ref.shape[0] // 4
+    loads = []
+    for number in range(4):
+        part = pl.ds(number * quarter, quarter)
+        load = pltpu.make_async_copy(field_hbm.at[part], field_ref.at[part], sem.at[number])
+        load.start()
+        loads.append(load)
     weight[...] = jnp.zeros_like(weight)
     frames, half_h, _ = estimate_ref.shape
 
@@ -481,8 +490,9 @@
         return carry
 
     lax.fori_loop(0, frames, one_frame, 0)
-    take_windows(weight, patterns, (window,), (0,), half_h)
-    load.wait()
+    take_windows(weight, patterns, (part_a, part_b), ((0, 0), (0, 1)), half_h)
+    for load in loads:
+        load.wait()
 
 
 def fetch(field, estimate, window, patterns):
@@ -494,30 +504,31 @@
             jax.ShapeDtypeStruct((leds, *estimate.shape[1:]), F32),
         ),
         in_specs=[pl.BlockSpec(memory_space=SMEM)]
-        + vmem_spec(2)
+        + vmem_spec(3)
         + [pl.BlockSpec(memory_space=pltpu.HBM)],
         out_specs=tuple(vmem_spec(2)),
-        scratch_shapes=[pltpu.SemaphoreType.DMA],
+        scratch_shapes=[pltpu.SemaphoreType.DMA((4,))],
         compiler_params=pltpu.CompilerParams(vmem_limit_bytes=LIMIT),
         cost_estimate=pl.CostEstimate(flops=0, bytes_accessed=16_000_000, transcendentals=0),
         name="fetch",
-    )(patterns, estimate, window, pltpu.with_memory_space_constraint(field, pltpu.HBM))
-
-
-def collect_kernel(patterns, w1, w2, weight_in, weight):
+    )(patterns, estimate, *window, pltpu.with_memory_space_constraint(field, pltpu.HBM))
+
+
+def collect_kernel(patterns, w1a, w1b, w2a, w2b, weight_in, weight):
     weight[...] = weight_in[...]
-    take_windows(weight, patterns, (w1, w2), (1, 2), weight.shape[1])
-
-
-def collect(weight, w1, w2, patterns):
+    places = ((1, 0), (1, 1), (2, 0), (2, 1))
+    take_windows(weight, patterns, (w1a, w1b, w2a, w2b), places, weight.shape[1])
+
+
+def collect(weight, here, patterns):
     return pl.pallas_call(
         collect_kernel,
         out_shape=jax.ShapeDtypeStruct(weight.shape, F32),
-        in_specs=[pl.BlockSpec(memory_space=SMEM)] + vmem_spec(3),
+        in_specs=[pl.BlockSpec(memory_space=SMEM)] + vmem_spec(5),
         out_specs=pl.BlockSpec(memory_space=VMEM),
         compiler_params=pltpu.CompilerParams(vmem_limit_bytes=LIMIT),
         name="collect",
-    )(patterns, w1, w2, weight)
+    )(patterns, *here, weight)
 
 
 def across(left, right):
@@ -526,7 +537,7 @@
 
 
 def update_kernel(
-    led_row, led_col, patterns, field_ref, weight_in, w3,
+    led_row, led_col, patterns, field_ref, weight_in, w3a, w3b,
     spec_ref, pupil_ref, back_ref, big_hbm,
     fresh_hbm, high_ref, low_ref, first_ref, second_ref,
     weight, grads, fresh_ref, big, sides_ref, big_sem, fresh_sems, *, group,
@@ -539,7 +550,7 @@
     big_load.start()
     grads[...] = jnp.zeros_like(grads)
     weight[...] = weight_in[...]
-    take_windows(weight, patterns, (w3,), (3,), half_h)
+    take_windows(weight, patterns, (w3a, w3b), ((3, 0), (3, 1)), half_h)
 
     left_rows = 2 * band_rows
     pair_rows, pair_cols = half_h // 2, half_w // 2
@@ -675,7 +686,7 @@
         functools.partial(update_kernel, group=group),
         out_shape=out_shape,
         in_specs=[pl.BlockSpec(memory_space=SMEM)] * 3
-        + vmem_spec(6)
+        + vmem_spec(7)
         + [pl.BlockSpec(memory_space=pltpu.HBM)],
         out_specs=(pl.BlockSpec(memory_space=pltpu.HBM), *vmem_spec(4)),
         scratch_shapes=[
@@ -690,7 +701,7 @@
         compiler_params=pltpu.CompilerParams(vmem_limit_bytes=LIMIT),
         name="update",
     )(
-        led_row, led_col, patterns, field, weight, window, spectrum, pupil, back,
+        led_row, led_col, patterns, field, weight, *window, spectrum, pupil, back,
         pltpu.with_memory_space_constraint(jnp.asarray(big), pltpu.HBM),
     )
 
@@ -845,11 +856,11 @@
     swap_core = [(i, i ^ 1) for i in range(4)]
     swap_chip = [(i, i ^ 2) for i in range(4)]
     other = functools.partial(lax.ppermute, axis_name="grp")
-    window_2 = other(window, perm=swap_chip)
-    window_1 = other(window, perm=swap_core)
-    window_2, field, weight = lax.optimization_barrier((window_2, field, weight))
-    window_3 = other(window_2, perm=swap_core)
-    weight = collect(weight, window_1, window_2, patterns)
+    early, late = (other(part, perm=swap_chip) for part in window)
+    window_1 = [other(part, perm=swap_core) for part in window]
+    late, field, weight = lax.optimization_barrier((late, field, weight))
+    window_3 = [other(part, perm=swap_core) for part in (early, late)]
+    weight = collect(weight, (*window_1, early, late), patterns)
 
     fresh, high, low, for_a, for_b = update(
         field, weight, window_3, spectrum_tile, pupil, patterns,

time: 62.6 us -> 62.5 us (level)
  waiting for transfers between devices: 8.41 us -> 7.13 us
  starting transfers between devices: 18 us -> 19.1 us
    ppermute x3 -> x6, waiting for transfers between devices: 2.11 us -> 0.83 us  [the longest x2 0.77 us: body(): early, late = (other(part, perm=swap_chip) for part in window)]
    ppermute x3 -> x6, starting transfers between devices: 1.56 us -> 2.67 us  [the longest x2 2.09 us: body(): early, late = (other(part, perm=swap_chip) for part in window)]
  transfers between devices with their start and end apart: 7 -> 10, of which waited for: 4 -> 4; matrix products, arithmetic and copies ran while one was open for 0% -> 0% of each run, Pallas kernels for 25% -> 25%
where the time goes in v10:
time: 62.5 us; the launch traced here: 62 us
  Pallas kernels  26.5 us (42%)
  starting transfers between devices  19.1 us (31%)
  local copies, waits for them, and re-layouts  8.37 us (13%)
  waiting for transfers between devices  7.13 us (11%)
  between operations  0.85 us (1%)
    unnamed x30, local copies, waits for them, and re-layouts  8.37 us
    pallas_call x1, Pallas kernels, all_fields(): pl.pallas_call(functools.partial(field_kernel, group=group), out_shape=(j...  7.31 us
    pallas_call x1, Pallas kernels, update(): pl.pallas_call(functools.partial(update_kernel, group=group), out_shape=o...  7.19 us
    all_to_all x1, starting transfers between devices, body(): lax.all_to_all(narrow, 'tile', split_axis=0, concat_axis=0, tiled=True)  6.29 us
    all_to_all x1, starting transfers between devices, body(): lax.all_to_all(by_rows, 'tile', split_axis=0, concat_axis=0, tiled=True)  6.07 us
    pallas_call x1, Pallas kernels, fetch(): pl.pallas_call(fetch_kernel, out_shape=(jax.ShapeDtypeStruct(field.shape,...  4.07 us
    all_to_all x1, waiting for transfers between devices, body(): lax.all_to_all(by_rows, 'tile', split_axis=0, concat_axis=0, tiled=True)  3.61 us
    ppermute x1, waiting for transfers between devices, neighbours(): lax.ppermute(for_b, 'tile', swap_b)  2.69 us
  transfers between devices with their start and end apart: 10, of which 4 were waited for; matrix products, arithmetic and copies ran while one was open for 0% of the time, Pallas kernels for 25%

profile of v10, /device:TPU:24, one launch (start us, length us, event | category | flops | bytes accessed | tf_op | source)
XLA Modules:
  0.0 62.0 jit_solution(7657488854471357936)
XLA Ops:
  0.6 1.0 %copy-done.4 = f32[256,480]{0,1:T(8,128)S(1)} copy-done((f32[256,480]{0,1:T(8,128)S(1)}, f32[256,480]{0,1:T(8,128)}, u32[]{:S(2)}) %copy-start.4) | copy-done | bytes 491544
  1.7 0.8 %gains.1.after = bf16[8,32,512]{2,1,0:T(8,128)(2,1)} custom-call(f32[480,256]{1,0:T(8,128)S(1)} %bitcast.9), custom_call_target="tpu_custom_call" | custom-call | tf_op jit(solution)/shard_map/gains/pallas_call | solution.py:116
  2.5 6.1 %all-to-all-start = ((bf16[8,32,512]{2,1,0:T(8,128)(2,1)}), bf16[8,32,512]{2,1,0:T(8,128)(2,1)S(1)}, u32[]{:S(2)}, u32[]{:S(2)}) async-start(bf16[8,32,512]{2,1,0:T(8,128)(2,1)} %gains.1.after), calls=%async_computation | async-start | bytes 524288 | tf_op jit(solution)/shard_map/all_to_all | solution.py:846
  8.6 1.2 %copy-done.10 = bf16[4,32,3840]{2,1,0:T(8,128)(2,1)S(1)} copy-done((bf16[4,32,3840]{2,1,0:T(8,128)(2,1)S(1)}, bf16[4,32,3840]{2,1,0:T(8,128)(2,1)}, u32[]{:S(2)}) %copy-start.10) | copy-done | bytes 983064
  9.8 0.7 %copy-done.11 = bf16[4,8,120]{2,1,0:T(8,128)(2,1)S(1)} copy-done((bf16[4,8,120]{2,1,0:T(8,128)(2,1)S(1)}, bf16[4,8,120]{2,1,0:T(8,128)(2,1)}, u32[]{:S(2)}) %copy-start.11) | copy-done | bytes 7704
  10.5 0.0 copy-start.13
  10.5 0.7 %dequantize.1.dq_ref = f32[8,128,512]{2,1,0:T(8,128)S(1)} custom-call(bf16[128,3840]{1,0:T(8,128)(2,1)S(1)} %bitcast.14, bf16[32,120]{1,0:T(8,128)(2,1)S(1)} %bitcast.15, bf16[8,32,512]{2,1,0:T(8,128)(2,1)} %gains.1.after), custom_call_target="tpu_custom_call" | custom-call | flops 2000000000 | bytes 4000000 | tf_op jit(solution)/shard_map/dequantize/pallas_call | solution.py:160
  11.2 3.6 %all-to-all-done.gains_ref = bf16[8,32,512]{2,1,0:T(8,128)(2,1)S(1)} async-done(((bf16[8,32,512]{2,1,0:T(8,128)(2,1)}), bf16[8,32,512]{2,1,0:T(8,128)(2,1)S(1)}, u32[]{:S(2)}, u32[]{:S(2)}) %all-to-all-start) | async-done | bytes 262176 | tf_op jit(solution)/shard_map/all_to_all | solution.py:846
  14.8 2.0 %strips.1 = bf16[8,272,128]{2,1,0:T(8,128)(2,1)} custom-call(f32[8,128,512]{2,1,0:T(8,128)S(1)} %dequantize.1.dq_ref, bf16[8,32,512]{2,1,0:T(8,128)(2,1)S(1)} %all-to-all-done.gains_ref, bf16[1024,256]{1,0:T(8,128)(2,1)S(1)} %copy-done.3), custom_call_target="tpu_custom_call" | custom-call | tf_op jit(solution)/shard_map/strips/pallas_call | solution.py:270
  16.8 6.3 %all-to-all-start.1 = ((bf16[8,272,128]{2,1,0:T(8,128)(2,1)}), bf16[8,272,128]{2,1,0:T(8,128)(2,1)S(1)}, u32[]{:S(2)}, u32[]{:S(2)}) async-start(bf16[8,272,128]{2,1,0:T(8,128)(2,1)} %strips.1), calls=%async_computation.1 | async-start | bytes 1114112 | tf_op jit(solution)/shard_map/all_to_all | solution.py:848
  23.1 0.0 copy-start.1
  23.1 1.2 %copy-done.1 = f32[1,2,256,512]{3,2,1,0:T(8,128)S(1)} copy-done((f32[1,2,256,512]{3,2,1,0:T(8,128)S(1)}, f32[1,2,256,512]{3,2,1,0:T(8,128)}, u32[]{:S(2)}) %copy-start.1) | copy-done | bytes 1048600
  24.3 0.9 %copy-done.14 = bf16[256,384]{1,0:T(8,128)(2,1)S(1)} copy-done((bf16[256,384]{1,0:T(8,128)(2,1)S(1)}, bf16[256,384]{1,0:T(8,128)(2,1)}, u32[]{:S(2)}) %copy-start.14) | copy-done | bytes 196632
  25.3 7.3 %fields.1 = (f32[32,256,256]{2,1,0:T(8,128)S(1)}, f32[16,128,256]{2,1,0:T(8,128)S(1)}, bf16[128,512]{1,0:T(8,128)(2,1)S(1)}, f32[136,256]{1,0:T(8,128)S(1)}) custom-call(s32[32]{0:T(128)S(1)} %copy-done.8, s32[32]{0:T(128)S(1)} %copy-done.9, s32[4,16]{1,0:T(4,128)S(1)} %bitcast.10, f32[2,256,512]{2,1,0:T(8,128)S(1)} %bitcast.7, f32[2,64,128]{2,1,0:T(8,128)S(1)} %copy-done.6, ...), custom_call_target="tpu_custom_call" | custom-call | flops 8000000000 | bytes 16000000 | tf_op jit(solution)/shard_map/fields/pallas_call | solution.py:353
  32.6 3.3 %copy-done = f32[32,256,256]{2,1,0:T(8,128)} copy-done((f32[32,256,256]{2,1,0:T(8,128)}, f32[32,256,256]{2,1,0:T(8,128)S(1)}, u32[]{:S(2)}) %copy-start) | copy-done | bytes 8388632
  35.9 0.5 windows.1
  36.3 1.5 %collective-permute-start = (bf16[272,256]{1,0:T(8,128)(2,1)S(1)}, bf16[272,256]{1,0:T(8,128)(2,1)S(1)}, u32[]{:S(2)}, u32[]{:S(2)}) collective-permute-start(bf16[272,256]{1,0:T(8,128)(2,1)S(1)} %get-tuple-element.22.part_b), channel_id=1, source_target_pairs={{0,16},{8,24},{16,0},{24,8},{1,17},{9,25},{17,1},{25,9},{2,18},{10... | collective-permute-start | bytes 417800 | tf_op jit(solution)/shard_map/ppermute | solution.py:859
  37.9 0.6 collective-permute-start.3
  38.4 0.5 collective-permute-start.2
  38.9 4.1 %fetch.1 = (f32[32,256,256]{2,1,0:T(8,128)S(1)}, f32[32,128,256]{2,1,0:T(8,128)S(1)}) custom-call(s32[4,16]{1,0:T(4,128)S(1)} %bitcast.11, f32[16,128,256]{2,1,0:T(8,128)S(1)} %get-tuple-element.23.estimate_ref, bf16[272,256]{1,0:T(8,128)(2,1)S(1)} %get-tuple-element.24.part_a, bf16[272,256]{1,0:T(8,128)(2,1)S(1)} %get-tuple-element.22.part_b, ...), custom_call_target="tpu_custom_call" | custom-call | bytes 16000000 | tf_op jit(solution)/shard_map/fetch/pallas_call | solution.py:500
  43.0 0.0 copy-start.5
  43.0 0.1 collective-permute-start.5
  43.1 0.8 %collective-permute-done.3.w2a = bf16[272,256]{1,0:T(8,128)(2,1)S(1)} collective-permute-done((bf16[272,256]{1,0:T(8,128)(2,1)S(1)}, bf16[272,256]{1,0:T(8,128)(2,1)S(1)}, u32[]{:S(2)}, u32[]{:S(2)}) %collective-permute-start.3) | collective-permute-done | bytes 139296 | tf_op jit(solution)/shard_map/ppermute | solution.py:859
  43.9 1.3 %collect.1.weight_in = f32[32,128,256]{2,1,0:T(8,128)S(1)} custom-call(s32[4,16]{1,0:T(4,128)S(1)} %bitcast.12, bf16[272,256]{1,0:T(8,128)(2,1)S(1)} %collective-permute-done.1.w1a, bf16[272,256]{1,0:T(8,128)(2,1)S(1)} %collective-permute-done.2.w1b, bf16[272,256]{1,0:T(8,128)(2,1)S(1)} %collective-permute-done.3.w2a, ...), custom_call_target="tpu_custom_call" | custom-call | tf_op jit(solution)/shard_map/collect/pallas_call | solution.py:524
  45.2 0.0 copy-start.12
  45.2 0.1 collective-permute-done.4.w3a
  45.3 7.2 %update.1 = (f32[2,256,512]{2,1,0:T(8,128)}, bf16[256,1024]{1,0:T(8,128)(2,1)S(1)}, bf16[256,1024]{1,0:T(8,128)(2,1)S(1)}, f32[32,256]{1,0:T(8,128)S(1)}, f32[32,256]{1,0:T(8,128)S(1)}) custom-call(s32[32]{0:T(128)S(1)} %copy-done.8, s32[32]{0:T(128)S(1)} %copy-done.9, s32[4,16]{1,0:T(4,128)S(1)} %bitcast.13, ...), custom_call_target="tpu_custom_call" | custom-call | tf_op jit(solution)/shard_map/update/pallas_call | solution.py:685
  52.5 2.2 %collective-permute-start.6 = (f32[32,256]{1,0:T(8,128)S(1)}, f32[32,256]{1,0:T(8,128)S(1)}, u32[]{:S(2)}, u32[]{:S(2)}) collective-permute-start(f32[32,256]{1,0:T(8,128)S(1)} %get-tuple-element.32), channel_id=1, source_target_pairs={{0,1},{1,0},{2,3},{3,2},{4,5},{5,4},{6,7},{7,6},{8,9},{9,8},{10,11... | collective-permute-start | bytes 98312 | tf_op jit(solution)/shard_map/ppermute | solution.py:839
  54.6 1.9 %collective-permute-start.7 = (f32[32,256]{1,0:T(8,128)S(1)}, f32[32,256]{1,0:T(8,128)S(1)}, u32[]{:S(2)}, u32[]{:S(2)}) collective-permute-start(f32[32,256]{1,0:T(8,128)S(1)} %get-tuple-element.33), channel_id=1, source_target_pairs={{1,2},{2,1},{3,4},{4,3},{5,6},{6,5},{9,10},{10,9},{11,12},{12,11},... | collective-permute-start | bytes 98312 | tf_op jit(solution)/shard_map/ppermute | solution.py:839
  56.6 2.1 %object.1 = (f32[2,480,256]{2,1,0:T(8,128)}, f32[2,2,16,256]{3,2,1,0:T(8,128)S(1)}) custom-call(bf16[256,1024]{1,0:T(8,128)(2,1)S(1)} %get-tuple-element.34.high_ref, bf16[256,1024]{1,0:T(8,128)(2,1)S(1)} %get-tuple-element.35.low_ref, bf16[1920,256]{1,0:T(8,128)(2,1)S(1)} %copy-done.12), custom_call_target="tpu_custom_call" | custom-call | flops 3000000000 | bytes 5000000 | tf_op jit(solution)/shard_map/object/pallas_call | solution.py:761
  58.6 2.7 %collective-permute-done.7.second_ref = f32[32,256]{1,0:T(8,128)S(1)} collective-permute-done((f32[32,256]{1,0:T(8,128)S(1)}, f32[32,256]{1,0:T(8,128)S(1)}, u32[]{:S(2)}, u32[]{:S(2)}) %collective-permute-start.7) | collective-permute-done | bytes 32800 | tf_op jit(solution)/shard_map/ppermute | solution.py:839
  61.3 0.7 %blend.1 = f32[2,480,256]{2,1,0:T(8,128)} custom-call(f32[32,256]{1,0:T(8,128)S(1)} %collective-permute-done.6.first_ref, f32[32,256]{1,0:T(8,128)S(1)} %collective-permute-done.7.second_ref, f32[2,2,16,256]{3,2,1,0:T(8,128)S(1)} %get-tuple-element.36.edges_ref, f32[2,480,256]{2,1,0:T(8,128)} %get-tuple-element.37.core_hbm), custom_call_target="tpu_custom_call", output_to_operand_aliasing={{}: (3, {})} | custom-call | tf_op jit(solution)/shard_map/blend/pallas_call | solution.py:813
  (28 shorter events, 0.1 us)
Async XLA Ops:
  0.6 1.0 %copy-start.4 = (f32[256,480]{0,1:T(8,128)S(1)}, f32[256,480]{0,1:T(8,128)}, u32[]{:S(2)}) copy-start(f32[256,480]{0,1:T(8,128)} %param.18) | copy-start | bytes 1474564
  1.7 13.1 %copy-start.3 = (bf16[1024,256]{1,0:T(8,128)(2,1)S(1)}, bf16[1024,256]{1,0:T(8,128)(2,1)}, u32[]{:S(2)}) copy-start(bf16[1024,256]{1,0:T(8,128)(2,1)} %constant.16.clone.lc_ref) | copy-start | bytes 1572868
  2.5 12.3 %all-to-all-start = ((bf16[8,32,512]{2,1,0:T(8,128)(2,1)}), bf16[8,32,512]{2,1,0:T(8,128)(2,1)S(1)}, u32[]{:S(2)}, u32[]{:S(2)}) async-start(bf16[8,32,512]{2,1,0:T(8,128)(2,1)} %gains.1.after), calls=%async_computation | async-start | bytes 524288 | tf_op jit(solution)/shard_map/all_to_all | solution.py:846
  8.6 1.2 %copy-start.10 = (bf16[4,32,3840]{2,1,0:T(8,128)(2,1)S(1)}, bf16[4,32,3840]{2,1,0:T(8,128)(2,1)}, u32[]{:S(2)}) copy-start(bf16[4,32,3840]{2,1,0:T(8,128)(2,1)} %param.16) | copy-start | bytes 2949124
  9.8 0.7 %copy-start.11 = (bf16[4,8,120]{2,1,0:T(8,128)(2,1)S(1)}, bf16[4,8,120]{2,1,0:T(8,128)(2,1)}, u32[]{:S(2)}) copy-start(bf16[4,8,120]{2,1,0:T(8,128)(2,1)} %param.17) | copy-start | bytes 23044
  10.5 12.6 %copy-start.6 = (f32[2,64,128]{2,1,0:T(8,128)S(1)}, f32[2,64,128]{2,1,0:T(8,128)}, u32[]{:S(2)}) copy-start(f32[2,64,128]{2,1,0:T(8,128)} %pupil_ref.3) | copy-start | bytes 196612
  10.5 12.6 %copy-start.7 = (s32[16,4]{0,1:T(4,128)S(1)}, s32[16,4]{0,1:T(4,128)}, u32[]{:S(2)}) copy-start(s32[16,4]{0,1:T(4,128)} %param.21) | copy-start | bytes 772
  10.5 12.6 %copy-start.8 = (s32[32]{0:T(128)S(1)}, s32[32]{0:T(128)}, u32[]{:S(2)}) copy-start(s32[32]{0:T(128)} %led_row.3) | copy-start | bytes 388
  10.5 12.6 %copy-start.9 = (s32[32]{0:T(128)S(1)}, s32[32]{0:T(128)}, u32[]{:S(2)}) copy-start(s32[32]{0:T(128)} %led_col.3) | copy-start | bytes 388
  10.5 12.6 %copy-start.13 = (bf16[512,512]{1,0:T(8,128)(2,1)S(1)}, bf16[512,512]{1,0:T(8,128)(2,1)}, u32[]{:S(2)}) copy-start(bf16[512,512]{1,0:T(8,128)(2,1)} %constant.19.clone.cols_ref) | copy-start | bytes 1572868
  16.8 19.1 %all-to-all-start.1 = ((bf16[8,272,128]{2,1,0:T(8,128)(2,1)}), bf16[8,272,128]{2,1,0:T(8,128)(2,1)S(1)}, u32[]{:S(2)}, u32[]{:S(2)}) async-start(bf16[8,272,128]{2,1,0:T(8,128)(2,1)} %strips.1), calls=%async_computation.1 | async-start | bytes 1114112 | tf_op jit(solution)/shard_map/all_to_all | solution.py:848
  23.1 1.2 %copy-start.1 = (f32[1,2,256,512]{3,2,1,0:T(8,128)S(1)}, f32[1,2,256,512]{3,2,1,0:T(8,128)}, u32[]{:S(2)}) copy-start(f32[1,2,256,512]{3,2,1,0:T(8,128)} %param.19) | copy-start | bytes 3145732
  24.3 0.9 %copy-start.14 = (bf16[256,384]{1,0:T(8,128)(2,1)S(1)}, bf16[256,384]{1,0:T(8,128)(2,1)}, u32[]{:S(2)}) copy-start(bf16[256,384]{1,0:T(8,128)(2,1)} %constant.20.clone.rows_ref) | copy-start | bytes 589828
  32.6 3.3 %copy-start = (f32[32,256,256]{2,1,0:T(8,128)}, f32[32,256,256]{2,1,0:T(8,128)S(1)}, u32[]{:S(2)}) copy-start(f32[32,256,256]{2,1,0:T(8,128)S(1)} %get-tuple-element.25.field_hbm) | copy-start | bytes 25165828
  36.3 6.7 %collective-permute-start = (bf16[272,256]{1,0:T(8,128)(2,1)S(1)}, bf16[272,256]{1,0:T(8,128)(2,1)S(1)}, u32[]{:S(2)}, u32[]{:S(2)}) collective-permute-start(bf16[272,256]{1,0:T(8,128)(2,1)S(1)} %get-tuple-element.22.part_b), channel_id=1, source_target_pairs={{0,16},{8,24},{16,0},{24,8},{1,17},{9,25},{17,1},{25,9},{2,18},{10... | collective-permute-start | bytes 417800 | tf_op jit(solution)/shard_map/ppermute | solution.py:859
  37.9 6.0 %collective-permute-start.3 = (bf16[272,256]{1,0:T(8,128)(2,1)S(1)}, bf16[272,256]{1,0:T(8,128)(2,1)S(1)}, u32[]{:S(2)}, u32[]{:S(2)}) collective-permute-start(bf16[272,256]{1,0:T(8,128)(2,1)S(1)} %get-tuple-element.24.part_a), channel_id=1, source_target_pairs={{0,16},{8,24},{16,0},{24,8},{1,17},{9,25},{17,1},{25,9},{2,18},{10... | collective-permute-start | bytes 417800 | tf_op jit(solution)/shard_map/ppermute | solution.py:859
  38.4 5.5 %collective-permute-start.1 = (bf16[272,256]{1,0:T(8,128)(2,1)S(1)}, bf16[272,256]{1,0:T(8,128)(2,1)S(1)}, u32[]{:S(2)}, u32[]{:S(2)}) collective-permute-start(bf16[272,256]{1,0:T(8,128)(2,1)S(1)} %get-tuple-element.24.part_a), channel_id=1, source_target_pairs={{0,8},{8,0},{16,24},{24,16},{1,9},{9,1},{17,25},{25,17},{2,10},{10... | collective-permute-start | bytes 417800 | tf_op jit(solution)/shard_map/ppermute | solution.py:860
  38.4 5.5 %collective-permute-start.2 = (bf16[272,256]{1,0:T(8,128)(2,1)S(1)}, bf16[272,256]{1,0:T(8,128)(2,1)S(1)}, u32[]{:S(2)}, u32[]{:S(2)}) collective-permute-start(bf16[272,256]{1,0:T(8,128)(2,1)S(1)} %get-tuple-element.22.part_b), channel_id=1, source_target_pairs={{0,8},{8,0},{16,24},{24,16},{1,9},{9,1},{17,25},{25,17},{2,10},{10... | collective-permute-start | bytes 417800 | tf_op jit(solution)/shard_map/ppermute | solution.py:860
  43.0 2.2 %copy-start.2 = (f32[1,2,256,512]{3,2,1,0:T(8,128)S(1)}, f32[1,2,256,512]{3,2,1,0:T(8,128)}, u32[]{:S(2)}) copy-start(f32[1,2,256,512]{3,2,1,0:T(8,128)} %param.19) | copy-start | bytes 3145732
  43.0 2.2 %copy-start.5 = (bf16[384,256]{1,0:T(8,128)(2,1)S(1)}, bf16[384,256]{1,0:T(8,128)(2,1)}, u32[]{:S(2)}) copy-start(bf16[384,256]{1,0:T(8,128)(2,1)} %constant.22.clone.back_ref) | copy-start | bytes 589828
  43.0 2.1 %collective-permute-start.5 = (bf16[272,256]{1,0:T(8,128)(2,1)S(1)}, bf16[272,256]{1,0:T(8,128)(2,1)S(1)}, u32[]{:S(2)}, u32[]{:S(2)}) collective-permute-start(bf16[272,256]{1,0:T(8,128)(2,1)S(1)} %collective-permute-done.w2b), channel_id=1, source_target_pairs={{0,8},{8,0},{16,24},{24,16},{1,9},{9,1},{17,25},{25,17},{2,10},{10... | collective-permute-start | bytes 417800 | tf_op jit(solution)/shard_map/ppermute | solution.py:862
  43.9 1.4 %collective-permute-start.4 = (bf16[272,256]{1,0:T(8,128)(2,1)S(1)}, bf16[272,256]{1,0:T(8,128)(2,1)S(1)}, u32[]{:S(2)}, u32[]{:S(2)}) collective-permute-start(bf16[272,256]{1,0:T(8,128)(2,1)S(1)} %collective-permute-done.3.w2a), channel_id=1, source_target_pairs={{0,8},{8,0},{16,24},{24,16},{1,9},{9,1},{17,25},{25,17},{2,10},{10... | collective-permute-start | bytes 417800 | tf_op jit(solution)/shard_map/ppermute | solution.py:862
  45.2 11.4 %copy-start.12 = (bf16[1920,256]{1,0:T(8,128)(2,1)S(1)}, bf16[1920,256]{1,0:T(8,128)(2,1)}, u32[]{:S(2)}) copy-start(bf16[1920,256]{1,0:T(8,128)(2,1)} %constant.23.clone.table_ref) | copy-start | bytes 2949124
  52.5 6.2 %collective-permute-start.6 = (f32[32,256]{1,0:T(8,128)S(1)}, f32[32,256]{1,0:T(8,128)S(1)}, u32[]{:S(2)}, u32[]{:S(2)}) collective-permute-start(f32[32,256]{1,0:T(8,128)S(1)} %get-tuple-element.32), channel_id=1, source_target_pairs={{0,1},{1,0},{2,3},{3,2},{4,5},{5,4},{6,7},{7,6},{8,9},{9,8},{10,11... | collective-permute-start | bytes 98312 | tf_op jit(solution)/shard_map/ppermute | solution.py:839
  54.6 6.7 %collective-permute-start.7 = (f32[32,256]{1,0:T(8,128)S(1)}, f32[32,256]{1,0:T(8,128)S(1)}, u32[]{:S(2)}, u32[]{:S(2)}) collective-permute-start(f32[32,256]{1,0:T(8,128)S(1)} %get-tuple-element.33), channel_id=1, source_target_pairs={{1,2},{2,1},{3,4},{4,3},{5,6},{6,5},{9,10},{10,9},{11,12},{12,11},... | collective-permute-start | bytes 98312 | tf_op jit(solution)/shard_map/ppermute | solution.py:839
